TPU v7x, 512 devices: a whole 4x4x16 slice. The times are simulated.
512 devices in a mesh: tm: 16 (over x, y), space: 32 (over z, core).
Axes of the slice: x: 4, y: 4, z: 16, core: 2. Of those that a mesh axis runs over, the one named last changes fastest.
Arguments:
- starts: float32 [16, 3, 64, 16, 512], P('tm', None, 'space'), may hold values from -1 to 1, as said below
- anisotropy: float32 [64, 16, 512], P('space'), may hold values from 0.1 to 1
- applied: float32 [3], replicated, may hold values from -1 to 1
Outputs:
- slice_ends: float32 [16, 3, 64, 16, 512], P('tm', None, 'space')
Inputs may be any that keep to these rules, and one draw needn't show every extreme that they name: `starts`: the three components of every site form a unit vector.
All inputs are finite; a program needn't handle non-finite values.
Results may differ from a plain program's by a relative error of at most 0.00002.
Values sent between devices are 32-bit elements; how exact they have to be, the bound alone decides.
No kernel may reach another device: no remote copies, remote signals or barrier semaphores. Data moves between devices by JAX's collectives and lax.ppermute only.
A program may use at most 64 MiB of HBM per device.

v0:
```python
import jax
import jax.numpy as jnp
from jax import lax
from jax.sharding import PartitionSpec as P

FINE_STEPS = 2


damping = 0.1
step_size = 0.02


def with_halo(array, sides, width):
    for axis, dim in sides:
        count, length = (lax.axis_size(axis), array.shape[dim])
        up = [(i, (i + 1) % count) for i in range(count)]
        down = [(j, i) for i, j in up]
        last = lax.slice_in_dim(array, length - width, length, axis=dim)
        initial = lax.slice_in_dim(array, 0, width, axis=dim)
        before = lax.ppermute(last, axis, up)
        after = lax.ppermute(initial, axis, down)
        array = jnp.concatenate([before, array, after], axis=dim)
    return array


def shifted(array, axis, by):
    count = lax.axis_size(axis)
    pairs = [(i, i + by) for i in range(count) if 0 <= i + by < count]
    return lax.ppermute(array, axis, pairs)


def layer_field(forward, behind):
    forward = forward + jnp.roll(forward, -1, axis=-1)
    behind = behind + jnp.roll(behind, 1, axis=-1)
    layers = forward.shape[-2]
    odd_layer = (lax.iota(jnp.int32, layers) % 2 == 1)[:, None]
    chosen = jnp.where(odd_layer, forward, behind)
    widths = [(0, 0)] * (chosen.ndim - 2) + [(1, 1), (0, 0)]
    padded = jnp.pad(chosen, widths)
    return padded[..., :-2, :] + padded[..., 2:, :]


def plane_sums(padded):
    forward = padded[..., 1:-1, :, :] + padded[..., 2:, :, :]
    behind = padded[..., :-2, :, :] + padded[..., 1:-1, :, :]
    return layer_field(forward, behind)


def spin_rate(near, spins, anisotropy, applied):
    spin_x = spins[..., 0, :, :, :]
    spin_y = spins[..., 1, :, :, :]
    spin_z = spins[..., 2, :, :, :]
    field_x = near[..., 0, :, :, :] + applied[0]
    field_y = near[..., 1, :, :, :] + applied[1]
    field_z = near[..., 2, :, :, :] + 2.0 * anisotropy * spin_z + applied[2]
    cross_x = spin_y * field_z - spin_z * field_y
    cross_y = spin_z * field_x - spin_x * field_z
    cross_z = spin_x * field_y - spin_y * field_x
    double_x = spin_y * cross_z - spin_z * cross_y
    double_y = spin_z * cross_x - spin_x * cross_z
    double_z = spin_x * cross_y - spin_y * cross_x
    factor = -1.0 / (1.0 + damping * damping)
    return jnp.stack(
        [
            factor * (cross_x + damping * double_x),
            factor * (cross_y + damping * double_y),
            factor * (cross_z + damping * double_z),
        ],
        axis=-4,
    )


def rim_planes(field):
    return with_halo(field, (("space", 1),), 1)


def per_device(starts, anisotropy, applied):
    current = starts[0]
    slice_index = lax.axis_index("tm")
    coarse_len = FINE_STEPS * step_size

    def heun_local(spins, step_len):
        rate_start = spin_rate(plane_sums(rim_planes(spins)), spins, anisotropy, applied)
        predicted = spins + step_len * rate_start
        rate_end = spin_rate(plane_sums(rim_planes(predicted)), predicted, anisotropy, applied)
        return spins + 0.5 * step_len * (rate_start + rate_end)

    fine_state = current
    for repeat in range(FINE_STEPS):
        fine_state = heun_local(fine_state, step_size)
    coarse_old = heun_local(current, coarse_len)
    correction = fine_state - coarse_old
    first_end = coarse_old + correction

    def relay_round(round_index, latest):
        received = shifted(latest, "tm", 1)
        chain_input = jnp.where(slice_index == 0, current, received)
        return heun_local(chain_input, coarse_len) + correction

    slice_end = lax.fori_loop(1, lax.axis_size("tm"), relay_round, first_end)
    return slice_end[None]


def solution(mesh):
    placed = (P("tm", None, "space", None, None), P("space", None, None), P())
    return jax.shard_map(
        per_device,
        mesh=mesh,
        in_specs=placed,
        out_specs=P("tm", None, "space", None, None),
        check_vma=False,
    )
```

profile of v0, /device:TPU:2, one launch (start us, length us, event | category | flops | bytes accessed | tf_op | source)
XLA Modules:
  0.0 462.8 jit_solution(9689442051244544331)
XLA Ops:
  1.0 8.9 %collective-permute-start.5 = (f32[3,1,16,512]{3,2,1,0:T(8,128)S(1)}, f32[3,1,16,512]{3,2,1,0:T(8,128)S(1)}, u32[]{:S(2)}, u32[]{:S(2)}) collective-permute-start(f32[3,1,16,512]{3,2,1,0:T(8,128)S(1)} %get-tuple-element.185), channel_id=1, source_target_pairs={{1,0},{2,1},{3,2},{4,3},{5,4},{6,5},{7,6},{8,7},{9,8},{10,9},{11,1... | collective-permute-start | bytes 294920 | tf_op jit(solution)/shard_map/ppermute | solution.py:21
  12.2 3.0 collective-permute-done.6
  29.2 3.0 collective-permute-start.7
  39.8 3.0 collective-permute-done.14
  45.5 416.6 %while.12 = (s32[]{:T(128)}, f32[3,2,16,512]{3,2,1,0:T(8,128)S(1)}, pred[]{:T(512)}, f32[3,2,16,512]{3,2,1,0:T(8,128)S(1)}, f32[2,16,512]{2,1,0:T(8,128)S(1)}, /...) while((s32[]{:T(128)}, f32[3,2,16,512]{3,2,1,0:T(8,128)S(1)}, pred[]{:T(512)}, ...), condition=%wide.region_1.2_spmd, body=%wide.region_0.1_spmd.sunk | while | flops 3063922 | bytes 12650382 | solution.py:100
  45.5 3.5 collective-permute-start
  49.7 5.6 %collective-permute-done = f32[3,2,16,512]{3,2,1,0:T(8,128)S(1)} collective-permute-done((f32[3,2,16,512]{3,2,1,0:T(8,128)S(1)}, f32[3,2,16,512]{3,2,1,0:T(8,128)S(1)}, u32[]{:S(2)}, u32[]{:S(2)}) %collective-permute-start) | collective-permute-done | bytes 196640 | tf_op jit(solution)/shard_map/while/body/eval_jaxpr/ppermute | solution.py:29
  75.9 7.1 %collective-permute-done = f32[3,2,16,512]{3,2,1,0:T(8,128)S(1)} collective-permute-done((f32[3,2,16,512]{3,2,1,0:T(8,128)S(1)}, f32[3,2,16,512]{3,2,1,0:T(8,128)S(1)}, u32[]{:S(2)}, u32[]{:S(2)}) %collective-permute-start) | collective-permute-done | bytes 196640 | tf_op jit(solution)/shard_map/while/body/eval_jaxpr/ppermute | solution.py:29
  103.6 7.1 %collective-permute-done = f32[3,2,16,512]{3,2,1,0:T(8,128)S(1)} collective-permute-done((f32[3,2,16,512]{3,2,1,0:T(8,128)S(1)}, f32[3,2,16,512]{3,2,1,0:T(8,128)S(1)}, u32[]{:S(2)}, u32[]{:S(2)}) %collective-permute-start) | collective-permute-done | bytes 196640 | tf_op jit(solution)/shard_map/while/body/eval_jaxpr/ppermute | solution.py:29
  119.9 3.0 collective-permute-start.4
  131.4 7.1 %collective-permute-done = f32[3,2,16,512]{3,2,1,0:T(8,128)S(1)} collective-permute-done((f32[3,2,16,512]{3,2,1,0:T(8,128)S(1)}, f32[3,2,16,512]{3,2,1,0:T(8,128)S(1)}, u32[]{:S(2)}, u32[]{:S(2)}) %collective-permute-start) | collective-permute-done | bytes 196640 | tf_op jit(solution)/shard_map/while/body/eval_jaxpr/ppermute | solution.py:29
  159.2 7.1 %collective-permute-done = f32[3,2,16,512]{3,2,1,0:T(8,128)S(1)} collective-permute-done((f32[3,2,16,512]{3,2,1,0:T(8,128)S(1)}, f32[3,2,16,512]{3,2,1,0:T(8,128)S(1)}, u32[]{:S(2)}, u32[]{:S(2)}) %collective-permute-start) | collective-permute-done | bytes 196640 | tf_op jit(solution)/shard_map/while/body/eval_jaxpr/ppermute | solution.py:29
  175.4 3.0 collective-permute-start.4
  187.0 7.1 %collective-permute-done = f32[3,2,16,512]{3,2,1,0:T(8,128)S(1)} collective-permute-done((f32[3,2,16,512]{3,2,1,0:T(8,128)S(1)}, f32[3,2,16,512]{3,2,1,0:T(8,128)S(1)}, u32[]{:S(2)}, u32[]{:S(2)}) %collective-permute-start) | collective-permute-done | bytes 196640 | tf_op jit(solution)/shard_map/while/body/eval_jaxpr/ppermute | solution.py:29
  214.7 7.1 %collective-permute-done = f32[3,2,16,512]{3,2,1,0:T(8,128)S(1)} collective-permute-done((f32[3,2,16,512]{3,2,1,0:T(8,128)S(1)}, f32[3,2,16,512]{3,2,1,0:T(8,128)S(1)}, u32[]{:S(2)}, u32[]{:S(2)}) %collective-permute-start) | collective-permute-done | bytes 196640 | tf_op jit(solution)/shard_map/while/body/eval_jaxpr/ppermute | solution.py:29
  231.0 3.0 collective-permute-start.4
  242.5 7.1 %collective-permute-done = f32[3,2,16,512]{3,2,1,0:T(8,128)S(1)} collective-permute-done((f32[3,2,16,512]{3,2,1,0:T(8,128)S(1)}, f32[3,2,16,512]{3,2,1,0:T(8,128)S(1)}, u32[]{:S(2)}, u32[]{:S(2)}) %collective-permute-start) | collective-permute-done | bytes 196640 | tf_op jit(solution)/shard_map/while/body/eval_jaxpr/ppermute | solution.py:29
  270.3 7.1 %collective-permute-done = f32[3,2,16,512]{3,2,1,0:T(8,128)S(1)} collective-permute-done((f32[3,2,16,512]{3,2,1,0:T(8,128)S(1)}, f32[3,2,16,512]{3,2,1,0:T(8,128)S(1)}, u32[]{:S(2)}, u32[]{:S(2)}) %collective-permute-start) | collective-permute-done | bytes 196640 | tf_op jit(solution)/shard_map/while/body/eval_jaxpr/ppermute | solution.py:29
  298.1 7.1 %collective-permute-done = f32[3,2,16,512]{3,2,1,0:T(8,128)S(1)} collective-permute-done((f32[3,2,16,512]{3,2,1,0:T(8,128)S(1)}, f32[3,2,16,512]{3,2,1,0:T(8,128)S(1)}, u32[]{:S(2)}, u32[]{:S(2)}) %collective-permute-start) | collective-permute-done | bytes 196640 | tf_op jit(solution)/shard_map/while/body/eval_jaxpr/ppermute | solution.py:29
  325.8 7.1 %collective-permute-done = f32[3,2,16,512]{3,2,1,0:T(8,128)S(1)} collective-permute-done((f32[3,2,16,512]{3,2,1,0:T(8,128)S(1)}, f32[3,2,16,512]{3,2,1,0:T(8,128)S(1)}, u32[]{:S(2)}, u32[]{:S(2)}) %collective-permute-start) | collective-permute-done | bytes 196640 | tf_op jit(solution)/shard_map/while/body/eval_jaxpr/ppermute | solution.py:29
  353.6 7.1 %collective-permute-done = f32[3,2,16,512]{3,2,1,0:T(8,128)S(1)} collective-permute-done((f32[3,2,16,512]{3,2,1,0:T(8,128)S(1)}, f32[3,2,16,512]{3,2,1,0:T(8,128)S(1)}, u32[]{:S(2)}, u32[]{:S(2)}) %collective-permute-start) | collective-permute-done | bytes 196640 | tf_op jit(solution)/shard_map/while/body/eval_jaxpr/ppermute | solution.py:29
  381.4 7.1 %collective-permute-done = f32[3,2,16,512]{3,2,1,0:T(8,128)S(1)} collective-permute-done((f32[3,2,16,512]{3,2,1,0:T(8,128)S(1)}, f32[3,2,16,512]{3,2,1,0:T(8,128)S(1)}, u32[]{:S(2)}, u32[]{:S(2)}) %collective-permute-start) | collective-permute-done | bytes 196640 | tf_op jit(solution)/shard_map/while/body/eval_jaxpr/ppermute | solution.py:29
  409.2 7.1 %collective-permute-done = f32[3,2,16,512]{3,2,1,0:T(8,128)S(1)} collective-permute-done((f32[3,2,16,512]{3,2,1,0:T(8,128)S(1)}, f32[3,2,16,512]{3,2,1,0:T(8,128)S(1)}, u32[]{:S(2)}, u32[]{:S(2)}) %collective-permute-start) | collective-permute-done | bytes 196640 | tf_op jit(solution)/shard_map/while/body/eval_jaxpr/ppermute | solution.py:29
  436.9 7.1 %collective-permute-done = f32[3,2,16,512]{3,2,1,0:T(8,128)S(1)} collective-permute-done((f32[3,2,16,512]{3,2,1,0:T(8,128)S(1)}, f32[3,2,16,512]{3,2,1,0:T(8,128)S(1)}, u32[]{:S(2)}, u32[]{:S(2)}) %collective-permute-start) | collective-permute-done | bytes 196640 | tf_op jit(solution)/shard_map/while/body/eval_jaxpr/ppermute | solution.py:29
  (548 shorter events, 324.2 us)
Async XLA Ops:
  1.0 11.2 %collective-permute-start.5 = (f32[3,1,16,512]{3,2,1,0:T(8,128)S(1)}, f32[3,1,16,512]{3,2,1,0:T(8,128)S(1)}, u32[]{:S(2)}, u32[]{:S(2)}) collective-permute-start(f32[3,1,16,512]{3,2,1,0:T(8,128)S(1)} %get-tuple-element.185), channel_id=1, source_target_pairs={{1,0},{2,1},{3,2},{4,3},{5,4},{6,5},{7,6},{8,7},{9,8},{10,9},{11,1... | collective-permute-start | bytes 294920 | tf_op jit(solution)/shard_map/ppermute | solution.py:21
  26.2 6.0 %collective-permute-start.11 = (f32[3,1,16,512]{3,2,1,0:T(8,128)S(1)}, f32[3,1,16,512]{3,2,1,0:T(8,128)S(1)}, u32[]{:S(2)}, u32[]{:S(2)}) collective-permute-start(f32[3,1,16,512]{3,2,1,0:T(8,128)S(1)} %get-tuple-element.173), channel_id=1, source_target_pairs={{1,0},{2,1},{3,2},{4,3},{5,4},{6,5},{7,6},{8,7},{9,8},{10,9},{11,1... | collective-permute-start | bytes 294920 | tf_op jit(solution)/shard_map/ppermute | solution.py:21
  29.2 8.4 %collective-permute-start.7 = (f32[3,1,16,512]{3,2,1,0:T(8,128)S(1)}, f32[3,1,16,512]{3,2,1,0:T(8,128)S(1)}, u32[]{:S(2)}, u32[]{:S(2)}) collective-permute-start(f32[3,1,16,512]{3,2,1,0:T(8,128)S(1)} %get-tuple-element.181), channel_id=1, source_target_pairs={{1,0},{2,1},{3,2},{4,3},{5,4},{6,5},{7,6},{8,7},{9,8},{10,9},{11,1... | collective-permute-start | bytes 294920 | tf_op jit(solution)/shard_map/ppermute | solution.py:21
  32.1 5.4 %collective-permute-start.8 = (f32[3,1,16,512]{3,2,1,0:T(8,128)S(1)}, f32[3,1,16,512]{3,2,1,0:T(8,128)S(1)}, u32[]{:S(2)}, u32[]{:S(2)}) collective-permute-start(f32[3,1,16,512]{3,2,1,0:T(8,128)S(1)} %get-tuple-element.180), channel_id=1, source_target_pairs={{0,1},{1,2},{2,3},{3,4},{4,5},{5,6},{6,7},{7,8},{8,9},{9,10},{10,1... | collective-permute-start | bytes 294920 | tf_op jit(solution)/shard_map/ppermute | solution.py:20
  45.5 9.7 %collective-permute-start = (f32[3,2,16,512]{3,2,1,0:T(8,128)S(1)}, f32[3,2,16,512]{3,2,1,0:T(8,128)S(1)}, u32[]{:S(2)}, u32[]{:S(2)}) collective-permute-start(f32[3,2,16,512]{3,2,1,0:T(8,128)S(1)} %get-tuple-element.287), channel_id=1, source_target_pairs={{0,32},{32,64},{64,96},{96,128},{128,160},{160,192},{192,224},{224... | collective-permute-start | bytes 589832 | tf_op jit(solution)/shard_map/while/body/eval_jaxpr/ppermute | solution.py:29
  73.3 9.7 %collective-permute-start = (f32[3,2,16,512]{3,2,1,0:T(8,128)S(1)}, f32[3,2,16,512]{3,2,1,0:T(8,128)S(1)}, u32[]{:S(2)}, u32[]{:S(2)}) collective-permute-start(f32[3,2,16,512]{3,2,1,0:T(8,128)S(1)} %get-tuple-element.287), channel_id=1, source_target_pairs={{0,32},{32,64},{64,96},{96,128},{128,160},{160,192},{192,224},{224... | collective-permute-start | bytes 589832 | tf_op jit(solution)/shard_map/while/body/eval_jaxpr/ppermute | solution.py:29
  101.1 9.7 %collective-permute-start = (f32[3,2,16,512]{3,2,1,0:T(8,128)S(1)}, f32[3,2,16,512]{3,2,1,0:T(8,128)S(1)}, u32[]{:S(2)}, u32[]{:S(2)}) collective-permute-start(f32[3,2,16,512]{3,2,1,0:T(8,128)S(1)} %get-tuple-element.287), channel_id=1, source_target_pairs={{0,32},{32,64},{64,96},{96,128},{128,160},{160,192},{192,224},{224... | collective-permute-start | bytes 589832 | tf_op jit(solution)/shard_map/while/body/eval_jaxpr/ppermute | solution.py:29
  128.9 9.7 %collective-permute-start = (f32[3,2,16,512]{3,2,1,0:T(8,128)S(1)}, f32[3,2,16,512]{3,2,1,0:T(8,128)S(1)}, u32[]{:S(2)}, u32[]{:S(2)}) collective-permute-start(f32[3,2,16,512]{3,2,1,0:T(8,128)S(1)} %get-tuple-element.287), channel_id=1, source_target_pairs={{0,32},{32,64},{64,96},{96,128},{128,160},{160,192},{192,224},{224... | collective-permute-start | bytes 589832 | tf_op jit(solution)/shard_map/while/body/eval_jaxpr/ppermute | solution.py:29
  147.6 5.3 %collective-permute-start.3 = (f32[3,1,16,512]{3,2,1,0:T(8,128)S(1)}, f32[3,1,16,512]{3,2,1,0:T(8,128)S(1)}, u32[]{:S(2)}, u32[]{:S(2)}) collective-permute-start(f32[3,1,16,512]{3,2,1,0:T(8,128)S(1)} %get-tuple-element.270), channel_id=1, source_target_pairs={{0,1},{1,2},{2,3},{3,4},{4,5},{5,6},{6,7},{7,8},{8,9},{9,10},{10,1... | collective-permute-start | bytes 294920 | tf_op jit(solution)/shard_map/while/body/eval_jaxpr/ppermute | solution.py:20
  156.6 9.7 %collective-permute-start = (f32[3,2,16,512]{3,2,1,0:T(8,128)S(1)}, f32[3,2,16,512]{3,2,1,0:T(8,128)S(1)}, u32[]{:S(2)}, u32[]{:S(2)}) collective-permute-start(f32[3,2,16,512]{3,2,1,0:T(8,128)S(1)} %get-tuple-element.287), channel_id=1, source_target_pairs={{0,32},{32,64},{64,96},{96,128},{128,160},{160,192},{192,224},{224... | collective-permute-start | bytes 589832 | tf_op jit(solution)/shard_map/while/body/eval_jaxpr/ppermute | solution.py:29
  184.4 9.7 %collective-permute-start = (f32[3,2,16,512]{3,2,1,0:T(8,128)S(1)}, f32[3,2,16,512]{3,2,1,0:T(8,128)S(1)}, u32[]{:S(2)}, u32[]{:S(2)}) collective-permute-start(f32[3,2,16,512]{3,2,1,0:T(8,128)S(1)} %get-tuple-element.287), channel_id=1, source_target_pairs={{0,32},{32,64},{64,96},{96,128},{128,160},{160,192},{192,224},{224... | collective-permute-start | bytes 589832 | tf_op jit(solution)/shard_map/while/body/eval_jaxpr/ppermute | solution.py:29
  203.2 5.3 %collective-permute-start.3 = (f32[3,1,16,512]{3,2,1,0:T(8,128)S(1)}, f32[3,1,16,512]{3,2,1,0:T(8,128)S(1)}, u32[]{:S(2)}, u32[]{:S(2)}) collective-permute-start(f32[3,1,16,512]{3,2,1,0:T(8,128)S(1)} %get-tuple-element.270), channel_id=1, source_target_pairs={{0,1},{1,2},{2,3},{3,4},{4,5},{5,6},{6,7},{7,8},{8,9},{9,10},{10,1... | collective-permute-start | bytes 294920 | tf_op jit(solution)/shard_map/while/body/eval_jaxpr/ppermute | solution.py:20
  212.2 9.7 %collective-permute-start = (f32[3,2,16,512]{3,2,1,0:T(8,128)S(1)}, f32[3,2,16,512]{3,2,1,0:T(8,128)S(1)}, u32[]{:S(2)}, u32[]{:S(2)}) collective-permute-start(f32[3,2,16,512]{3,2,1,0:T(8,128)S(1)} %get-tuple-element.287), channel_id=1, source_target_pairs={{0,32},{32,64},{64,96},{96,128},{128,160},{160,192},{192,224},{224... | collective-permute-start | bytes 589832 | tf_op jit(solution)/shard_map/while/body/eval_jaxpr/ppermute | solution.py:29
  240.0 9.7 %collective-permute-start = (f32[3,2,16,512]{3,2,1,0:T(8,128)S(1)}, f32[3,2,16,512]{3,2,1,0:T(8,128)S(1)}, u32[]{:S(2)}, u32[]{:S(2)}) collective-permute-start(f32[3,2,16,512]{3,2,1,0:T(8,128)S(1)} %get-tuple-element.287), channel_id=1, source_target_pairs={{0,32},{32,64},{64,96},{96,128},{128,160},{160,192},{192,224},{224... | collective-permute-start | bytes 589832 | tf_op jit(solution)/shard_map/while/body/eval_jaxpr/ppermute | solution.py:29
  258.7 5.3 %collective-permute-start.3 = (f32[3,1,16,512]{3,2,1,0:T(8,128)S(1)}, f32[3,1,16,512]{3,2,1,0:T(8,128)S(1)}, u32[]{:S(2)}, u32[]{:S(2)}) collective-permute-start(f32[3,1,16,512]{3,2,1,0:T(8,128)S(1)} %get-tuple-element.270), channel_id=1, source_target_pairs={{0,1},{1,2},{2,3},{3,4},{4,5},{5,6},{6,7},{7,8},{8,9},{9,10},{10,1... | collective-permute-start | bytes 294920 | tf_op jit(solution)/shard_map/while/body/eval_jaxpr/ppermute | solution.py:20
  267.7 9.7 %collective-permute-start = (f32[3,2,16,512]{3,2,1,0:T(8,128)S(1)}, f32[3,2,16,512]{3,2,1,0:T(8,128)S(1)}, u32[]{:S(2)}, u32[]{:S(2)}) collective-permute-start(f32[3,2,16,512]{3,2,1,0:T(8,128)S(1)} %get-tuple-element.287), channel_id=1, source_target_pairs={{0,32},{32,64},{64,96},{96,128},{128,160},{160,192},{192,224},{224... | collective-permute-start | bytes 589832 | tf_op jit(solution)/shard_map/while/body/eval_jaxpr/ppermute | solution.py:29
  295.5 9.7 %collective-permute-start = (f32[3,2,16,512]{3,2,1,0:T(8,128)S(1)}, f32[3,2,16,512]{3,2,1,0:T(8,128)S(1)}, u32[]{:S(2)}, u32[]{:S(2)}) collective-permute-start(f32[3,2,16,512]{3,2,1,0:T(8,128)S(1)} %get-tuple-element.287), channel_id=1, source_target_pairs={{0,32},{32,64},{64,96},{96,128},{128,160},{160,192},{192,224},{224... | collective-permute-start | bytes 589832 | tf_op jit(solution)/shard_map/while/body/eval_jaxpr/ppermute | solution.py:29
  314.3 5.3 %collective-permute-start.3 = (f32[3,1,16,512]{3,2,1,0:T(8,128)S(1)}, f32[3,1,16,512]{3,2,1,0:T(8,128)S(1)}, u32[]{:S(2)}, u32[]{:S(2)}) collective-permute-start(f32[3,1,16,512]{3,2,1,0:T(8,128)S(1)} %get-tuple-element.270), channel_id=1, source_target_pairs={{0,1},{1,2},{2,3},{3,4},{4,5},{5,6},{6,7},{7,8},{8,9},{9,10},{10,1... | collective-permute-start | bytes 294920 | tf_op jit(solution)/shard_map/while/body/eval_jaxpr/ppermute | solution.py:20
  323.3 9.7 %collective-permute-start = (f32[3,2,16,512]{3,2,1,0:T(8,128)S(1)}, f32[3,2,16,512]{3,2,1,0:T(8,128)S(1)}, u32[]{:S(2)}, u32[]{:S(2)}) collective-permute-start(f32[3,2,16,512]{3,2,1,0:T(8,128)S(1)} %get-tuple-element.287), channel_id=1, source_target_pairs={{0,32},{32,64},{64,96},{96,128},{128,160},{160,192},{192,224},{224... | collective-permute-start | bytes 589832 | tf_op jit(solution)/shard_map/while/body/eval_jaxpr/ppermute | solution.py:29
  351.1 9.7 %collective-permute-start = (f32[3,2,16,512]{3,2,1,0:T(8,128)S(1)}, f32[3,2,16,512]{3,2,1,0:T(8,128)S(1)}, u32[]{:S(2)}, u32[]{:S(2)}) collective-permute-start(f32[3,2,16,512]{3,2,1,0:T(8,128)S(1)} %get-tuple-element.287), channel_id=1, source_target_pairs={{0,32},{32,64},{64,96},{96,128},{128,160},{160,192},{192,224},{224... | collective-permute-start | bytes 589832 | tf_op jit(solution)/shard_map/while/body/eval_jaxpr/ppermute | solution.py:29
  369.8 5.3 %collective-permute-start.3 = (f32[3,1,16,512]{3,2,1,0:T(8,128)S(1)}, f32[3,1,16,512]{3,2,1,0:T(8,128)S(1)}, u32[]{:S(2)}, u32[]{:S(2)}) collective-permute-start(f32[3,1,16,512]{3,2,1,0:T(8,128)S(1)} %get-tuple-element.270), channel_id=1, source_target_pairs={{0,1},{1,2},{2,3},{3,4},{4,5},{5,6},{6,7},{7,8},{8,9},{9,10},{10,1... | collective-permute-start | bytes 294920 | tf_op jit(solution)/shard_map/while/body/eval_jaxpr/ppermute | solution.py:20
  378.8 9.7 %collective-permute-start = (f32[3,2,16,512]{3,2,1,0:T(8,128)S(1)}, f32[3,2,16,512]{3,2,1,0:T(8,128)S(1)}, u32[]{:S(2)}, u32[]{:S(2)}) collective-permute-start(f32[3,2,16,512]{3,2,1,0:T(8,128)S(1)} %get-tuple-element.287), channel_id=1, source_target_pairs={{0,32},{32,64},{64,96},{96,128},{128,160},{160,192},{192,224},{224... | collective-permute-start | bytes 589832 | tf_op jit(solution)/shard_map/while/body/eval_jaxpr/ppermute | solution.py:29
  406.6 9.7 %collective-permute-start = (f32[3,2,16,512]{3,2,1,0:T(8,128)S(1)}, f32[3,2,16,512]{3,2,1,0:T(8,128)S(1)}, u32[]{:S(2)}, u32[]{:S(2)}) collective-permute-start(f32[3,2,16,512]{3,2,1,0:T(8,128)S(1)} %get-tuple-element.287), channel_id=1, source_target_pairs={{0,32},{32,64},{64,96},{96,128},{128,160},{160,192},{192,224},{224... | collective-permute-start | bytes 589832 | tf_op jit(solution)/shard_map/while/body/eval_jaxpr/ppermute | solution.py:29
  434.4 9.7 %collective-permute-start = (f32[3,2,16,512]{3,2,1,0:T(8,128)S(1)}, f32[3,2,16,512]{3,2,1,0:T(8,128)S(1)}, u32[]{:S(2)}, u32[]{:S(2)}) collective-permute-start(f32[3,2,16,512]{3,2,1,0:T(8,128)S(1)} %get-tuple-element.287), channel_id=1, source_target_pairs={{0,32},{32,64},{64,96},{96,128},{128,160},{160,192},{192,224},{224... | collective-permute-start | bytes 589832 | tf_op jit(solution)/shard_map/while/body/eval_jaxpr/ppermute | solution.py:29
  (65 other events, 343.8 us)
where the time goes:
time: 465 us; the launch traced here: 463 us
  waiting for transfers between devices  188 us (40%)
  starting transfers between devices  138 us (30%)
  other arithmetic  114 us (25%)
  local copies, waits for them, and re-layouts  19.7 us (4%)
    ppermute x35, starting transfers between devices, with_halo(): after = lax.ppermute(initial, axis, down)  107 us
    ppermute x15, waiting for transfers between devices, shifted(): return lax.ppermute(array, axis, pairs)  105 us
    ppermute x35, waiting for transfers between devices, with_halo(): before = lax.ppermute(last, axis, up)  79.1 us
    mul x30, other arithmetic, spin_rate(): factor * (cross_x + damping * double_x)  56.7 us
    mul x30, other arithmetic, spin_rate(): factor * (cross_y + damping * double_y)  40.1 us
    ppermute x15, starting transfers between devices, shifted(): return lax.ppermute(array, axis, pairs)  30.4 us
  transfers between devices with their start and end apart: 85, of which 51 were waited for; matrix products, arithmetic and copies ran while one was open for 3% of the time, Pallas kernels for 0%

commit v1 on v0

v1 whole, which is shorter than its diff:
```python
import functools

import jax
import jax.numpy as jnp
from jax import lax
from jax.experimental import pallas as pl
from jax.experimental.pallas import tpu as pltpu
from jax.sharding import PartitionSpec as P

DAMPING = 0.1
STEP = 0.02
COARSE = 2 * STEP
GAIN = -1.0 / (1.0 + DAMPING * DAMPING)
F32 = jnp.float32
VMEM = pl.BlockSpec(memory_space=pltpu.VMEM)
SMEM = pl.BlockSpec(memory_space=pltpu.SMEM)


def near_odd(even_below, even_here):
    out = []
    for below, here in zip(even_below, even_here):
        pair = below + here
        pair = pair + pltpu.roll(pair, 1, axis=1)
        row = lax.broadcasted_iota(jnp.int32, pair.shape, 0)
        out.append(pair + jnp.where(row < 7, pltpu.roll(pair, 7, axis=0), 0.0))
    return out


def near_even(odd_here, odd_above):
    out = []
    for here, above in zip(odd_here, odd_above):
        pair = here + above
        pair = pair + pltpu.roll(pair, pair.shape[1] - 1, axis=1)
        row = lax.broadcasted_iota(jnp.int32, pair.shape, 0)
        out.append(pair + jnp.where(row > 0, pltpu.roll(pair, 1, axis=0), 0.0))
    return out


def cross(a, b):
    return [a[1] * b[2] - a[2] * b[1], a[2] * b[0] - a[0] * b[2], a[0] * b[1] - a[1] * b[0]]


def bare_rate(spin, near, twice_aniso, applied):
    field = [n + h for n, h in zip(near, applied)]
    field[2] = field[2] + twice_aniso * spin[2]
    turn = cross(spin, field)
    return cross(spin, [f + DAMPING * c for f, c in zip(field, turn)])


def rates(even, odd, aniso_even, aniso_odd, applied, evens, odds):
    rate_even = {x: bare_rate(even[x], near_even(odd[x], odd[x + 1]), aniso_even(x), applied) for x in evens}
    rate_odd = {x: bare_rate(odd[x], near_odd(even[x - 1], even[x]), aniso_odd(x), applied) for x in odds}
    return rate_even, rate_odd


def ahead(spins, rate, length):
    return {x: [s + (length * GAIN) * r for s, r in zip(spins[x], rate[x])] for x in rate}


def finish(spins, first, second, length, planes):
    return {
        x: [s + (0.5 * length * GAIN) * (f + g) for s, f, g in zip(spins[x], first[x], second[x])]
        for x in planes
    }


def heun(even, odd, aniso_even, aniso_odd, applied, length, low, high):
    evens, odds, inner = range(low, high), range(low + 1, high + 1), range(low + 1, high)
    first_e, first_o = rates(even, odd, aniso_even, aniso_odd, applied, evens, odds)
    pred_e, pred_o = ahead(even, first_e, length), ahead(odd, first_o, length)
    second_e, second_o = rates(pred_e, pred_o, aniso_even, aniso_odd, applied, inner, inner)
    return finish(even, first_e, second_e, length, inner), finish(odd, first_o, second_o, length, inner)


def lane_select(tile, low, high, a, b):
    lane = lax.broadcasted_iota(jnp.int32, (8, 128), 1) % tile
    return jnp.where((lane >= low) & (lane < high), a, b)


def tiles_of(wide):
    return [wide[:, 128 * q : 128 * (q + 1)] for q in range(wide.shape[1] // 128)]


def turn(x, by):
    by = by % x.shape[1]
    return pltpu.roll(x, by, axis=1) if by else x


def prologue(own, left, right, applied_ref, row_ref, payload, windows, layers):
    applied = [applied_ref[c] for c in range(3)]
    tiles = own.shape[3] // 128
    for base, ref in enumerate((left, own, right)):
        for q in range(tiles):
            layers[:, 2 * base : 2 * base + 2, q] = ref[:, :, :, 128 * q : 128 * (q + 1)]

    def load(comp, plane, parity):
        parts = [layers[comp, plane + 2, q, pl.ds(parity, 8, stride=2), :] for q in range(tiles)]
        return jnp.concatenate(parts, axis=1)

    planes = range(-2, 4)
    even = {x: [load(c, x, 0) for c in range(3)] for x in planes}
    odd = {x: [load(c, x, 1) for c in range(3)] for x in planes}

    def aniso_even(x):
        return 2.0 * load(3, x, 0)

    def aniso_odd(x):
        return 2.0 * load(3, x, 1)

    sides = (aniso_even, aniso_odd, applied)
    first_e, first_o = rates(even, odd, *sides, range(-2, 3), range(-1, 4))
    pred_e, pred_o = ahead(even, first_e, STEP), ahead(odd, first_o, STEP)
    second_e, second_o = rates(pred_e, pred_o, *sides, range(-1, 3), range(-1, 3))
    fine_e = finish(even, first_e, second_e, STEP, range(-1, 3))
    fine_o = finish(odd, first_o, second_o, STEP, range(-1, 3))
    fine_e, fine_o = heun(fine_e, fine_o, *sides, STEP, -1, 2)
    pred_e, pred_o = ahead(even, first_e, COARSE), ahead(odd, first_o, COARSE)
    second_e, second_o = rates(pred_e, pred_o, *sides, range(2), range(2))
    coarse_e = finish(even, first_e, second_e, COARSE, range(2))
    coarse_o = finish(odd, first_o, second_o, COARSE, range(2))

    row = row_ref[0]
    keep = jnp.where(row == 0, 0.0, 1.0).astype(F32)
    for comp in range(3):
        for parity, fine, coarse in ((0, fine_e, coarse_e), (1, fine_o, coarse_o)):
            moved = []
            for x in range(2):
                wide = fine[x][comp] - keep * coarse[x][comp]
                moved.append(tiles_of(pltpu.roll(wide, 16, axis=1)))
            count = len(moved[0])
            for q in range(count):
                a, b = moved[0][q], moved[1][q]
                after = (q + 1) % count
                c, d = (lane_select(128, 96, 128, m[q], m[after]) for m in moved)
                for i, (p, r) in enumerate(((a, b), (a, b), (a, b), (c, d))):
                    payload[4 * q + i, comp, parity] = lane_select(
                        128, 0, 64, turn(p, -32 * i), turn(r, 64 - 32 * i)
                    )

    for at in range(payload.shape[0]):

        @pl.when(row == at)
        def _():
            for parity, planes_used in ((0, range(-2, 3)), (1, range(-1, 4))):
                for k, x in enumerate(planes_used):
                    wide = 2.0 * load(3, x, parity)
                    windows[parity, k] = turn(wide, 16 - 32 * at)[:, :128]


def dense(even_pair, odd_pair):
    return lane_select(64, 0, 32, turn(even_pair, -16), turn(odd_pair, 16))


def chain(block, last, own, left, right, corr, windows, applied_ref, *rest):
    applied = [applied_ref[c] for c in range(3)]
    first_slice = 2 * block + 1

    def pair(ref, field, comp, parity):
        packed = ref[field, comp, parity]
        return packed, turn(packed, 64)

    def spread(field, parity, planes):
        out = {}
        for ref, base in ((left, -2), (own, 0), (right, 2)):
            pairs = [pair(ref, field, c, parity) for c in range(3)]
            for k in range(2):
                if base + k in planes:
                    out[base + k] = [p[k] for p in pairs]
        return out

    def aniso_even(x):
        return windows[0, x + 2]

    def aniso_odd(x):
        return windows[1, x + 1]

    sides = (aniso_even, aniso_odd, applied)
    reach = range(-1, 3) if last else range(-2, 4)
    inner = range(reach[0] + 1, reach[-1])
    even, odd = spread(0, 0, reach), spread(0, 1, reach)
    corr_e, corr_o = spread(1, 0, inner), spread(1, 1, inner)

    def add(spins, extra):
        return {x: [s + e for s, e in zip(spins[x], extra[x])] for x in extra}

    even, odd = heun(even, odd, *sides, COARSE, reach[0], reach[-1])
    even, odd = add(even, corr_e), add(odd, corr_o)

    def packed(spins):
        return [lane_select(128, 0, 64, spins[0][c], turn(spins[1][c], 64)) for c in range(3)]

    def emit(ref, at, packed_e, packed_o):
        for c in range(3):
            ref[at, c] = dense(packed_e[c], packed_o[c])

    if last:
        *earlier, sent = rest
        at = 0
        for ref in earlier:
            for k in range(ref.shape[0]):
                sent[at] = ref[k]
                at += 1
        emit(sent, at, packed(even), packed(odd))
        return

    message, ends = rest
    at = 0
    if block == 0:
        emit(ends, 0, [own[0, c, 0] for c in range(3)], [own[0, c, 1] for c in range(3)])
        at = 1
    emit(ends, at, packed(even), packed(odd))
    even, odd = heun(even, odd, *sides, COARSE, -1, 2)
    end_e = [s + corr[first_slice + 1, c, 0] for c, s in enumerate(packed(even))]
    end_o = [s + corr[first_slice + 1, c, 1] for c, s in enumerate(packed(odd))]
    emit(ends, at + 1, end_e, end_o)
    for c in range(3):
        message[0, c, 0] = end_e[c]
        message[0, c, 1] = end_o[c]
    message[1] = corr[first_slice + 2]


def assemble(sent, out, layers):
    for comp in range(3):
        for q in range(4):
            tiles = [sent[4 * q + i, comp] for i in range(4)]
            for k in range(4):
                whole = None
                for i in range(4):
                    part = turn(tiles[i], 32 * (i - k))
                    whole = part if whole is None else lane_select(128, 32 * i, 32 * i + 32, part, whole)
                layers[comp, k // 2, q, pl.ds(k % 2, 8, stride=2), :] = whole
            out[0, comp, :, :, 128 * q : 128 * (q + 1)] = layers[comp, :, q]


def both_sides(array):
    count = lax.axis_size("space")
    up = [(i, (i + 1) % count) for i in range(count)]
    down = [(j, i) for i, j in up]
    return lax.ppermute(array, "space", up), lax.ppermute(array, "space", down)


def call(kernel, shapes, in_specs, *args, scratch=()):
    return pl.pallas_call(
        kernel,
        out_shape=[jax.ShapeDtypeStruct(s, F32) for s in shapes],
        in_specs=in_specs,
        out_specs=[VMEM] * len(shapes),
        scratch_shapes=[pltpu.VMEM(s, F32) for s in scratch],
        compiler_params=pltpu.CompilerParams(vmem_limit_bytes=32 * 1024 * 1024),
    )(*args)


def per_device(starts, anisotropy, applied):
    slices = lax.axis_size("tm")
    row = lax.axis_index("tm").astype(jnp.int32)[None]
    own = jnp.concatenate([starts[0], anisotropy[None]], axis=0)
    left, right = both_sides(own)
    payload, windows = call(
        prologue,
        [(slices, 3, 2, 8, 128), (2, 5, 8, 128)],
        [VMEM] * 3 + [SMEM] * 2,
        *(own, left, right, applied, row),
        scratch=[(4, 6, starts.shape[-1] // 128, 16, 128)],
    )
    corr = lax.all_to_all(payload, "tm", 0, 0, tiled=True)
    message = corr[:2]
    done = []
    blocks = slices // 2
    for block in range(blocks):
        left, right = both_sides(message)
        last = block == blocks - 1
        kernel = functools.partial(chain, block, last)
        args = (message, left, right, corr, windows, applied)
        specs = [VMEM] * 5 + [SMEM]
        if last:
            (sent,) = call(kernel, [(slices, 3, 8, 128)], specs + [VMEM] * len(done), *args, *done)
        else:
            message, ends = call(kernel, [message.shape, (3 if block == 0 else 2, 3, 8, 128)], specs, *args)
            done.append(ends)
    sent = lax.all_to_all(sent, "tm", 0, 0, tiled=True)
    (out,) = call(assemble, [starts.shape], [VMEM], sent, scratch=[(3, 2, starts.shape[-1] // 128, 16, 128)])
    return out


def solution(mesh):
    placed = (P("tm", None, "space", None, None), P("space", None, None), P())
    return jax.shard_map(
        per_device,
        mesh=mesh,
        in_specs=placed,
        out_specs=P("tm", None, "space", None, None),
        check_vma=False,
    )
```

time: 465 us -> 94.6 us (0.20)
  waiting for transfers between devices: 188 us -> 40.9 us
  starting transfers between devices: 138 us -> 13.1 us
  other arithmetic: 114 us -> 0.98 us
  blocking collectives: 0 us -> 26.8 us
  local copies, waits for them, and re-layouts: 19.7 us -> 0.01 us
  Pallas kernels: 0 us -> 12.5 us
    ppermute x85 -> x18, waiting for transfers between devices: 188 us -> 40.9 us  [the longest x9 27.1 us: both_sides(): lax.ppermute(array, 'space', up)]
    ppermute x85 -> x18, starting transfers between devices: 138 us -> 13.1 us  [the longest x9 9.08 us: both_sides(): lax.ppermute(array, 'space', down)]
    mul x60 -> x0, other arithmetic: 96.8 us -> none  [the longest x30 56.7 us: spin_rate(): factor * (cross_x + damping * double_x)]
    all_to_all x0 -> x2, blocking collectives: none -> 26.8 us  [the longest x1 14.5 us: per_device(): corr = lax.all_to_all(payload, 'tm', 0, 0, tiled=True)]
    slice x156 -> x1, local copies, waits for them, and re-layouts: 18.2 us -> 0.01 us  [per_device(): message = corr[:2]]
    pallas_call x0 -> x10, Pallas kernels: none -> 12.5 us  [call(): pl.pallas_call(kernel, out_shape=[jax.ShapeDtypeStruct(s, F32) for s in s...]
    another operation x9 -> x0, other arithmetic: 7.8 us -> none  [spin_rate(): jnp.stack([factor * (cross_x + damping * double_x), factor * (cross_y + d...]
    select_n x49 -> x0, other arithmetic: 5.39 us -> none  [the longest x34 4.99 us: layer_field(): chosen = jnp.where(odd_layer, forward, behind)]
  transfers between devices with their start and end apart: 85 -> 18, of which waited for: 51 -> 18; matrix products, arithmetic and copies ran while one was open for 3% -> 0% of each run, Pallas kernels for 0% -> 0%
where the time goes in v1:
time: 94.6 us; the launch traced here: 94.4 us
  waiting for transfers between devices  40.9 us (43%)
  blocking collectives  26.8 us (28%)
  starting transfers between devices  13.1 us (14%)
  Pallas kernels  12.5 us (13%)
  other arithmetic  0.98 us (1%)
    ppermute x9, waiting for transfers between devices, both_sides(): lax.ppermute(array, 'space', up)  27.1 us
    all_to_all x1, blocking collectives, per_device(): corr = lax.all_to_all(payload, 'tm', 0, 0, tiled=True)  14.5 us
    ppermute x9, waiting for transfers between devices, both_sides(): lax.ppermute(array, 'space', down)  13.9 us
    pallas_call x10, Pallas kernels, call(): pl.pallas_call(kernel, out_shape=[jax.ShapeDtypeStruct(s, F32) for s in s...  12.5 us
    all_to_all x1, blocking collectives, per_device(): sent = lax.all_to_all(sent, 'tm', 0, 0, tiled=True)  12.3 us
    ppermute x9, starting transfers between devices, both_sides(): lax.ppermute(array, 'space', down)  9.08 us
    ppermute x9, starting transfers between devices, both_sides(): lax.ppermute(array, 'space', up)  3.99 us
  transfers between devices with their start and end apart: 18, of which 18 were waited for; matrix products, arithmetic and copies ran while one was open for 0% of the time, Pallas kernels for 0%

profile of v1, /device:TPU:2, one launch (start us, length us, event | category | flops | bytes accessed | tf_op | source)
XLA Modules:
  0.0 94.4 jit_solution(4286952870281281141)
XLA Ops:
  1.0 8.9 %collective-permute-start.1 = (f32[4,2,16,512]{3,2,1,0:T(8,128)S(1)}, f32[4,2,16,512]{3,2,1,0:T(8,128)S(1)}, u32[]{:S(2)}, u32[]{:S(2)}) collective-permute-start(f32[4,2,16,512]{3,2,1,0:T(8,128)S(1)} %pad_maximum_fusion.own), channel_id=1, source_target_pairs={{1,0},{2,1},{3,2},{4,3},{5,4},{6,5},{7,6},{8,7},{9,8},{10,9},{11,1... | collective-permute-start | bytes 786440 | tf_op jit(solution)/shard_map/ppermute | solution.py:239
  9.9 3.9 %collective-permute-done.1.right = f32[4,2,16,512]{3,2,1,0:T(8,128)S(1)} collective-permute-done((f32[4,2,16,512]{3,2,1,0:T(8,128)S(1)}, f32[4,2,16,512]{3,2,1,0:T(8,128)S(1)}, u32[]{:S(2)}, u32[]{:S(2)}) %collective-permute-start.1) | collective-permute-done | bytes 262176 | tf_op jit(solution)/shard_map/ppermute | solution.py:239
  13.8 3.1 %collective-permute-done.left = f32[4,2,16,512]{3,2,1,0:T(8,128)S(1)} collective-permute-done((f32[4,2,16,512]{3,2,1,0:T(8,128)S(1)}, f32[4,2,16,512]{3,2,1,0:T(8,128)S(1)}, u32[]{:S(2)}, u32[]{:S(2)}) %collective-permute-start) | collective-permute-done | bytes 262176 | tf_op jit(solution)/shard_map/ppermute | solution.py:239
  16.9 2.3 %shard_map.37 = (f32[16,3,2,8,128]{4,3,2,1,0:T(8,128)S(1)}, f32[2,5,8,128]{3,2,1,0:T(8,128)S(1)}) custom-call(f32[4,2,16,512]{3,2,1,0:T(8,128)S(1)} %pad_maximum_fusion.own, f32[4,2,16,512]{3,2,1,0:T(8,128)S(1)} %collective-permute-done.left, f32[4,2,16,512]{3,2,1,0:T(8,128)S(1)} %collective-permute-done.1.right, f32[3]{0:T(128)S(1)} %copy-done, ...), custom_call_target="tpu_custom_call" | custom-call | tf_op jit(solution)/shard_map/pallas_call | solution.py:243
  19.2 14.5 %all_to_all.10.corr = f32[16,3,2,8,128]{4,3,2,1,0:T(8,128)S(1)} all-to-all(f32[16,3,2,8,128]{4,3,2,1,0:T(8,128)S(1)} %get-tuple-element.21), channel_id=1, replica_groups=mesh['tm'=16,'space'=32] {'tm'}, dimensions={0} | all-to-all | bytes 786432 | tf_op jit(solution)/shard_map/all_to_all | solution.py:265
  34.3 1.2 %collective-permute-done.3.right = f32[2,3,2,8,128]{4,3,2,1,0:T(8,128)S(1)} collective-permute-done((f32[2,3,2,8,128]{4,3,2,1,0:T(8,128)S(1)}, f32[2,3,2,8,128]{4,3,2,1,0:T(8,128)S(1)}, u32[]{:S(2)}, u32[]{:S(2)}) %collective-permute-start.3) | collective-permute-done | bytes 49184 | tf_op jit(solution)/shard_map/ppermute | solution.py:239
  35.5 3.0 %collective-permute-done.2.left = f32[2,3,2,8,128]{4,3,2,1,0:T(8,128)S(1)} collective-permute-done((f32[2,3,2,8,128]{4,3,2,1,0:T(8,128)S(1)}, f32[2,3,2,8,128]{4,3,2,1,0:T(8,128)S(1)}, u32[]{:S(2)}, u32[]{:S(2)}) %collective-permute-start.2) | collective-permute-done | bytes 49184 | tf_op jit(solution)/shard_map/ppermute | solution.py:239
  40.2 1.2 %collective-permute-done.5.right = f32[2,3,2,8,128]{4,3,2,1,0:T(8,128)S(1)} collective-permute-done((f32[2,3,2,8,128]{4,3,2,1,0:T(8,128)S(1)}, f32[2,3,2,8,128]{4,3,2,1,0:T(8,128)S(1)}, u32[]{:S(2)}, u32[]{:S(2)}) %collective-permute-start.5) | collective-permute-done | bytes 49184 | tf_op jit(solution)/shard_map/ppermute | solution.py:239
  41.5 3.0 %collective-permute-done.4.left = f32[2,3,2,8,128]{4,3,2,1,0:T(8,128)S(1)} collective-permute-done((f32[2,3,2,8,128]{4,3,2,1,0:T(8,128)S(1)}, f32[2,3,2,8,128]{4,3,2,1,0:T(8,128)S(1)}, u32[]{:S(2)}, u32[]{:S(2)}) %collective-permute-start.4) | collective-permute-done | bytes 49184 | tf_op jit(solution)/shard_map/ppermute | solution.py:239
  44.5 1.2 %shard_map.39 = (f32[2,3,2,8,128]{4,3,2,1,0:T(8,128)S(1)}, f32[2,3,8,128]{3,2,1,0:T(8,128)S(1)}) custom-call(f32[2,3,2,8,128]{4,3,2,1,0:T(8,128)S(1)} %get-tuple-element.23.own, f32[2,3,2,8,128]{4,3,2,1,0:T(8,128)S(1)} %collective-permute-done.4.left, f32[2,3,2,8,128]{4,3,2,1,0:T(8,128)S(1)} %collective-permute-done.5.right, ...), custom_call_target="tpu_custom_call" | custom-call | tf_op jit(solution)/shard_map/pallas_call | solution.py:243
  46.2 1.2 %collective-permute-done.7.right = f32[2,3,2,8,128]{4,3,2,1,0:T(8,128)S(1)} collective-permute-done((f32[2,3,2,8,128]{4,3,2,1,0:T(8,128)S(1)}, f32[2,3,2,8,128]{4,3,2,1,0:T(8,128)S(1)}, u32[]{:S(2)}, u32[]{:S(2)}) %collective-permute-start.7) | collective-permute-done | bytes 49184 | tf_op jit(solution)/shard_map/ppermute | solution.py:239
  47.4 3.0 %collective-permute-done.6.left = f32[2,3,2,8,128]{4,3,2,1,0:T(8,128)S(1)} collective-permute-done((f32[2,3,2,8,128]{4,3,2,1,0:T(8,128)S(1)}, f32[2,3,2,8,128]{4,3,2,1,0:T(8,128)S(1)}, u32[]{:S(2)}, u32[]{:S(2)}) %collective-permute-start.6) | collective-permute-done | bytes 49184 | tf_op jit(solution)/shard_map/ppermute | solution.py:239
  50.4 1.2 %shard_map.40 = (f32[2,3,2,8,128]{4,3,2,1,0:T(8,128)S(1)}, f32[2,3,8,128]{3,2,1,0:T(8,128)S(1)}) custom-call(f32[2,3,2,8,128]{4,3,2,1,0:T(8,128)S(1)} %get-tuple-element.24.own, f32[2,3,2,8,128]{4,3,2,1,0:T(8,128)S(1)} %collective-permute-done.6.left, f32[2,3,2,8,128]{4,3,2,1,0:T(8,128)S(1)} %collective-permute-done.7.right, ...), custom_call_target="tpu_custom_call" | custom-call | tf_op jit(solution)/shard_map/pallas_call | solution.py:243
  52.1 1.2 %collective-permute-done.9.right = f32[2,3,2,8,128]{4,3,2,1,0:T(8,128)S(1)} collective-permute-done((f32[2,3,2,8,128]{4,3,2,1,0:T(8,128)S(1)}, f32[2,3,2,8,128]{4,3,2,1,0:T(8,128)S(1)}, u32[]{:S(2)}, u32[]{:S(2)}) %collective-permute-start.9) | collective-permute-done | bytes 49184 | tf_op jit(solution)/shard_map/ppermute | solution.py:239
  53.4 3.0 %collective-permute-done.8.left = f32[2,3,2,8,128]{4,3,2,1,0:T(8,128)S(1)} collective-permute-done((f32[2,3,2,8,128]{4,3,2,1,0:T(8,128)S(1)}, f32[2,3,2,8,128]{4,3,2,1,0:T(8,128)S(1)}, u32[]{:S(2)}, u32[]{:S(2)}) %collective-permute-start.8) | collective-permute-done | bytes 49184 | tf_op jit(solution)/shard_map/ppermute | solution.py:239
  58.1 1.2 %collective-permute-done.11.right = f32[2,3,2,8,128]{4,3,2,1,0:T(8,128)S(1)} collective-permute-done((f32[2,3,2,8,128]{4,3,2,1,0:T(8,128)S(1)}, f32[2,3,2,8,128]{4,3,2,1,0:T(8,128)S(1)}, u32[]{:S(2)}, u32[]{:S(2)}) %collective-permute-start.11) | collective-permute-done | bytes 49184 | tf_op jit(solution)/shard_map/ppermute | solution.py:239
  59.3 3.0 %collective-permute-done.10.left = f32[2,3,2,8,128]{4,3,2,1,0:T(8,128)S(1)} collective-permute-done((f32[2,3,2,8,128]{4,3,2,1,0:T(8,128)S(1)}, f32[2,3,2,8,128]{4,3,2,1,0:T(8,128)S(1)}, u32[]{:S(2)}, u32[]{:S(2)}) %collective-permute-start.10) | collective-permute-done | bytes 49184 | tf_op jit(solution)/shard_map/ppermute | solution.py:239
  64.1 1.2 %collective-permute-done.13.right = f32[2,3,2,8,128]{4,3,2,1,0:T(8,128)S(1)} collective-permute-done((f32[2,3,2,8,128]{4,3,2,1,0:T(8,128)S(1)}, f32[2,3,2,8,128]{4,3,2,1,0:T(8,128)S(1)}, u32[]{:S(2)}, u32[]{:S(2)}) %collective-permute-start.13) | collective-permute-done | bytes 49184 | tf_op jit(solution)/shard_map/ppermute | solution.py:239
  65.3 3.0 %collective-permute-done.12.left = f32[2,3,2,8,128]{4,3,2,1,0:T(8,128)S(1)} collective-permute-done((f32[2,3,2,8,128]{4,3,2,1,0:T(8,128)S(1)}, f32[2,3,2,8,128]{4,3,2,1,0:T(8,128)S(1)}, u32[]{:S(2)}, u32[]{:S(2)}) %collective-permute-start.12) | collective-permute-done | bytes 49184 | tf_op jit(solution)/shard_map/ppermute | solution.py:239
  70.0 1.2 %collective-permute-done.15.right = f32[2,3,2,8,128]{4,3,2,1,0:T(8,128)S(1)} collective-permute-done((f32[2,3,2,8,128]{4,3,2,1,0:T(8,128)S(1)}, f32[2,3,2,8,128]{4,3,2,1,0:T(8,128)S(1)}, u32[]{:S(2)}, u32[]{:S(2)}) %collective-permute-start.15) | collective-permute-done | bytes 49184 | tf_op jit(solution)/shard_map/ppermute | solution.py:239
  71.3 3.0 %collective-permute-done.14.left = f32[2,3,2,8,128]{4,3,2,1,0:T(8,128)S(1)} collective-permute-done((f32[2,3,2,8,128]{4,3,2,1,0:T(8,128)S(1)}, f32[2,3,2,8,128]{4,3,2,1,0:T(8,128)S(1)}, u32[]{:S(2)}, u32[]{:S(2)}) %collective-permute-start.14) | collective-permute-done | bytes 49184 | tf_op jit(solution)/shard_map/ppermute | solution.py:239
  76.0 1.2 %collective-permute-done.17.right = f32[2,3,2,8,128]{4,3,2,1,0:T(8,128)S(1)} collective-permute-done((f32[2,3,2,8,128]{4,3,2,1,0:T(8,128)S(1)}, f32[2,3,2,8,128]{4,3,2,1,0:T(8,128)S(1)}, u32[]{:S(2)}, u32[]{:S(2)}) %collective-permute-start.17) | collective-permute-done | bytes 49184 | tf_op jit(solution)/shard_map/ppermute | solution.py:239
  77.2 3.0 %collective-permute-done.16.left = f32[2,3,2,8,128]{4,3,2,1,0:T(8,128)S(1)} collective-permute-done((f32[2,3,2,8,128]{4,3,2,1,0:T(8,128)S(1)}, f32[2,3,2,8,128]{4,3,2,1,0:T(8,128)S(1)}, u32[]{:S(2)}, u32[]{:S(2)}) %collective-permute-start.16) | collective-permute-done | bytes 49184 | tf_op jit(solution)/shard_map/ppermute | solution.py:239
  81.2 12.3 %all_to_all.11.sent = f32[16,3,8,128]{3,2,1,0:T(8,128)S(1)} all-to-all(f32[16,3,8,128]{3,2,1,0:T(8,128)S(1)} %shard_map.45), channel_id=1, replica_groups=mesh['tm'=16,'space'=32] {'tm'}, dimensions={0} | all-to-all | bytes 393216 | tf_op jit(solution)/shard_map/all_to_all | solution.py:280
  (28 shorter events, 12.9 us)
Async XLA Ops:
  1.0 12.8 %collective-permute-start.1 = (f32[4,2,16,512]{3,2,1,0:T(8,128)S(1)}, f32[4,2,16,512]{3,2,1,0:T(8,128)S(1)}, u32[]{:S(2)}, u32[]{:S(2)}) collective-permute-start(f32[4,2,16,512]{3,2,1,0:T(8,128)S(1)} %pad_maximum_fusion.own), channel_id=1, source_target_pairs={{1,0},{2,1},{3,2},{4,3},{5,4},{6,5},{7,6},{8,7},{9,8},{10,9},{11,1... | collective-permute-start | bytes 786440 | tf_op jit(solution)/shard_map/ppermute | solution.py:239
  9.9 7.0 %collective-permute-start = (f32[4,2,16,512]{3,2,1,0:T(8,128)S(1)}, f32[4,2,16,512]{3,2,1,0:T(8,128)S(1)}, u32[]{:S(2)}, u32[]{:S(2)}) collective-permute-start(f32[4,2,16,512]{3,2,1,0:T(8,128)S(1)} %pad_maximum_fusion.own), channel_id=1, source_target_pairs={{0,1},{1,2},{2,3},{3,4},{4,5},{5,6},{6,7},{7,8},{8,9},{9,10},{10,1... | collective-permute-start | bytes 786440 | tf_op jit(solution)/shard_map/ppermute | solution.py:239
  9.9 7.0 %copy-start = (f32[3]{0:T(128)S(1)}, f32[3]{0:T(128)}, u32[]{:S(2)}) copy-start(f32[3]{0:T(128)} %applied_ref.17) | copy-start | bytes 40
  33.8 1.8 %collective-permute-start.3 = (f32[2,3,2,8,128]{4,3,2,1,0:T(8,128)S(1)}, f32[2,3,2,8,128]{4,3,2,1,0:T(8,128)S(1)}, u32[]{:S(2)}, u32[]{:S(2)}) collective-permute-start(f32[2,3,2,8,128]{4,3,2,1,0:T(8,128)S(1)} %slice.4.own), channel_id=1, source_target_pairs={{1,0},{2,1},{3,2},{4,3},{5,4},{6,5},{7,6},{8,7},{9,8},{10,9},{11,1... | collective-permute-start | bytes 147464 | tf_op jit(solution)/shard_map/ppermute | solution.py:239
  33.8 4.7 %collective-permute-start.2 = (f32[2,3,2,8,128]{4,3,2,1,0:T(8,128)S(1)}, f32[2,3,2,8,128]{4,3,2,1,0:T(8,128)S(1)}, u32[]{:S(2)}, u32[]{:S(2)}) collective-permute-start(f32[2,3,2,8,128]{4,3,2,1,0:T(8,128)S(1)} %slice.4.own), channel_id=1, source_target_pairs={{0,1},{1,2},{2,3},{3,4},{4,5},{5,6},{6,7},{7,8},{8,9},{9,10},{10,1... | collective-permute-start | bytes 147464 | tf_op jit(solution)/shard_map/ppermute | solution.py:239
  39.7 1.8 %collective-permute-start.5 = (f32[2,3,2,8,128]{4,3,2,1,0:T(8,128)S(1)}, f32[2,3,2,8,128]{4,3,2,1,0:T(8,128)S(1)}, u32[]{:S(2)}, u32[]{:S(2)}) collective-permute-start(f32[2,3,2,8,128]{4,3,2,1,0:T(8,128)S(1)} %get-tuple-element.23.own), channel_id=1, source_target_pairs={{1,0},{2,1},{3,2},{4,3},{5,4},{6,5},{7,6},{8,7},{9,8},{10,9},{11,1... | collective-permute-start | bytes 147464 | tf_op jit(solution)/shard_map/ppermute | solution.py:239
  39.7 4.7 %collective-permute-start.4 = (f32[2,3,2,8,128]{4,3,2,1,0:T(8,128)S(1)}, f32[2,3,2,8,128]{4,3,2,1,0:T(8,128)S(1)}, u32[]{:S(2)}, u32[]{:S(2)}) collective-permute-start(f32[2,3,2,8,128]{4,3,2,1,0:T(8,128)S(1)} %get-tuple-element.23.own), channel_id=1, source_target_pairs={{0,1},{1,2},{2,3},{3,4},{4,5},{5,6},{6,7},{7,8},{8,9},{9,10},{10,1... | collective-permute-start | bytes 147464 | tf_op jit(solution)/shard_map/ppermute | solution.py:239
  45.7 1.8 %collective-permute-start.7 = (f32[2,3,2,8,128]{4,3,2,1,0:T(8,128)S(1)}, f32[2,3,2,8,128]{4,3,2,1,0:T(8,128)S(1)}, u32[]{:S(2)}, u32[]{:S(2)}) collective-permute-start(f32[2,3,2,8,128]{4,3,2,1,0:T(8,128)S(1)} %get-tuple-element.24.own), channel_id=1, source_target_pairs={{1,0},{2,1},{3,2},{4,3},{5,4},{6,5},{7,6},{8,7},{9,8},{10,9},{11,1... | collective-permute-start | bytes 147464 | tf_op jit(solution)/shard_map/ppermute | solution.py:239
  45.7 4.7 %collective-permute-start.6 = (f32[2,3,2,8,128]{4,3,2,1,0:T(8,128)S(1)}, f32[2,3,2,8,128]{4,3,2,1,0:T(8,128)S(1)}, u32[]{:S(2)}, u32[]{:S(2)}) collective-permute-start(f32[2,3,2,8,128]{4,3,2,1,0:T(8,128)S(1)} %get-tuple-element.24.own), channel_id=1, source_target_pairs={{0,1},{1,2},{2,3},{3,4},{4,5},{5,6},{6,7},{7,8},{8,9},{9,10},{10,1... | collective-permute-start | bytes 147464 | tf_op jit(solution)/shard_map/ppermute | solution.py:239
  51.6 1.8 %collective-permute-start.9 = (f32[2,3,2,8,128]{4,3,2,1,0:T(8,128)S(1)}, f32[2,3,2,8,128]{4,3,2,1,0:T(8,128)S(1)}, u32[]{:S(2)}, u32[]{:S(2)}) collective-permute-start(f32[2,3,2,8,128]{4,3,2,1,0:T(8,128)S(1)} %get-tuple-element.25.own), channel_id=1, source_target_pairs={{1,0},{2,1},{3,2},{4,3},{5,4},{6,5},{7,6},{8,7},{9,8},{10,9},{11,1... | collective-permute-start | bytes 147464 | tf_op jit(solution)/shard_map/ppermute | solution.py:239
  51.6 4.7 %collective-permute-start.8 = (f32[2,3,2,8,128]{4,3,2,1,0:T(8,128)S(1)}, f32[2,3,2,8,128]{4,3,2,1,0:T(8,128)S(1)}, u32[]{:S(2)}, u32[]{:S(2)}) collective-permute-start(f32[2,3,2,8,128]{4,3,2,1,0:T(8,128)S(1)} %get-tuple-element.25.own), channel_id=1, source_target_pairs={{0,1},{1,2},{2,3},{3,4},{4,5},{5,6},{6,7},{7,8},{8,9},{9,10},{10,1... | collective-permute-start | bytes 147464 | tf_op jit(solution)/shard_map/ppermute | solution.py:239
  57.6 1.8 %collective-permute-start.11 = (f32[2,3,2,8,128]{4,3,2,1,0:T(8,128)S(1)}, f32[2,3,2,8,128]{4,3,2,1,0:T(8,128)S(1)}, u32[]{:S(2)}, u32[]{:S(2)}) collective-permute-start(f32[2,3,2,8,128]{4,3,2,1,0:T(8,128)S(1)} %get-tuple-element.26.own), channel_id=1, source_target_pairs={{1,0},{2,1},{3,2},{4,3},{5,4},{6,5},{7,6},{8,7},{9,8},{10,9},{11,1... | collective-permute-start | bytes 147464 | tf_op jit(solution)/shard_map/ppermute | solution.py:239
  57.6 4.7 %collective-permute-start.10 = (f32[2,3,2,8,128]{4,3,2,1,0:T(8,128)S(1)}, f32[2,3,2,8,128]{4,3,2,1,0:T(8,128)S(1)}, u32[]{:S(2)}, u32[]{:S(2)}) collective-permute-start(f32[2,3,2,8,128]{4,3,2,1,0:T(8,128)S(1)} %get-tuple-element.26.own), channel_id=1, source_target_pairs={{0,1},{1,2},{2,3},{3,4},{4,5},{5,6},{6,7},{7,8},{8,9},{9,10},{10,1... | collective-permute-start | bytes 147464 | tf_op jit(solution)/shard_map/ppermute | solution.py:239
  63.5 1.8 %collective-permute-start.13 = (f32[2,3,2,8,128]{4,3,2,1,0:T(8,128)S(1)}, f32[2,3,2,8,128]{4,3,2,1,0:T(8,128)S(1)}, u32[]{:S(2)}, u32[]{:S(2)}) collective-permute-start(f32[2,3,2,8,128]{4,3,2,1,0:T(8,128)S(1)} %get-tuple-element.27.own), channel_id=1, source_target_pairs={{1,0},{2,1},{3,2},{4,3},{5,4},{6,5},{7,6},{8,7},{9,8},{10,9},{11,1... | collective-permute-start | bytes 147464 | tf_op jit(solution)/shard_map/ppermute | solution.py:239
  63.6 4.7 %collective-permute-start.12 = (f32[2,3,2,8,128]{4,3,2,1,0:T(8,128)S(1)}, f32[2,3,2,8,128]{4,3,2,1,0:T(8,128)S(1)}, u32[]{:S(2)}, u32[]{:S(2)}) collective-permute-start(f32[2,3,2,8,128]{4,3,2,1,0:T(8,128)S(1)} %get-tuple-element.27.own), channel_id=1, source_target_pairs={{0,1},{1,2},{2,3},{3,4},{4,5},{5,6},{6,7},{7,8},{8,9},{9,10},{10,1... | collective-permute-start | bytes 147464 | tf_op jit(solution)/shard_map/ppermute | solution.py:239
  69.5 1.8 %collective-permute-start.15 = (f32[2,3,2,8,128]{4,3,2,1,0:T(8,128)S(1)}, f32[2,3,2,8,128]{4,3,2,1,0:T(8,128)S(1)}, u32[]{:S(2)}, u32[]{:S(2)}) collective-permute-start(f32[2,3,2,8,128]{4,3,2,1,0:T(8,128)S(1)} %get-tuple-element.28.own), channel_id=1, source_target_pairs={{1,0},{2,1},{3,2},{4,3},{5,4},{6,5},{7,6},{8,7},{9,8},{10,9},{11,1... | collective-permute-start | bytes 147464 | tf_op jit(solution)/shard_map/ppermute | solution.py:239
  69.5 4.7 %collective-permute-start.14 = (f32[2,3,2,8,128]{4,3,2,1,0:T(8,128)S(1)}, f32[2,3,2,8,128]{4,3,2,1,0:T(8,128)S(1)}, u32[]{:S(2)}, u32[]{:S(2)}) collective-permute-start(f32[2,3,2,8,128]{4,3,2,1,0:T(8,128)S(1)} %get-tuple-element.28.own), channel_id=1, source_target_pairs={{0,1},{1,2},{2,3},{3,4},{4,5},{5,6},{6,7},{7,8},{8,9},{9,10},{10,1... | collective-permute-start | bytes 147464 | tf_op jit(solution)/shard_map/ppermute | solution.py:239
  75.5 1.8 %collective-permute-start.17 = (f32[2,3,2,8,128]{4,3,2,1,0:T(8,128)S(1)}, f32[2,3,2,8,128]{4,3,2,1,0:T(8,128)S(1)}, u32[]{:S(2)}, u32[]{:S(2)}) collective-permute-start(f32[2,3,2,8,128]{4,3,2,1,0:T(8,128)S(1)} %get-tuple-element.29.own), channel_id=1, source_target_pairs={{1,0},{2,1},{3,2},{4,3},{5,4},{6,5},{7,6},{8,7},{9,8},{10,9},{11,1... | collective-permute-start | bytes 147464 | tf_op jit(solution)/shard_map/ppermute | solution.py:239
  75.5 4.7 %collective-permute-start.16 = (f32[2,3,2,8,128]{4,3,2,1,0:T(8,128)S(1)}, f32[2,3,2,8,128]{4,3,2,1,0:T(8,128)S(1)}, u32[]{:S(2)}, u32[]{:S(2)}) collective-permute-start(f32[2,3,2,8,128]{4,3,2,1,0:T(8,128)S(1)} %get-tuple-element.29.own), channel_id=1, source_target_pairs={{0,1},{1,2},{2,3},{3,4},{4,5},{5,6},{6,7},{7,8},{8,9},{9,10},{10,1... | collective-permute-start | bytes 147464 | tf_op jit(solution)/shard_map/ppermute | solution.py:239

commit v2 on v1

--- a/solution.py
+++ b/solution.py
@@ -13,7 +13,6 @@
 GAIN = -1.0 / (1.0 + DAMPING * DAMPING)
 F32 = jnp.float32
 VMEM = pl.BlockSpec(memory_space=pltpu.VMEM)
-SMEM = pl.BlockSpec(memory_space=pltpu.SMEM)
 
 
 def near_odd(even_below, even_here):
@@ -86,16 +85,17 @@
     return pltpu.roll(x, by, axis=1) if by else x
 
 
-def prologue(own, left, right, applied_ref, row_ref, payload, windows, layers):
-    applied = [applied_ref[c] for c in range(3)]
-    tiles = own.shape[3] // 128
-    for base, ref in enumerate((left, own, right)):
-        for q in range(tiles):
-            layers[:, 2 * base : 2 * base + 2, q] = ref[:, :, :, 128 * q : 128 * (q + 1)]
-
+def laid(own, left, right):
     def load(comp, plane, parity):
-        parts = [layers[comp, plane + 2, q, pl.ds(parity, 8, stride=2), :] for q in range(tiles)]
-        return jnp.concatenate(parts, axis=1)
+        ref, at = (left, plane + 2) if plane < 0 else (own, plane) if plane < 2 else (right, plane - 2)
+        return ref[comp, at, parity]
+
+    return load
+
+
+def prologue(own, left, right, field, payload):
+    applied = [jnp.concatenate([field[c]] * (own.shape[-1] // 128), axis=1) for c in range(3)]
+    load = laid(own, left, right)
 
     planes = range(-2, 4)
     even = {x: [load(c, x, 0) for c in range(3)] for x in planes}
@@ -119,8 +119,7 @@
     coarse_e = finish(even, first_e, second_e, COARSE, range(2))
     coarse_o = finish(odd, first_o, second_o, COARSE, range(2))
 
-    row = row_ref[0]
-    keep = jnp.where(row == 0, 0.0, 1.0).astype(F32)
+    keep = jnp.where(lax.axis_index("tm") == 0, 0.0, 1.0).astype(F32)
     for comp in range(3):
         for parity, fine, coarse in ((0, fine_e, coarse_e), (1, fine_o, coarse_o)):
             moved = []
@@ -137,36 +136,54 @@
                         128, 0, 64, turn(p, -32 * i), turn(r, 64 - 32 * i)
                     )
 
-    for at in range(payload.shape[0]):
+
+def window(own, left, right, windows):
+    load = laid(own, left, right)
+    row = lax.axis_index("tm")
+    for at in range(own.shape[-1] // 32):
 
         @pl.when(row == at)
         def _():
-            for parity, planes_used in ((0, range(-2, 3)), (1, range(-1, 4))):
-                for k, x in enumerate(planes_used):
-                    wide = 2.0 * load(3, x, parity)
-                    windows[parity, k] = turn(wide, 16 - 32 * at)[:, :128]
+            for parity, planes in ((0, range(-2, 3)), (1, range(-1, 4))):
+                for k, x in enumerate(planes):
+                    windows[parity, k] = turn(2.0 * load(3, x, parity), 16 - 32 * at)[:, :128]
 
 
 def dense(even_pair, odd_pair):
     return lane_select(64, 0, 32, turn(even_pair, -16), turn(odd_pair, 16))
 
 
-def chain(block, last, own, left, right, corr, windows, applied_ref, *rest):
-    applied = [applied_ref[c] for c in range(3)]
+def chain(block, last, own, left, right, corr, windows, field, *rest):
+    applied = [field[c] for c in range(3)]
     first_slice = 2 * block + 1
-
-    def pair(ref, field, comp, parity):
-        packed = ref[field, comp, parity]
-        return packed, turn(packed, 64)
-
-    def spread(field, parity, planes):
+    start = block == 0
+    reach = range(-1, 3) if last else range(-2, 4)
+    inner = range(reach[0] + 1, reach[-1])
+
+    def state(ref, comp, parity):
+        return ref[0, comp, parity] if start else ref[parity, comp]
+
+    def spread(parity):
         out = {}
         for ref, base in ((left, -2), (own, 0), (right, 2)):
-            pairs = [pair(ref, field, c, parity) for c in range(3)]
-            for k in range(2):
-                if base + k in planes:
-                    out[base + k] = [p[k] for p in pairs]
+            pairs = [state(ref, c, parity) for c in range(3)]
+            for x, shift in ((base, 0), (base + 1, 64)):
+                if x in reach:
+                    out[x] = [turn(p, shift) for p in pairs]
         return out
+
+    def extra(parity):
+        pairs = [corr[first_slice, c, parity] for c in range(3)]
+        out = {0: pairs, 1: [turn(p, 64) for p in pairs]}
+        for ref, x, shift in ((left, -1, 64), (right, 2, 0)):
+            if x in inner and start:
+                out[x] = [turn(ref[1, c, parity], shift) for c in range(3)]
+            elif x in inner:
+                out[x] = [turn(ref[2, c], 64 * parity) for c in range(3)]
+        return out
+
+    def add(spins, more):
+        return {x: [s + e for s, e in zip(spins[x], more[x])] for x in inner}
 
     def aniso_even(x):
         return windows[0, x + 2]
@@ -175,16 +192,8 @@
         return windows[1, x + 1]
 
     sides = (aniso_even, aniso_odd, applied)
-    reach = range(-1, 3) if last else range(-2, 4)
-    inner = range(reach[0] + 1, reach[-1])
-    even, odd = spread(0, 0, reach), spread(0, 1, reach)
-    corr_e, corr_o = spread(1, 0, inner), spread(1, 1, inner)
-
-    def add(spins, extra):
-        return {x: [s + e for s, e in zip(spins[x], extra[x])] for x in extra}
-
-    even, odd = heun(even, odd, *sides, COARSE, reach[0], reach[-1])
-    even, odd = add(even, corr_e), add(odd, corr_o)
+    even, odd = heun(spread(0), spread(1), *sides, COARSE, reach[0], reach[-1])
+    even, odd = add(even, extra(0)), add(odd, extra(1))
 
     def packed(spins):
         return [lane_select(128, 0, 64, spins[0][c], turn(spins[1][c], 64)) for c in range(3)]
@@ -203,9 +212,9 @@
         emit(sent, at, packed(even), packed(odd))
         return
 
-    message, ends = rest
+    up, down, ends = rest
     at = 0
-    if block == 0:
+    if start:
         emit(ends, 0, [own[0, c, 0] for c in range(3)], [own[0, c, 1] for c in range(3)])
         at = 1
     emit(ends, at, packed(even), packed(odd))
@@ -214,9 +223,11 @@
     end_o = [s + corr[first_slice + 1, c, 1] for c, s in enumerate(packed(odd))]
     emit(ends, at + 1, end_e, end_o)
     for c in range(3):
-        message[0, c, 0] = end_e[c]
-        message[0, c, 1] = end_o[c]
-    message[1] = corr[first_slice + 2]
+        later_e, later_o = corr[first_slice + 2, c, 0], corr[first_slice + 2, c, 1]
+        up[2, c] = lane_select(128, 0, 64, turn(later_e, 64), later_o)
+        down[2, c] = lane_select(128, 0, 64, later_e, turn(later_o, 64))
+        up[0, c], up[1, c] = end_e[c], end_o[c]
+        down[0, c], down[1, c] = end_e[c], end_o[c]
 
 
 def assemble(sent, out, layers):
@@ -232,18 +243,18 @@
             out[0, comp, :, :, 128 * q : 128 * (q + 1)] = layers[comp, :, q]
 
 
-def both_sides(array):
+def both_sides(to_above, to_below):
     count = lax.axis_size("space")
     up = [(i, (i + 1) % count) for i in range(count)]
     down = [(j, i) for i, j in up]
-    return lax.ppermute(array, "space", up), lax.ppermute(array, "space", down)
-
-
-def call(kernel, shapes, in_specs, *args, scratch=()):
+    return lax.ppermute(to_above, "space", up), lax.ppermute(to_below, "space", down)
+
+
+def call(kernel, shapes, *args, scratch=()):
     return pl.pallas_call(
         kernel,
         out_shape=[jax.ShapeDtypeStruct(s, F32) for s in shapes],
-        in_specs=in_specs,
+        in_specs=[VMEM] * len(args),
         out_specs=[VMEM] * len(shapes),
         scratch_shapes=[pltpu.VMEM(s, F32) for s in scratch],
         compiler_params=pltpu.CompilerParams(vmem_limit_bytes=32 * 1024 * 1024),
@@ -252,33 +263,29 @@
 
 def per_device(starts, anisotropy, applied):
     slices = lax.axis_size("tm")
-    row = lax.axis_index("tm").astype(jnp.int32)[None]
+    width = starts.shape[-1]
     own = jnp.concatenate([starts[0], anisotropy[None]], axis=0)
-    left, right = both_sides(own)
-    payload, windows = call(
-        prologue,
-        [(slices, 3, 2, 8, 128), (2, 5, 8, 128)],
-        [VMEM] * 3 + [SMEM] * 2,
-        *(own, left, right, applied, row),
-        scratch=[(4, 6, starts.shape[-1] // 128, 16, 128)],
-    )
+    own = own.reshape(4, 2, 8, 2, width).swapaxes(2, 3)
+    field = jnp.broadcast_to(applied[:, None, None], (3, 8, 128))
+    slabs = (own, *both_sides(own, own))
+    (payload,) = call(prologue, [(slices, 3, 2, 8, 128)], *slabs, field)
+    (windows,) = call(window, [(2, 5, 8, 128)], *slabs)
     corr = lax.all_to_all(payload, "tm", 0, 0, tiled=True)
-    message = corr[:2]
+    up = down = corr[:2]
     done = []
     blocks = slices // 2
     for block in range(blocks):
-        left, right = both_sides(message)
         last = block == blocks - 1
         kernel = functools.partial(chain, block, last)
-        args = (message, left, right, corr, windows, applied)
-        specs = [VMEM] * 5 + [SMEM]
+        args = (up, *both_sides(up, down), corr, windows, field)
         if last:
-            (sent,) = call(kernel, [(slices, 3, 8, 128)], specs + [VMEM] * len(done), *args, *done)
+            (sent,) = call(kernel, [(slices, 3, 8, 128)], *args, *done)
         else:
-            message, ends = call(kernel, [message.shape, (3 if block == 0 else 2, 3, 8, 128)], specs, *args)
+            shapes = [(3, 3, 8, 128)] * 2 + [(3 if block == 0 else 2, 3, 8, 128)]
+            up, down, ends = call(kernel, shapes, *args)
             done.append(ends)
     sent = lax.all_to_all(sent, "tm", 0, 0, tiled=True)
-    (out,) = call(assemble, [starts.shape], [VMEM], sent, scratch=[(3, 2, starts.shape[-1] // 128, 16, 128)])
+    (out,) = call(assemble, [starts.shape], sent, scratch=[(3, 2, width // 128, 16, 128)])
     return out
 
 

time: 94.6 us -> 89.1 us (0.942)
  Pallas kernels: 12.5 us -> 7.66 us
  local copies, waits for them, and re-layouts: 0.01 us -> 1.26 us
  waiting for transfers between devices: 40.9 us -> 39.8 us
  other arithmetic: 0.98 us -> 0.02 us
    pallas_call x10 -> x11, Pallas kernels: 12.5 us -> 7.66 us  [call(): pl.pallas_call(kernel, out_shape=[jax.ShapeDtypeStruct(s, F32) for s in s...]
    unnamed x2 -> x6, local copies, waits for them, and re-layouts: 0.01 us -> 1.1 us
    ppermute x18, waiting for transfers between devices: 40.9 us -> 39.8 us  [the longest x9 26.9 us: both_sides(): lax.ppermute(to_above, 'space', up)]
    concatenate x1 -> x0, other arithmetic: 0.98 us -> none  [per_device(): own = jnp.concatenate([starts[0], anisotropy[None]], axis=0)]
where the time goes in v2:
time: 89.1 us; the launch traced here: 88.9 us
  waiting for transfers between devices  39.8 us (45%)
  blocking collectives  26.8 us (30%)
  starting transfers between devices  13.1 us (15%)
  Pallas kernels  7.66 us (9%)
  local copies, waits for them, and re-layouts  1.26 us (1%)
    ppermute x9, waiting for transfers between devices, both_sides(): lax.ppermute(to_above, 'space', up)  26.9 us
    all_to_all x1, blocking collectives, per_device(): corr = lax.all_to_all(payload, 'tm', 0, 0, tiled=True)  14.5 us
    ppermute x9, waiting for transfers between devices, both_sides(): lax.ppermute(to_below, 'space', down)  12.9 us
    all_to_all x1, blocking collectives, per_device(): sent = lax.all_to_all(sent, 'tm', 0, 0, tiled=True)  12.3 us
    ppermute x9, starting transfers between devices, both_sides(): lax.ppermute(to_below, 'space', down)  9.08 us
    pallas_call x11, Pallas kernels, call(): pl.pallas_call(kernel, out_shape=[jax.ShapeDtypeStruct(s, F32) for s in s...  7.66 us
    ppermute x9, starting transfers between devices, both_sides(): lax.ppermute(to_above, 'space', up)  3.99 us
  transfers between devices with their start and end apart: 18, of which 18 were waited for; matrix products, arithmetic and copies ran while one was open for 0% of the time, Pallas kernels for 0%

profile of v2, /device:TPU:2, one launch (start us, length us, event | category | flops | bytes accessed | tf_op | source)
XLA Modules:
  0.0 88.9 jit_solution(8945235927767104443)
XLA Ops:
  0.0 0.9 %copy.5 = f32[2,16,512]{2,0,1:T(2,128)S(1)} copy(f32[2,16,512]{2,1,0:T(8,128)} %param.4) | data formatting | bytes 131072 | tf_op args[1]
  1.3 8.9 %collective-permute-start.1 = (f32[4,2,2,8,512]{4,3,2,1,0:T(8,128)S(1)}, f32[4,2,2,8,512]{4,3,2,1,0:T(8,128)S(1)}, u32[]{:S(2)}, u32[]{:S(2)}) collective-permute-start(f32[4,2,2,8,512]{4,3,2,1,0:T(8,128)S(1)} %maximum_bitcast_fusion.own), channel_id=1, source_target_pairs={{1,0},{2,1},{3,2},{4,3},{5,4},{6,5},{7,6},{8,7},{9,8},{10,9},{11,1... | collective-permute-start | bytes 786440 | tf_op jit(solution)/shard_map/ppermute | solution.py:250
  10.2 3.9 %collective-permute-done.1.right = f32[4,2,2,8,512]{4,3,2,1,0:T(8,128)S(1)} collective-permute-done((f32[4,2,2,8,512]{4,3,2,1,0:T(8,128)S(1)}, f32[4,2,2,8,512]{4,3,2,1,0:T(8,128)S(1)}, u32[]{:S(2)}, u32[]{:S(2)}) %collective-permute-start.1) | collective-permute-done | bytes 262176 | tf_op jit(solution)/shard_map/ppermute | solution.py:250
  14.1 3.1 %collective-permute-done.left = f32[4,2,2,8,512]{4,3,2,1,0:T(8,128)S(1)} collective-permute-done((f32[4,2,2,8,512]{4,3,2,1,0:T(8,128)S(1)}, f32[4,2,2,8,512]{4,3,2,1,0:T(8,128)S(1)}, u32[]{:S(2)}, u32[]{:S(2)}) %collective-permute-start) | collective-permute-done | bytes 262176 | tf_op jit(solution)/shard_map/ppermute | solution.py:250
  17.3 1.6 %shard_map.37 = f32[16,3,2,8,128]{4,3,2,1,0:T(8,128)S(1)} custom-call(f32[4,2,2,8,512]{4,3,2,1,0:T(8,128)S(1)} %maximum_bitcast_fusion.own, f32[4,2,2,8,512]{4,3,2,1,0:T(8,128)S(1)} %collective-permute-done.left, f32[4,2,2,8,512]{4,3,2,1,0:T(8,128)S(1)} %collective-permute-done.1.right, f32[3,8,128]{2,1,0:T(8,128)S(1)} %broadcast_in_dim.2.field), custom_call_target="tpu_custom_call" | custom-call | tf_op jit(solution)/shard_map/pallas_call | solution.py:254
  18.9 14.5 %all_to_all.10.corr = f32[16,3,2,8,128]{4,3,2,1,0:T(8,128)S(1)} all-to-all(f32[16,3,2,8,128]{4,3,2,1,0:T(8,128)S(1)} %shard_map.37), channel_id=1, replica_groups=mesh['tm'=16,'space'=32] {'tm'}, dimensions={0} | all-to-all | bytes 786432 | tf_op jit(solution)/shard_map/all_to_all | solution.py:273
  34.1 1.1 %collective-permute-done.3.right = f32[2,3,2,8,128]{4,3,2,1,0:T(8,128)S(1)} collective-permute-done((f32[2,3,2,8,128]{4,3,2,1,0:T(8,128)S(1)}, f32[2,3,2,8,128]{4,3,2,1,0:T(8,128)S(1)}, u32[]{:S(2)}, u32[]{:S(2)}) %collective-permute-start.3) | collective-permute-done | bytes 49184 | tf_op jit(solution)/shard_map/ppermute | solution.py:250
  35.2 3.0 %collective-permute-done.2.left = f32[2,3,2,8,128]{4,3,2,1,0:T(8,128)S(1)} collective-permute-done((f32[2,3,2,8,128]{4,3,2,1,0:T(8,128)S(1)}, f32[2,3,2,8,128]{4,3,2,1,0:T(8,128)S(1)}, u32[]{:S(2)}, u32[]{:S(2)}) %collective-permute-start.2) | collective-permute-done | bytes 49184 | tf_op jit(solution)/shard_map/ppermute | solution.py:250
  39.3 1.1 %collective-permute-done.5.right = f32[3,3,8,128]{3,2,1,0:T(8,128)S(1)} collective-permute-done((f32[3,3,8,128]{3,2,1,0:T(8,128)S(1)}, f32[3,3,8,128]{3,2,1,0:T(8,128)S(1)}, u32[]{:S(2)}, u32[]{:S(2)}) %collective-permute-start.5) | collective-permute-done | bytes 36896 | tf_op jit(solution)/shard_map/ppermute | solution.py:250
  40.5 3.0 %collective-permute-done.4.left = f32[3,3,8,128]{3,2,1,0:T(8,128)S(1)} collective-permute-done((f32[3,3,8,128]{3,2,1,0:T(8,128)S(1)}, f32[3,3,8,128]{3,2,1,0:T(8,128)S(1)}, u32[]{:S(2)}, u32[]{:S(2)}) %collective-permute-start.4) | collective-permute-done | bytes 36896 | tf_op jit(solution)/shard_map/ppermute | solution.py:250
  44.6 1.1 %collective-permute-done.7.right = f32[3,3,8,128]{3,2,1,0:T(8,128)S(1)} collective-permute-done((f32[3,3,8,128]{3,2,1,0:T(8,128)S(1)}, f32[3,3,8,128]{3,2,1,0:T(8,128)S(1)}, u32[]{:S(2)}, u32[]{:S(2)}) %collective-permute-start.7) | collective-permute-done | bytes 36896 | tf_op jit(solution)/shard_map/ppermute | solution.py:250
  45.8 3.0 %collective-permute-done.6.left = f32[3,3,8,128]{3,2,1,0:T(8,128)S(1)} collective-permute-done((f32[3,3,8,128]{3,2,1,0:T(8,128)S(1)}, f32[3,3,8,128]{3,2,1,0:T(8,128)S(1)}, u32[]{:S(2)}, u32[]{:S(2)}) %collective-permute-start.6) | collective-permute-done | bytes 36896 | tf_op jit(solution)/shard_map/ppermute | solution.py:250
  49.9 1.1 %collective-permute-done.9.right = f32[3,3,8,128]{3,2,1,0:T(8,128)S(1)} collective-permute-done((f32[3,3,8,128]{3,2,1,0:T(8,128)S(1)}, f32[3,3,8,128]{3,2,1,0:T(8,128)S(1)}, u32[]{:S(2)}, u32[]{:S(2)}) %collective-permute-start.9) | collective-permute-done | bytes 36896 | tf_op jit(solution)/shard_map/ppermute | solution.py:250
  51.1 3.0 %collective-permute-done.8.left = f32[3,3,8,128]{3,2,1,0:T(8,128)S(1)} collective-permute-done((f32[3,3,8,128]{3,2,1,0:T(8,128)S(1)}, f32[3,3,8,128]{3,2,1,0:T(8,128)S(1)}, u32[]{:S(2)}, u32[]{:S(2)}) %collective-permute-start.8) | collective-permute-done | bytes 36896 | tf_op jit(solution)/shard_map/ppermute | solution.py:250
  55.2 1.1 %collective-permute-done.11.right = f32[3,3,8,128]{3,2,1,0:T(8,128)S(1)} collective-permute-done((f32[3,3,8,128]{3,2,1,0:T(8,128)S(1)}, f32[3,3,8,128]{3,2,1,0:T(8,128)S(1)}, u32[]{:S(2)}, u32[]{:S(2)}) %collective-permute-start.11) | collective-permute-done | bytes 36896 | tf_op jit(solution)/shard_map/ppermute | solution.py:250
  56.4 3.0 %collective-permute-done.10.left = f32[3,3,8,128]{3,2,1,0:T(8,128)S(1)} collective-permute-done((f32[3,3,8,128]{3,2,1,0:T(8,128)S(1)}, f32[3,3,8,128]{3,2,1,0:T(8,128)S(1)}, u32[]{:S(2)}, u32[]{:S(2)}) %collective-permute-start.10) | collective-permute-done | bytes 36896 | tf_op jit(solution)/shard_map/ppermute | solution.py:250
  60.5 1.1 %collective-permute-done.13.right = f32[3,3,8,128]{3,2,1,0:T(8,128)S(1)} collective-permute-done((f32[3,3,8,128]{3,2,1,0:T(8,128)S(1)}, f32[3,3,8,128]{3,2,1,0:T(8,128)S(1)}, u32[]{:S(2)}, u32[]{:S(2)}) %collective-permute-start.13) | collective-permute-done | bytes 36896 | tf_op jit(solution)/shard_map/ppermute | solution.py:250
  61.7 3.0 %collective-permute-done.12.left = f32[3,3,8,128]{3,2,1,0:T(8,128)S(1)} collective-permute-done((f32[3,3,8,128]{3,2,1,0:T(8,128)S(1)}, f32[3,3,8,128]{3,2,1,0:T(8,128)S(1)}, u32[]{:S(2)}, u32[]{:S(2)}) %collective-permute-start.12) | collective-permute-done | bytes 36896 | tf_op jit(solution)/shard_map/ppermute | solution.py:250
  65.8 1.1 %collective-permute-done.15.right = f32[3,3,8,128]{3,2,1,0:T(8,128)S(1)} collective-permute-done((f32[3,3,8,128]{3,2,1,0:T(8,128)S(1)}, f32[3,3,8,128]{3,2,1,0:T(8,128)S(1)}, u32[]{:S(2)}, u32[]{:S(2)}) %collective-permute-start.15) | collective-permute-done | bytes 36896 | tf_op jit(solution)/shard_map/ppermute | solution.py:250
  67.0 3.0 %collective-permute-done.14.left = f32[3,3,8,128]{3,2,1,0:T(8,128)S(1)} collective-permute-done((f32[3,3,8,128]{3,2,1,0:T(8,128)S(1)}, f32[3,3,8,128]{3,2,1,0:T(8,128)S(1)}, u32[]{:S(2)}, u32[]{:S(2)}) %collective-permute-start.14) | collective-permute-done | bytes 36896 | tf_op jit(solution)/shard_map/ppermute | solution.py:250
  71.1 1.1 %collective-permute-done.17.right = f32[3,3,8,128]{3,2,1,0:T(8,128)S(1)} collective-permute-done((f32[3,3,8,128]{3,2,1,0:T(8,128)S(1)}, f32[3,3,8,128]{3,2,1,0:T(8,128)S(1)}, u32[]{:S(2)}, u32[]{:S(2)}) %collective-permute-start.17) | collective-permute-done | bytes 36896 | tf_op jit(solution)/shard_map/ppermute | solution.py:250
  72.3 3.0 %collective-permute-done.16.left = f32[3,3,8,128]{3,2,1,0:T(8,128)S(1)} collective-permute-done((f32[3,3,8,128]{3,2,1,0:T(8,128)S(1)}, f32[3,3,8,128]{3,2,1,0:T(8,128)S(1)}, u32[]{:S(2)}, u32[]{:S(2)}) %collective-permute-start.16) | collective-permute-done | bytes 36896 | tf_op jit(solution)/shard_map/ppermute | solution.py:250
  75.6 12.3 %all_to_all.11.sent = f32[16,3,8,128]{3,2,1,0:T(8,128)S(1)} all-to-all(f32[16,3,8,128]{3,2,1,0:T(8,128)S(1)} %shard_map.46), channel_id=1, replica_groups=mesh['tm'=16,'space'=32] {'tm'}, dimensions={0} | all-to-all | bytes 393216 | tf_op jit(solution)/shard_map/all_to_all | solution.py:287
  88.0 0.9 %shard_map.47 = f32[1,3,2,16,512]{4,3,2,1,0:T(8,128)} custom-call(f32[16,3,8,128]{3,2,1,0:T(8,128)S(1)} %all_to_all.11.sent), custom_call_target="tpu_custom_call" | custom-call | tf_op jit(solution)/shard_map/pallas_call | solution.py:254
  (36 shorter events, 9.6 us)
Async XLA Ops:
  0.0 1.0 %copy-start = (f32[1,3,2,16,512]{4,3,2,1,0:T(8,128)S(1)}, f32[1,3,2,16,512]{4,3,2,1,0:T(8,128)}, u32[]{:S(2)}) copy-start(f32[1,3,2,16,512]{4,3,2,1,0:T(8,128)} %param.3) | copy-start | bytes 589828
  1.2 16.0 %copy-start.1 = (f32[3]{0:T(128)S(1)}, f32[3]{0:T(128)}, u32[]{:S(2)}) copy-start(f32[3]{0:T(128)} %param.5) | copy-start | bytes 40
  1.3 12.8 %collective-permute-start.1 = (f32[4,2,2,8,512]{4,3,2,1,0:T(8,128)S(1)}, f32[4,2,2,8,512]{4,3,2,1,0:T(8,128)S(1)}, u32[]{:S(2)}, u32[]{:S(2)}) collective-permute-start(f32[4,2,2,8,512]{4,3,2,1,0:T(8,128)S(1)} %maximum_bitcast_fusion.own), channel_id=1, source_target_pairs={{1,0},{2,1},{3,2},{4,3},{5,4},{6,5},{7,6},{8,7},{9,8},{10,9},{11,1... | collective-permute-start | bytes 786440 | tf_op jit(solution)/shard_map/ppermute | solution.py:250
  10.2 7.0 %collective-permute-start = (f32[4,2,2,8,512]{4,3,2,1,0:T(8,128)S(1)}, f32[4,2,2,8,512]{4,3,2,1,0:T(8,128)S(1)}, u32[]{:S(2)}, u32[]{:S(2)}) collective-permute-start(f32[4,2,2,8,512]{4,3,2,1,0:T(8,128)S(1)} %maximum_bitcast_fusion.own), channel_id=1, source_target_pairs={{0,1},{1,2},{2,3},{3,4},{4,5},{5,6},{6,7},{7,8},{8,9},{9,10},{10,1... | collective-permute-start | bytes 786440 | tf_op jit(solution)/shard_map/ppermute | solution.py:250
  33.4 1.8 %collective-permute-start.3 = (f32[2,3,2,8,128]{4,3,2,1,0:T(8,128)S(1)}, f32[2,3,2,8,128]{4,3,2,1,0:T(8,128)S(1)}, u32[]{:S(2)}, u32[]{:S(2)}) collective-permute-start(f32[2,3,2,8,128]{4,3,2,1,0:T(8,128)S(1)} %slice.4.own), channel_id=1, source_target_pairs={{1,0},{2,1},{3,2},{4,3},{5,4},{6,5},{7,6},{8,7},{9,8},{10,9},{11,1... | collective-permute-start | bytes 147464 | tf_op jit(solution)/shard_map/ppermute | solution.py:250
  33.4 4.7 %collective-permute-start.2 = (f32[2,3,2,8,128]{4,3,2,1,0:T(8,128)S(1)}, f32[2,3,2,8,128]{4,3,2,1,0:T(8,128)S(1)}, u32[]{:S(2)}, u32[]{:S(2)}) collective-permute-start(f32[2,3,2,8,128]{4,3,2,1,0:T(8,128)S(1)} %slice.4.own), channel_id=1, source_target_pairs={{0,1},{1,2},{2,3},{3,4},{4,5},{5,6},{6,7},{7,8},{8,9},{9,10},{10,1... | collective-permute-start | bytes 147464 | tf_op jit(solution)/shard_map/ppermute | solution.py:250
  38.8 1.7 %collective-permute-start.5 = (f32[3,3,8,128]{3,2,1,0:T(8,128)S(1)}, f32[3,3,8,128]{3,2,1,0:T(8,128)S(1)}, u32[]{:S(2)}, u32[]{:S(2)}) collective-permute-start(f32[3,3,8,128]{3,2,1,0:T(8,128)S(1)} %get-tuple-element.27), channel_id=1, source_target_pairs={{1,0},{2,1},{3,2},{4,3},{5,4},{6,5},{7,6},{8,7},{9,8},{10,9},{11,1... | collective-permute-start | bytes 110600 | tf_op jit(solution)/shard_map/ppermute | solution.py:250
  38.8 4.6 %collective-permute-start.4 = (f32[3,3,8,128]{3,2,1,0:T(8,128)S(1)}, f32[3,3,8,128]{3,2,1,0:T(8,128)S(1)}, u32[]{:S(2)}, u32[]{:S(2)}) collective-permute-start(f32[3,3,8,128]{3,2,1,0:T(8,128)S(1)} %get-tuple-element.26.own), channel_id=1, source_target_pairs={{0,1},{1,2},{2,3},{3,4},{4,5},{5,6},{6,7},{7,8},{8,9},{9,10},{10,1... | collective-permute-start | bytes 110600 | tf_op jit(solution)/shard_map/ppermute | solution.py:250
  44.1 1.7 %collective-permute-start.7 = (f32[3,3,8,128]{3,2,1,0:T(8,128)S(1)}, f32[3,3,8,128]{3,2,1,0:T(8,128)S(1)}, u32[]{:S(2)}, u32[]{:S(2)}) collective-permute-start(f32[3,3,8,128]{3,2,1,0:T(8,128)S(1)} %get-tuple-element.29), channel_id=1, source_target_pairs={{1,0},{2,1},{3,2},{4,3},{5,4},{6,5},{7,6},{8,7},{9,8},{10,9},{11,1... | collective-permute-start | bytes 110600 | tf_op jit(solution)/shard_map/ppermute | solution.py:250
  44.1 4.6 %collective-permute-start.6 = (f32[3,3,8,128]{3,2,1,0:T(8,128)S(1)}, f32[3,3,8,128]{3,2,1,0:T(8,128)S(1)}, u32[]{:S(2)}, u32[]{:S(2)}) collective-permute-start(f32[3,3,8,128]{3,2,1,0:T(8,128)S(1)} %get-tuple-element.28.own), channel_id=1, source_target_pairs={{0,1},{1,2},{2,3},{3,4},{4,5},{5,6},{6,7},{7,8},{8,9},{9,10},{10,1... | collective-permute-start | bytes 110600 | tf_op jit(solution)/shard_map/ppermute | solution.py:250
  49.4 1.7 %collective-permute-start.9 = (f32[3,3,8,128]{3,2,1,0:T(8,128)S(1)}, f32[3,3,8,128]{3,2,1,0:T(8,128)S(1)}, u32[]{:S(2)}, u32[]{:S(2)}) collective-permute-start(f32[3,3,8,128]{3,2,1,0:T(8,128)S(1)} %get-tuple-element.31), channel_id=1, source_target_pairs={{1,0},{2,1},{3,2},{4,3},{5,4},{6,5},{7,6},{8,7},{9,8},{10,9},{11,1... | collective-permute-start | bytes 110600 | tf_op jit(solution)/shard_map/ppermute | solution.py:250
  49.4 4.6 %collective-permute-start.8 = (f32[3,3,8,128]{3,2,1,0:T(8,128)S(1)}, f32[3,3,8,128]{3,2,1,0:T(8,128)S(1)}, u32[]{:S(2)}, u32[]{:S(2)}) collective-permute-start(f32[3,3,8,128]{3,2,1,0:T(8,128)S(1)} %get-tuple-element.30.own), channel_id=1, source_target_pairs={{0,1},{1,2},{2,3},{3,4},{4,5},{5,6},{6,7},{7,8},{8,9},{9,10},{10,1... | collective-permute-start | bytes 110600 | tf_op jit(solution)/shard_map/ppermute | solution.py:250
  54.7 1.7 %collective-permute-start.11 = (f32[3,3,8,128]{3,2,1,0:T(8,128)S(1)}, f32[3,3,8,128]{3,2,1,0:T(8,128)S(1)}, u32[]{:S(2)}, u32[]{:S(2)}) collective-permute-start(f32[3,3,8,128]{3,2,1,0:T(8,128)S(1)} %get-tuple-element.33), channel_id=1, source_target_pairs={{1,0},{2,1},{3,2},{4,3},{5,4},{6,5},{7,6},{8,7},{9,8},{10,9},{11,1... | collective-permute-start | bytes 110600 | tf_op jit(solution)/shard_map/ppermute | solution.py:250
  54.7 4.6 %collective-permute-start.10 = (f32[3,3,8,128]{3,2,1,0:T(8,128)S(1)}, f32[3,3,8,128]{3,2,1,0:T(8,128)S(1)}, u32[]{:S(2)}, u32[]{:S(2)}) collective-permute-start(f32[3,3,8,128]{3,2,1,0:T(8,128)S(1)} %get-tuple-element.32.own), channel_id=1, source_target_pairs={{0,1},{1,2},{2,3},{3,4},{4,5},{5,6},{6,7},{7,8},{8,9},{9,10},{10,1... | collective-permute-start | bytes 110600 | tf_op jit(solution)/shard_map/ppermute | solution.py:250
  60.0 1.7 %collective-permute-start.13 = (f32[3,3,8,128]{3,2,1,0:T(8,128)S(1)}, f32[3,3,8,128]{3,2,1,0:T(8,128)S(1)}, u32[]{:S(2)}, u32[]{:S(2)}) collective-permute-start(f32[3,3,8,128]{3,2,1,0:T(8,128)S(1)} %get-tuple-element.35), channel_id=1, source_target_pairs={{1,0},{2,1},{3,2},{4,3},{5,4},{6,5},{7,6},{8,7},{9,8},{10,9},{11,1... | collective-permute-start | bytes 110600 | tf_op jit(solution)/shard_map/ppermute | solution.py:250
  60.0 4.6 %collective-permute-start.12 = (f32[3,3,8,128]{3,2,1,0:T(8,128)S(1)}, f32[3,3,8,128]{3,2,1,0:T(8,128)S(1)}, u32[]{:S(2)}, u32[]{:S(2)}) collective-permute-start(f32[3,3,8,128]{3,2,1,0:T(8,128)S(1)} %get-tuple-element.34.own), channel_id=1, source_target_pairs={{0,1},{1,2},{2,3},{3,4},{4,5},{5,6},{6,7},{7,8},{8,9},{9,10},{10,1... | collective-permute-start | bytes 110600 | tf_op jit(solution)/shard_map/ppermute | solution.py:250
  65.3 1.7 %collective-permute-start.15 = (f32[3,3,8,128]{3,2,1,0:T(8,128)S(1)}, f32[3,3,8,128]{3,2,1,0:T(8,128)S(1)}, u32[]{:S(2)}, u32[]{:S(2)}) collective-permute-start(f32[3,3,8,128]{3,2,1,0:T(8,128)S(1)} %get-tuple-element.37), channel_id=1, source_target_pairs={{1,0},{2,1},{3,2},{4,3},{5,4},{6,5},{7,6},{8,7},{9,8},{10,9},{11,1... | collective-permute-start | bytes 110600 | tf_op jit(solution)/shard_map/ppermute | solution.py:250
  65.3 4.6 %collective-permute-start.14 = (f32[3,3,8,128]{3,2,1,0:T(8,128)S(1)}, f32[3,3,8,128]{3,2,1,0:T(8,128)S(1)}, u32[]{:S(2)}, u32[]{:S(2)}) collective-permute-start(f32[3,3,8,128]{3,2,1,0:T(8,128)S(1)} %get-tuple-element.36.own), channel_id=1, source_target_pairs={{0,1},{1,2},{2,3},{3,4},{4,5},{5,6},{6,7},{7,8},{8,9},{9,10},{10,1... | collective-permute-start | bytes 110600 | tf_op jit(solution)/shard_map/ppermute | solution.py:250
  70.6 1.7 %collective-permute-start.17 = (f32[3,3,8,128]{3,2,1,0:T(8,128)S(1)}, f32[3,3,8,128]{3,2,1,0:T(8,128)S(1)}, u32[]{:S(2)}, u32[]{:S(2)}) collective-permute-start(f32[3,3,8,128]{3,2,1,0:T(8,128)S(1)} %get-tuple-element.39), channel_id=1, source_target_pairs={{1,0},{2,1},{3,2},{4,3},{5,4},{6,5},{7,6},{8,7},{9,8},{10,9},{11,1... | collective-permute-start | bytes 110600 | tf_op jit(solution)/shard_map/ppermute | solution.py:250
  70.6 4.6 %collective-permute-start.16 = (f32[3,3,8,128]{3,2,1,0:T(8,128)S(1)}, f32[3,3,8,128]{3,2,1,0:T(8,128)S(1)}, u32[]{:S(2)}, u32[]{:S(2)}) collective-permute-start(f32[3,3,8,128]{3,2,1,0:T(8,128)S(1)} %get-tuple-element.38.own), channel_id=1, source_target_pairs={{0,1},{1,2},{2,3},{3,4},{4,5},{5,6},{6,7},{7,8},{8,9},{9,10},{10,1... | collective-permute-start | bytes 110600 | tf_op jit(solution)/shard_map/ppermute | solution.py:250

commit v3 on v2

v3 whole, which is shorter than its diff:
```python
import functools

import jax
import jax.numpy as jnp
from jax import lax
from jax.experimental import pallas as pl
from jax.experimental.pallas import tpu as pltpu
from jax.sharding import PartitionSpec as P

DAMPING = 0.1
STEP = 0.02
COARSE = 2 * STEP
GAIN = -1.0 / (1.0 + DAMPING * DAMPING)
F32 = jnp.float32
VMEM = pl.BlockSpec(memory_space=pltpu.VMEM)


def near_odd(even_below, even_here):
    out = []
    for below, here in zip(even_below, even_here):
        pair = below + here
        pair = pair + pltpu.roll(pair, 1, axis=1)
        row = lax.broadcasted_iota(jnp.int32, pair.shape, 0)
        out.append(pair + jnp.where(row < 7, pltpu.roll(pair, 7, axis=0), 0.0))
    return out


def near_even(odd_here, odd_above):
    out = []
    for here, above in zip(odd_here, odd_above):
        pair = here + above
        pair = pair + pltpu.roll(pair, pair.shape[1] - 1, axis=1)
        row = lax.broadcasted_iota(jnp.int32, pair.shape, 0)
        out.append(pair + jnp.where(row > 0, pltpu.roll(pair, 1, axis=0), 0.0))
    return out


def cross(a, b):
    return [a[1] * b[2] - a[2] * b[1], a[2] * b[0] - a[0] * b[2], a[0] * b[1] - a[1] * b[0]]


def bare_rate(spin, near, twice_aniso, applied):
    field = [n + h for n, h in zip(near, applied)]
    field[2] = field[2] + twice_aniso * spin[2]
    turn = cross(spin, field)
    return cross(spin, [f + DAMPING * c for f, c in zip(field, turn)])


def rates(even, odd, aniso_even, aniso_odd, applied, evens, odds):
    rate_even = {x: bare_rate(even[x], near_even(odd[x], odd[x + 1]), aniso_even(x), applied) for x in evens}
    rate_odd = {x: bare_rate(odd[x], near_odd(even[x - 1], even[x]), aniso_odd(x), applied) for x in odds}
    return rate_even, rate_odd


def ahead(spins, rate, length):
    return {x: [s + (length * GAIN) * r for s, r in zip(spins[x], rate[x])] for x in rate}


def finish(spins, first, second, length, planes):
    return {
        x: [s + (0.5 * length * GAIN) * (f + g) for s, f, g in zip(spins[x], first[x], second[x])]
        for x in planes
    }


def heun(even, odd, aniso_even, aniso_odd, applied, length, low, high):
    evens, odds, inner = range(low, high), range(low + 1, high + 1), range(low + 1, high)
    first_e, first_o = rates(even, odd, aniso_even, aniso_odd, applied, evens, odds)
    pred_e, pred_o = ahead(even, first_e, length), ahead(odd, first_o, length)
    second_e, second_o = rates(pred_e, pred_o, aniso_even, aniso_odd, applied, inner, inner)
    return finish(even, first_e, second_e, length, inner), finish(odd, first_o, second_o, length, inner)


def lane_select(tile, low, high, a, b):
    lane = lax.broadcasted_iota(jnp.int32, (8, 128), 1) % tile
    return jnp.where((lane >= low) & (lane < high), a, b)


def tiles_of(wide):
    return [wide[:, 128 * q : 128 * (q + 1)] for q in range(wide.shape[1] // 128)]


def turn(x, by):
    by = by % x.shape[1]
    return pltpu.roll(x, by, axis=1) if by else x


def laid(own, left, right):
    def load(comp, plane, parity):
        ref, at = (left, plane + 2) if plane < 0 else (own, plane) if plane < 2 else (right, plane - 2)
        return ref[comp, at, parity]

    return load


def prologue(own, left, right, field, payload):
    applied = [jnp.concatenate([field[c]] * (own.shape[-1] // 128), axis=1) for c in range(3)]
    load = laid(own, left, right)

    planes = range(-2, 4)
    even = {x: [load(c, x, 0) for c in range(3)] for x in planes}
    odd = {x: [load(c, x, 1) for c in range(3)] for x in planes}

    def aniso_even(x):
        return 2.0 * load(3, x, 0)

    def aniso_odd(x):
        return 2.0 * load(3, x, 1)

    sides = (aniso_even, aniso_odd, applied)
    first_e, first_o = rates(even, odd, *sides, range(-2, 3), range(-1, 4))
    pred_e, pred_o = ahead(even, first_e, STEP), ahead(odd, first_o, STEP)
    second_e, second_o = rates(pred_e, pred_o, *sides, range(-1, 3), range(-1, 3))
    fine_e = finish(even, first_e, second_e, STEP, range(-1, 3))
    fine_o = finish(odd, first_o, second_o, STEP, range(-1, 3))
    fine_e, fine_o = heun(fine_e, fine_o, *sides, STEP, -1, 2)
    pred_e, pred_o = ahead(even, first_e, COARSE), ahead(odd, first_o, COARSE)
    second_e, second_o = rates(pred_e, pred_o, *sides, range(2), range(2))
    coarse_e = finish(even, first_e, second_e, COARSE, range(2))
    coarse_o = finish(odd, first_o, second_o, COARSE, range(2))

    keep = jnp.where(lax.axis_index("tm") == 0, 0.0, 1.0).astype(F32)
    for comp in range(3):
        for x in range(2):
            evens = tiles_of(fine_e[x][comp] - keep * coarse_e[x][comp])
            odds = [turn(t, 64) for t in tiles_of(fine_o[x][comp] - keep * coarse_o[x][comp])]
            for at in range(payload.shape[0]):
                payload[at, x, comp] = cut(evens, odds, at)


def cut(evens, odds, at):
    q, part = divmod(at, 4)
    if part == 0:
        return lanes(48, lanes(64, lanes(112, evens[q - 1], odds[q]), odds[q - 1]), evens[q])
    if part == 3:
        after = (q + 1) % len(evens)
        return lanes(16, lanes(64, lanes(80, evens[q], odds[after]), odds[q]), evens[after])
    first = 32 * part - 16
    return lanes(first, lanes(first + 64, odds[q], evens[q]), odds[q])


def lanes(count, here, before):
    return jnp.where(lax.broadcasted_iota(jnp.int32, (8, 128), 1) < count, before, here)


def logical_lane(row):
    return (lax.broadcasted_iota(jnp.int32, (8, 128), 1) + 16 - 32 * (row % 4)) & 127


def window(own, left, right, windows):
    load = laid(own, left, right)
    row = lax.axis_index("tm")
    windows[6] = logical_lane(row).astype(F32)
    for at in range(own.shape[-1] // 32):

        @pl.when(row == at)
        def _():
            for k in range(6):
                even, odd = (tiles_of(2.0 * load(3, k - 2, parity)) for parity in range(2))
                windows[k] = cut(even, [turn(t, 64) for t in odd], at)


def near_pair(pair, is_even):
    row = lax.broadcasted_iota(jnp.int32, (8, 128), 0)
    lane = lax.broadcasted_iota(jnp.int32, (8, 128), 1)
    source = (lane + jnp.where(is_even, 65, 63)) & 127
    out = []
    for p in pair:
        near = turn(p, 64) + jnp.take_along_axis(p, source, axis=1)
        lower = jnp.where(is_even & (row > 0), pltpu.roll(near, 1, axis=0), 0.0)
        out.append(near + jnp.where(~is_even & (row < 7), pltpu.roll(near, 7, axis=0), lower))
    return out


def pair_heun(spins, aniso, applied, is_even, length, low, high):
    def pick(a, b):
        return [jnp.where(is_even, p, r) for p, r in zip(a, b)]

    def plus(a, b):
        return [p + r for p, r in zip(a, b)]

    def rate(spins, x):
        pair = plus(spins[x], pick(spins[x - 1], spins[x + 1]))
        return bare_rate(spins[x], near_pair(pair, is_even), aniso(x), applied)

    inner = range(low + 1, high)
    first = {x: rate(spins, x) for x in inner}
    pair = pick(plus(spins[high - 1], spins[high]), plus(spins[low], spins[low + 1]))
    edge = pick(spins[low], spins[high])
    edge_aniso = jnp.where(is_even, aniso(low), aniso(high))
    edge_rate = bare_rate(edge, near_pair(pair, is_even), edge_aniso, applied)
    predicted = ahead(spins, first, length)
    predicted[low] = predicted[high] = ahead({0: edge}, {0: edge_rate}, length)[0]
    second = {x: rate(predicted, x) for x in inner}
    return finish(spins, first, second, length, inner)


def emit(ref, at, below, above, logical):
    inside = (logical & 63 >= 16) & (logical & 63 < 48)
    for c in range(3):
        ref[at, c] = jnp.where(inside, below[c], turn(above[c], 32))


def triple(ref, *at):
    return [ref[(*at, c)] for c in range(3)]


def chain(block, blocks, own, left, right, corr, windows, field, *rest):
    applied = [field[c] for c in range(3)]
    is_even = windows[6] < 64.0
    first_slice = 2 * block + 1
    start, last = block == 0, block == blocks - 1

    if last:
        below, above = own
        spins = {-1: triple(left, 0), 0: triple(below, 0), 1: triple(above, 0), 2: triple(right, 0)}
    elif start:
        spins = {base + k: triple(ref, 0, k) for ref, base in ((left, -2), (own, 0), (right, 2)) for k in range(2)}
        extra = {-1: triple(left, 1, 1), 2: triple(right, 1, 0)}
    else:
        spins = {base + k: triple(ref, k) for ref, base in ((left, -2), (own, 0), (right, 2)) for k in range(2)}
        extra = {-1: triple(left, 2), 2: triple(right, 2)}

    def added(spins, extra):
        return {x: [s + e for s, e in zip(spins[x], extra[x])] for x in spins}

    def aniso(x):
        return windows[x + 2]

    reach = (-1, 2) if last else (-2, 3)
    inside = {x: triple(corr, first_slice, x) for x in range(2)}
    ends = pair_heun(spins, aniso, applied, is_even, COARSE, *reach)
    if last:
        earlier, sent = rest
        ends = added(ends, inside)
        emit(sent, sent.shape[0] - 1, ends[0], ends[1], windows[6].astype(jnp.int32))
        return

    up, down, middle = rest
    ends = added(ends, inside | extra)
    for x in range(2):
        for c in range(3):
            middle[x, c] = ends[x][c]
    inside = {x: triple(corr, first_slice + 1, x) for x in range(2)}
    ends = added(pair_heun(ends, aniso, applied, is_even, COARSE, -1, 2), inside)
    for c in range(3):
        if block == blocks - 2:
            up[0, c], down[0, c] = ends[1][c], ends[0][c]
        else:
            for x in range(2):
                up[x, c] = down[x, c] = ends[x][c]
            up[2, c] = corr[first_slice + 2, 1, c]
            down[2, c] = corr[first_slice + 2, 0, c]


def final(block, blocks, below, above, *rest):
    chain(block, blocks, (below, above), *rest)


def pack(corr, windows, below, above, *rest):
    *kept, sent = rest
    logical = windows[6].astype(jnp.int32)
    emit(sent, 0, triple(corr, 0, 0), triple(corr, 0, 1), logical)
    for k, ref in enumerate(kept):
        emit(sent, k + 1, triple(ref, 0), triple(ref, 1), logical)
    emit(sent, len(kept) + 1, triple(below, 0), triple(above, 0), logical)


def assemble(sent, out, layers):
    for comp in range(3):
        for q in range(layers.shape[2]):
            tiles = [sent[4 * q + i, comp] for i in range(4)]
            for k in range(4):
                whole = tiles[0]
                for i in range(1, 4):
                    at = 32 * ((k + i) % 4)
                    whole = lane_select(128, at, at + 32, tiles[i], whole)
                layers[comp, k % 2, q, pl.ds(k // 2, 8, stride=2), :] = turn(whole, -32 * k)
            out[0, comp, :, :, 128 * q : 128 * (q + 1)] = layers[comp, :, q]


def both_sides(to_above, to_below):
    count = lax.axis_size("space")
    up = [(i, (i + 1) % count) for i in range(count)]
    down = [(j, i) for i, j in up]
    return lax.ppermute(to_above, "space", up), lax.ppermute(to_below, "space", down)


def call(kernel, shapes, *args, scratch=(), **more):
    return pl.pallas_call(
        kernel,
        out_shape=[jax.ShapeDtypeStruct(s, F32) for s in shapes],
        in_specs=[VMEM] * len(args),
        out_specs=[VMEM] * len(shapes),
        scratch_shapes=[pltpu.VMEM(s, F32) for s in scratch],
        **more,
        compiler_params=pltpu.CompilerParams(vmem_limit_bytes=32 * 1024 * 1024),
    )(*args)


def per_device(starts, anisotropy, applied):
    slices = lax.axis_size("tm")
    width = starts.shape[-1]
    own = jnp.concatenate([starts[0], anisotropy[None]], axis=0)
    own = own.reshape(4, 2, 8, 2, width).swapaxes(2, 3)
    field = jnp.broadcast_to(applied[:, None, None], (3, 8, 128))
    slabs = (own, *both_sides(own, own))
    (payload,) = call(prologue, [(slices, 2, 3, 8, 128)], *slabs, field)
    (windows,) = call(window, [(7, 8, 128)], *slabs)
    corr = lax.all_to_all(payload, "tm", 0, 0, tiled=True)
    up = down = corr[:2]
    kept = []
    blocks = slices // 2
    for block in range(blocks - 1):
        kernel = functools.partial(chain, block, blocks)
        ahead_of_last = block == blocks - 2
        shapes = [(1 if ahead_of_last else 3, 3, 8, 128)] * 2 + [(2, 3, 8, 128)]
        up, down, middle = call(kernel, shapes, up, *both_sides(up, down), corr, windows, field)
        kept += [middle] if ahead_of_last else [middle, up]
    left, right = both_sides(up, down)
    (sent,) = call(pack, [(slices, 3, 8, 128)], corr, windows, down, up, *kept)
    kernel = functools.partial(final, blocks - 1, blocks)
    (sent,) = call(
        kernel, [sent.shape], down, up, left, right, corr, windows, field, sent, input_output_aliases={7: 0}
    )
    sent = lax.all_to_all(sent, "tm", 0, 0, tiled=True)
    (out,) = call(assemble, [starts.shape], sent, scratch=[(3, 2, width // 128, 16, 128)])
    return out


def solution(mesh):
    placed = (P("tm", None, "space", None, None), P("space", None, None), P())
    return jax.shard_map(
        per_device,
        mesh=mesh,
        in_specs=placed,
        out_specs=P("tm", None, "space", None, None),
        check_vma=False,
    )
```

time: 89.1 us -> 86.5 us (0.971)
  Pallas kernels: 7.66 us -> 5.43 us
    pallas_call x11 -> x12, Pallas kernels: 7.66 us -> 5.43 us  [call(): pl.pallas_call(kernel, out_shape=[jax.ShapeDtypeStruct(s, F32) for s in s...]
where the time goes in v3:
time: 86.5 us; the launch traced here: 86.3 us
  waiting for transfers between devices  39.5 us (46%)
  blocking collectives  26.8 us (31%)
  starting transfers between devices  13.1 us (15%)
  Pallas kernels  5.43 us (6%)
  local copies, waits for them, and re-layouts  1.26 us (1%)
    ppermute x9, waiting for transfers between devices, both_sides(): lax.ppermute(to_above, 'space', up)  26.9 us
    all_to_all x1, blocking collectives, per_device(): corr = lax.all_to_all(payload, 'tm', 0, 0, tiled=True)  14.5 us
    ppermute x9, waiting for transfers between devices, both_sides(): lax.ppermute(to_below, 'space', down)  12.6 us
    all_to_all x1, blocking collectives, per_device(): sent = lax.all_to_all(sent, 'tm', 0, 0, tiled=True)  12.3 us
    ppermute x9, starting transfers between devices, both_sides(): lax.ppermute(to_below, 'space', down)  9.08 us
    pallas_call x12, Pallas kernels, call(): pl.pallas_call(kernel, out_shape=[jax.ShapeDtypeStruct(s, F32) for s in s...  5.43 us
    ppermute x9, starting transfers between devices, both_sides(): lax.ppermute(to_above, 'space', up)  3.99 us
  transfers between devices with their start and end apart: 18, of which 18 were waited for; matrix products, arithmetic and copies ran while one was open for 0% of the time, Pallas kernels for 0%

profile of v3, /device:TPU:2, one launch (start us, length us, event | category | flops | bytes accessed | tf_op | source)
XLA Modules:
  0.0 86.3 jit_solution(15234437832548191414)
XLA Ops:
  0.0 0.9 %copy.6 = f32[2,16,512]{2,0,1:T(2,128)S(1)} copy(f32[2,16,512]{2,1,0:T(8,128)} %param.4) | data formatting | bytes 131072 | tf_op args[1]
  1.3 8.9 %collective-permute-start.1 = (f32[4,2,2,8,512]{4,3,2,1,0:T(8,128)S(1)}, f32[4,2,2,8,512]{4,3,2,1,0:T(8,128)S(1)}, u32[]{:S(2)}, u32[]{:S(2)}) collective-permute-start(f32[4,2,2,8,512]{4,3,2,1,0:T(8,128)S(1)} %maximum_bitcast_fusion.own), channel_id=1, source_target_pairs={{1,0},{2,1},{3,2},{4,3},{5,4},{6,5},{7,6},{8,7},{9,8},{10,9},{11,1... | collective-permute-start | bytes 786440 | tf_op jit(solution)/shard_map/ppermute | solution.py:286
  10.2 3.9 %collective-permute-done.1.right = f32[4,2,2,8,512]{4,3,2,1,0:T(8,128)S(1)} collective-permute-done((f32[4,2,2,8,512]{4,3,2,1,0:T(8,128)S(1)}, f32[4,2,2,8,512]{4,3,2,1,0:T(8,128)S(1)}, u32[]{:S(2)}, u32[]{:S(2)}) %collective-permute-start.1) | collective-permute-done | bytes 262176 | tf_op jit(solution)/shard_map/ppermute | solution.py:286
  14.1 3.1 %collective-permute-done.left = f32[4,2,2,8,512]{4,3,2,1,0:T(8,128)S(1)} collective-permute-done((f32[4,2,2,8,512]{4,3,2,1,0:T(8,128)S(1)}, f32[4,2,2,8,512]{4,3,2,1,0:T(8,128)S(1)}, u32[]{:S(2)}, u32[]{:S(2)}) %collective-permute-start) | collective-permute-done | bytes 262176 | tf_op jit(solution)/shard_map/ppermute | solution.py:286
  17.3 1.1 %shard_map.37 = f32[16,2,3,8,128]{4,3,2,1,0:T(8,128)S(1)} custom-call(f32[4,2,2,8,512]{4,3,2,1,0:T(8,128)S(1)} %maximum_bitcast_fusion.own, f32[4,2,2,8,512]{4,3,2,1,0:T(8,128)S(1)} %collective-permute-done.left, f32[4,2,2,8,512]{4,3,2,1,0:T(8,128)S(1)} %collective-permute-done.1.right, f32[3,8,128]{2,1,0:T(8,128)S(1)} %broadcast_in_dim.2.field.rest_4_), custom_call_target="tpu_custom_call" | custom-call | tf_op jit(solution)/shard_map/pallas_call | solution.py:290
  18.4 14.5 %all_to_all.10.corr.rest_2_ = f32[16,2,3,8,128]{4,3,2,1,0:T(8,128)S(1)} all-to-all(f32[16,2,3,8,128]{4,3,2,1,0:T(8,128)S(1)} %shard_map.37), channel_id=1, replica_groups=mesh['tm'=16,'space'=32] {'tm'}, dimensions={0} | all-to-all | bytes 786432 | tf_op jit(solution)/shard_map/all_to_all | solution.py:310
  33.6 1.1 %collective-permute-done.3.right = f32[2,2,3,8,128]{4,3,2,1,0:T(8,128)S(1)} collective-permute-done((f32[2,2,3,8,128]{4,3,2,1,0:T(8,128)S(1)}, f32[2,2,3,8,128]{4,3,2,1,0:T(8,128)S(1)}, u32[]{:S(2)}, u32[]{:S(2)}) %collective-permute-start.3) | collective-permute-done | bytes 49184 | tf_op jit(solution)/shard_map/ppermute | solution.py:286
  34.7 3.0 %collective-permute-done.2.left = f32[2,2,3,8,128]{4,3,2,1,0:T(8,128)S(1)} collective-permute-done((f32[2,2,3,8,128]{4,3,2,1,0:T(8,128)S(1)}, f32[2,2,3,8,128]{4,3,2,1,0:T(8,128)S(1)}, u32[]{:S(2)}, u32[]{:S(2)}) %collective-permute-start.2) | collective-permute-done | bytes 49184 | tf_op jit(solution)/shard_map/ppermute | solution.py:286
  38.6 1.1 %collective-permute-done.5.right = f32[3,3,8,128]{3,2,1,0:T(8,128)S(1)} collective-permute-done((f32[3,3,8,128]{3,2,1,0:T(8,128)S(1)}, f32[3,3,8,128]{3,2,1,0:T(8,128)S(1)}, u32[]{:S(2)}, u32[]{:S(2)}) %collective-permute-start.5) | collective-permute-done | bytes 36896 | tf_op jit(solution)/shard_map/ppermute | solution.py:286
  39.8 3.0 %collective-permute-done.4.left = f32[3,3,8,128]{3,2,1,0:T(8,128)S(1)} collective-permute-done((f32[3,3,8,128]{3,2,1,0:T(8,128)S(1)}, f32[3,3,8,128]{3,2,1,0:T(8,128)S(1)}, u32[]{:S(2)}, u32[]{:S(2)}) %collective-permute-start.4) | collective-permute-done | bytes 36896 | tf_op jit(solution)/shard_map/ppermute | solution.py:286
  43.7 1.1 %collective-permute-done.7.right = f32[3,3,8,128]{3,2,1,0:T(8,128)S(1)} collective-permute-done((f32[3,3,8,128]{3,2,1,0:T(8,128)S(1)}, f32[3,3,8,128]{3,2,1,0:T(8,128)S(1)}, u32[]{:S(2)}, u32[]{:S(2)}) %collective-permute-start.7) | collective-permute-done | bytes 36896 | tf_op jit(solution)/shard_map/ppermute | solution.py:286
  44.8 3.0 %collective-permute-done.6.left = f32[3,3,8,128]{3,2,1,0:T(8,128)S(1)} collective-permute-done((f32[3,3,8,128]{3,2,1,0:T(8,128)S(1)}, f32[3,3,8,128]{3,2,1,0:T(8,128)S(1)}, u32[]{:S(2)}, u32[]{:S(2)}) %collective-permute-start.6) | collective-permute-done | bytes 36896 | tf_op jit(solution)/shard_map/ppermute | solution.py:286
  48.8 1.1 %collective-permute-done.9.right = f32[3,3,8,128]{3,2,1,0:T(8,128)S(1)} collective-permute-done((f32[3,3,8,128]{3,2,1,0:T(8,128)S(1)}, f32[3,3,8,128]{3,2,1,0:T(8,128)S(1)}, u32[]{:S(2)}, u32[]{:S(2)}) %collective-permute-start.9) | collective-permute-done | bytes 36896 | tf_op jit(solution)/shard_map/ppermute | solution.py:286
  49.9 3.0 %collective-permute-done.8.left = f32[3,3,8,128]{3,2,1,0:T(8,128)S(1)} collective-permute-done((f32[3,3,8,128]{3,2,1,0:T(8,128)S(1)}, f32[3,3,8,128]{3,2,1,0:T(8,128)S(1)}, u32[]{:S(2)}, u32[]{:S(2)}) %collective-permute-start.8) | collective-permute-done | bytes 36896 | tf_op jit(solution)/shard_map/ppermute | solution.py:286
  53.8 1.1 %collective-permute-done.11.right = f32[3,3,8,128]{3,2,1,0:T(8,128)S(1)} collective-permute-done((f32[3,3,8,128]{3,2,1,0:T(8,128)S(1)}, f32[3,3,8,128]{3,2,1,0:T(8,128)S(1)}, u32[]{:S(2)}, u32[]{:S(2)}) %collective-permute-start.11) | collective-permute-done | bytes 36896 | tf_op jit(solution)/shard_map/ppermute | solution.py:286
  55.0 3.0 %collective-permute-done.10.left = f32[3,3,8,128]{3,2,1,0:T(8,128)S(1)} collective-permute-done((f32[3,3,8,128]{3,2,1,0:T(8,128)S(1)}, f32[3,3,8,128]{3,2,1,0:T(8,128)S(1)}, u32[]{:S(2)}, u32[]{:S(2)}) %collective-permute-start.10) | collective-permute-done | bytes 36896 | tf_op jit(solution)/shard_map/ppermute | solution.py:286
  58.9 1.1 %collective-permute-done.13.right = f32[3,3,8,128]{3,2,1,0:T(8,128)S(1)} collective-permute-done((f32[3,3,8,128]{3,2,1,0:T(8,128)S(1)}, f32[3,3,8,128]{3,2,1,0:T(8,128)S(1)}, u32[]{:S(2)}, u32[]{:S(2)}) %collective-permute-start.13) | collective-permute-done | bytes 36896 | tf_op jit(solution)/shard_map/ppermute | solution.py:286
  60.0 3.0 %collective-permute-done.12.left = f32[3,3,8,128]{3,2,1,0:T(8,128)S(1)} collective-permute-done((f32[3,3,8,128]{3,2,1,0:T(8,128)S(1)}, f32[3,3,8,128]{3,2,1,0:T(8,128)S(1)}, u32[]{:S(2)}, u32[]{:S(2)}) %collective-permute-start.12) | collective-permute-done | bytes 36896 | tf_op jit(solution)/shard_map/ppermute | solution.py:286
  64.0 1.1 %collective-permute-done.15.right = f32[3,3,8,128]{3,2,1,0:T(8,128)S(1)} collective-permute-done((f32[3,3,8,128]{3,2,1,0:T(8,128)S(1)}, f32[3,3,8,128]{3,2,1,0:T(8,128)S(1)}, u32[]{:S(2)}, u32[]{:S(2)}) %collective-permute-start.15) | collective-permute-done | bytes 36896 | tf_op jit(solution)/shard_map/ppermute | solution.py:286
  65.1 3.0 %collective-permute-done.14.left = f32[3,3,8,128]{3,2,1,0:T(8,128)S(1)} collective-permute-done((f32[3,3,8,128]{3,2,1,0:T(8,128)S(1)}, f32[3,3,8,128]{3,2,1,0:T(8,128)S(1)}, u32[]{:S(2)}, u32[]{:S(2)}) %collective-permute-start.14) | collective-permute-done | bytes 36896 | tf_op jit(solution)/shard_map/ppermute | solution.py:286
  69.2 0.8 collective-permute-done.17.rest_1_
  69.9 2.9 %collective-permute-done.16.rest_0_ = f32[1,3,8,128]{3,2,1,0:T(8,128)S(1)} collective-permute-done((f32[1,3,8,128]{3,2,1,0:T(8,128)S(1)}, f32[1,3,8,128]{3,2,1,0:T(8,128)S(1)}, u32[]{:S(2)}, u32[]{:S(2)}) %collective-permute-start.16) | collective-permute-done | bytes 12320 | tf_op jit(solution)/shard_map/ppermute | solution.py:286
  73.1 12.3 %all_to_all.11.sent = f32[16,3,8,128]{3,2,1,0:T(8,128)S(1)} all-to-all(f32[16,3,8,128]{3,2,1,0:T(8,128)S(1)} %shard_map.47), channel_id=1, replica_groups=mesh['tm'=16,'space'=32] {'tm'}, dimensions={0} | all-to-all | bytes 393216 | tf_op jit(solution)/shard_map/all_to_all | solution.py:326
  85.5 0.8 shard_map.48
  (37 shorter events, 7.9 us)
Async XLA Ops:
  0.0 1.0 %copy-start = (f32[1,3,2,16,512]{4,3,2,1,0:T(8,128)S(1)}, f32[1,3,2,16,512]{4,3,2,1,0:T(8,128)}, u32[]{:S(2)}) copy-start(f32[1,3,2,16,512]{4,3,2,1,0:T(8,128)} %param.3) | copy-start | bytes 589828
  1.2 16.0 %copy-start.1 = (f32[3]{0:T(128)S(1)}, f32[3]{0:T(128)}, u32[]{:S(2)}) copy-start(f32[3]{0:T(128)} %param.5) | copy-start | bytes 40
  1.3 12.8 %collective-permute-start.1 = (f32[4,2,2,8,512]{4,3,2,1,0:T(8,128)S(1)}, f32[4,2,2,8,512]{4,3,2,1,0:T(8,128)S(1)}, u32[]{:S(2)}, u32[]{:S(2)}) collective-permute-start(f32[4,2,2,8,512]{4,3,2,1,0:T(8,128)S(1)} %maximum_bitcast_fusion.own), channel_id=1, source_target_pairs={{1,0},{2,1},{3,2},{4,3},{5,4},{6,5},{7,6},{8,7},{9,8},{10,9},{11,1... | collective-permute-start | bytes 786440 | tf_op jit(solution)/shard_map/ppermute | solution.py:286
  10.2 7.0 %collective-permute-start = (f32[4,2,2,8,512]{4,3,2,1,0:T(8,128)S(1)}, f32[4,2,2,8,512]{4,3,2,1,0:T(8,128)S(1)}, u32[]{:S(2)}, u32[]{:S(2)}) collective-permute-start(f32[4,2,2,8,512]{4,3,2,1,0:T(8,128)S(1)} %maximum_bitcast_fusion.own), channel_id=1, source_target_pairs={{0,1},{1,2},{2,3},{3,4},{4,5},{5,6},{6,7},{7,8},{8,9},{9,10},{10,1... | collective-permute-start | bytes 786440 | tf_op jit(solution)/shard_map/ppermute | solution.py:286
  33.0 1.8 %collective-permute-start.3 = (f32[2,2,3,8,128]{4,3,2,1,0:T(8,128)S(1)}, f32[2,2,3,8,128]{4,3,2,1,0:T(8,128)S(1)}, u32[]{:S(2)}, u32[]{:S(2)}) collective-permute-start(f32[2,2,3,8,128]{4,3,2,1,0:T(8,128)S(1)} %slice.4.own), channel_id=1, source_target_pairs={{1,0},{2,1},{3,2},{4,3},{5,4},{6,5},{7,6},{8,7},{9,8},{10,9},{11,1... | collective-permute-start | bytes 147464 | tf_op jit(solution)/shard_map/ppermute | solution.py:286
  33.0 4.7 %collective-permute-start.2 = (f32[2,2,3,8,128]{4,3,2,1,0:T(8,128)S(1)}, f32[2,2,3,8,128]{4,3,2,1,0:T(8,128)S(1)}, u32[]{:S(2)}, u32[]{:S(2)}) collective-permute-start(f32[2,2,3,8,128]{4,3,2,1,0:T(8,128)S(1)} %slice.4.own), channel_id=1, source_target_pairs={{0,1},{1,2},{2,3},{3,4},{4,5},{5,6},{6,7},{7,8},{8,9},{9,10},{10,1... | collective-permute-start | bytes 147464 | tf_op jit(solution)/shard_map/ppermute | solution.py:286
  38.1 1.7 %collective-permute-start.5 = (f32[3,3,8,128]{3,2,1,0:T(8,128)S(1)}, f32[3,3,8,128]{3,2,1,0:T(8,128)S(1)}, u32[]{:S(2)}, u32[]{:S(2)}) collective-permute-start(f32[3,3,8,128]{3,2,1,0:T(8,128)S(1)} %get-tuple-element.27), channel_id=1, source_target_pairs={{1,0},{2,1},{3,2},{4,3},{5,4},{6,5},{7,6},{8,7},{9,8},{10,9},{11,1... | collective-permute-start | bytes 110600 | tf_op jit(solution)/shard_map/ppermute | solution.py:286
  38.2 4.6 %collective-permute-start.4 = (f32[3,3,8,128]{3,2,1,0:T(8,128)S(1)}, f32[3,3,8,128]{3,2,1,0:T(8,128)S(1)}, u32[]{:S(2)}, u32[]{:S(2)}) collective-permute-start(f32[3,3,8,128]{3,2,1,0:T(8,128)S(1)} %get-tuple-element.26.own.rest_1_), channel_id=1, source_target_pairs={{0,1},{1,2},{2,3},{3,4},{4,5},{5,6},{6,7},{7,8},{8,9},{9,10},{10,1... | collective-permute-start | bytes 110600 | tf_op jit(solution)/shard_map/ppermute | solution.py:286
  43.2 1.7 %collective-permute-start.7 = (f32[3,3,8,128]{3,2,1,0:T(8,128)S(1)}, f32[3,3,8,128]{3,2,1,0:T(8,128)S(1)}, u32[]{:S(2)}, u32[]{:S(2)}) collective-permute-start(f32[3,3,8,128]{3,2,1,0:T(8,128)S(1)} %get-tuple-element.29), channel_id=1, source_target_pairs={{1,0},{2,1},{3,2},{4,3},{5,4},{6,5},{7,6},{8,7},{9,8},{10,9},{11,1... | collective-permute-start | bytes 110600 | tf_op jit(solution)/shard_map/ppermute | solution.py:286
  43.2 4.6 %collective-permute-start.6 = (f32[3,3,8,128]{3,2,1,0:T(8,128)S(1)}, f32[3,3,8,128]{3,2,1,0:T(8,128)S(1)}, u32[]{:S(2)}, u32[]{:S(2)}) collective-permute-start(f32[3,3,8,128]{3,2,1,0:T(8,128)S(1)} %get-tuple-element.28.own.rest_3_), channel_id=1, source_target_pairs={{0,1},{1,2},{2,3},{3,4},{4,5},{5,6},{6,7},{7,8},{8,9},{9,10},{10,1... | collective-permute-start | bytes 110600 | tf_op jit(solution)/shard_map/ppermute | solution.py:286
  48.3 1.7 %collective-permute-start.9 = (f32[3,3,8,128]{3,2,1,0:T(8,128)S(1)}, f32[3,3,8,128]{3,2,1,0:T(8,128)S(1)}, u32[]{:S(2)}, u32[]{:S(2)}) collective-permute-start(f32[3,3,8,128]{3,2,1,0:T(8,128)S(1)} %get-tuple-element.31), channel_id=1, source_target_pairs={{1,0},{2,1},{3,2},{4,3},{5,4},{6,5},{7,6},{8,7},{9,8},{10,9},{11,1... | collective-permute-start | bytes 110600 | tf_op jit(solution)/shard_map/ppermute | solution.py:286
  48.3 4.6 %collective-permute-start.8 = (f32[3,3,8,128]{3,2,1,0:T(8,128)S(1)}, f32[3,3,8,128]{3,2,1,0:T(8,128)S(1)}, u32[]{:S(2)}, u32[]{:S(2)}) collective-permute-start(f32[3,3,8,128]{3,2,1,0:T(8,128)S(1)} %get-tuple-element.30.own.rest_5_), channel_id=1, source_target_pairs={{0,1},{1,2},{2,3},{3,4},{4,5},{5,6},{6,7},{7,8},{8,9},{9,10},{10,1... | collective-permute-start | bytes 110600 | tf_op jit(solution)/shard_map/ppermute | solution.py:286
  53.3 1.7 %collective-permute-start.11 = (f32[3,3,8,128]{3,2,1,0:T(8,128)S(1)}, f32[3,3,8,128]{3,2,1,0:T(8,128)S(1)}, u32[]{:S(2)}, u32[]{:S(2)}) collective-permute-start(f32[3,3,8,128]{3,2,1,0:T(8,128)S(1)} %get-tuple-element.33), channel_id=1, source_target_pairs={{1,0},{2,1},{3,2},{4,3},{5,4},{6,5},{7,6},{8,7},{9,8},{10,9},{11,1... | collective-permute-start | bytes 110600 | tf_op jit(solution)/shard_map/ppermute | solution.py:286
  53.3 4.6 %collective-permute-start.10 = (f32[3,3,8,128]{3,2,1,0:T(8,128)S(1)}, f32[3,3,8,128]{3,2,1,0:T(8,128)S(1)}, u32[]{:S(2)}, u32[]{:S(2)}) collective-permute-start(f32[3,3,8,128]{3,2,1,0:T(8,128)S(1)} %get-tuple-element.32.own.rest_7_), channel_id=1, source_target_pairs={{0,1},{1,2},{2,3},{3,4},{4,5},{5,6},{6,7},{7,8},{8,9},{9,10},{10,1... | collective-permute-start | bytes 110600 | tf_op jit(solution)/shard_map/ppermute | solution.py:286
  58.4 1.7 %collective-permute-start.13 = (f32[3,3,8,128]{3,2,1,0:T(8,128)S(1)}, f32[3,3,8,128]{3,2,1,0:T(8,128)S(1)}, u32[]{:S(2)}, u32[]{:S(2)}) collective-permute-start(f32[3,3,8,128]{3,2,1,0:T(8,128)S(1)} %get-tuple-element.35), channel_id=1, source_target_pairs={{1,0},{2,1},{3,2},{4,3},{5,4},{6,5},{7,6},{8,7},{9,8},{10,9},{11,1... | collective-permute-start | bytes 110600 | tf_op jit(solution)/shard_map/ppermute | solution.py:286
  58.4 4.6 %collective-permute-start.12 = (f32[3,3,8,128]{3,2,1,0:T(8,128)S(1)}, f32[3,3,8,128]{3,2,1,0:T(8,128)S(1)}, u32[]{:S(2)}, u32[]{:S(2)}) collective-permute-start(f32[3,3,8,128]{3,2,1,0:T(8,128)S(1)} %get-tuple-element.34.own.rest_9_), channel_id=1, source_target_pairs={{0,1},{1,2},{2,3},{3,4},{4,5},{5,6},{6,7},{7,8},{8,9},{9,10},{10,1... | collective-permute-start | bytes 110600 | tf_op jit(solution)/shard_map/ppermute | solution.py:286
  63.5 1.7 %collective-permute-start.15 = (f32[3,3,8,128]{3,2,1,0:T(8,128)S(1)}, f32[3,3,8,128]{3,2,1,0:T(8,128)S(1)}, u32[]{:S(2)}, u32[]{:S(2)}) collective-permute-start(f32[3,3,8,128]{3,2,1,0:T(8,128)S(1)} %get-tuple-element.37), channel_id=1, source_target_pairs={{1,0},{2,1},{3,2},{4,3},{5,4},{6,5},{7,6},{8,7},{9,8},{10,9},{11,1... | collective-permute-start | bytes 110600 | tf_op jit(solution)/shard_map/ppermute | solution.py:286
  63.5 4.6 %collective-permute-start.14 = (f32[3,3,8,128]{3,2,1,0:T(8,128)S(1)}, f32[3,3,8,128]{3,2,1,0:T(8,128)S(1)}, u32[]{:S(2)}, u32[]{:S(2)}) collective-permute-start(f32[3,3,8,128]{3,2,1,0:T(8,128)S(1)} %get-tuple-element.36.own.rest_11_), channel_id=1, source_target_pairs={{0,1},{1,2},{2,3},{3,4},{4,5},{5,6},{6,7},{7,8},{8,9},{9,10},{10,1... | collective-permute-start | bytes 110600 | tf_op jit(solution)/shard_map/ppermute | solution.py:286
  68.5 1.4 %collective-permute-start.17 = (f32[1,3,8,128]{3,2,1,0:T(8,128)S(1)}, f32[1,3,8,128]{3,2,1,0:T(8,128)S(1)}, u32[]{:S(2)}, u32[]{:S(2)}) collective-permute-start(f32[1,3,8,128]{3,2,1,0:T(8,128)S(1)} %get-tuple-element.38.below), channel_id=1, source_target_pairs={{1,0},{2,1},{3,2},{4,3},{5,4},{6,5},{7,6},{8,7},{9,8},{10,9},{11,1... | collective-permute-start | bytes 36872 | tf_op jit(solution)/shard_map/ppermute | solution.py:286
  68.5 4.3 %collective-permute-start.16 = (f32[1,3,8,128]{3,2,1,0:T(8,128)S(1)}, f32[1,3,8,128]{3,2,1,0:T(8,128)S(1)}, u32[]{:S(2)}, u32[]{:S(2)}) collective-permute-start(f32[1,3,8,128]{3,2,1,0:T(8,128)S(1)} %get-tuple-element.39.above), channel_id=1, source_target_pairs={{0,1},{1,2},{2,3},{3,4},{4,5},{5,6},{6,7},{7,8},{8,9},{9,10},{10,1... | collective-permute-start | bytes 36872 | tf_op jit(solution)/shard_map/ppermute | solution.py:286

commit v4 on v3

--- a/solution.py
+++ b/solution.py
@@ -85,17 +85,35 @@
     return pltpu.roll(x, by, axis=1) if by else x
 
 
-def laid(own, left, right):
+def by_parity(spins, aniso, out, layers):
+    for comp in range(4):
+        for x in range(2):
+            for q in range(layers.shape[2]):
+                at = slice(128 * q, 128 * (q + 1))
+                layers[comp, x, q] = aniso[x, :, at] if comp == 3 else spins[comp, x, :, at]
+                for parity in range(2):
+                    out[comp, x, parity, :, at] = layers[comp, x, q, pl.ds(parity, 8, stride=2), :]
+
+
+def prepare(spins, aniso, applied, out, field, layers):
+    by_parity(spins, aniso, out, layers)
+    for c in range(3):
+        field[c] = jnp.full(field.shape[1:], applied[c], F32)
+
+
+def beside(own, sides):
     def load(comp, plane, parity):
-        ref, at = (left, plane + 2) if plane < 0 else (own, plane) if plane < 2 else (right, plane - 2)
+        ref, at = (sides.at[0], plane + 2) if plane < 0 else (own, plane) if plane < 2 else (sides.at[1], plane - 2)
         return ref[comp, at, parity]
 
     return load
 
 
-def prologue(own, left, right, field, payload):
-    applied = [jnp.concatenate([field[c]] * (own.shape[-1] // 128), axis=1) for c in range(3)]
-    load = laid(own, left, right)
+def prologue(own, left, left_a, right, right_a, field, payload, sides, layers):
+    by_parity(left, left_a, sides.at[0], layers.at[0])
+    by_parity(right, right_a, sides.at[1], layers.at[1])
+    load = beside(own, sides)
+    applied = [jnp.concatenate([field[c]] * layers.shape[3], axis=1) for c in range(3)]
 
     planes = range(-2, 4)
     even = {x: [load(c, x, 0) for c in range(3)] for x in planes}
@@ -147,8 +165,8 @@
     return (lax.broadcasted_iota(jnp.int32, (8, 128), 1) + 16 - 32 * (row % 4)) & 127
 
 
-def window(own, left, right, windows):
-    load = laid(own, left, right)
+def window(own, sides, windows):
+    load = beside(own, sides)
     row = lax.axis_index("tm")
     windows[6] = logical_lane(row).astype(F32)
     for at in range(own.shape[-1] // 32):
@@ -290,10 +308,9 @@
     return pl.pallas_call(
         kernel,
         out_shape=[jax.ShapeDtypeStruct(s, F32) for s in shapes],
-        in_specs=[VMEM] * len(args),
         out_specs=[VMEM] * len(shapes),
         scratch_shapes=[pltpu.VMEM(s, F32) for s in scratch],
-        **more,
+        **({"in_specs": [VMEM] * len(args)} | more),
         compiler_params=pltpu.CompilerParams(vmem_limit_bytes=32 * 1024 * 1024),
     )(*args)
 
@@ -301,12 +318,23 @@
 def per_device(starts, anisotropy, applied):
     slices = lax.axis_size("tm")
     width = starts.shape[-1]
-    own = jnp.concatenate([starts[0], anisotropy[None]], axis=0)
-    own = own.reshape(4, 2, 8, 2, width).swapaxes(2, 3)
-    field = jnp.broadcast_to(applied[:, None, None], (3, 8, 128))
-    slabs = (own, *both_sides(own, own))
-    (payload,) = call(prologue, [(slices, 2, 3, 8, 128)], *slabs, field)
-    (windows,) = call(window, [(7, 8, 128)], *slabs)
+    layers = (4, 2, width // 128, 16, 128)
+    left, right = both_sides(starts[0], starts[0])
+    left_a, right_a = both_sides(anisotropy, anisotropy)
+    own, field = call(
+        prepare,
+        [(4, 2, 2, 8, width), (3, 8, 128)],
+        *(starts[0], anisotropy, applied),
+        scratch=[layers],
+        in_specs=[VMEM] * 2 + [pl.BlockSpec(memory_space=pltpu.SMEM)],
+    )
+    payload, sides = call(
+        prologue,
+        [(slices, 2, 3, 8, 128), (2, 4, 2, 2, 8, width)],
+        *(own, left, left_a, right, right_a, field),
+        scratch=[(2, *layers)],
+    )
+    (windows,) = call(window, [(7, 8, 128)], own, sides)
     corr = lax.all_to_all(payload, "tm", 0, 0, tiled=True)
     up = down = corr[:2]
     kept = []

time: 86.5 us -> 86.5 us (level)
  waiting for transfers between devices: 39.5 us -> 35.5 us
  starting transfers between devices: 13.1 us -> 16 us
    ppermute x9 -> x10, waiting for transfers between devices: 12.6 us -> 8.98 us  [both_sides(): lax.ppermute(to_below, 'space', down)]
    ppermute x9 -> x10, starting transfers between devices: 9.08 us -> 12.3 us  [both_sides(): lax.ppermute(to_below, 'space', down)]
    pallas_call x12 -> x13, Pallas kernels: 5.43 us -> 6.11 us  [call(): pl.pallas_call(kernel, out_shape=[jax.ShapeDtypeStruct(s, F32) for s in s...]
    ppermute x9 -> x10, waiting for transfers between devices: 26.9 us -> 26.5 us  [both_sides(): lax.ppermute(to_above, 'space', up)]
    ppermute x9 -> x10, starting transfers between devices: 3.99 us -> 3.68 us  [both_sides(): lax.ppermute(to_above, 'space', up)]
  transfers between devices with their start and end apart: 18 -> 20, of which waited for: 18 -> 17; matrix products, arithmetic and copies ran while one was open for 0% -> 0% of each run, Pallas kernels for 0% -> 1%
where the time goes in v4:
time: 86.5 us; the launch traced here: 86.2 us
  waiting for transfers between devices  35.5 us (41%)
  blocking collectives  26.7 us (31%)
  starting transfers between devices  16 us (18%)
  Pallas kernels  6.11 us (7%)
  local copies, waits for them, and re-layouts  1.77 us (2%)
    ppermute x10, waiting for transfers between devices, both_sides(): lax.ppermute(to_above, 'space', up)  26.5 us
    all_to_all x1, blocking collectives, per_device(): corr = lax.all_to_all(payload, 'tm', 0, 0, tiled=True)  14.5 us
    ppermute x10, starting transfers between devices, both_sides(): lax.ppermute(to_below, 'space', down)  12.3 us
    all_to_all x1, blocking collectives, per_device(): sent = lax.all_to_all(sent, 'tm', 0, 0, tiled=True)  12.1 us
    ppermute x10, waiting for transfers between devices, both_sides(): lax.ppermute(to_below, 'space', down)  8.98 us
    pallas_call x13, Pallas kernels, call(): pl.pallas_call(kernel, out_shape=[jax.ShapeDtypeStruct(s, F32) for s in s...  6.11 us
    ppermute x10, starting transfers between devices, both_sides(): lax.ppermute(to_above, 'space', up)  3.68 us
    unnamed x6, local copies, waits for them, and re-layouts  1.77 us
  transfers between devices with their start and end apart: 20, of which 17 were waited for; matrix products, arithmetic and copies ran while one was open for 0% of the time, Pallas kernels for 1%

profile of v4, /device:TPU:2, one launch (start us, length us, event | category | flops | bytes accessed | tf_op | source)
XLA Modules:
  0.0 86.2 jit_solution(3371765672438578926)
XLA Ops:
  0.0 8.9 %collective-permute-start.2 = (f32[3,2,16,512]{3,2,1,0:T(8,128)}, f32[3,2,16,512]{3,2,1,0:T(8,128)S(1)}, u32[]{:S(2)}, u32[]{:S(2)}) collective-permute-start(f32[3,2,16,512]{3,2,1,0:T(8,128)} %bitcast.1), channel_id=1, source_target_pairs={{1,0},{2,1},{3,2},{4,3},{5,4},{6,5},{7,6},{8,7},{9,8},{10,9},{11,1... | collective-permute-start | bytes 589832 | tf_op jit(solution)/shard_map/ppermute | solution.py:304
  8.9 3.0 %collective-permute-start.3 = (f32[2,16,512]{2,1,0:T(8,128)}, f32[2,16,512]{2,1,0:T(8,128)S(1)}, u32[]{:S(2)}, u32[]{:S(2)}) collective-permute-start(f32[2,16,512]{2,1,0:T(8,128)} %aniso.1), channel_id=1, source_target_pairs={{1,0},{2,1},{3,2},{4,3},{5,4},{6,5},{7,6},{8,7},{9,8},{10,9},{11,1... | collective-permute-start | bytes 196616 | tf_op jit(solution)/shard_map/ppermute | solution.py:304
  11.9 0.9 %copy-done = f32[1,3,2,16,512]{4,3,2,1,0:T(8,128)S(1)} copy-done((f32[1,3,2,16,512]{4,3,2,1,0:T(8,128)S(1)}, f32[1,3,2,16,512]{4,3,2,1,0:T(8,128)}, u32[]{:S(2)}) %copy-start) | copy-done | bytes 196632
  12.8 0.8 copy-done.1
  14.3 2.7 %collective-permute-done.1.left_a = f32[2,16,512]{2,1,0:T(8,128)S(1)} collective-permute-done((f32[2,16,512]{2,1,0:T(8,128)}, f32[2,16,512]{2,1,0:T(8,128)S(1)}, u32[]{:S(2)}, u32[]{:S(2)}) %collective-permute-start.1) | collective-permute-done | bytes 65568 | tf_op jit(solution)/shard_map/ppermute | solution.py:304
  17.0 1.2 %shard_map.38 = (f32[16,2,3,8,128]{4,3,2,1,0:T(8,128)S(1)}, f32[2,4,2,2,8,512]{5,4,3,2,1,0:T(8,128)S(1)}) custom-call(f32[4,2,2,8,512]{4,3,2,1,0:T(8,128)S(1)} %get-tuple-element.30.own, f32[3,2,16,512]{3,2,1,0:T(8,128)S(1)} %collective-permute-done.left, f32[2,16,512]{2,1,0:T(8,128)S(1)} %collective-permute-done.1.left_a, ...), custom_call_target="tpu_custom_call" | custom-call | tf_op jit(solution)/shard_map/pallas_call | solution.py:308
  18.3 14.5 %all_to_all.10.corr.rest_2_ = f32[16,2,3,8,128]{4,3,2,1,0:T(8,128)S(1)} all-to-all(f32[16,2,3,8,128]{4,3,2,1,0:T(8,128)S(1)} %get-tuple-element.32), channel_id=1, replica_groups=mesh['tm'=16,'space'=32] {'tm'}, dimensions={0} | all-to-all | bytes 786432 | tf_op jit(solution)/shard_map/all_to_all | solution.py:338
  33.4 1.4 %collective-permute-done.5.right = f32[2,2,3,8,128]{4,3,2,1,0:T(8,128)S(1)} collective-permute-done((f32[2,2,3,8,128]{4,3,2,1,0:T(8,128)S(1)}, f32[2,2,3,8,128]{4,3,2,1,0:T(8,128)S(1)}, u32[]{:S(2)}, u32[]{:S(2)}) %collective-permute-start.5) | collective-permute-done | bytes 49184 | tf_op jit(solution)/shard_map/ppermute | solution.py:304
  34.8 3.0 %collective-permute-done.4.left = f32[2,2,3,8,128]{4,3,2,1,0:T(8,128)S(1)} collective-permute-done((f32[2,2,3,8,128]{4,3,2,1,0:T(8,128)S(1)}, f32[2,2,3,8,128]{4,3,2,1,0:T(8,128)S(1)}, u32[]{:S(2)}, u32[]{:S(2)}) %collective-permute-start.4) | collective-permute-done | bytes 49184 | tf_op jit(solution)/shard_map/ppermute | solution.py:304
  38.8 1.1 %collective-permute-done.7.right = f32[3,3,8,128]{3,2,1,0:T(8,128)S(1)} collective-permute-done((f32[3,3,8,128]{3,2,1,0:T(8,128)S(1)}, f32[3,3,8,128]{3,2,1,0:T(8,128)S(1)}, u32[]{:S(2)}, u32[]{:S(2)}) %collective-permute-start.7) | collective-permute-done | bytes 36896 | tf_op jit(solution)/shard_map/ppermute | solution.py:304
  39.9 3.0 %collective-permute-done.6.left = f32[3,3,8,128]{3,2,1,0:T(8,128)S(1)} collective-permute-done((f32[3,3,8,128]{3,2,1,0:T(8,128)S(1)}, f32[3,3,8,128]{3,2,1,0:T(8,128)S(1)}, u32[]{:S(2)}, u32[]{:S(2)}) %collective-permute-start.6) | collective-permute-done | bytes 36896 | tf_op jit(solution)/shard_map/ppermute | solution.py:304
  43.8 1.1 %collective-permute-done.9.right = f32[3,3,8,128]{3,2,1,0:T(8,128)S(1)} collective-permute-done((f32[3,3,8,128]{3,2,1,0:T(8,128)S(1)}, f32[3,3,8,128]{3,2,1,0:T(8,128)S(1)}, u32[]{:S(2)}, u32[]{:S(2)}) %collective-permute-start.9) | collective-permute-done | bytes 36896 | tf_op jit(solution)/shard_map/ppermute | solution.py:304
  45.0 3.0 %collective-permute-done.8.left = f32[3,3,8,128]{3,2,1,0:T(8,128)S(1)} collective-permute-done((f32[3,3,8,128]{3,2,1,0:T(8,128)S(1)}, f32[3,3,8,128]{3,2,1,0:T(8,128)S(1)}, u32[]{:S(2)}, u32[]{:S(2)}) %collective-permute-start.8) | collective-permute-done | bytes 36896 | tf_op jit(solution)/shard_map/ppermute | solution.py:304
  48.9 1.1 %collective-permute-done.11.right = f32[3,3,8,128]{3,2,1,0:T(8,128)S(1)} collective-permute-done((f32[3,3,8,128]{3,2,1,0:T(8,128)S(1)}, f32[3,3,8,128]{3,2,1,0:T(8,128)S(1)}, u32[]{:S(2)}, u32[]{:S(2)}) %collective-permute-start.11) | collective-permute-done | bytes 36896 | tf_op jit(solution)/shard_map/ppermute | solution.py:304
  50.0 3.0 %collective-permute-done.10.left = f32[3,3,8,128]{3,2,1,0:T(8,128)S(1)} collective-permute-done((f32[3,3,8,128]{3,2,1,0:T(8,128)S(1)}, f32[3,3,8,128]{3,2,1,0:T(8,128)S(1)}, u32[]{:S(2)}, u32[]{:S(2)}) %collective-permute-start.10) | collective-permute-done | bytes 36896 | tf_op jit(solution)/shard_map/ppermute | solution.py:304
  54.0 1.1 %collective-permute-done.13.right = f32[3,3,8,128]{3,2,1,0:T(8,128)S(1)} collective-permute-done((f32[3,3,8,128]{3,2,1,0:T(8,128)S(1)}, f32[3,3,8,128]{3,2,1,0:T(8,128)S(1)}, u32[]{:S(2)}, u32[]{:S(2)}) %collective-permute-start.13) | collective-permute-done | bytes 36896 | tf_op jit(solution)/shard_map/ppermute | solution.py:304
  55.1 3.0 %collective-permute-done.12.left = f32[3,3,8,128]{3,2,1,0:T(8,128)S(1)} collective-permute-done((f32[3,3,8,128]{3,2,1,0:T(8,128)S(1)}, f32[3,3,8,128]{3,2,1,0:T(8,128)S(1)}, u32[]{:S(2)}, u32[]{:S(2)}) %collective-permute-start.12) | collective-permute-done | bytes 36896 | tf_op jit(solution)/shard_map/ppermute | solution.py:304
  59.0 1.1 %collective-permute-done.15.right = f32[3,3,8,128]{3,2,1,0:T(8,128)S(1)} collective-permute-done((f32[3,3,8,128]{3,2,1,0:T(8,128)S(1)}, f32[3,3,8,128]{3,2,1,0:T(8,128)S(1)}, u32[]{:S(2)}, u32[]{:S(2)}) %collective-permute-start.15) | collective-permute-done | bytes 36896 | tf_op jit(solution)/shard_map/ppermute | solution.py:304
  60.2 3.0 %collective-permute-done.14.left = f32[3,3,8,128]{3,2,1,0:T(8,128)S(1)} collective-permute-done((f32[3,3,8,128]{3,2,1,0:T(8,128)S(1)}, f32[3,3,8,128]{3,2,1,0:T(8,128)S(1)}, u32[]{:S(2)}, u32[]{:S(2)}) %collective-permute-start.14) | collective-permute-done | bytes 36896 | tf_op jit(solution)/shard_map/ppermute | solution.py:304
  64.1 1.1 %collective-permute-done.17.right = f32[3,3,8,128]{3,2,1,0:T(8,128)S(1)} collective-permute-done((f32[3,3,8,128]{3,2,1,0:T(8,128)S(1)}, f32[3,3,8,128]{3,2,1,0:T(8,128)S(1)}, u32[]{:S(2)}, u32[]{:S(2)}) %collective-permute-start.17) | collective-permute-done | bytes 36896 | tf_op jit(solution)/shard_map/ppermute | solution.py:304
  65.2 3.0 %collective-permute-done.16.left = f32[3,3,8,128]{3,2,1,0:T(8,128)S(1)} collective-permute-done((f32[3,3,8,128]{3,2,1,0:T(8,128)S(1)}, f32[3,3,8,128]{3,2,1,0:T(8,128)S(1)}, u32[]{:S(2)}, u32[]{:S(2)}) %collective-permute-start.16) | collective-permute-done | bytes 36896 | tf_op jit(solution)/shard_map/ppermute | solution.py:304
  70.1 2.9 %collective-permute-done.18.rest_0_ = f32[1,3,8,128]{3,2,1,0:T(8,128)S(1)} collective-permute-done((f32[1,3,8,128]{3,2,1,0:T(8,128)S(1)}, f32[1,3,8,128]{3,2,1,0:T(8,128)S(1)}, u32[]{:S(2)}, u32[]{:S(2)}) %collective-permute-start.18) | collective-permute-done | bytes 12320 | tf_op jit(solution)/shard_map/ppermute | solution.py:304
  73.3 12.1 %all_to_all.11.sent = f32[16,3,8,128]{3,2,1,0:T(8,128)S(1)} all-to-all(f32[16,3,8,128]{3,2,1,0:T(8,128)S(1)} %shard_map.48), channel_id=1, replica_groups=mesh['tm'=16,'space'=32] {'tm'}, dimensions={0} | all-to-all | bytes 393216 | tf_op jit(solution)/shard_map/all_to_all | solution.py:354
  85.4 0.8 shard_map.49
  (38 shorter events, 9.0 us)
Async XLA Ops:
  0.0 11.9 %copy-start.2 = (f32[3]{0:T(128)S(1)}, f32[3]{0:T(128)}, u32[]{:S(2)}) copy-start(f32[3]{0:T(128)} %applied.1) | copy-start | bytes 40
  0.0 17.0 %collective-permute-start.2 = (f32[3,2,16,512]{3,2,1,0:T(8,128)}, f32[3,2,16,512]{3,2,1,0:T(8,128)S(1)}, u32[]{:S(2)}, u32[]{:S(2)}) collective-permute-start(f32[3,2,16,512]{3,2,1,0:T(8,128)} %bitcast.1), channel_id=1, source_target_pairs={{1,0},{2,1},{3,2},{4,3},{5,4},{6,5},{7,6},{8,7},{9,8},{10,9},{11,1... | collective-permute-start | bytes 589832 | tf_op jit(solution)/shard_map/ppermute | solution.py:304
  8.9 8.1 %collective-permute-start = (f32[3,2,16,512]{3,2,1,0:T(8,128)}, f32[3,2,16,512]{3,2,1,0:T(8,128)S(1)}, u32[]{:S(2)}, u32[]{:S(2)}) collective-permute-start(f32[3,2,16,512]{3,2,1,0:T(8,128)} %bitcast.2), channel_id=1, source_target_pairs={{0,1},{1,2},{2,3},{3,4},{4,5},{5,6},{6,7},{7,8},{8,9},{9,10},{10,1... | collective-permute-start | bytes 589832 | tf_op jit(solution)/shard_map/ppermute | solution.py:304
  8.9 5.3 %collective-permute-start.3 = (f32[2,16,512]{2,1,0:T(8,128)}, f32[2,16,512]{2,1,0:T(8,128)S(1)}, u32[]{:S(2)}, u32[]{:S(2)}) collective-permute-start(f32[2,16,512]{2,1,0:T(8,128)} %aniso.1), channel_id=1, source_target_pairs={{1,0},{2,1},{3,2},{4,3},{5,4},{6,5},{7,6},{8,7},{9,8},{10,9},{11,1... | collective-permute-start | bytes 196616 | tf_op jit(solution)/shard_map/ppermute | solution.py:304
  11.9 5.1 %collective-permute-start.1 = (f32[2,16,512]{2,1,0:T(8,128)}, f32[2,16,512]{2,1,0:T(8,128)S(1)}, u32[]{:S(2)}, u32[]{:S(2)}) collective-permute-start(f32[2,16,512]{2,1,0:T(8,128)} %aniso.1), channel_id=1, source_target_pairs={{0,1},{1,2},{2,3},{3,4},{4,5},{5,6},{6,7},{7,8},{8,9},{9,10},{10,1... | collective-permute-start | bytes 196616 | tf_op jit(solution)/shard_map/ppermute | solution.py:304
  11.9 0.9 %copy-start = (f32[1,3,2,16,512]{4,3,2,1,0:T(8,128)S(1)}, f32[1,3,2,16,512]{4,3,2,1,0:T(8,128)}, u32[]{:S(2)}) copy-start(f32[1,3,2,16,512]{4,3,2,1,0:T(8,128)} %param.3) | copy-start | bytes 589828
  12.8 0.8 copy-start.1
  32.8 2.1 %collective-permute-start.5 = (f32[2,2,3,8,128]{4,3,2,1,0:T(8,128)S(1)}, f32[2,2,3,8,128]{4,3,2,1,0:T(8,128)S(1)}, u32[]{:S(2)}, u32[]{:S(2)}) collective-permute-start(f32[2,2,3,8,128]{4,3,2,1,0:T(8,128)S(1)} %slice.4.own), channel_id=1, source_target_pairs={{1,0},{2,1},{3,2},{4,3},{5,4},{6,5},{7,6},{8,7},{9,8},{10,9},{11,1... | collective-permute-start | bytes 147464 | tf_op jit(solution)/shard_map/ppermute | solution.py:304
  33.1 4.7 %collective-permute-start.4 = (f32[2,2,3,8,128]{4,3,2,1,0:T(8,128)S(1)}, f32[2,2,3,8,128]{4,3,2,1,0:T(8,128)S(1)}, u32[]{:S(2)}, u32[]{:S(2)}) collective-permute-start(f32[2,2,3,8,128]{4,3,2,1,0:T(8,128)S(1)} %slice.4.own), channel_id=1, source_target_pairs={{0,1},{1,2},{2,3},{3,4},{4,5},{5,6},{6,7},{7,8},{8,9},{9,10},{10,1... | collective-permute-start | bytes 147464 | tf_op jit(solution)/shard_map/ppermute | solution.py:304
  38.2 1.7 %collective-permute-start.7 = (f32[3,3,8,128]{3,2,1,0:T(8,128)S(1)}, f32[3,3,8,128]{3,2,1,0:T(8,128)S(1)}, u32[]{:S(2)}, u32[]{:S(2)}) collective-permute-start(f32[3,3,8,128]{3,2,1,0:T(8,128)S(1)} %get-tuple-element.35), channel_id=1, source_target_pairs={{1,0},{2,1},{3,2},{4,3},{5,4},{6,5},{7,6},{8,7},{9,8},{10,9},{11,1... | collective-permute-start | bytes 110600 | tf_op jit(solution)/shard_map/ppermute | solution.py:304
  38.3 4.6 %collective-permute-start.6 = (f32[3,3,8,128]{3,2,1,0:T(8,128)S(1)}, f32[3,3,8,128]{3,2,1,0:T(8,128)S(1)}, u32[]{:S(2)}, u32[]{:S(2)}) collective-permute-start(f32[3,3,8,128]{3,2,1,0:T(8,128)S(1)} %get-tuple-element.34.own.rest_1_), channel_id=1, source_target_pairs={{0,1},{1,2},{2,3},{3,4},{4,5},{5,6},{6,7},{7,8},{8,9},{9,10},{10,1... | collective-permute-start | bytes 110600 | tf_op jit(solution)/shard_map/ppermute | solution.py:304
  43.3 1.7 %collective-permute-start.9 = (f32[3,3,8,128]{3,2,1,0:T(8,128)S(1)}, f32[3,3,8,128]{3,2,1,0:T(8,128)S(1)}, u32[]{:S(2)}, u32[]{:S(2)}) collective-permute-start(f32[3,3,8,128]{3,2,1,0:T(8,128)S(1)} %get-tuple-element.37), channel_id=1, source_target_pairs={{1,0},{2,1},{3,2},{4,3},{5,4},{6,5},{7,6},{8,7},{9,8},{10,9},{11,1... | collective-permute-start | bytes 110600 | tf_op jit(solution)/shard_map/ppermute | solution.py:304
  43.3 4.6 %collective-permute-start.8 = (f32[3,3,8,128]{3,2,1,0:T(8,128)S(1)}, f32[3,3,8,128]{3,2,1,0:T(8,128)S(1)}, u32[]{:S(2)}, u32[]{:S(2)}) collective-permute-start(f32[3,3,8,128]{3,2,1,0:T(8,128)S(1)} %get-tuple-element.36.own.rest_3_), channel_id=1, source_target_pairs={{0,1},{1,2},{2,3},{3,4},{4,5},{5,6},{6,7},{7,8},{8,9},{9,10},{10,1... | collective-permute-start | bytes 110600 | tf_op jit(solution)/shard_map/ppermute | solution.py:304
  48.4 1.7 %collective-permute-start.11 = (f32[3,3,8,128]{3,2,1,0:T(8,128)S(1)}, f32[3,3,8,128]{3,2,1,0:T(8,128)S(1)}, u32[]{:S(2)}, u32[]{:S(2)}) collective-permute-start(f32[3,3,8,128]{3,2,1,0:T(8,128)S(1)} %get-tuple-element.39), channel_id=1, source_target_pairs={{1,0},{2,1},{3,2},{4,3},{5,4},{6,5},{7,6},{8,7},{9,8},{10,9},{11,1... | collective-permute-start | bytes 110600 | tf_op jit(solution)/shard_map/ppermute | solution.py:304
  48.4 4.6 %collective-permute-start.10 = (f32[3,3,8,128]{3,2,1,0:T(8,128)S(1)}, f32[3,3,8,128]{3,2,1,0:T(8,128)S(1)}, u32[]{:S(2)}, u32[]{:S(2)}) collective-permute-start(f32[3,3,8,128]{3,2,1,0:T(8,128)S(1)} %get-tuple-element.38.own.rest_5_), channel_id=1, source_target_pairs={{0,1},{1,2},{2,3},{3,4},{4,5},{5,6},{6,7},{7,8},{8,9},{9,10},{10,1... | collective-permute-start | bytes 110600 | tf_op jit(solution)/shard_map/ppermute | solution.py:304
  53.4 1.7 %collective-permute-start.13 = (f32[3,3,8,128]{3,2,1,0:T(8,128)S(1)}, f32[3,3,8,128]{3,2,1,0:T(8,128)S(1)}, u32[]{:S(2)}, u32[]{:S(2)}) collective-permute-start(f32[3,3,8,128]{3,2,1,0:T(8,128)S(1)} %get-tuple-element.41), channel_id=1, source_target_pairs={{1,0},{2,1},{3,2},{4,3},{5,4},{6,5},{7,6},{8,7},{9,8},{10,9},{11,1... | collective-permute-start | bytes 110600 | tf_op jit(solution)/shard_map/ppermute | solution.py:304
  53.5 4.6 %collective-permute-start.12 = (f32[3,3,8,128]{3,2,1,0:T(8,128)S(1)}, f32[3,3,8,128]{3,2,1,0:T(8,128)S(1)}, u32[]{:S(2)}, u32[]{:S(2)}) collective-permute-start(f32[3,3,8,128]{3,2,1,0:T(8,128)S(1)} %get-tuple-element.40.own.rest_7_), channel_id=1, source_target_pairs={{0,1},{1,2},{2,3},{3,4},{4,5},{5,6},{6,7},{7,8},{8,9},{9,10},{10,1... | collective-permute-start | bytes 110600 | tf_op jit(solution)/shard_map/ppermute | solution.py:304
  58.5 1.7 %collective-permute-start.15 = (f32[3,3,8,128]{3,2,1,0:T(8,128)S(1)}, f32[3,3,8,128]{3,2,1,0:T(8,128)S(1)}, u32[]{:S(2)}, u32[]{:S(2)}) collective-permute-start(f32[3,3,8,128]{3,2,1,0:T(8,128)S(1)} %get-tuple-element.43), channel_id=1, source_target_pairs={{1,0},{2,1},{3,2},{4,3},{5,4},{6,5},{7,6},{8,7},{9,8},{10,9},{11,1... | collective-permute-start | bytes 110600 | tf_op jit(solution)/shard_map/ppermute | solution.py:304
  58.5 4.6 %collective-permute-start.14 = (f32[3,3,8,128]{3,2,1,0:T(8,128)S(1)}, f32[3,3,8,128]{3,2,1,0:T(8,128)S(1)}, u32[]{:S(2)}, u32[]{:S(2)}) collective-permute-start(f32[3,3,8,128]{3,2,1,0:T(8,128)S(1)} %get-tuple-element.42.own.rest_9_), channel_id=1, source_target_pairs={{0,1},{1,2},{2,3},{3,4},{4,5},{5,6},{6,7},{7,8},{8,9},{9,10},{10,1... | collective-permute-start | bytes 110600 | tf_op jit(solution)/shard_map/ppermute | solution.py:304
  63.6 1.7 %collective-permute-start.17 = (f32[3,3,8,128]{3,2,1,0:T(8,128)S(1)}, f32[3,3,8,128]{3,2,1,0:T(8,128)S(1)}, u32[]{:S(2)}, u32[]{:S(2)}) collective-permute-start(f32[3,3,8,128]{3,2,1,0:T(8,128)S(1)} %get-tuple-element.45), channel_id=1, source_target_pairs={{1,0},{2,1},{3,2},{4,3},{5,4},{6,5},{7,6},{8,7},{9,8},{10,9},{11,1... | collective-permute-start | bytes 110600 | tf_op jit(solution)/shard_map/ppermute | solution.py:304
  63.6 4.6 %collective-permute-start.16 = (f32[3,3,8,128]{3,2,1,0:T(8,128)S(1)}, f32[3,3,8,128]{3,2,1,0:T(8,128)S(1)}, u32[]{:S(2)}, u32[]{:S(2)}) collective-permute-start(f32[3,3,8,128]{3,2,1,0:T(8,128)S(1)} %get-tuple-element.44.own.rest_11_), channel_id=1, source_target_pairs={{0,1},{1,2},{2,3},{3,4},{4,5},{5,6},{6,7},{7,8},{8,9},{9,10},{10,1... | collective-permute-start | bytes 110600 | tf_op jit(solution)/shard_map/ppermute | solution.py:304
  68.6 1.4 %collective-permute-start.19 = (f32[1,3,8,128]{3,2,1,0:T(8,128)S(1)}, f32[1,3,8,128]{3,2,1,0:T(8,128)S(1)}, u32[]{:S(2)}, u32[]{:S(2)}) collective-permute-start(f32[1,3,8,128]{3,2,1,0:T(8,128)S(1)} %get-tuple-element.46.below), channel_id=1, source_target_pairs={{1,0},{2,1},{3,2},{4,3},{5,4},{6,5},{7,6},{8,7},{9,8},{10,9},{11,1... | collective-permute-start | bytes 36872 | tf_op jit(solution)/shard_map/ppermute | solution.py:304
  68.7 4.3 %collective-permute-start.18 = (f32[1,3,8,128]{3,2,1,0:T(8,128)S(1)}, f32[1,3,8,128]{3,2,1,0:T(8,128)S(1)}, u32[]{:S(2)}, u32[]{:S(2)}) collective-permute-start(f32[1,3,8,128]{3,2,1,0:T(8,128)S(1)} %get-tuple-element.47.above), channel_id=1, source_target_pairs={{0,1},{1,2},{2,3},{3,4},{4,5},{5,6},{6,7},{7,8},{8,9},{9,10},{10,1... | collective-permute-start | bytes 36872 | tf_op jit(solution)/shard_map/ppermute | solution.py:304

commit v5 on v4

--- a/solution.py
+++ b/solution.py
@@ -85,18 +85,18 @@
     return pltpu.roll(x, by, axis=1) if by else x
 
 
-def by_parity(spins, aniso, out, layers):
+def by_parity(slab, out, layers):
     for comp in range(4):
         for x in range(2):
             for q in range(layers.shape[2]):
                 at = slice(128 * q, 128 * (q + 1))
-                layers[comp, x, q] = aniso[x, :, at] if comp == 3 else spins[comp, x, :, at]
+                layers[comp, x, q] = slab[comp, x, :, at]
                 for parity in range(2):
                     out[comp, x, parity, :, at] = layers[comp, x, q, pl.ds(parity, 8, stride=2), :]
 
 
-def prepare(spins, aniso, applied, out, field, layers):
-    by_parity(spins, aniso, out, layers)
+def prepare(slab, applied, out, field, layers):
+    by_parity(slab, out, layers)
     for c in range(3):
         field[c] = jnp.full(field.shape[1:], applied[c], F32)
 
@@ -109,9 +109,9 @@
     return load
 
 
-def prologue(own, left, left_a, right, right_a, field, payload, sides, layers):
-    by_parity(left, left_a, sides.at[0], layers.at[0])
-    by_parity(right, right_a, sides.at[1], layers.at[1])
+def prologue(own, left, right, field, payload, sides, layers):
+    by_parity(left, sides.at[0], layers.at[0])
+    by_parity(right, sides.at[1], layers.at[1])
     load = beside(own, sides)
     applied = [jnp.concatenate([field[c]] * layers.shape[3], axis=1) for c in range(3)]
 
@@ -319,19 +319,19 @@
     slices = lax.axis_size("tm")
     width = starts.shape[-1]
     layers = (4, 2, width // 128, 16, 128)
-    left, right = both_sides(starts[0], starts[0])
-    left_a, right_a = both_sides(anisotropy, anisotropy)
+    slab = jnp.concatenate([starts[0], anisotropy[None]], axis=0)
+    left, right = both_sides(slab, slab)
     own, field = call(
         prepare,
         [(4, 2, 2, 8, width), (3, 8, 128)],
-        *(starts[0], anisotropy, applied),
+        *(slab, applied),
         scratch=[layers],
-        in_specs=[VMEM] * 2 + [pl.BlockSpec(memory_space=pltpu.SMEM)],
+        in_specs=[VMEM, pl.BlockSpec(memory_space=pltpu.SMEM)],
     )
     payload, sides = call(
         prologue,
         [(slices, 2, 3, 8, 128), (2, 4, 2, 2, 8, width)],
-        *(own, left, left_a, right, right_a, field),
+        *(own, left, right, field),
         scratch=[(2, *layers)],
     )
     (windows,) = call(window, [(7, 8, 128)], own, sides)

time: 86.5 us -> 86.2 us (level)
  waiting for transfers between devices: 35.5 us -> 38.9 us
  starting transfers between devices: 16 us -> 13.1 us
  local copies, waits for them, and re-layouts: 1.77 us -> 0.01 us
  other arithmetic: 0 us -> 0.99 us
    ppermute x10 -> x9, starting transfers between devices: 12.3 us -> 9.08 us  [both_sides(): lax.ppermute(to_below, 'space', down)]
    ppermute x10 -> x9, waiting for transfers between devices: 8.98 us -> 12 us  [both_sides(): lax.ppermute(to_below, 'space', down)]
    unnamed x6 -> x2, local copies, waits for them, and re-layouts: 1.77 us -> 0.01 us
    concatenate x0 -> x1, other arithmetic: none -> 0.99 us  [per_device(): slab = jnp.concatenate([starts[0], anisotropy[None]], axis=0)]
    ppermute x10 -> x9, waiting for transfers between devices: 26.5 us -> 26.9 us  [both_sides(): lax.ppermute(to_above, 'space', up)]
    ppermute x10 -> x9, starting transfers between devices: 3.68 us -> 3.99 us  [both_sides(): lax.ppermute(to_above, 'space', up)]
  transfers between devices with their start and end apart: 20 -> 18, of which waited for: 17 -> 18; matrix products, arithmetic and copies ran while one was open for 0% -> 0% of each run, Pallas kernels for 1% -> 1%
where the time goes in v5:
time: 86.2 us; the launch traced here: 86 us
  waiting for transfers between devices  38.9 us (45%)
  blocking collectives  26.8 us (31%)
  starting transfers between devices  13.1 us (15%)
  Pallas kernels  6.1 us (7%)
  other arithmetic  0.99 us (1%)
    ppermute x9, waiting for transfers between devices, both_sides(): lax.ppermute(to_above, 'space', up)  26.9 us
    all_to_all x1, blocking collectives, per_device(): corr = lax.all_to_all(payload, 'tm', 0, 0, tiled=True)  14.5 us
    all_to_all x1, blocking collectives, per_device(): sent = lax.all_to_all(sent, 'tm', 0, 0, tiled=True)  12.3 us
    ppermute x9, waiting for transfers between devices, both_sides(): lax.ppermute(to_below, 'space', down)  12 us
    ppermute x9, starting transfers between devices, both_sides(): lax.ppermute(to_below, 'space', down)  9.08 us
    pallas_call x13, Pallas kernels, call(): pl.pallas_call(kernel, out_shape=[jax.ShapeDtypeStruct(s, F32) for s in s...  6.1 us
    ppermute x9, starting transfers between devices, both_sides(): lax.ppermute(to_above, 'space', up)  3.99 us
  transfers between devices with their start and end apart: 18, of which 18 were waited for; matrix products, arithmetic and copies ran while one was open for 0% of the time, Pallas kernels for 1%

profile of v5, /device:TPU:2, one launch (start us, length us, event | category | flops | bytes accessed | tf_op | source)
XLA Modules:
  0.0 86.0 jit_solution(11866448094577545591)
XLA Ops:
  0.0 1.0 %pad_maximum_fusion.slab = f32[4,2,16,512]{3,2,1,0:T(8,128)S(1)} fusion(f32[1,2,16,512]{3,2,1,0:T(8,128)} %bitcast.3, f32[3,2,16,512]{3,2,1,0:T(8,128)} %bitcast.2), kind=kLoop, calls=%fused_computation | loop fusion | flops 65536 | bytes 524288 | tf_op jit(solution)/shard_map/concatenate | solution.py:322
  1.0 8.9 %collective-permute-start.1 = (f32[4,2,16,512]{3,2,1,0:T(8,128)S(1)}, f32[4,2,16,512]{3,2,1,0:T(8,128)S(1)}, u32[]{:S(2)}, u32[]{:S(2)}) collective-permute-start(f32[4,2,16,512]{3,2,1,0:T(8,128)S(1)} %pad_maximum_fusion.slab), channel_id=1, source_target_pairs={{1,0},{2,1},{3,2},{4,3},{5,4},{6,5},{7,6},{8,7},{9,8},{10,9},{11,1... | collective-permute-start | bytes 786440 | tf_op jit(solution)/shard_map/ppermute | solution.py:304
  10.5 3.3 %collective-permute-done.1.right = f32[4,2,16,512]{3,2,1,0:T(8,128)S(1)} collective-permute-done((f32[4,2,16,512]{3,2,1,0:T(8,128)S(1)}, f32[4,2,16,512]{3,2,1,0:T(8,128)S(1)}, u32[]{:S(2)}, u32[]{:S(2)}) %collective-permute-start.1) | collective-permute-done | bytes 262176 | tf_op jit(solution)/shard_map/ppermute | solution.py:304
  13.8 3.1 %collective-permute-done.left = f32[4,2,16,512]{3,2,1,0:T(8,128)S(1)} collective-permute-done((f32[4,2,16,512]{3,2,1,0:T(8,128)S(1)}, f32[4,2,16,512]{3,2,1,0:T(8,128)S(1)}, u32[]{:S(2)}, u32[]{:S(2)}) %collective-permute-start) | collective-permute-done | bytes 262176 | tf_op jit(solution)/shard_map/ppermute | solution.py:304
  17.0 1.2 %shard_map.38 = (f32[16,2,3,8,128]{4,3,2,1,0:T(8,128)S(1)}, f32[2,4,2,2,8,512]{5,4,3,2,1,0:T(8,128)S(1)}) custom-call(f32[4,2,2,8,512]{4,3,2,1,0:T(8,128)S(1)} %get-tuple-element.30.own, f32[4,2,16,512]{3,2,1,0:T(8,128)S(1)} %collective-permute-done.left, f32[4,2,16,512]{3,2,1,0:T(8,128)S(1)} %collective-permute-done.1.right, ...), custom_call_target="tpu_custom_call" | custom-call | tf_op jit(solution)/shard_map/pallas_call | solution.py:308
  18.2 14.5 %all_to_all.10.corr.rest_2_ = f32[16,2,3,8,128]{4,3,2,1,0:T(8,128)S(1)} all-to-all(f32[16,2,3,8,128]{4,3,2,1,0:T(8,128)S(1)} %get-tuple-element.32), channel_id=1, replica_groups=mesh['tm'=16,'space'=32] {'tm'}, dimensions={0} | all-to-all | bytes 786432 | tf_op jit(solution)/shard_map/all_to_all | solution.py:338
  33.4 1.1 %collective-permute-done.3.right = f32[2,2,3,8,128]{4,3,2,1,0:T(8,128)S(1)} collective-permute-done((f32[2,2,3,8,128]{4,3,2,1,0:T(8,128)S(1)}, f32[2,2,3,8,128]{4,3,2,1,0:T(8,128)S(1)}, u32[]{:S(2)}, u32[]{:S(2)}) %collective-permute-start.3) | collective-permute-done | bytes 49184 | tf_op jit(solution)/shard_map/ppermute | solution.py:304
  34.5 3.0 %collective-permute-done.2.left = f32[2,2,3,8,128]{4,3,2,1,0:T(8,128)S(1)} collective-permute-done((f32[2,2,3,8,128]{4,3,2,1,0:T(8,128)S(1)}, f32[2,2,3,8,128]{4,3,2,1,0:T(8,128)S(1)}, u32[]{:S(2)}, u32[]{:S(2)}) %collective-permute-start.2) | collective-permute-done | bytes 49184 | tf_op jit(solution)/shard_map/ppermute | solution.py:304
  38.4 1.1 %collective-permute-done.5.right = f32[3,3,8,128]{3,2,1,0:T(8,128)S(1)} collective-permute-done((f32[3,3,8,128]{3,2,1,0:T(8,128)S(1)}, f32[3,3,8,128]{3,2,1,0:T(8,128)S(1)}, u32[]{:S(2)}, u32[]{:S(2)}) %collective-permute-start.5) | collective-permute-done | bytes 36896 | tf_op jit(solution)/shard_map/ppermute | solution.py:304
  39.5 3.0 %collective-permute-done.4.left = f32[3,3,8,128]{3,2,1,0:T(8,128)S(1)} collective-permute-done((f32[3,3,8,128]{3,2,1,0:T(8,128)S(1)}, f32[3,3,8,128]{3,2,1,0:T(8,128)S(1)}, u32[]{:S(2)}, u32[]{:S(2)}) %collective-permute-start.4) | collective-permute-done | bytes 36896 | tf_op jit(solution)/shard_map/ppermute | solution.py:304
  43.5 1.1 %collective-permute-done.7.right = f32[3,3,8,128]{3,2,1,0:T(8,128)S(1)} collective-permute-done((f32[3,3,8,128]{3,2,1,0:T(8,128)S(1)}, f32[3,3,8,128]{3,2,1,0:T(8,128)S(1)}, u32[]{:S(2)}, u32[]{:S(2)}) %collective-permute-start.7) | collective-permute-done | bytes 36896 | tf_op jit(solution)/shard_map/ppermute | solution.py:304
  44.6 3.0 %collective-permute-done.6.left = f32[3,3,8,128]{3,2,1,0:T(8,128)S(1)} collective-permute-done((f32[3,3,8,128]{3,2,1,0:T(8,128)S(1)}, f32[3,3,8,128]{3,2,1,0:T(8,128)S(1)}, u32[]{:S(2)}, u32[]{:S(2)}) %collective-permute-start.6) | collective-permute-done | bytes 36896 | tf_op jit(solution)/shard_map/ppermute | solution.py:304
  48.5 1.1 %collective-permute-done.9.right = f32[3,3,8,128]{3,2,1,0:T(8,128)S(1)} collective-permute-done((f32[3,3,8,128]{3,2,1,0:T(8,128)S(1)}, f32[3,3,8,128]{3,2,1,0:T(8,128)S(1)}, u32[]{:S(2)}, u32[]{:S(2)}) %collective-permute-start.9) | collective-permute-done | bytes 36896 | tf_op jit(solution)/shard_map/ppermute | solution.py:304
  49.7 3.0 %collective-permute-done.8.left = f32[3,3,8,128]{3,2,1,0:T(8,128)S(1)} collective-permute-done((f32[3,3,8,128]{3,2,1,0:T(8,128)S(1)}, f32[3,3,8,128]{3,2,1,0:T(8,128)S(1)}, u32[]{:S(2)}, u32[]{:S(2)}) %collective-permute-start.8) | collective-permute-done | bytes 36896 | tf_op jit(solution)/shard_map/ppermute | solution.py:304
  53.6 1.1 %collective-permute-done.11.right = f32[3,3,8,128]{3,2,1,0:T(8,128)S(1)} collective-permute-done((f32[3,3,8,128]{3,2,1,0:T(8,128)S(1)}, f32[3,3,8,128]{3,2,1,0:T(8,128)S(1)}, u32[]{:S(2)}, u32[]{:S(2)}) %collective-permute-start.11) | collective-permute-done | bytes 36896 | tf_op jit(solution)/shard_map/ppermute | solution.py:304
  54.7 3.0 %collective-permute-done.10.left = f32[3,3,8,128]{3,2,1,0:T(8,128)S(1)} collective-permute-done((f32[3,3,8,128]{3,2,1,0:T(8,128)S(1)}, f32[3,3,8,128]{3,2,1,0:T(8,128)S(1)}, u32[]{:S(2)}, u32[]{:S(2)}) %collective-permute-start.10) | collective-permute-done | bytes 36896 | tf_op jit(solution)/shard_map/ppermute | solution.py:304
  58.7 1.1 %collective-permute-done.13.right = f32[3,3,8,128]{3,2,1,0:T(8,128)S(1)} collective-permute-done((f32[3,3,8,128]{3,2,1,0:T(8,128)S(1)}, f32[3,3,8,128]{3,2,1,0:T(8,128)S(1)}, u32[]{:S(2)}, u32[]{:S(2)}) %collective-permute-start.13) | collective-permute-done | bytes 36896 | tf_op jit(solution)/shard_map/ppermute | solution.py:304
  59.8 3.0 %collective-permute-done.12.left = f32[3,3,8,128]{3,2,1,0:T(8,128)S(1)} collective-permute-done((f32[3,3,8,128]{3,2,1,0:T(8,128)S(1)}, f32[3,3,8,128]{3,2,1,0:T(8,128)S(1)}, u32[]{:S(2)}, u32[]{:S(2)}) %collective-permute-start.12) | collective-permute-done | bytes 36896 | tf_op jit(solution)/shard_map/ppermute | solution.py:304
  63.7 1.1 %collective-permute-done.15.right = f32[3,3,8,128]{3,2,1,0:T(8,128)S(1)} collective-permute-done((f32[3,3,8,128]{3,2,1,0:T(8,128)S(1)}, f32[3,3,8,128]{3,2,1,0:T(8,128)S(1)}, u32[]{:S(2)}, u32[]{:S(2)}) %collective-permute-start.15) | collective-permute-done | bytes 36896 | tf_op jit(solution)/shard_map/ppermute | solution.py:304
  64.9 3.0 %collective-permute-done.14.left = f32[3,3,8,128]{3,2,1,0:T(8,128)S(1)} collective-permute-done((f32[3,3,8,128]{3,2,1,0:T(8,128)S(1)}, f32[3,3,8,128]{3,2,1,0:T(8,128)S(1)}, u32[]{:S(2)}, u32[]{:S(2)}) %collective-permute-start.14) | collective-permute-done | bytes 36896 | tf_op jit(solution)/shard_map/ppermute | solution.py:304
  68.9 0.8 collective-permute-done.17.rest_1_
  69.7 2.9 %collective-permute-done.16.rest_0_ = f32[1,3,8,128]{3,2,1,0:T(8,128)S(1)} collective-permute-done((f32[1,3,8,128]{3,2,1,0:T(8,128)S(1)}, f32[1,3,8,128]{3,2,1,0:T(8,128)S(1)}, u32[]{:S(2)}, u32[]{:S(2)}) %collective-permute-start.16) | collective-permute-done | bytes 12320 | tf_op jit(solution)/shard_map/ppermute | solution.py:304
  72.9 12.3 %all_to_all.11.sent = f32[16,3,8,128]{3,2,1,0:T(8,128)S(1)} all-to-all(f32[16,3,8,128]{3,2,1,0:T(8,128)S(1)} %shard_map.48), channel_id=1, replica_groups=mesh['tm'=16,'space'=32] {'tm'}, dimensions={0} | all-to-all | bytes 393216 | tf_op jit(solution)/shard_map/all_to_all | solution.py:354
  85.2 0.8 shard_map.49
  (31 shorter events, 8.2 us)
Async XLA Ops:
  0.0 9.9 %copy-start = (f32[3]{0:T(128)S(1)}, f32[3]{0:T(128)}, u32[]{:S(2)}) copy-start(f32[3]{0:T(128)} %applied.1) | copy-start | bytes 40
  1.0 12.8 %collective-permute-start.1 = (f32[4,2,16,512]{3,2,1,0:T(8,128)S(1)}, f32[4,2,16,512]{3,2,1,0:T(8,128)S(1)}, u32[]{:S(2)}, u32[]{:S(2)}) collective-permute-start(f32[4,2,16,512]{3,2,1,0:T(8,128)S(1)} %pad_maximum_fusion.slab), channel_id=1, source_target_pairs={{1,0},{2,1},{3,2},{4,3},{5,4},{6,5},{7,6},{8,7},{9,8},{10,9},{11,1... | collective-permute-start | bytes 786440 | tf_op jit(solution)/shard_map/ppermute | solution.py:304
  9.9 7.0 %collective-permute-start = (f32[4,2,16,512]{3,2,1,0:T(8,128)S(1)}, f32[4,2,16,512]{3,2,1,0:T(8,128)S(1)}, u32[]{:S(2)}, u32[]{:S(2)}) collective-permute-start(f32[4,2,16,512]{3,2,1,0:T(8,128)S(1)} %pad_maximum_fusion.slab), channel_id=1, source_target_pairs={{0,1},{1,2},{2,3},{3,4},{4,5},{5,6},{6,7},{7,8},{8,9},{9,10},{10,1... | collective-permute-start | bytes 786440 | tf_op jit(solution)/shard_map/ppermute | solution.py:304
  32.7 1.8 %collective-permute-start.3 = (f32[2,2,3,8,128]{4,3,2,1,0:T(8,128)S(1)}, f32[2,2,3,8,128]{4,3,2,1,0:T(8,128)S(1)}, u32[]{:S(2)}, u32[]{:S(2)}) collective-permute-start(f32[2,2,3,8,128]{4,3,2,1,0:T(8,128)S(1)} %slice.4.own), channel_id=1, source_target_pairs={{1,0},{2,1},{3,2},{4,3},{5,4},{6,5},{7,6},{8,7},{9,8},{10,9},{11,1... | collective-permute-start | bytes 147464 | tf_op jit(solution)/shard_map/ppermute | solution.py:304
  32.7 4.7 %collective-permute-start.2 = (f32[2,2,3,8,128]{4,3,2,1,0:T(8,128)S(1)}, f32[2,2,3,8,128]{4,3,2,1,0:T(8,128)S(1)}, u32[]{:S(2)}, u32[]{:S(2)}) collective-permute-start(f32[2,2,3,8,128]{4,3,2,1,0:T(8,128)S(1)} %slice.4.own), channel_id=1, source_target_pairs={{0,1},{1,2},{2,3},{3,4},{4,5},{5,6},{6,7},{7,8},{8,9},{9,10},{10,1... | collective-permute-start | bytes 147464 | tf_op jit(solution)/shard_map/ppermute | solution.py:304
  37.9 1.7 %collective-permute-start.5 = (f32[3,3,8,128]{3,2,1,0:T(8,128)S(1)}, f32[3,3,8,128]{3,2,1,0:T(8,128)S(1)}, u32[]{:S(2)}, u32[]{:S(2)}) collective-permute-start(f32[3,3,8,128]{3,2,1,0:T(8,128)S(1)} %get-tuple-element.35), channel_id=1, source_target_pairs={{1,0},{2,1},{3,2},{4,3},{5,4},{6,5},{7,6},{8,7},{9,8},{10,9},{11,1... | collective-permute-start | bytes 110600 | tf_op jit(solution)/shard_map/ppermute | solution.py:304
  37.9 4.6 %collective-permute-start.4 = (f32[3,3,8,128]{3,2,1,0:T(8,128)S(1)}, f32[3,3,8,128]{3,2,1,0:T(8,128)S(1)}, u32[]{:S(2)}, u32[]{:S(2)}) collective-permute-start(f32[3,3,8,128]{3,2,1,0:T(8,128)S(1)} %get-tuple-element.34.own.rest_1_), channel_id=1, source_target_pairs={{0,1},{1,2},{2,3},{3,4},{4,5},{5,6},{6,7},{7,8},{8,9},{9,10},{10,1... | collective-permute-start | bytes 110600 | tf_op jit(solution)/shard_map/ppermute | solution.py:304
  43.0 1.7 %collective-permute-start.7 = (f32[3,3,8,128]{3,2,1,0:T(8,128)S(1)}, f32[3,3,8,128]{3,2,1,0:T(8,128)S(1)}, u32[]{:S(2)}, u32[]{:S(2)}) collective-permute-start(f32[3,3,8,128]{3,2,1,0:T(8,128)S(1)} %get-tuple-element.37), channel_id=1, source_target_pairs={{1,0},{2,1},{3,2},{4,3},{5,4},{6,5},{7,6},{8,7},{9,8},{10,9},{11,1... | collective-permute-start | bytes 110600 | tf_op jit(solution)/shard_map/ppermute | solution.py:304
  43.0 4.6 %collective-permute-start.6 = (f32[3,3,8,128]{3,2,1,0:T(8,128)S(1)}, f32[3,3,8,128]{3,2,1,0:T(8,128)S(1)}, u32[]{:S(2)}, u32[]{:S(2)}) collective-permute-start(f32[3,3,8,128]{3,2,1,0:T(8,128)S(1)} %get-tuple-element.36.own.rest_3_), channel_id=1, source_target_pairs={{0,1},{1,2},{2,3},{3,4},{4,5},{5,6},{6,7},{7,8},{8,9},{9,10},{10,1... | collective-permute-start | bytes 110600 | tf_op jit(solution)/shard_map/ppermute | solution.py:304
  48.0 1.7 %collective-permute-start.9 = (f32[3,3,8,128]{3,2,1,0:T(8,128)S(1)}, f32[3,3,8,128]{3,2,1,0:T(8,128)S(1)}, u32[]{:S(2)}, u32[]{:S(2)}) collective-permute-start(f32[3,3,8,128]{3,2,1,0:T(8,128)S(1)} %get-tuple-element.39), channel_id=1, source_target_pairs={{1,0},{2,1},{3,2},{4,3},{5,4},{6,5},{7,6},{8,7},{9,8},{10,9},{11,1... | collective-permute-start | bytes 110600 | tf_op jit(solution)/shard_map/ppermute | solution.py:304
  48.0 4.6 %collective-permute-start.8 = (f32[3,3,8,128]{3,2,1,0:T(8,128)S(1)}, f32[3,3,8,128]{3,2,1,0:T(8,128)S(1)}, u32[]{:S(2)}, u32[]{:S(2)}) collective-permute-start(f32[3,3,8,128]{3,2,1,0:T(8,128)S(1)} %get-tuple-element.38.own.rest_5_), channel_id=1, source_target_pairs={{0,1},{1,2},{2,3},{3,4},{4,5},{5,6},{6,7},{7,8},{8,9},{9,10},{10,1... | collective-permute-start | bytes 110600 | tf_op jit(solution)/shard_map/ppermute | solution.py:304
  53.1 1.7 %collective-permute-start.11 = (f32[3,3,8,128]{3,2,1,0:T(8,128)S(1)}, f32[3,3,8,128]{3,2,1,0:T(8,128)S(1)}, u32[]{:S(2)}, u32[]{:S(2)}) collective-permute-start(f32[3,3,8,128]{3,2,1,0:T(8,128)S(1)} %get-tuple-element.41), channel_id=1, source_target_pairs={{1,0},{2,1},{3,2},{4,3},{5,4},{6,5},{7,6},{8,7},{9,8},{10,9},{11,1... | collective-permute-start | bytes 110600 | tf_op jit(solution)/shard_map/ppermute | solution.py:304
  53.1 4.6 %collective-permute-start.10 = (f32[3,3,8,128]{3,2,1,0:T(8,128)S(1)}, f32[3,3,8,128]{3,2,1,0:T(8,128)S(1)}, u32[]{:S(2)}, u32[]{:S(2)}) collective-permute-start(f32[3,3,8,128]{3,2,1,0:T(8,128)S(1)} %get-tuple-element.40.own.rest_7_), channel_id=1, source_target_pairs={{0,1},{1,2},{2,3},{3,4},{4,5},{5,6},{6,7},{7,8},{8,9},{9,10},{10,1... | collective-permute-start | bytes 110600 | tf_op jit(solution)/shard_map/ppermute | solution.py:304
  58.1 1.7 %collective-permute-start.13 = (f32[3,3,8,128]{3,2,1,0:T(8,128)S(1)}, f32[3,3,8,128]{3,2,1,0:T(8,128)S(1)}, u32[]{:S(2)}, u32[]{:S(2)}) collective-permute-start(f32[3,3,8,128]{3,2,1,0:T(8,128)S(1)} %get-tuple-element.43), channel_id=1, source_target_pairs={{1,0},{2,1},{3,2},{4,3},{5,4},{6,5},{7,6},{8,7},{9,8},{10,9},{11,1... | collective-permute-start | bytes 110600 | tf_op jit(solution)/shard_map/ppermute | solution.py:304
  58.2 4.6 %collective-permute-start.12 = (f32[3,3,8,128]{3,2,1,0:T(8,128)S(1)}, f32[3,3,8,128]{3,2,1,0:T(8,128)S(1)}, u32[]{:S(2)}, u32[]{:S(2)}) collective-permute-start(f32[3,3,8,128]{3,2,1,0:T(8,128)S(1)} %get-tuple-element.42.own.rest_9_), channel_id=1, source_target_pairs={{0,1},{1,2},{2,3},{3,4},{4,5},{5,6},{6,7},{7,8},{8,9},{9,10},{10,1... | collective-permute-start | bytes 110600 | tf_op jit(solution)/shard_map/ppermute | solution.py:304
  63.2 1.7 %collective-permute-start.15 = (f32[3,3,8,128]{3,2,1,0:T(8,128)S(1)}, f32[3,3,8,128]{3,2,1,0:T(8,128)S(1)}, u32[]{:S(2)}, u32[]{:S(2)}) collective-permute-start(f32[3,3,8,128]{3,2,1,0:T(8,128)S(1)} %get-tuple-element.45), channel_id=1, source_target_pairs={{1,0},{2,1},{3,2},{4,3},{5,4},{6,5},{7,6},{8,7},{9,8},{10,9},{11,1... | collective-permute-start | bytes 110600 | tf_op jit(solution)/shard_map/ppermute | solution.py:304
  63.2 4.6 %collective-permute-start.14 = (f32[3,3,8,128]{3,2,1,0:T(8,128)S(1)}, f32[3,3,8,128]{3,2,1,0:T(8,128)S(1)}, u32[]{:S(2)}, u32[]{:S(2)}) collective-permute-start(f32[3,3,8,128]{3,2,1,0:T(8,128)S(1)} %get-tuple-element.44.own.rest_11_), channel_id=1, source_target_pairs={{0,1},{1,2},{2,3},{3,4},{4,5},{5,6},{6,7},{7,8},{8,9},{9,10},{10,1... | collective-permute-start | bytes 110600 | tf_op jit(solution)/shard_map/ppermute | solution.py:304
  68.3 1.4 %collective-permute-start.17 = (f32[1,3,8,128]{3,2,1,0:T(8,128)S(1)}, f32[1,3,8,128]{3,2,1,0:T(8,128)S(1)}, u32[]{:S(2)}, u32[]{:S(2)}) collective-permute-start(f32[1,3,8,128]{3,2,1,0:T(8,128)S(1)} %get-tuple-element.46.below), channel_id=1, source_target_pairs={{1,0},{2,1},{3,2},{4,3},{5,4},{6,5},{7,6},{8,7},{9,8},{10,9},{11,1... | collective-permute-start | bytes 36872 | tf_op jit(solution)/shard_map/ppermute | solution.py:304
  68.3 4.3 %collective-permute-start.16 = (f32[1,3,8,128]{3,2,1,0:T(8,128)S(1)}, f32[1,3,8,128]{3,2,1,0:T(8,128)S(1)}, u32[]{:S(2)}, u32[]{:S(2)}) collective-permute-start(f32[1,3,8,128]{3,2,1,0:T(8,128)S(1)} %get-tuple-element.47.above), channel_id=1, source_target_pairs={{0,1},{1,2},{2,3},{3,4},{4,5},{5,6},{6,7},{7,8},{8,9},{9,10},{10,1... | collective-permute-start | bytes 36872 | tf_op jit(solution)/shard_map/ppermute | solution.py:304

commit v6 on v5

--- a/solution.py
+++ b/solution.py
@@ -109,7 +109,7 @@
     return load
 
 
-def prologue(own, left, right, field, payload, sides, layers):
+def prologue(own, right, left, field, payload, sides, layers):
     by_parity(left, sides.at[0], layers.at[0])
     by_parity(right, sides.at[1], layers.at[1])
     load = beside(own, sides)
@@ -223,7 +223,7 @@
     return [ref[(*at, c)] for c in range(3)]
 
 
-def chain(block, blocks, own, left, right, corr, windows, field, *rest):
+def chain(block, blocks, own, right, left, corr, windows, field, *rest):
     applied = [field[c] for c in range(3)]
     is_even = windows[6] < 64.0
     first_slice = 2 * block + 1
@@ -301,7 +301,8 @@
     count = lax.axis_size("space")
     up = [(i, (i + 1) % count) for i in range(count)]
     down = [(j, i) for i, j in up]
-    return lax.ppermute(to_above, "space", up), lax.ppermute(to_below, "space", down)
+    from_above = lax.ppermute(to_below, "space", down)
+    return from_above, lax.ppermute(to_above, "space", up)
 
 
 def call(kernel, shapes, *args, scratch=(), **more):
@@ -320,7 +321,7 @@
     width = starts.shape[-1]
     layers = (4, 2, width // 128, 16, 128)
     slab = jnp.concatenate([starts[0], anisotropy[None]], axis=0)
-    left, right = both_sides(slab, slab)
+    right, left = both_sides(slab, slab)
     own, field = call(
         prepare,
         [(4, 2, 2, 8, width), (3, 8, 128)],
@@ -331,7 +332,7 @@
     payload, sides = call(
         prologue,
         [(slices, 2, 3, 8, 128), (2, 4, 2, 2, 8, width)],
-        *(own, left, right, field),
+        *(own, right, left, field),
         scratch=[(2, *layers)],
     )
     (windows,) = call(window, [(7, 8, 128)], own, sides)
@@ -345,11 +346,11 @@
         shapes = [(1 if ahead_of_last else 3, 3, 8, 128)] * 2 + [(2, 3, 8, 128)]
         up, down, middle = call(kernel, shapes, up, *both_sides(up, down), corr, windows, field)
         kept += [middle] if ahead_of_last else [middle, up]
-    left, right = both_sides(up, down)
+    right, left = both_sides(up, down)
     (sent,) = call(pack, [(slices, 3, 8, 128)], corr, windows, down, up, *kept)
     kernel = functools.partial(final, blocks - 1, blocks)
     (sent,) = call(
-        kernel, [sent.shape], down, up, left, right, corr, windows, field, sent, input_output_aliases={7: 0}
+        kernel, [sent.shape], down, up, right, left, corr, windows, field, sent, input_output_aliases={7: 0}
     )
     sent = lax.all_to_all(sent, "tm", 0, 0, tiled=True)
     (out,) = call(assemble, [starts.shape], sent, scratch=[(3, 2, width // 128, 16, 128)])

time: 86.2 us -> 86.7 us (level)
  starting transfers between devices: 13.1 us -> 18.4 us
  waiting for transfers between devices: 38.9 us -> 33.9 us
    ppermute x18, starting transfers between devices: 13.1 us -> 18.4 us  [the longest x9 15.4 us: both_sides(): from_above = lax.ppermute(to_below, 'space', down)]
    ppermute x18, waiting for transfers between devices: 38.9 us -> 33.9 us  [the longest x9 25.8 us: both_sides(): return (from_above, lax.ppermute(to_above, 'space', up))]
  transfers between devices with their start and end apart: 18 -> 18, of which waited for: 18 -> 16; matrix products, arithmetic and copies ran while one was open for 0% -> 0% of each run, Pallas kernels for 1% -> 1%
where the time goes in v6:
time: 86.7 us; the launch traced here: 86.5 us
  waiting for transfers between devices  33.9 us (39%)
  blocking collectives  26.9 us (31%)
  starting transfers between devices  18.4 us (21%)
  Pallas kernels  6.1 us (7%)
  other arithmetic  0.99 us (1%)
    ppermute x9, waiting for transfers between devices, both_sides(): return (from_above, lax.ppermute(to_above, 'space', up))  25.8 us
    ppermute x9, starting transfers between devices, both_sides(): from_above = lax.ppermute(to_below, 'space', down)  15.4 us
    all_to_all x1, blocking collectives, per_device(): corr = lax.all_to_all(payload, 'tm', 0, 0, tiled=True)  14.5 us
    all_to_all x1, blocking collectives, per_device(): sent = lax.all_to_all(sent, 'tm', 0, 0, tiled=True)  12.4 us
    ppermute x9, waiting for transfers between devices, both_sides(): from_above = lax.ppermute(to_below, 'space', down)  8.07 us
    pallas_call x13, Pallas kernels, call(): pl.pallas_call(kernel, out_shape=[jax.ShapeDtypeStruct(s, F32) for s in s...  6.1 us
    ppermute x9, starting transfers between devices, both_sides(): return (from_above, lax.ppermute(to_above, 'space', up))  3 us
  transfers between devices with their start and end apart: 18, of which 16 were waited for; matrix products, arithmetic and copies ran while one was open for 0% of the time, Pallas kernels for 1%

profile of v6, /device:TPU:2, one launch (start us, length us, event | category | flops | bytes accessed | tf_op | source)
XLA Modules:
  0.0 86.5 jit_solution(4652110359253081445)
XLA Ops:
  0.0 1.0 %pad_maximum_fusion.slab = f32[4,2,16,512]{3,2,1,0:T(8,128)S(1)} fusion(f32[1,2,16,512]{3,2,1,0:T(8,128)} %bitcast.3, f32[3,2,16,512]{3,2,1,0:T(8,128)} %bitcast.2), kind=kLoop, calls=%fused_computation | loop fusion | flops 65536 | bytes 524288 | tf_op jit(solution)/shard_map/concatenate | solution.py:323
  1.0 8.9 %collective-permute-start = (f32[4,2,16,512]{3,2,1,0:T(8,128)S(1)}, f32[4,2,16,512]{3,2,1,0:T(8,128)S(1)}, u32[]{:S(2)}, u32[]{:S(2)}) collective-permute-start(f32[4,2,16,512]{3,2,1,0:T(8,128)S(1)} %pad_maximum_fusion.slab), channel_id=1, source_target_pairs={{1,0},{2,1},{3,2},{4,3},{5,4},{6,5},{7,6},{8,7},{9,8},{10,9},{11,1... | collective-permute-start | bytes 786440 | tf_op jit(solution)/shard_map/ppermute | solution.py:304
  10.6 3.4 %collective-permute-done.1.left = f32[4,2,16,512]{3,2,1,0:T(8,128)S(1)} collective-permute-done((f32[4,2,16,512]{3,2,1,0:T(8,128)S(1)}, f32[4,2,16,512]{3,2,1,0:T(8,128)S(1)}, u32[]{:S(2)}, u32[]{:S(2)}) %collective-permute-start.1) | collective-permute-done | bytes 262176 | tf_op jit(solution)/shard_map/ppermute | solution.py:305
  14.0 1.2 %shard_map.38 = (f32[16,2,3,8,128]{4,3,2,1,0:T(8,128)S(1)}, f32[2,4,2,2,8,512]{5,4,3,2,1,0:T(8,128)S(1)}) custom-call(f32[4,2,2,8,512]{4,3,2,1,0:T(8,128)S(1)} %get-tuple-element.30.own, f32[4,2,16,512]{3,2,1,0:T(8,128)S(1)} %collective-permute-done.right, f32[4,2,16,512]{3,2,1,0:T(8,128)S(1)} %collective-permute-done.1.left, ...), custom_call_target="tpu_custom_call" | custom-call | tf_op jit(solution)/shard_map/pallas_call | solution.py:309
  15.2 14.5 %all_to_all.10.corr.rest_2_ = f32[16,2,3,8,128]{4,3,2,1,0:T(8,128)S(1)} all-to-all(f32[16,2,3,8,128]{4,3,2,1,0:T(8,128)S(1)} %get-tuple-element.32), channel_id=1, replica_groups=mesh['tm'=16,'space'=32] {'tm'}, dimensions={0} | all-to-all | bytes 786432 | tf_op jit(solution)/shard_map/all_to_all | solution.py:339
  29.8 3.3 %collective-permute-start.2 = (f32[2,2,3,8,128]{4,3,2,1,0:T(8,128)S(1)}, f32[2,2,3,8,128]{4,3,2,1,0:T(8,128)S(1)}, u32[]{:S(2)}, u32[]{:S(2)}) collective-permute-start(f32[2,2,3,8,128]{4,3,2,1,0:T(8,128)S(1)} %slice.4.own), channel_id=1, source_target_pairs={{1,0},{2,1},{3,2},{4,3},{5,4},{6,5},{7,6},{8,7},{9,8},{10,9},{11,1... | collective-permute-start | bytes 147464 | tf_op jit(solution)/shard_map/ppermute | solution.py:304
  33.3 1.6 %collective-permute-done.3.left = f32[2,2,3,8,128]{4,3,2,1,0:T(8,128)S(1)} collective-permute-done((f32[2,2,3,8,128]{4,3,2,1,0:T(8,128)S(1)}, f32[2,2,3,8,128]{4,3,2,1,0:T(8,128)S(1)}, u32[]{:S(2)}, u32[]{:S(2)}) %collective-permute-start.3) | collective-permute-done | bytes 49184 | tf_op jit(solution)/shard_map/ppermute | solution.py:305
  35.3 3.0 %collective-permute-start.4 = (f32[3,3,8,128]{3,2,1,0:T(8,128)S(1)}, f32[3,3,8,128]{3,2,1,0:T(8,128)S(1)}, u32[]{:S(2)}, u32[]{:S(2)}) collective-permute-start(f32[3,3,8,128]{3,2,1,0:T(8,128)S(1)} %get-tuple-element.35), channel_id=1, source_target_pairs={{1,0},{2,1},{3,2},{4,3},{5,4},{6,5},{7,6},{8,7},{9,8},{10,9},{11,1... | collective-permute-start | bytes 110600 | tf_op jit(solution)/shard_map/ppermute | solution.py:304
  38.3 1.6 %collective-permute-done.4.right = f32[3,3,8,128]{3,2,1,0:T(8,128)S(1)} collective-permute-done((f32[3,3,8,128]{3,2,1,0:T(8,128)S(1)}, f32[3,3,8,128]{3,2,1,0:T(8,128)S(1)}, u32[]{:S(2)}, u32[]{:S(2)}) %collective-permute-start.4) | collective-permute-done | bytes 36896 | tf_op jit(solution)/shard_map/ppermute | solution.py:304
  39.9 3.0 %collective-permute-done.5.left = f32[3,3,8,128]{3,2,1,0:T(8,128)S(1)} collective-permute-done((f32[3,3,8,128]{3,2,1,0:T(8,128)S(1)}, f32[3,3,8,128]{3,2,1,0:T(8,128)S(1)}, u32[]{:S(2)}, u32[]{:S(2)}) %collective-permute-start.5) | collective-permute-done | bytes 36896 | tf_op jit(solution)/shard_map/ppermute | solution.py:305
  43.8 1.1 %collective-permute-done.6.right = f32[3,3,8,128]{3,2,1,0:T(8,128)S(1)} collective-permute-done((f32[3,3,8,128]{3,2,1,0:T(8,128)S(1)}, f32[3,3,8,128]{3,2,1,0:T(8,128)S(1)}, u32[]{:S(2)}, u32[]{:S(2)}) %collective-permute-start.6) | collective-permute-done | bytes 36896 | tf_op jit(solution)/shard_map/ppermute | solution.py:304
  45.0 3.0 %collective-permute-done.7.left = f32[3,3,8,128]{3,2,1,0:T(8,128)S(1)} collective-permute-done((f32[3,3,8,128]{3,2,1,0:T(8,128)S(1)}, f32[3,3,8,128]{3,2,1,0:T(8,128)S(1)}, u32[]{:S(2)}, u32[]{:S(2)}) %collective-permute-start.7) | collective-permute-done | bytes 36896 | tf_op jit(solution)/shard_map/ppermute | solution.py:305
  48.9 1.1 %collective-permute-done.8.right = f32[3,3,8,128]{3,2,1,0:T(8,128)S(1)} collective-permute-done((f32[3,3,8,128]{3,2,1,0:T(8,128)S(1)}, f32[3,3,8,128]{3,2,1,0:T(8,128)S(1)}, u32[]{:S(2)}, u32[]{:S(2)}) %collective-permute-start.8) | collective-permute-done | bytes 36896 | tf_op jit(solution)/shard_map/ppermute | solution.py:304
  50.0 3.0 %collective-permute-done.9.left = f32[3,3,8,128]{3,2,1,0:T(8,128)S(1)} collective-permute-done((f32[3,3,8,128]{3,2,1,0:T(8,128)S(1)}, f32[3,3,8,128]{3,2,1,0:T(8,128)S(1)}, u32[]{:S(2)}, u32[]{:S(2)}) %collective-permute-start.9) | collective-permute-done | bytes 36896 | tf_op jit(solution)/shard_map/ppermute | solution.py:305
  54.0 1.1 %collective-permute-done.10.right = f32[3,3,8,128]{3,2,1,0:T(8,128)S(1)} collective-permute-done((f32[3,3,8,128]{3,2,1,0:T(8,128)S(1)}, f32[3,3,8,128]{3,2,1,0:T(8,128)S(1)}, u32[]{:S(2)}, u32[]{:S(2)}) %collective-permute-start.10) | collective-permute-done | bytes 36896 | tf_op jit(solution)/shard_map/ppermute | solution.py:304
  55.1 3.0 %collective-permute-done.11.left = f32[3,3,8,128]{3,2,1,0:T(8,128)S(1)} collective-permute-done((f32[3,3,8,128]{3,2,1,0:T(8,128)S(1)}, f32[3,3,8,128]{3,2,1,0:T(8,128)S(1)}, u32[]{:S(2)}, u32[]{:S(2)}) %collective-permute-start.11) | collective-permute-done | bytes 36896 | tf_op jit(solution)/shard_map/ppermute | solution.py:305
  59.0 1.1 %collective-permute-done.12.right = f32[3,3,8,128]{3,2,1,0:T(8,128)S(1)} collective-permute-done((f32[3,3,8,128]{3,2,1,0:T(8,128)S(1)}, f32[3,3,8,128]{3,2,1,0:T(8,128)S(1)}, u32[]{:S(2)}, u32[]{:S(2)}) %collective-permute-start.12) | collective-permute-done | bytes 36896 | tf_op jit(solution)/shard_map/ppermute | solution.py:304
  60.2 3.0 %collective-permute-done.13.left = f32[3,3,8,128]{3,2,1,0:T(8,128)S(1)} collective-permute-done((f32[3,3,8,128]{3,2,1,0:T(8,128)S(1)}, f32[3,3,8,128]{3,2,1,0:T(8,128)S(1)}, u32[]{:S(2)}, u32[]{:S(2)}) %collective-permute-start.13) | collective-permute-done | bytes 36896 | tf_op jit(solution)/shard_map/ppermute | solution.py:305
  64.1 1.1 %collective-permute-done.14.right = f32[3,3,8,128]{3,2,1,0:T(8,128)S(1)} collective-permute-done((f32[3,3,8,128]{3,2,1,0:T(8,128)S(1)}, f32[3,3,8,128]{3,2,1,0:T(8,128)S(1)}, u32[]{:S(2)}, u32[]{:S(2)}) %collective-permute-start.14) | collective-permute-done | bytes 36896 | tf_op jit(solution)/shard_map/ppermute | solution.py:304
  65.2 3.0 %collective-permute-done.15.left = f32[3,3,8,128]{3,2,1,0:T(8,128)S(1)} collective-permute-done((f32[3,3,8,128]{3,2,1,0:T(8,128)S(1)}, f32[3,3,8,128]{3,2,1,0:T(8,128)S(1)}, u32[]{:S(2)}, u32[]{:S(2)}) %collective-permute-start.15) | collective-permute-done | bytes 36896 | tf_op jit(solution)/shard_map/ppermute | solution.py:305
  69.3 0.8 collective-permute-done.16.rest_0_
  70.1 2.9 %collective-permute-done.17.rest_1_ = f32[1,3,8,128]{3,2,1,0:T(8,128)S(1)} collective-permute-done((f32[1,3,8,128]{3,2,1,0:T(8,128)S(1)}, f32[1,3,8,128]{3,2,1,0:T(8,128)S(1)}, u32[]{:S(2)}, u32[]{:S(2)}) %collective-permute-start.17) | collective-permute-done | bytes 12320 | tf_op jit(solution)/shard_map/ppermute | solution.py:305
  73.3 12.4 %all_to_all.11.sent = f32[16,3,8,128]{3,2,1,0:T(8,128)S(1)} all-to-all(f32[16,3,8,128]{3,2,1,0:T(8,128)S(1)} %shard_map.48), channel_id=1, replica_groups=mesh['tm'=16,'space'=32] {'tm'}, dimensions={0} | all-to-all | bytes 393216 | tf_op jit(solution)/shard_map/all_to_all | solution.py:355
  85.7 0.8 shard_map.49
  (31 shorter events, 7.2 us)
Async XLA Ops:
  0.0 10.0 %copy-start = (f32[3]{0:T(128)S(1)}, f32[3]{0:T(128)}, u32[]{:S(2)}) copy-start(f32[3]{0:T(128)} %applied.1) | copy-start | bytes 40
  1.0 13.0 %collective-permute-start.1 = (f32[4,2,16,512]{3,2,1,0:T(8,128)S(1)}, f32[4,2,16,512]{3,2,1,0:T(8,128)S(1)}, u32[]{:S(2)}, u32[]{:S(2)}) collective-permute-start(f32[4,2,16,512]{3,2,1,0:T(8,128)S(1)} %pad_maximum_fusion.slab), channel_id=1, source_target_pairs={{0,1},{1,2},{2,3},{3,4},{4,5},{5,6},{6,7},{7,8},{8,9},{9,10},{10,1... | collective-permute-start | bytes 786440 | tf_op jit(solution)/shard_map/ppermute | solution.py:305
  1.0 13.0 %collective-permute-start = (f32[4,2,16,512]{3,2,1,0:T(8,128)S(1)}, f32[4,2,16,512]{3,2,1,0:T(8,128)S(1)}, u32[]{:S(2)}, u32[]{:S(2)}) collective-permute-start(f32[4,2,16,512]{3,2,1,0:T(8,128)S(1)} %pad_maximum_fusion.slab), channel_id=1, source_target_pairs={{1,0},{2,1},{3,2},{4,3},{5,4},{6,5},{7,6},{8,7},{9,8},{10,9},{11,1... | collective-permute-start | bytes 786440 | tf_op jit(solution)/shard_map/ppermute | solution.py:304
  29.8 5.1 %collective-permute-start.3 = (f32[2,2,3,8,128]{4,3,2,1,0:T(8,128)S(1)}, f32[2,2,3,8,128]{4,3,2,1,0:T(8,128)S(1)}, u32[]{:S(2)}, u32[]{:S(2)}) collective-permute-start(f32[2,2,3,8,128]{4,3,2,1,0:T(8,128)S(1)} %slice.4.own), channel_id=1, source_target_pairs={{0,1},{1,2},{2,3},{3,4},{4,5},{5,6},{6,7},{7,8},{8,9},{9,10},{10,1... | collective-permute-start | bytes 147464 | tf_op jit(solution)/shard_map/ppermute | solution.py:305
  29.8 5.1 %collective-permute-start.2 = (f32[2,2,3,8,128]{4,3,2,1,0:T(8,128)S(1)}, f32[2,2,3,8,128]{4,3,2,1,0:T(8,128)S(1)}, u32[]{:S(2)}, u32[]{:S(2)}) collective-permute-start(f32[2,2,3,8,128]{4,3,2,1,0:T(8,128)S(1)} %slice.4.own), channel_id=1, source_target_pairs={{1,0},{2,1},{3,2},{4,3},{5,4},{6,5},{7,6},{8,7},{9,8},{10,9},{11,1... | collective-permute-start | bytes 147464 | tf_op jit(solution)/shard_map/ppermute | solution.py:304
  35.3 4.6 %collective-permute-start.4 = (f32[3,3,8,128]{3,2,1,0:T(8,128)S(1)}, f32[3,3,8,128]{3,2,1,0:T(8,128)S(1)}, u32[]{:S(2)}, u32[]{:S(2)}) collective-permute-start(f32[3,3,8,128]{3,2,1,0:T(8,128)S(1)} %get-tuple-element.35), channel_id=1, source_target_pairs={{1,0},{2,1},{3,2},{4,3},{5,4},{6,5},{7,6},{8,7},{9,8},{10,9},{11,1... | collective-permute-start | bytes 110600 | tf_op jit(solution)/shard_map/ppermute | solution.py:304
  38.3 4.6 %collective-permute-start.5 = (f32[3,3,8,128]{3,2,1,0:T(8,128)S(1)}, f32[3,3,8,128]{3,2,1,0:T(8,128)S(1)}, u32[]{:S(2)}, u32[]{:S(2)}) collective-permute-start(f32[3,3,8,128]{3,2,1,0:T(8,128)S(1)} %get-tuple-element.34.own.rest_1_), channel_id=1, source_target_pairs={{0,1},{1,2},{2,3},{3,4},{4,5},{5,6},{6,7},{7,8},{8,9},{9,10},{10,1... | collective-permute-start | bytes 110600 | tf_op jit(solution)/shard_map/ppermute | solution.py:305
  43.3 1.7 %collective-permute-start.6 = (f32[3,3,8,128]{3,2,1,0:T(8,128)S(1)}, f32[3,3,8,128]{3,2,1,0:T(8,128)S(1)}, u32[]{:S(2)}, u32[]{:S(2)}) collective-permute-start(f32[3,3,8,128]{3,2,1,0:T(8,128)S(1)} %get-tuple-element.37), channel_id=1, source_target_pairs={{1,0},{2,1},{3,2},{4,3},{5,4},{6,5},{7,6},{8,7},{9,8},{10,9},{11,1... | collective-permute-start | bytes 110600 | tf_op jit(solution)/shard_map/ppermute | solution.py:304
  43.3 4.6 %collective-permute-start.7 = (f32[3,3,8,128]{3,2,1,0:T(8,128)S(1)}, f32[3,3,8,128]{3,2,1,0:T(8,128)S(1)}, u32[]{:S(2)}, u32[]{:S(2)}) collective-permute-start(f32[3,3,8,128]{3,2,1,0:T(8,128)S(1)} %get-tuple-element.36.own.rest_3_), channel_id=1, source_target_pairs={{0,1},{1,2},{2,3},{3,4},{4,5},{5,6},{6,7},{7,8},{8,9},{9,10},{10,1... | collective-permute-start | bytes 110600 | tf_op jit(solution)/shard_map/ppermute | solution.py:305
  48.4 1.7 %collective-permute-start.8 = (f32[3,3,8,128]{3,2,1,0:T(8,128)S(1)}, f32[3,3,8,128]{3,2,1,0:T(8,128)S(1)}, u32[]{:S(2)}, u32[]{:S(2)}) collective-permute-start(f32[3,3,8,128]{3,2,1,0:T(8,128)S(1)} %get-tuple-element.39), channel_id=1, source_target_pairs={{1,0},{2,1},{3,2},{4,3},{5,4},{6,5},{7,6},{8,7},{9,8},{10,9},{11,1... | collective-permute-start | bytes 110600 | tf_op jit(solution)/shard_map/ppermute | solution.py:304
  48.4 4.6 %collective-permute-start.9 = (f32[3,3,8,128]{3,2,1,0:T(8,128)S(1)}, f32[3,3,8,128]{3,2,1,0:T(8,128)S(1)}, u32[]{:S(2)}, u32[]{:S(2)}) collective-permute-start(f32[3,3,8,128]{3,2,1,0:T(8,128)S(1)} %get-tuple-element.38.own.rest_5_), channel_id=1, source_target_pairs={{0,1},{1,2},{2,3},{3,4},{4,5},{5,6},{6,7},{7,8},{8,9},{9,10},{10,1... | collective-permute-start | bytes 110600 | tf_op jit(solution)/shard_map/ppermute | solution.py:305
  53.4 1.7 %collective-permute-start.10 = (f32[3,3,8,128]{3,2,1,0:T(8,128)S(1)}, f32[3,3,8,128]{3,2,1,0:T(8,128)S(1)}, u32[]{:S(2)}, u32[]{:S(2)}) collective-permute-start(f32[3,3,8,128]{3,2,1,0:T(8,128)S(1)} %get-tuple-element.41), channel_id=1, source_target_pairs={{1,0},{2,1},{3,2},{4,3},{5,4},{6,5},{7,6},{8,7},{9,8},{10,9},{11,1... | collective-permute-start | bytes 110600 | tf_op jit(solution)/shard_map/ppermute | solution.py:304
  53.5 4.6 %collective-permute-start.11 = (f32[3,3,8,128]{3,2,1,0:T(8,128)S(1)}, f32[3,3,8,128]{3,2,1,0:T(8,128)S(1)}, u32[]{:S(2)}, u32[]{:S(2)}) collective-permute-start(f32[3,3,8,128]{3,2,1,0:T(8,128)S(1)} %get-tuple-element.40.own.rest_7_), channel_id=1, source_target_pairs={{0,1},{1,2},{2,3},{3,4},{4,5},{5,6},{6,7},{7,8},{8,9},{9,10},{10,1... | collective-permute-start | bytes 110600 | tf_op jit(solution)/shard_map/ppermute | solution.py:305
  58.5 1.7 %collective-permute-start.12 = (f32[3,3,8,128]{3,2,1,0:T(8,128)S(1)}, f32[3,3,8,128]{3,2,1,0:T(8,128)S(1)}, u32[]{:S(2)}, u32[]{:S(2)}) collective-permute-start(f32[3,3,8,128]{3,2,1,0:T(8,128)S(1)} %get-tuple-element.43), channel_id=1, source_target_pairs={{1,0},{2,1},{3,2},{4,3},{5,4},{6,5},{7,6},{8,7},{9,8},{10,9},{11,1... | collective-permute-start | bytes 110600 | tf_op jit(solution)/shard_map/ppermute | solution.py:304
  58.5 4.6 %collective-permute-start.13 = (f32[3,3,8,128]{3,2,1,0:T(8,128)S(1)}, f32[3,3,8,128]{3,2,1,0:T(8,128)S(1)}, u32[]{:S(2)}, u32[]{:S(2)}) collective-permute-start(f32[3,3,8,128]{3,2,1,0:T(8,128)S(1)} %get-tuple-element.42.own.rest_9_), channel_id=1, source_target_pairs={{0,1},{1,2},{2,3},{3,4},{4,5},{5,6},{6,7},{7,8},{8,9},{9,10},{10,1... | collective-permute-start | bytes 110600 | tf_op jit(solution)/shard_map/ppermute | solution.py:305
  63.6 1.7 %collective-permute-start.14 = (f32[3,3,8,128]{3,2,1,0:T(8,128)S(1)}, f32[3,3,8,128]{3,2,1,0:T(8,128)S(1)}, u32[]{:S(2)}, u32[]{:S(2)}) collective-permute-start(f32[3,3,8,128]{3,2,1,0:T(8,128)S(1)} %get-tuple-element.45), channel_id=1, source_target_pairs={{1,0},{2,1},{3,2},{4,3},{5,4},{6,5},{7,6},{8,7},{9,8},{10,9},{11,1... | collective-permute-start | bytes 110600 | tf_op jit(solution)/shard_map/ppermute | solution.py:304
  63.6 4.6 %collective-permute-start.15 = (f32[3,3,8,128]{3,2,1,0:T(8,128)S(1)}, f32[3,3,8,128]{3,2,1,0:T(8,128)S(1)}, u32[]{:S(2)}, u32[]{:S(2)}) collective-permute-start(f32[3,3,8,128]{3,2,1,0:T(8,128)S(1)} %get-tuple-element.44.own.rest_11_), channel_id=1, source_target_pairs={{0,1},{1,2},{2,3},{3,4},{4,5},{5,6},{6,7},{7,8},{8,9},{9,10},{10,1... | collective-permute-start | bytes 110600 | tf_op jit(solution)/shard_map/ppermute | solution.py:305
  68.6 1.4 %collective-permute-start.16 = (f32[1,3,8,128]{3,2,1,0:T(8,128)S(1)}, f32[1,3,8,128]{3,2,1,0:T(8,128)S(1)}, u32[]{:S(2)}, u32[]{:S(2)}) collective-permute-start(f32[1,3,8,128]{3,2,1,0:T(8,128)S(1)} %get-tuple-element.46.below), channel_id=1, source_target_pairs={{1,0},{2,1},{3,2},{4,3},{5,4},{6,5},{7,6},{8,7},{9,8},{10,9},{11,1... | collective-permute-start | bytes 36872 | tf_op jit(solution)/shard_map/ppermute | solution.py:304
  68.7 4.3 %collective-permute-start.17 = (f32[1,3,8,128]{3,2,1,0:T(8,128)S(1)}, f32[1,3,8,128]{3,2,1,0:T(8,128)S(1)}, u32[]{:S(2)}, u32[]{:S(2)}) collective-permute-start(f32[1,3,8,128]{3,2,1,0:T(8,128)S(1)} %get-tuple-element.47.above), channel_id=1, source_target_pairs={{0,1},{1,2},{2,3},{3,4},{4,5},{5,6},{6,7},{7,8},{8,9},{9,10},{10,1... | collective-permute-start | bytes 36872 | tf_op jit(solution)/shard_map/ppermute | solution.py:305

commit v7 on v6

--- a/solution.py
+++ b/solution.py
@@ -271,7 +271,7 @@
             down[2, c] = corr[first_slice + 2, 0, c]
 
 
-def final(block, blocks, below, above, *rest):
+def final(block, blocks, above, below, *rest):
     chain(block, blocks, (below, above), *rest)
 
 
@@ -344,13 +344,13 @@
         kernel = functools.partial(chain, block, blocks)
         ahead_of_last = block == blocks - 2
         shapes = [(1 if ahead_of_last else 3, 3, 8, 128)] * 2 + [(2, 3, 8, 128)]
-        up, down, middle = call(kernel, shapes, up, *both_sides(up, down), corr, windows, field)
-        kept += [middle] if ahead_of_last else [middle, up]
+        up, down, middle = call(kernel, shapes, down, *both_sides(up, down), corr, windows, field)
+        kept += [middle] if ahead_of_last else [middle, down]
     right, left = both_sides(up, down)
     (sent,) = call(pack, [(slices, 3, 8, 128)], corr, windows, down, up, *kept)
     kernel = functools.partial(final, blocks - 1, blocks)
     (sent,) = call(
-        kernel, [sent.shape], down, up, right, left, corr, windows, field, sent, input_output_aliases={7: 0}
+        kernel, [sent.shape], up, down, right, left, corr, windows, field, sent, input_output_aliases={7: 0}
     )
     sent = lax.all_to_all(sent, "tm", 0, 0, tiled=True)
     (out,) = call(assemble, [starts.shape], sent, scratch=[(3, 2, width // 128, 16, 128)])

time: 86.7 us -> 83.8 us (0.967)
  waiting for transfers between devices: 33.9 us -> 16.2 us
  starting transfers between devices: 18.4 us -> 33.2 us
    ppermute x9, starting transfers between devices: 15.4 us -> 33.1 us  [both_sides(): from_above = lax.ppermute(to_below, 'space', down)]
    ppermute x9, waiting for transfers between devices: 25.8 us -> 16 us  [both_sides(): return (from_above, lax.ppermute(to_above, 'space', up))]
    ppermute x9, waiting for transfers between devices: 8.07 us -> 0.17 us  [both_sides(): from_above = lax.ppermute(to_below, 'space', down)]
    ppermute x9, starting transfers between devices: 3 us -> 0.15 us  [both_sides(): return (from_above, lax.ppermute(to_above, 'space', up))]
  transfers between devices with their start and end apart: 18 -> 18, of which waited for: 16 -> 10; matrix products, arithmetic and copies ran while one was open for 0% -> 0% of each run, Pallas kernels for 1% -> 1%
where the time goes in v7:
time: 83.8 us; the launch traced here: 83.6 us
  starting transfers between devices  33.2 us (40%)
  blocking collectives  26.9 us (32%)
  waiting for transfers between devices  16.2 us (19%)
  Pallas kernels  6.1 us (7%)
  other arithmetic  0.99 us (1%)
    ppermute x9, starting transfers between devices, both_sides(): from_above = lax.ppermute(to_below, 'space', down)  33.1 us
    ppermute x9, waiting for transfers between devices, both_sides(): return (from_above, lax.ppermute(to_above, 'space', up))  16 us
    all_to_all x1, blocking collectives, per_device(): corr = lax.all_to_all(payload, 'tm', 0, 0, tiled=True)  14.5 us
    all_to_all x1, blocking collectives, per_device(): sent = lax.all_to_all(sent, 'tm', 0, 0, tiled=True)  12.4 us
    pallas_call x13, Pallas kernels, call(): pl.pallas_call(kernel, out_shape=[jax.ShapeDtypeStruct(s, F32) for s in s...  6.1 us
  transfers between devices with their start and end apart: 18, of which 10 were waited for; matrix products, arithmetic and copies ran while one was open for 0% of the time, Pallas kernels for 1%

profile of v7, /device:TPU:2, one launch (start us, length us, event | category | flops | bytes accessed | tf_op | source)
XLA Modules:
  0.0 83.6 jit_solution(9781999550794415188)
XLA Ops:
  0.0 1.0 %pad_maximum_fusion.slab = f32[4,2,16,512]{3,2,1,0:T(8,128)S(1)} fusion(f32[1,2,16,512]{3,2,1,0:T(8,128)} %bitcast.3, f32[3,2,16,512]{3,2,1,0:T(8,128)} %bitcast.2), kind=kLoop, calls=%fused_computation | loop fusion | flops 65536 | bytes 524288 | tf_op jit(solution)/shard_map/concatenate | solution.py:323
  1.0 8.9 %collective-permute-start = (f32[4,2,16,512]{3,2,1,0:T(8,128)S(1)}, f32[4,2,16,512]{3,2,1,0:T(8,128)S(1)}, u32[]{:S(2)}, u32[]{:S(2)}) collective-permute-start(f32[4,2,16,512]{3,2,1,0:T(8,128)S(1)} %pad_maximum_fusion.slab), channel_id=1, source_target_pairs={{1,0},{2,1},{3,2},{4,3},{5,4},{6,5},{7,6},{8,7},{9,8},{10,9},{11,1... | collective-permute-start | bytes 786440 | tf_op jit(solution)/shard_map/ppermute | solution.py:304
  10.0 0.6 shard_map.37
  10.6 3.4 %collective-permute-done.1.left = f32[4,2,16,512]{3,2,1,0:T(8,128)S(1)} collective-permute-done((f32[4,2,16,512]{3,2,1,0:T(8,128)S(1)}, f32[4,2,16,512]{3,2,1,0:T(8,128)S(1)}, u32[]{:S(2)}, u32[]{:S(2)}) %collective-permute-start.1) | collective-permute-done | bytes 262176 | tf_op jit(solution)/shard_map/ppermute | solution.py:305
  14.0 1.2 %shard_map.38 = (f32[16,2,3,8,128]{4,3,2,1,0:T(8,128)S(1)}, f32[2,4,2,2,8,512]{5,4,3,2,1,0:T(8,128)S(1)}) custom-call(f32[4,2,2,8,512]{4,3,2,1,0:T(8,128)S(1)} %get-tuple-element.30.own, f32[4,2,16,512]{3,2,1,0:T(8,128)S(1)} %collective-permute-done.right, f32[4,2,16,512]{3,2,1,0:T(8,128)S(1)} %collective-permute-done.1.left, ...), custom_call_target="tpu_custom_call" | custom-call | tf_op jit(solution)/shard_map/pallas_call | solution.py:309
  15.2 14.5 %all_to_all.10.corr.rest_2_ = f32[16,2,3,8,128]{4,3,2,1,0:T(8,128)S(1)} all-to-all(f32[16,2,3,8,128]{4,3,2,1,0:T(8,128)S(1)} %get-tuple-element.32), channel_id=1, replica_groups=mesh['tm'=16,'space'=32] {'tm'}, dimensions={0} | all-to-all | bytes 786432 | tf_op jit(solution)/shard_map/all_to_all | solution.py:339
  29.8 3.3 %collective-permute-start.2 = (f32[2,2,3,8,128]{4,3,2,1,0:T(8,128)S(1)}, f32[2,2,3,8,128]{4,3,2,1,0:T(8,128)S(1)}, u32[]{:S(2)}, u32[]{:S(2)}) collective-permute-start(f32[2,2,3,8,128]{4,3,2,1,0:T(8,128)S(1)} %slice.4.own), channel_id=1, source_target_pairs={{1,0},{2,1},{3,2},{4,3},{5,4},{6,5},{7,6},{8,7},{9,8},{10,9},{11,1... | collective-permute-start | bytes 147464 | tf_op jit(solution)/shard_map/ppermute | solution.py:304
  33.3 1.6 %collective-permute-done.3.left = f32[2,2,3,8,128]{4,3,2,1,0:T(8,128)S(1)} collective-permute-done((f32[2,2,3,8,128]{4,3,2,1,0:T(8,128)S(1)}, f32[2,2,3,8,128]{4,3,2,1,0:T(8,128)S(1)}, u32[]{:S(2)}, u32[]{:S(2)}) %collective-permute-start.3) | collective-permute-done | bytes 49184 | tf_op jit(solution)/shard_map/ppermute | solution.py:305
  35.3 3.0 %collective-permute-start.4 = (f32[3,3,8,128]{3,2,1,0:T(8,128)S(1)}, f32[3,3,8,128]{3,2,1,0:T(8,128)S(1)}, u32[]{:S(2)}, u32[]{:S(2)}) collective-permute-start(f32[3,3,8,128]{3,2,1,0:T(8,128)S(1)} %get-tuple-element.34.own.rest_1_), channel_id=1, source_target_pairs={{1,0},{2,1},{3,2},{4,3},{5,4},{6,5},{7,6},{8,7},{9,8},{10,9},{11,1... | collective-permute-start | bytes 110600 | tf_op jit(solution)/shard_map/ppermute | solution.py:304
  38.3 1.6 %collective-permute-done.5.left = f32[3,3,8,128]{3,2,1,0:T(8,128)S(1)} collective-permute-done((f32[3,3,8,128]{3,2,1,0:T(8,128)S(1)}, f32[3,3,8,128]{3,2,1,0:T(8,128)S(1)}, u32[]{:S(2)}, u32[]{:S(2)}) %collective-permute-start.5) | collective-permute-done | bytes 36896 | tf_op jit(solution)/shard_map/ppermute | solution.py:305
  40.4 3.0 %collective-permute-start.6 = (f32[3,3,8,128]{3,2,1,0:T(8,128)S(1)}, f32[3,3,8,128]{3,2,1,0:T(8,128)S(1)}, u32[]{:S(2)}, u32[]{:S(2)}) collective-permute-start(f32[3,3,8,128]{3,2,1,0:T(8,128)S(1)} %get-tuple-element.36.own.rest_3_), channel_id=1, source_target_pairs={{1,0},{2,1},{3,2},{4,3},{5,4},{6,5},{7,6},{8,7},{9,8},{10,9},{11,1... | collective-permute-start | bytes 110600 | tf_op jit(solution)/shard_map/ppermute | solution.py:304
  43.4 1.6 %collective-permute-done.7.left = f32[3,3,8,128]{3,2,1,0:T(8,128)S(1)} collective-permute-done((f32[3,3,8,128]{3,2,1,0:T(8,128)S(1)}, f32[3,3,8,128]{3,2,1,0:T(8,128)S(1)}, u32[]{:S(2)}, u32[]{:S(2)}) %collective-permute-start.7) | collective-permute-done | bytes 36896 | tf_op jit(solution)/shard_map/ppermute | solution.py:305
  45.5 3.0 %collective-permute-start.8 = (f32[3,3,8,128]{3,2,1,0:T(8,128)S(1)}, f32[3,3,8,128]{3,2,1,0:T(8,128)S(1)}, u32[]{:S(2)}, u32[]{:S(2)}) collective-permute-start(f32[3,3,8,128]{3,2,1,0:T(8,128)S(1)} %get-tuple-element.38.own.rest_5_), channel_id=1, source_target_pairs={{1,0},{2,1},{3,2},{4,3},{5,4},{6,5},{7,6},{8,7},{9,8},{10,9},{11,1... | collective-permute-start | bytes 110600 | tf_op jit(solution)/shard_map/ppermute | solution.py:304
  48.4 1.6 %collective-permute-done.9.left = f32[3,3,8,128]{3,2,1,0:T(8,128)S(1)} collective-permute-done((f32[3,3,8,128]{3,2,1,0:T(8,128)S(1)}, f32[3,3,8,128]{3,2,1,0:T(8,128)S(1)}, u32[]{:S(2)}, u32[]{:S(2)}) %collective-permute-start.9) | collective-permute-done | bytes 36896 | tf_op jit(solution)/shard_map/ppermute | solution.py:305
  50.5 3.0 %collective-permute-start.10 = (f32[3,3,8,128]{3,2,1,0:T(8,128)S(1)}, f32[3,3,8,128]{3,2,1,0:T(8,128)S(1)}, u32[]{:S(2)}, u32[]{:S(2)}) collective-permute-start(f32[3,3,8,128]{3,2,1,0:T(8,128)S(1)} %get-tuple-element.40.own.rest_7_), channel_id=1, source_target_pairs={{1,0},{2,1},{3,2},{4,3},{5,4},{6,5},{7,6},{8,7},{9,8},{10,9},{11,1... | collective-permute-start | bytes 110600 | tf_op jit(solution)/shard_map/ppermute | solution.py:304
  53.5 1.6 %collective-permute-done.11.left = f32[3,3,8,128]{3,2,1,0:T(8,128)S(1)} collective-permute-done((f32[3,3,8,128]{3,2,1,0:T(8,128)S(1)}, f32[3,3,8,128]{3,2,1,0:T(8,128)S(1)}, u32[]{:S(2)}, u32[]{:S(2)}) %collective-permute-start.11) | collective-permute-done | bytes 36896 | tf_op jit(solution)/shard_map/ppermute | solution.py:305
  55.6 3.0 %collective-permute-start.12 = (f32[3,3,8,128]{3,2,1,0:T(8,128)S(1)}, f32[3,3,8,128]{3,2,1,0:T(8,128)S(1)}, u32[]{:S(2)}, u32[]{:S(2)}) collective-permute-start(f32[3,3,8,128]{3,2,1,0:T(8,128)S(1)} %get-tuple-element.42.own.rest_9_), channel_id=1, source_target_pairs={{1,0},{2,1},{3,2},{4,3},{5,4},{6,5},{7,6},{8,7},{9,8},{10,9},{11,1... | collective-permute-start | bytes 110600 | tf_op jit(solution)/shard_map/ppermute | solution.py:304
  58.6 1.6 %collective-permute-done.13.left = f32[3,3,8,128]{3,2,1,0:T(8,128)S(1)} collective-permute-done((f32[3,3,8,128]{3,2,1,0:T(8,128)S(1)}, f32[3,3,8,128]{3,2,1,0:T(8,128)S(1)}, u32[]{:S(2)}, u32[]{:S(2)}) %collective-permute-start.13) | collective-permute-done | bytes 36896 | tf_op jit(solution)/shard_map/ppermute | solution.py:305
  60.7 3.0 %collective-permute-start.14 = (f32[3,3,8,128]{3,2,1,0:T(8,128)S(1)}, f32[3,3,8,128]{3,2,1,0:T(8,128)S(1)}, u32[]{:S(2)}, u32[]{:S(2)}) collective-permute-start(f32[3,3,8,128]{3,2,1,0:T(8,128)S(1)} %get-tuple-element.44.own.rest_11_), channel_id=1, source_target_pairs={{1,0},{2,1},{3,2},{4,3},{5,4},{6,5},{7,6},{8,7},{9,8},{10,9},{11,1... | collective-permute-start | bytes 110600 | tf_op jit(solution)/shard_map/ppermute | solution.py:304
  63.6 1.6 %collective-permute-done.15.left = f32[3,3,8,128]{3,2,1,0:T(8,128)S(1)} collective-permute-done((f32[3,3,8,128]{3,2,1,0:T(8,128)S(1)}, f32[3,3,8,128]{3,2,1,0:T(8,128)S(1)}, u32[]{:S(2)}, u32[]{:S(2)}) %collective-permute-start.15) | collective-permute-done | bytes 36896 | tf_op jit(solution)/shard_map/ppermute | solution.py:305
  65.7 3.0 %collective-permute-start.16 = (f32[1,3,8,128]{3,2,1,0:T(8,128)S(1)}, f32[1,3,8,128]{3,2,1,0:T(8,128)S(1)}, u32[]{:S(2)}, u32[]{:S(2)}) collective-permute-start(f32[1,3,8,128]{3,2,1,0:T(8,128)S(1)} %get-tuple-element.47.below), channel_id=1, source_target_pairs={{1,0},{2,1},{3,2},{4,3},{5,4},{6,5},{7,6},{8,7},{9,8},{10,9},{11,1... | collective-permute-start | bytes 36872 | tf_op jit(solution)/shard_map/ppermute | solution.py:304
  68.8 1.2 %collective-permute-done.17.rest_1_ = f32[1,3,8,128]{3,2,1,0:T(8,128)S(1)} collective-permute-done((f32[1,3,8,128]{3,2,1,0:T(8,128)S(1)}, f32[1,3,8,128]{3,2,1,0:T(8,128)S(1)}, u32[]{:S(2)}, u32[]{:S(2)}) %collective-permute-start.17) | collective-permute-done | bytes 12320 | tf_op jit(solution)/shard_map/ppermute | solution.py:305
  70.4 12.4 %all_to_all.11.sent = f32[16,3,8,128]{3,2,1,0:T(8,128)S(1)} all-to-all(f32[16,3,8,128]{3,2,1,0:T(8,128)S(1)} %shard_map.48), channel_id=1, replica_groups=mesh['tm'=16,'space'=32] {'tm'}, dimensions={0} | all-to-all | bytes 393216 | tf_op jit(solution)/shard_map/all_to_all | solution.py:355
  82.8 0.8 shard_map.49
  (31 shorter events, 3.8 us)
Async XLA Ops:
  0.0 10.0 %copy-start = (f32[3]{0:T(128)S(1)}, f32[3]{0:T(128)}, u32[]{:S(2)}) copy-start(f32[3]{0:T(128)} %applied.1) | copy-start | bytes 40
  1.0 13.0 %collective-permute-start.1 = (f32[4,2,16,512]{3,2,1,0:T(8,128)S(1)}, f32[4,2,16,512]{3,2,1,0:T(8,128)S(1)}, u32[]{:S(2)}, u32[]{:S(2)}) collective-permute-start(f32[4,2,16,512]{3,2,1,0:T(8,128)S(1)} %pad_maximum_fusion.slab), channel_id=1, source_target_pairs={{0,1},{1,2},{2,3},{3,4},{4,5},{5,6},{6,7},{7,8},{8,9},{9,10},{10,1... | collective-permute-start | bytes 786440 | tf_op jit(solution)/shard_map/ppermute | solution.py:305
  1.0 13.0 %collective-permute-start = (f32[4,2,16,512]{3,2,1,0:T(8,128)S(1)}, f32[4,2,16,512]{3,2,1,0:T(8,128)S(1)}, u32[]{:S(2)}, u32[]{:S(2)}) collective-permute-start(f32[4,2,16,512]{3,2,1,0:T(8,128)S(1)} %pad_maximum_fusion.slab), channel_id=1, source_target_pairs={{1,0},{2,1},{3,2},{4,3},{5,4},{6,5},{7,6},{8,7},{9,8},{10,9},{11,1... | collective-permute-start | bytes 786440 | tf_op jit(solution)/shard_map/ppermute | solution.py:304
  29.8 5.1 %collective-permute-start.3 = (f32[2,2,3,8,128]{4,3,2,1,0:T(8,128)S(1)}, f32[2,2,3,8,128]{4,3,2,1,0:T(8,128)S(1)}, u32[]{:S(2)}, u32[]{:S(2)}) collective-permute-start(f32[2,2,3,8,128]{4,3,2,1,0:T(8,128)S(1)} %slice.4.own), channel_id=1, source_target_pairs={{0,1},{1,2},{2,3},{3,4},{4,5},{5,6},{6,7},{7,8},{8,9},{9,10},{10,1... | collective-permute-start | bytes 147464 | tf_op jit(solution)/shard_map/ppermute | solution.py:305
  29.8 5.1 %collective-permute-start.2 = (f32[2,2,3,8,128]{4,3,2,1,0:T(8,128)S(1)}, f32[2,2,3,8,128]{4,3,2,1,0:T(8,128)S(1)}, u32[]{:S(2)}, u32[]{:S(2)}) collective-permute-start(f32[2,2,3,8,128]{4,3,2,1,0:T(8,128)S(1)} %slice.4.own), channel_id=1, source_target_pairs={{1,0},{2,1},{3,2},{4,3},{5,4},{6,5},{7,6},{8,7},{9,8},{10,9},{11,1... | collective-permute-start | bytes 147464 | tf_op jit(solution)/shard_map/ppermute | solution.py:304
  35.3 4.6 %collective-permute-start.5 = (f32[3,3,8,128]{3,2,1,0:T(8,128)S(1)}, f32[3,3,8,128]{3,2,1,0:T(8,128)S(1)}, u32[]{:S(2)}, u32[]{:S(2)}) collective-permute-start(f32[3,3,8,128]{3,2,1,0:T(8,128)S(1)} %get-tuple-element.35), channel_id=1, source_target_pairs={{0,1},{1,2},{2,3},{3,4},{4,5},{5,6},{6,7},{7,8},{8,9},{9,10},{10,1... | collective-permute-start | bytes 110600 | tf_op jit(solution)/shard_map/ppermute | solution.py:305
  35.3 4.6 %collective-permute-start.4 = (f32[3,3,8,128]{3,2,1,0:T(8,128)S(1)}, f32[3,3,8,128]{3,2,1,0:T(8,128)S(1)}, u32[]{:S(2)}, u32[]{:S(2)}) collective-permute-start(f32[3,3,8,128]{3,2,1,0:T(8,128)S(1)} %get-tuple-element.34.own.rest_1_), channel_id=1, source_target_pairs={{1,0},{2,1},{3,2},{4,3},{5,4},{6,5},{7,6},{8,7},{9,8},{10,9},{11,1... | collective-permute-start | bytes 110600 | tf_op jit(solution)/shard_map/ppermute | solution.py:304
  40.4 4.6 %collective-permute-start.7 = (f32[3,3,8,128]{3,2,1,0:T(8,128)S(1)}, f32[3,3,8,128]{3,2,1,0:T(8,128)S(1)}, u32[]{:S(2)}, u32[]{:S(2)}) collective-permute-start(f32[3,3,8,128]{3,2,1,0:T(8,128)S(1)} %get-tuple-element.37), channel_id=1, source_target_pairs={{0,1},{1,2},{2,3},{3,4},{4,5},{5,6},{6,7},{7,8},{8,9},{9,10},{10,1... | collective-permute-start | bytes 110600 | tf_op jit(solution)/shard_map/ppermute | solution.py:305
  40.4 4.6 %collective-permute-start.6 = (f32[3,3,8,128]{3,2,1,0:T(8,128)S(1)}, f32[3,3,8,128]{3,2,1,0:T(8,128)S(1)}, u32[]{:S(2)}, u32[]{:S(2)}) collective-permute-start(f32[3,3,8,128]{3,2,1,0:T(8,128)S(1)} %get-tuple-element.36.own.rest_3_), channel_id=1, source_target_pairs={{1,0},{2,1},{3,2},{4,3},{5,4},{6,5},{7,6},{8,7},{9,8},{10,9},{11,1... | collective-permute-start | bytes 110600 | tf_op jit(solution)/shard_map/ppermute | solution.py:304
  45.4 4.6 %collective-permute-start.9 = (f32[3,3,8,128]{3,2,1,0:T(8,128)S(1)}, f32[3,3,8,128]{3,2,1,0:T(8,128)S(1)}, u32[]{:S(2)}, u32[]{:S(2)}) collective-permute-start(f32[3,3,8,128]{3,2,1,0:T(8,128)S(1)} %get-tuple-element.39), channel_id=1, source_target_pairs={{0,1},{1,2},{2,3},{3,4},{4,5},{5,6},{6,7},{7,8},{8,9},{9,10},{10,1... | collective-permute-start | bytes 110600 | tf_op jit(solution)/shard_map/ppermute | solution.py:305
  45.5 4.6 %collective-permute-start.8 = (f32[3,3,8,128]{3,2,1,0:T(8,128)S(1)}, f32[3,3,8,128]{3,2,1,0:T(8,128)S(1)}, u32[]{:S(2)}, u32[]{:S(2)}) collective-permute-start(f32[3,3,8,128]{3,2,1,0:T(8,128)S(1)} %get-tuple-element.38.own.rest_5_), channel_id=1, source_target_pairs={{1,0},{2,1},{3,2},{4,3},{5,4},{6,5},{7,6},{8,7},{9,8},{10,9},{11,1... | collective-permute-start | bytes 110600 | tf_op jit(solution)/shard_map/ppermute | solution.py:304
  50.5 4.6 %collective-permute-start.11 = (f32[3,3,8,128]{3,2,1,0:T(8,128)S(1)}, f32[3,3,8,128]{3,2,1,0:T(8,128)S(1)}, u32[]{:S(2)}, u32[]{:S(2)}) collective-permute-start(f32[3,3,8,128]{3,2,1,0:T(8,128)S(1)} %get-tuple-element.41), channel_id=1, source_target_pairs={{0,1},{1,2},{2,3},{3,4},{4,5},{5,6},{6,7},{7,8},{8,9},{9,10},{10,1... | collective-permute-start | bytes 110600 | tf_op jit(solution)/shard_map/ppermute | solution.py:305
  50.5 4.6 %collective-permute-start.10 = (f32[3,3,8,128]{3,2,1,0:T(8,128)S(1)}, f32[3,3,8,128]{3,2,1,0:T(8,128)S(1)}, u32[]{:S(2)}, u32[]{:S(2)}) collective-permute-start(f32[3,3,8,128]{3,2,1,0:T(8,128)S(1)} %get-tuple-element.40.own.rest_7_), channel_id=1, source_target_pairs={{1,0},{2,1},{3,2},{4,3},{5,4},{6,5},{7,6},{8,7},{9,8},{10,9},{11,1... | collective-permute-start | bytes 110600 | tf_op jit(solution)/shard_map/ppermute | solution.py:304
  55.6 4.6 %collective-permute-start.13 = (f32[3,3,8,128]{3,2,1,0:T(8,128)S(1)}, f32[3,3,8,128]{3,2,1,0:T(8,128)S(1)}, u32[]{:S(2)}, u32[]{:S(2)}) collective-permute-start(f32[3,3,8,128]{3,2,1,0:T(8,128)S(1)} %get-tuple-element.43), channel_id=1, source_target_pairs={{0,1},{1,2},{2,3},{3,4},{4,5},{5,6},{6,7},{7,8},{8,9},{9,10},{10,1... | collective-permute-start | bytes 110600 | tf_op jit(solution)/shard_map/ppermute | solution.py:305
  55.6 4.6 %collective-permute-start.12 = (f32[3,3,8,128]{3,2,1,0:T(8,128)S(1)}, f32[3,3,8,128]{3,2,1,0:T(8,128)S(1)}, u32[]{:S(2)}, u32[]{:S(2)}) collective-permute-start(f32[3,3,8,128]{3,2,1,0:T(8,128)S(1)} %get-tuple-element.42.own.rest_9_), channel_id=1, source_target_pairs={{1,0},{2,1},{3,2},{4,3},{5,4},{6,5},{7,6},{8,7},{9,8},{10,9},{11,1... | collective-permute-start | bytes 110600 | tf_op jit(solution)/shard_map/ppermute | solution.py:304
  60.6 4.6 %collective-permute-start.15 = (f32[3,3,8,128]{3,2,1,0:T(8,128)S(1)}, f32[3,3,8,128]{3,2,1,0:T(8,128)S(1)}, u32[]{:S(2)}, u32[]{:S(2)}) collective-permute-start(f32[3,3,8,128]{3,2,1,0:T(8,128)S(1)} %get-tuple-element.45), channel_id=1, source_target_pairs={{0,1},{1,2},{2,3},{3,4},{4,5},{5,6},{6,7},{7,8},{8,9},{9,10},{10,1... | collective-permute-start | bytes 110600 | tf_op jit(solution)/shard_map/ppermute | solution.py:305
  60.7 4.6 %collective-permute-start.14 = (f32[3,3,8,128]{3,2,1,0:T(8,128)S(1)}, f32[3,3,8,128]{3,2,1,0:T(8,128)S(1)}, u32[]{:S(2)}, u32[]{:S(2)}) collective-permute-start(f32[3,3,8,128]{3,2,1,0:T(8,128)S(1)} %get-tuple-element.44.own.rest_11_), channel_id=1, source_target_pairs={{1,0},{2,1},{3,2},{4,3},{5,4},{6,5},{7,6},{8,7},{9,8},{10,9},{11,1... | collective-permute-start | bytes 110600 | tf_op jit(solution)/shard_map/ppermute | solution.py:304
  65.7 4.4 %collective-permute-start.17 = (f32[1,3,8,128]{3,2,1,0:T(8,128)S(1)}, f32[1,3,8,128]{3,2,1,0:T(8,128)S(1)}, u32[]{:S(2)}, u32[]{:S(2)}) collective-permute-start(f32[1,3,8,128]{3,2,1,0:T(8,128)S(1)} %get-tuple-element.46.above), channel_id=1, source_target_pairs={{0,1},{1,2},{2,3},{3,4},{4,5},{5,6},{6,7},{7,8},{8,9},{9,10},{10,1... | collective-permute-start | bytes 36872 | tf_op jit(solution)/shard_map/ppermute | solution.py:305
  65.7 4.4 %collective-permute-start.16 = (f32[1,3,8,128]{3,2,1,0:T(8,128)S(1)}, f32[1,3,8,128]{3,2,1,0:T(8,128)S(1)}, u32[]{:S(2)}, u32[]{:S(2)}) collective-permute-start(f32[1,3,8,128]{3,2,1,0:T(8,128)S(1)} %get-tuple-element.47.below), channel_id=1, source_target_pairs={{1,0},{2,1},{3,2},{4,3},{5,4},{6,5},{7,6},{8,7},{9,8},{10,9},{11,1... | collective-permute-start | bytes 36872 | tf_op jit(solution)/shard_map/ppermute | solution.py:304

commit v8 on v4

--- a/solution.py
+++ b/solution.py
@@ -109,7 +109,7 @@
     return load
 
 
-def prologue(own, left, left_a, right, right_a, field, payload, sides, layers):
+def prologue(own, right, left, right_a, left_a, field, payload, sides, layers):
     by_parity(left, left_a, sides.at[0], layers.at[0])
     by_parity(right, right_a, sides.at[1], layers.at[1])
     load = beside(own, sides)
@@ -223,7 +223,7 @@
     return [ref[(*at, c)] for c in range(3)]
 
 
-def chain(block, blocks, own, left, right, corr, windows, field, *rest):
+def chain(block, blocks, own, right, left, corr, windows, field, *rest):
     applied = [field[c] for c in range(3)]
     is_even = windows[6] < 64.0
     first_slice = 2 * block + 1
@@ -271,7 +271,7 @@
             down[2, c] = corr[first_slice + 2, 0, c]
 
 
-def final(block, blocks, below, above, *rest):
+def final(block, blocks, above, below, *rest):
     chain(block, blocks, (below, above), *rest)
 
 
@@ -301,7 +301,8 @@
     count = lax.axis_size("space")
     up = [(i, (i + 1) % count) for i in range(count)]
     down = [(j, i) for i, j in up]
-    return lax.ppermute(to_above, "space", up), lax.ppermute(to_below, "space", down)
+    from_above = lax.ppermute(to_below, "space", down)
+    return from_above, lax.ppermute(to_above, "space", up)
 
 
 def call(kernel, shapes, *args, scratch=(), **more):
@@ -319,8 +320,8 @@
     slices = lax.axis_size("tm")
     width = starts.shape[-1]
     layers = (4, 2, width // 128, 16, 128)
-    left, right = both_sides(starts[0], starts[0])
-    left_a, right_a = both_sides(anisotropy, anisotropy)
+    right, left = both_sides(starts[0], starts[0])
+    right_a, left_a = both_sides(anisotropy, anisotropy)
     own, field = call(
         prepare,
         [(4, 2, 2, 8, width), (3, 8, 128)],
@@ -331,7 +332,7 @@
     payload, sides = call(
         prologue,
         [(slices, 2, 3, 8, 128), (2, 4, 2, 2, 8, width)],
-        *(own, left, left_a, right, right_a, field),
+        *(own, right, left, right_a, left_a, field),
         scratch=[(2, *layers)],
     )
     (windows,) = call(window, [(7, 8, 128)], own, sides)
@@ -343,13 +344,13 @@
         kernel = functools.partial(chain, block, blocks)
         ahead_of_last = block == blocks - 2
         shapes = [(1 if ahead_of_last else 3, 3, 8, 128)] * 2 + [(2, 3, 8, 128)]
-        up, down, middle = call(kernel, shapes, up, *both_sides(up, down), corr, windows, field)
-        kept += [middle] if ahead_of_last else [middle, up]
-    left, right = both_sides(up, down)
+        up, down, middle = call(kernel, shapes, down, *both_sides(up, down), corr, windows, field)
+        kept += [middle] if ahead_of_last else [middle, down]
+    right, left = both_sides(up, down)
     (sent,) = call(pack, [(slices, 3, 8, 128)], corr, windows, down, up, *kept)
     kernel = functools.partial(final, blocks - 1, blocks)
     (sent,) = call(
-        kernel, [sent.shape], down, up, left, right, corr, windows, field, sent, input_output_aliases={7: 0}
+        kernel, [sent.shape], up, down, right, left, corr, windows, field, sent, input_output_aliases={7: 0}
     )
     sent = lax.all_to_all(sent, "tm", 0, 0, tiled=True)
     (out,) = call(assemble, [starts.shape], sent, scratch=[(3, 2, width // 128, 16, 128)])

time: 86.5 us -> 83.3 us (0.963)
  waiting for transfers between devices: 35.5 us -> 12.7 us
  starting transfers between devices: 16 us -> 35.8 us
    ppermute x20, waiting for transfers between devices: 35.5 us -> 12.7 us  [the longest x10 12.6 us: both_sides(): return (from_above, lax.ppermute(to_above, 'space', up))]
    ppermute x20, starting transfers between devices: 16 us -> 35.8 us  [the longest x10 35.6 us: both_sides(): from_above = lax.ppermute(to_below, 'space', down)]
  transfers between devices with their start and end apart: 20 -> 20, of which waited for: 17 -> 9; matrix products, arithmetic and copies ran while one was open for 0% -> 0% of each run, Pallas kernels for 1% -> 1%
where the time goes in v8:
time: 83.3 us; the launch traced here: 83.1 us
  starting transfers between devices  35.8 us (43%)
  blocking collectives  26.5 us (32%)
  waiting for transfers between devices  12.7 us (15%)
  Pallas kernels  6.1 us (7%)
  local copies, waits for them, and re-layouts  1.77 us (2%)
    ppermute x10, starting transfers between devices, both_sides(): from_above = lax.ppermute(to_below, 'space', down)  35.6 us
    all_to_all x1, blocking collectives, per_device(): corr = lax.all_to_all(payload, 'tm', 0, 0, tiled=True)  14.5 us
    ppermute x10, waiting for transfers between devices, both_sides(): return (from_above, lax.ppermute(to_above, 'space', up))  12.6 us
    all_to_all x1, blocking collectives, per_device(): sent = lax.all_to_all(sent, 'tm', 0, 0, tiled=True)  12 us
    pallas_call x13, Pallas kernels, call(): pl.pallas_call(kernel, out_shape=[jax.ShapeDtypeStruct(s, F32) for s in s...  6.1 us
    unnamed x6, local copies, waits for them, and re-layouts  1.77 us
  transfers between devices with their start and end apart: 20, of which 9 were waited for; matrix products, arithmetic and copies ran while one was open for 0% of the time, Pallas kernels for 1%

profile of v8, /device:TPU:2, one launch (start us, length us, event | category | flops | bytes accessed | tf_op | source)
XLA Modules:
  0.0 83.1 jit_solution(12732329512890021331)
XLA Ops:
  0.0 8.9 %collective-permute-start = (f32[3,2,16,512]{3,2,1,0:T(8,128)}, f32[3,2,16,512]{3,2,1,0:T(8,128)S(1)}, u32[]{:S(2)}, u32[]{:S(2)}) collective-permute-start(f32[3,2,16,512]{3,2,1,0:T(8,128)} %bitcast.2), channel_id=1, source_target_pairs={{1,0},{2,1},{3,2},{4,3},{5,4},{6,5},{7,6},{8,7},{9,8},{10,9},{11,1... | collective-permute-start | bytes 589832 | tf_op jit(solution)/shard_map/ppermute | solution.py:304
  9.0 3.0 %collective-permute-start.2 = (f32[2,16,512]{2,1,0:T(8,128)}, f32[2,16,512]{2,1,0:T(8,128)S(1)}, u32[]{:S(2)}, u32[]{:S(2)}) collective-permute-start(f32[2,16,512]{2,1,0:T(8,128)} %aniso.1), channel_id=1, source_target_pairs={{1,0},{2,1},{3,2},{4,3},{5,4},{6,5},{7,6},{8,7},{9,8},{10,9},{11,1... | collective-permute-start | bytes 196616 | tf_op jit(solution)/shard_map/ppermute | solution.py:304
  11.9 0.9 %copy-done = f32[1,3,2,16,512]{4,3,2,1,0:T(8,128)S(1)} copy-done((f32[1,3,2,16,512]{4,3,2,1,0:T(8,128)S(1)}, f32[1,3,2,16,512]{4,3,2,1,0:T(8,128)}, u32[]{:S(2)}) %copy-start) | copy-done | bytes 196632
  12.8 0.8 %copy-done.1 = f32[2,16,512]{2,1,0:T(8,128)S(1)} copy-done((f32[2,16,512]{2,1,0:T(8,128)S(1)}, f32[2,16,512]{2,1,0:T(8,128)}, u32[]{:S(2)}) %copy-start.1) | copy-done | bytes 65560
  14.3 1.2 %shard_map.38 = (f32[16,2,3,8,128]{4,3,2,1,0:T(8,128)S(1)}, f32[2,4,2,2,8,512]{5,4,3,2,1,0:T(8,128)S(1)}) custom-call(f32[4,2,2,8,512]{4,3,2,1,0:T(8,128)S(1)} %get-tuple-element.30.own, f32[3,2,16,512]{3,2,1,0:T(8,128)S(1)} %collective-permute-done.right, f32[3,2,16,512]{3,2,1,0:T(8,128)S(1)} %collective-permute-done.1.left, ...), custom_call_target="tpu_custom_call" | custom-call | tf_op jit(solution)/shard_map/pallas_call | solution.py:309
  15.6 14.5 %all_to_all.10.corr.rest_2_ = f32[16,2,3,8,128]{4,3,2,1,0:T(8,128)S(1)} all-to-all(f32[16,2,3,8,128]{4,3,2,1,0:T(8,128)S(1)} %get-tuple-element.32), channel_id=1, replica_groups=mesh['tm'=16,'space'=32] {'tm'}, dimensions={0} | all-to-all | bytes 786432 | tf_op jit(solution)/shard_map/all_to_all | solution.py:339
  30.1 3.0 %collective-permute-start.4 = (f32[2,2,3,8,128]{4,3,2,1,0:T(8,128)S(1)}, f32[2,2,3,8,128]{4,3,2,1,0:T(8,128)S(1)}, u32[]{:S(2)}, u32[]{:S(2)}) collective-permute-start(f32[2,2,3,8,128]{4,3,2,1,0:T(8,128)S(1)} %slice.4.own), channel_id=1, source_target_pairs={{1,0},{2,1},{3,2},{4,3},{5,4},{6,5},{7,6},{8,7},{9,8},{10,9},{11,1... | collective-permute-start | bytes 147464 | tf_op jit(solution)/shard_map/ppermute | solution.py:304
  33.2 1.6 %collective-permute-done.5.left = f32[2,2,3,8,128]{4,3,2,1,0:T(8,128)S(1)} collective-permute-done((f32[2,2,3,8,128]{4,3,2,1,0:T(8,128)S(1)}, f32[2,2,3,8,128]{4,3,2,1,0:T(8,128)S(1)}, u32[]{:S(2)}, u32[]{:S(2)}) %collective-permute-start.5) | collective-permute-done | bytes 49184 | tf_op jit(solution)/shard_map/ppermute | solution.py:305
  35.3 3.0 %collective-permute-start.6 = (f32[3,3,8,128]{3,2,1,0:T(8,128)S(1)}, f32[3,3,8,128]{3,2,1,0:T(8,128)S(1)}, u32[]{:S(2)}, u32[]{:S(2)}) collective-permute-start(f32[3,3,8,128]{3,2,1,0:T(8,128)S(1)} %get-tuple-element.34.own.rest_1_), channel_id=1, source_target_pairs={{1,0},{2,1},{3,2},{4,3},{5,4},{6,5},{7,6},{8,7},{9,8},{10,9},{11,1... | collective-permute-start | bytes 110600 | tf_op jit(solution)/shard_map/ppermute | solution.py:304
  38.2 1.6 %collective-permute-done.7.left = f32[3,3,8,128]{3,2,1,0:T(8,128)S(1)} collective-permute-done((f32[3,3,8,128]{3,2,1,0:T(8,128)S(1)}, f32[3,3,8,128]{3,2,1,0:T(8,128)S(1)}, u32[]{:S(2)}, u32[]{:S(2)}) %collective-permute-start.7) | collective-permute-done | bytes 36896 | tf_op jit(solution)/shard_map/ppermute | solution.py:305
  40.3 3.0 %collective-permute-start.8 = (f32[3,3,8,128]{3,2,1,0:T(8,128)S(1)}, f32[3,3,8,128]{3,2,1,0:T(8,128)S(1)}, u32[]{:S(2)}, u32[]{:S(2)}) collective-permute-start(f32[3,3,8,128]{3,2,1,0:T(8,128)S(1)} %get-tuple-element.36.own.rest_3_), channel_id=1, source_target_pairs={{1,0},{2,1},{3,2},{4,3},{5,4},{6,5},{7,6},{8,7},{9,8},{10,9},{11,1... | collective-permute-start | bytes 110600 | tf_op jit(solution)/shard_map/ppermute | solution.py:304
  43.3 1.6 %collective-permute-done.9.left = f32[3,3,8,128]{3,2,1,0:T(8,128)S(1)} collective-permute-done((f32[3,3,8,128]{3,2,1,0:T(8,128)S(1)}, f32[3,3,8,128]{3,2,1,0:T(8,128)S(1)}, u32[]{:S(2)}, u32[]{:S(2)}) %collective-permute-start.9) | collective-permute-done | bytes 36896 | tf_op jit(solution)/shard_map/ppermute | solution.py:305
  45.4 3.0 %collective-permute-start.10 = (f32[3,3,8,128]{3,2,1,0:T(8,128)S(1)}, f32[3,3,8,128]{3,2,1,0:T(8,128)S(1)}, u32[]{:S(2)}, u32[]{:S(2)}) collective-permute-start(f32[3,3,8,128]{3,2,1,0:T(8,128)S(1)} %get-tuple-element.38.own.rest_5_), channel_id=1, source_target_pairs={{1,0},{2,1},{3,2},{4,3},{5,4},{6,5},{7,6},{8,7},{9,8},{10,9},{11,1... | collective-permute-start | bytes 110600 | tf_op jit(solution)/shard_map/ppermute | solution.py:304
  48.4 1.6 %collective-permute-done.11.left = f32[3,3,8,128]{3,2,1,0:T(8,128)S(1)} collective-permute-done((f32[3,3,8,128]{3,2,1,0:T(8,128)S(1)}, f32[3,3,8,128]{3,2,1,0:T(8,128)S(1)}, u32[]{:S(2)}, u32[]{:S(2)}) %collective-permute-start.11) | collective-permute-done | bytes 36896 | tf_op jit(solution)/shard_map/ppermute | solution.py:305
  50.4 3.0 %collective-permute-start.12 = (f32[3,3,8,128]{3,2,1,0:T(8,128)S(1)}, f32[3,3,8,128]{3,2,1,0:T(8,128)S(1)}, u32[]{:S(2)}, u32[]{:S(2)}) collective-permute-start(f32[3,3,8,128]{3,2,1,0:T(8,128)S(1)} %get-tuple-element.40.own.rest_7_), channel_id=1, source_target_pairs={{1,0},{2,1},{3,2},{4,3},{5,4},{6,5},{7,6},{8,7},{9,8},{10,9},{11,1... | collective-permute-start | bytes 110600 | tf_op jit(solution)/shard_map/ppermute | solution.py:304
  53.4 1.6 %collective-permute-done.13.left = f32[3,3,8,128]{3,2,1,0:T(8,128)S(1)} collective-permute-done((f32[3,3,8,128]{3,2,1,0:T(8,128)S(1)}, f32[3,3,8,128]{3,2,1,0:T(8,128)S(1)}, u32[]{:S(2)}, u32[]{:S(2)}) %collective-permute-start.13) | collective-permute-done | bytes 36896 | tf_op jit(solution)/shard_map/ppermute | solution.py:305
  55.5 3.0 %collective-permute-start.14 = (f32[3,3,8,128]{3,2,1,0:T(8,128)S(1)}, f32[3,3,8,128]{3,2,1,0:T(8,128)S(1)}, u32[]{:S(2)}, u32[]{:S(2)}) collective-permute-start(f32[3,3,8,128]{3,2,1,0:T(8,128)S(1)} %get-tuple-element.42.own.rest_9_), channel_id=1, source_target_pairs={{1,0},{2,1},{3,2},{4,3},{5,4},{6,5},{7,6},{8,7},{9,8},{10,9},{11,1... | collective-permute-start | bytes 110600 | tf_op jit(solution)/shard_map/ppermute | solution.py:304
  58.5 1.6 %collective-permute-done.15.left = f32[3,3,8,128]{3,2,1,0:T(8,128)S(1)} collective-permute-done((f32[3,3,8,128]{3,2,1,0:T(8,128)S(1)}, f32[3,3,8,128]{3,2,1,0:T(8,128)S(1)}, u32[]{:S(2)}, u32[]{:S(2)}) %collective-permute-start.15) | collective-permute-done | bytes 36896 | tf_op jit(solution)/shard_map/ppermute | solution.py:305
  60.6 3.0 %collective-permute-start.16 = (f32[3,3,8,128]{3,2,1,0:T(8,128)S(1)}, f32[3,3,8,128]{3,2,1,0:T(8,128)S(1)}, u32[]{:S(2)}, u32[]{:S(2)}) collective-permute-start(f32[3,3,8,128]{3,2,1,0:T(8,128)S(1)} %get-tuple-element.44.own.rest_11_), channel_id=1, source_target_pairs={{1,0},{2,1},{3,2},{4,3},{5,4},{6,5},{7,6},{8,7},{9,8},{10,9},{11,1... | collective-permute-start | bytes 110600 | tf_op jit(solution)/shard_map/ppermute | solution.py:304
  63.5 1.6 %collective-permute-done.17.left = f32[3,3,8,128]{3,2,1,0:T(8,128)S(1)} collective-permute-done((f32[3,3,8,128]{3,2,1,0:T(8,128)S(1)}, f32[3,3,8,128]{3,2,1,0:T(8,128)S(1)}, u32[]{:S(2)}, u32[]{:S(2)}) %collective-permute-start.17) | collective-permute-done | bytes 36896 | tf_op jit(solution)/shard_map/ppermute | solution.py:305
  65.6 3.0 %collective-permute-start.18 = (f32[1,3,8,128]{3,2,1,0:T(8,128)S(1)}, f32[1,3,8,128]{3,2,1,0:T(8,128)S(1)}, u32[]{:S(2)}, u32[]{:S(2)}) collective-permute-start(f32[1,3,8,128]{3,2,1,0:T(8,128)S(1)} %get-tuple-element.47.below), channel_id=1, source_target_pairs={{1,0},{2,1},{3,2},{4,3},{5,4},{6,5},{7,6},{8,7},{9,8},{10,9},{11,1... | collective-permute-start | bytes 36872 | tf_op jit(solution)/shard_map/ppermute | solution.py:304
  68.7 1.2 %collective-permute-done.19.rest_1_ = f32[1,3,8,128]{3,2,1,0:T(8,128)S(1)} collective-permute-done((f32[1,3,8,128]{3,2,1,0:T(8,128)S(1)}, f32[1,3,8,128]{3,2,1,0:T(8,128)S(1)}, u32[]{:S(2)}, u32[]{:S(2)}) %collective-permute-start.19) | collective-permute-done | bytes 12320 | tf_op jit(solution)/shard_map/ppermute | solution.py:305
  70.3 12.0 %all_to_all.11.sent = f32[16,3,8,128]{3,2,1,0:T(8,128)S(1)} all-to-all(f32[16,3,8,128]{3,2,1,0:T(8,128)S(1)} %shard_map.48), channel_id=1, replica_groups=mesh['tm'=16,'space'=32] {'tm'}, dimensions={0} | all-to-all | bytes 393216 | tf_op jit(solution)/shard_map/all_to_all | solution.py:355
  82.3 0.8 shard_map.49
  (38 shorter events, 4.4 us)
Async XLA Ops:
  0.0 11.9 %copy-start.2 = (f32[3]{0:T(128)S(1)}, f32[3]{0:T(128)}, u32[]{:S(2)}) copy-start(f32[3]{0:T(128)} %applied.1) | copy-start | bytes 40
  0.0 14.3 %collective-permute-start.1 = (f32[3,2,16,512]{3,2,1,0:T(8,128)}, f32[3,2,16,512]{3,2,1,0:T(8,128)S(1)}, u32[]{:S(2)}, u32[]{:S(2)}) collective-permute-start(f32[3,2,16,512]{3,2,1,0:T(8,128)} %bitcast.1), channel_id=1, source_target_pairs={{0,1},{1,2},{2,3},{3,4},{4,5},{5,6},{6,7},{7,8},{8,9},{9,10},{10,1... | collective-permute-start | bytes 589832 | tf_op jit(solution)/shard_map/ppermute | solution.py:305
  0.0 14.3 %collective-permute-start = (f32[3,2,16,512]{3,2,1,0:T(8,128)}, f32[3,2,16,512]{3,2,1,0:T(8,128)S(1)}, u32[]{:S(2)}, u32[]{:S(2)}) collective-permute-start(f32[3,2,16,512]{3,2,1,0:T(8,128)} %bitcast.2), channel_id=1, source_target_pairs={{1,0},{2,1},{3,2},{4,3},{5,4},{6,5},{7,6},{8,7},{9,8},{10,9},{11,1... | collective-permute-start | bytes 589832 | tf_op jit(solution)/shard_map/ppermute | solution.py:304
  8.9 5.3 %collective-permute-start.3 = (f32[2,16,512]{2,1,0:T(8,128)}, f32[2,16,512]{2,1,0:T(8,128)S(1)}, u32[]{:S(2)}, u32[]{:S(2)}) collective-permute-start(f32[2,16,512]{2,1,0:T(8,128)} %aniso.1), channel_id=1, source_target_pairs={{0,1},{1,2},{2,3},{3,4},{4,5},{5,6},{6,7},{7,8},{8,9},{9,10},{10,1... | collective-permute-start | bytes 196616 | tf_op jit(solution)/shard_map/ppermute | solution.py:305
  9.0 5.3 %collective-permute-start.2 = (f32[2,16,512]{2,1,0:T(8,128)}, f32[2,16,512]{2,1,0:T(8,128)S(1)}, u32[]{:S(2)}, u32[]{:S(2)}) collective-permute-start(f32[2,16,512]{2,1,0:T(8,128)} %aniso.1), channel_id=1, source_target_pairs={{1,0},{2,1},{3,2},{4,3},{5,4},{6,5},{7,6},{8,7},{9,8},{10,9},{11,1... | collective-permute-start | bytes 196616 | tf_op jit(solution)/shard_map/ppermute | solution.py:304
  11.9 0.9 %copy-start = (f32[1,3,2,16,512]{4,3,2,1,0:T(8,128)S(1)}, f32[1,3,2,16,512]{4,3,2,1,0:T(8,128)}, u32[]{:S(2)}) copy-start(f32[1,3,2,16,512]{4,3,2,1,0:T(8,128)} %param.3) | copy-start | bytes 589828
  12.8 0.8 %copy-start.1 = (f32[2,16,512]{2,1,0:T(8,128)S(1)}, f32[2,16,512]{2,1,0:T(8,128)}, u32[]{:S(2)}) copy-start(f32[2,16,512]{2,1,0:T(8,128)} %aniso.1) | copy-start | bytes 196612
  30.1 4.7 %collective-permute-start.5 = (f32[2,2,3,8,128]{4,3,2,1,0:T(8,128)S(1)}, f32[2,2,3,8,128]{4,3,2,1,0:T(8,128)S(1)}, u32[]{:S(2)}, u32[]{:S(2)}) collective-permute-start(f32[2,2,3,8,128]{4,3,2,1,0:T(8,128)S(1)} %slice.4.own), channel_id=1, source_target_pairs={{0,1},{1,2},{2,3},{3,4},{4,5},{5,6},{6,7},{7,8},{8,9},{9,10},{10,1... | collective-permute-start | bytes 147464 | tf_op jit(solution)/shard_map/ppermute | solution.py:305
  30.1 4.7 %collective-permute-start.4 = (f32[2,2,3,8,128]{4,3,2,1,0:T(8,128)S(1)}, f32[2,2,3,8,128]{4,3,2,1,0:T(8,128)S(1)}, u32[]{:S(2)}, u32[]{:S(2)}) collective-permute-start(f32[2,2,3,8,128]{4,3,2,1,0:T(8,128)S(1)} %slice.4.own), channel_id=1, source_target_pairs={{1,0},{2,1},{3,2},{4,3},{5,4},{6,5},{7,6},{8,7},{9,8},{10,9},{11,1... | collective-permute-start | bytes 147464 | tf_op jit(solution)/shard_map/ppermute | solution.py:304
  35.2 4.6 %collective-permute-start.7 = (f32[3,3,8,128]{3,2,1,0:T(8,128)S(1)}, f32[3,3,8,128]{3,2,1,0:T(8,128)S(1)}, u32[]{:S(2)}, u32[]{:S(2)}) collective-permute-start(f32[3,3,8,128]{3,2,1,0:T(8,128)S(1)} %get-tuple-element.35), channel_id=1, source_target_pairs={{0,1},{1,2},{2,3},{3,4},{4,5},{5,6},{6,7},{7,8},{8,9},{9,10},{10,1... | collective-permute-start | bytes 110600 | tf_op jit(solution)/shard_map/ppermute | solution.py:305
  35.3 4.6 %collective-permute-start.6 = (f32[3,3,8,128]{3,2,1,0:T(8,128)S(1)}, f32[3,3,8,128]{3,2,1,0:T(8,128)S(1)}, u32[]{:S(2)}, u32[]{:S(2)}) collective-permute-start(f32[3,3,8,128]{3,2,1,0:T(8,128)S(1)} %get-tuple-element.34.own.rest_1_), channel_id=1, source_target_pairs={{1,0},{2,1},{3,2},{4,3},{5,4},{6,5},{7,6},{8,7},{9,8},{10,9},{11,1... | collective-permute-start | bytes 110600 | tf_op jit(solution)/shard_map/ppermute | solution.py:304
  40.3 4.6 %collective-permute-start.9 = (f32[3,3,8,128]{3,2,1,0:T(8,128)S(1)}, f32[3,3,8,128]{3,2,1,0:T(8,128)S(1)}, u32[]{:S(2)}, u32[]{:S(2)}) collective-permute-start(f32[3,3,8,128]{3,2,1,0:T(8,128)S(1)} %get-tuple-element.37), channel_id=1, source_target_pairs={{0,1},{1,2},{2,3},{3,4},{4,5},{5,6},{6,7},{7,8},{8,9},{9,10},{10,1... | collective-permute-start | bytes 110600 | tf_op jit(solution)/shard_map/ppermute | solution.py:305
  40.3 4.6 %collective-permute-start.8 = (f32[3,3,8,128]{3,2,1,0:T(8,128)S(1)}, f32[3,3,8,128]{3,2,1,0:T(8,128)S(1)}, u32[]{:S(2)}, u32[]{:S(2)}) collective-permute-start(f32[3,3,8,128]{3,2,1,0:T(8,128)S(1)} %get-tuple-element.36.own.rest_3_), channel_id=1, source_target_pairs={{1,0},{2,1},{3,2},{4,3},{5,4},{6,5},{7,6},{8,7},{9,8},{10,9},{11,1... | collective-permute-start | bytes 110600 | tf_op jit(solution)/shard_map/ppermute | solution.py:304
  45.4 4.6 %collective-permute-start.11 = (f32[3,3,8,128]{3,2,1,0:T(8,128)S(1)}, f32[3,3,8,128]{3,2,1,0:T(8,128)S(1)}, u32[]{:S(2)}, u32[]{:S(2)}) collective-permute-start(f32[3,3,8,128]{3,2,1,0:T(8,128)S(1)} %get-tuple-element.39), channel_id=1, source_target_pairs={{0,1},{1,2},{2,3},{3,4},{4,5},{5,6},{6,7},{7,8},{8,9},{9,10},{10,1... | collective-permute-start | bytes 110600 | tf_op jit(solution)/shard_map/ppermute | solution.py:305
  45.4 4.6 %collective-permute-start.10 = (f32[3,3,8,128]{3,2,1,0:T(8,128)S(1)}, f32[3,3,8,128]{3,2,1,0:T(8,128)S(1)}, u32[]{:S(2)}, u32[]{:S(2)}) collective-permute-start(f32[3,3,8,128]{3,2,1,0:T(8,128)S(1)} %get-tuple-element.38.own.rest_5_), channel_id=1, source_target_pairs={{1,0},{2,1},{3,2},{4,3},{5,4},{6,5},{7,6},{8,7},{9,8},{10,9},{11,1... | collective-permute-start | bytes 110600 | tf_op jit(solution)/shard_map/ppermute | solution.py:304
  50.4 4.6 %collective-permute-start.13 = (f32[3,3,8,128]{3,2,1,0:T(8,128)S(1)}, f32[3,3,8,128]{3,2,1,0:T(8,128)S(1)}, u32[]{:S(2)}, u32[]{:S(2)}) collective-permute-start(f32[3,3,8,128]{3,2,1,0:T(8,128)S(1)} %get-tuple-element.41), channel_id=1, source_target_pairs={{0,1},{1,2},{2,3},{3,4},{4,5},{5,6},{6,7},{7,8},{8,9},{9,10},{10,1... | collective-permute-start | bytes 110600 | tf_op jit(solution)/shard_map/ppermute | solution.py:305
  50.4 4.6 %collective-permute-start.12 = (f32[3,3,8,128]{3,2,1,0:T(8,128)S(1)}, f32[3,3,8,128]{3,2,1,0:T(8,128)S(1)}, u32[]{:S(2)}, u32[]{:S(2)}) collective-permute-start(f32[3,3,8,128]{3,2,1,0:T(8,128)S(1)} %get-tuple-element.40.own.rest_7_), channel_id=1, source_target_pairs={{1,0},{2,1},{3,2},{4,3},{5,4},{6,5},{7,6},{8,7},{9,8},{10,9},{11,1... | collective-permute-start | bytes 110600 | tf_op jit(solution)/shard_map/ppermute | solution.py:304
  55.5 4.6 %collective-permute-start.15 = (f32[3,3,8,128]{3,2,1,0:T(8,128)S(1)}, f32[3,3,8,128]{3,2,1,0:T(8,128)S(1)}, u32[]{:S(2)}, u32[]{:S(2)}) collective-permute-start(f32[3,3,8,128]{3,2,1,0:T(8,128)S(1)} %get-tuple-element.43), channel_id=1, source_target_pairs={{0,1},{1,2},{2,3},{3,4},{4,5},{5,6},{6,7},{7,8},{8,9},{9,10},{10,1... | collective-permute-start | bytes 110600 | tf_op jit(solution)/shard_map/ppermute | solution.py:305
  55.5 4.6 %collective-permute-start.14 = (f32[3,3,8,128]{3,2,1,0:T(8,128)S(1)}, f32[3,3,8,128]{3,2,1,0:T(8,128)S(1)}, u32[]{:S(2)}, u32[]{:S(2)}) collective-permute-start(f32[3,3,8,128]{3,2,1,0:T(8,128)S(1)} %get-tuple-element.42.own.rest_9_), channel_id=1, source_target_pairs={{1,0},{2,1},{3,2},{4,3},{5,4},{6,5},{7,6},{8,7},{9,8},{10,9},{11,1... | collective-permute-start | bytes 110600 | tf_op jit(solution)/shard_map/ppermute | solution.py:304
  60.5 4.6 %collective-permute-start.17 = (f32[3,3,8,128]{3,2,1,0:T(8,128)S(1)}, f32[3,3,8,128]{3,2,1,0:T(8,128)S(1)}, u32[]{:S(2)}, u32[]{:S(2)}) collective-permute-start(f32[3,3,8,128]{3,2,1,0:T(8,128)S(1)} %get-tuple-element.45), channel_id=1, source_target_pairs={{0,1},{1,2},{2,3},{3,4},{4,5},{5,6},{6,7},{7,8},{8,9},{9,10},{10,1... | collective-permute-start | bytes 110600 | tf_op jit(solution)/shard_map/ppermute | solution.py:305
  60.6 4.6 %collective-permute-start.16 = (f32[3,3,8,128]{3,2,1,0:T(8,128)S(1)}, f32[3,3,8,128]{3,2,1,0:T(8,128)S(1)}, u32[]{:S(2)}, u32[]{:S(2)}) collective-permute-start(f32[3,3,8,128]{3,2,1,0:T(8,128)S(1)} %get-tuple-element.44.own.rest_11_), channel_id=1, source_target_pairs={{1,0},{2,1},{3,2},{4,3},{5,4},{6,5},{7,6},{8,7},{9,8},{10,9},{11,1... | collective-permute-start | bytes 110600 | tf_op jit(solution)/shard_map/ppermute | solution.py:304
  65.6 4.4 %collective-permute-start.19 = (f32[1,3,8,128]{3,2,1,0:T(8,128)S(1)}, f32[1,3,8,128]{3,2,1,0:T(8,128)S(1)}, u32[]{:S(2)}, u32[]{:S(2)}) collective-permute-start(f32[1,3,8,128]{3,2,1,0:T(8,128)S(1)} %get-tuple-element.46.above), channel_id=1, source_target_pairs={{0,1},{1,2},{2,3},{3,4},{4,5},{5,6},{6,7},{7,8},{8,9},{9,10},{10,1... | collective-permute-start | bytes 36872 | tf_op jit(solution)/shard_map/ppermute | solution.py:305
  65.6 4.4 %collective-permute-start.18 = (f32[1,3,8,128]{3,2,1,0:T(8,128)S(1)}, f32[1,3,8,128]{3,2,1,0:T(8,128)S(1)}, u32[]{:S(2)}, u32[]{:S(2)}) collective-permute-start(f32[1,3,8,128]{3,2,1,0:T(8,128)S(1)} %get-tuple-element.47.below), channel_id=1, source_target_pairs={{1,0},{2,1},{3,2},{4,3},{5,4},{6,5},{7,6},{8,7},{9,8},{10,9},{11,1... | collective-permute-start | bytes 36872 | tf_op jit(solution)/shard_map/ppermute | solution.py:304

commit v9 on v8

--- a/solution.py
+++ b/solution.py
@@ -95,8 +95,8 @@
                     out[comp, x, parity, :, at] = layers[comp, x, q, pl.ds(parity, 8, stride=2), :]
 
 
-def prepare(spins, aniso, applied, out, field, layers):
-    by_parity(spins, aniso, out, layers)
+def prepare(slab, applied, out, field, layers):
+    by_parity(slab, slab.at[3], out, layers)
     for c in range(3):
         field[c] = jnp.full(field.shape[1:], applied[c], F32)
 
@@ -320,14 +320,15 @@
     slices = lax.axis_size("tm")
     width = starts.shape[-1]
     layers = (4, 2, width // 128, 16, 128)
+    slab = jnp.concatenate([starts[0], anisotropy[None]], axis=0)
     right, left = both_sides(starts[0], starts[0])
     right_a, left_a = both_sides(anisotropy, anisotropy)
     own, field = call(
         prepare,
         [(4, 2, 2, 8, width), (3, 8, 128)],
-        *(starts[0], anisotropy, applied),
+        *(slab, applied),
         scratch=[layers],
-        in_specs=[VMEM] * 2 + [pl.BlockSpec(memory_space=pltpu.SMEM)],
+        in_specs=[VMEM, pl.BlockSpec(memory_space=pltpu.SMEM)],
     )
     payload, sides = call(
         prologue,

time: 83.3 us -> 83.1 us (level)
  local copies, waits for them, and re-layouts: 1.77 us -> 0.01 us
  other arithmetic: 0 us -> 0.99 us
    unnamed x6 -> x2, local copies, waits for them, and re-layouts: 1.77 us -> 0.01 us
    concatenate x0 -> x1, other arithmetic: none -> 0.99 us  [per_device(): slab = jnp.concatenate([starts[0], anisotropy[None]], axis=0)]
  transfers between devices with their start and end apart: 20 -> 20, of which waited for: 9 -> 11; matrix products, arithmetic and copies ran while one was open for 0% -> 1% of each run, Pallas kernels for 1% -> 1%
where the time goes in v9:
time: 83.1 us; the launch traced here: 82.9 us
  starting transfers between devices  35.8 us (43%)
  blocking collectives  26.5 us (32%)
  waiting for transfers between devices  13.4 us (16%)
  Pallas kernels  6.11 us (7%)
  other arithmetic  0.99 us (1%)
    ppermute x10, starting transfers between devices, both_sides(): from_above = lax.ppermute(to_below, 'space', down)  35.6 us
    all_to_all x1, blocking collectives, per_device(): corr = lax.all_to_all(payload, 'tm', 0, 0, tiled=True)  14.5 us
    ppermute x10, waiting for transfers between devices, both_sides(): return (from_above, lax.ppermute(to_above, 'space', up))  13.1 us
    all_to_all x1, blocking collectives, per_device(): sent = lax.all_to_all(sent, 'tm', 0, 0, tiled=True)  12 us
    pallas_call x13, Pallas kernels, call(): pl.pallas_call(kernel, out_shape=[jax.ShapeDtypeStruct(s, F32) for s in s...  6.11 us
  transfers between devices with their start and end apart: 20, of which 11 were waited for; matrix products, arithmetic and copies ran while one was open for 1% of the time, Pallas kernels for 1%

profile of v9, /device:TPU:2, one launch (start us, length us, event | category | flops | bytes accessed | tf_op | source)
XLA Modules:
  0.0 82.9 jit_solution(15308256567199027640)
XLA Ops:
  0.0 8.9 %collective-permute-start = (f32[3,2,16,512]{3,2,1,0:T(8,128)}, f32[3,2,16,512]{3,2,1,0:T(8,128)S(1)}, u32[]{:S(2)}, u32[]{:S(2)}) collective-permute-start(f32[3,2,16,512]{3,2,1,0:T(8,128)} %bitcast.3), channel_id=1, source_target_pairs={{1,0},{2,1},{3,2},{4,3},{5,4},{6,5},{7,6},{8,7},{9,8},{10,9},{11,1... | collective-permute-start | bytes 589832 | tf_op jit(solution)/shard_map/ppermute | solution.py:304
  8.9 3.0 %collective-permute-start.2 = (f32[2,16,512]{2,1,0:T(8,128)}, f32[2,16,512]{2,1,0:T(8,128)S(1)}, u32[]{:S(2)}, u32[]{:S(2)}) collective-permute-start(f32[2,16,512]{2,1,0:T(8,128)} %param.4), channel_id=1, source_target_pairs={{1,0},{2,1},{3,2},{4,3},{5,4},{6,5},{7,6},{8,7},{9,8},{10,9},{11,1... | collective-permute-start | bytes 196616 | tf_op jit(solution)/shard_map/ppermute | solution.py:304
  11.9 1.0 %pad_maximum_fusion.slab = f32[4,2,16,512]{3,2,1,0:T(8,128)S(1)} fusion(f32[1,2,16,512]{3,2,1,0:T(8,128)} %bitcast.5, f32[3,2,16,512]{3,2,1,0:T(8,128)} %bitcast.4), kind=kLoop, calls=%fused_computation | loop fusion | flops 65536 | bytes 524288 | tf_op jit(solution)/shard_map/concatenate | solution.py:323
  12.9 0.6 shard_map.37
  14.1 1.2 %shard_map.38 = (f32[16,2,3,8,128]{4,3,2,1,0:T(8,128)S(1)}, f32[2,4,2,2,8,512]{5,4,3,2,1,0:T(8,128)S(1)}) custom-call(f32[4,2,2,8,512]{4,3,2,1,0:T(8,128)S(1)} %get-tuple-element.30.own, f32[3,2,16,512]{3,2,1,0:T(8,128)S(1)} %collective-permute-done.right, f32[3,2,16,512]{3,2,1,0:T(8,128)S(1)} %collective-permute-done.1.left, ...), custom_call_target="tpu_custom_call" | custom-call | tf_op jit(solution)/shard_map/pallas_call | solution.py:309
  15.4 14.5 %all_to_all.10.corr.rest_2_ = f32[16,2,3,8,128]{4,3,2,1,0:T(8,128)S(1)} all-to-all(f32[16,2,3,8,128]{4,3,2,1,0:T(8,128)S(1)} %get-tuple-element.32), channel_id=1, replica_groups=mesh['tm'=16,'space'=32] {'tm'}, dimensions={0} | all-to-all | bytes 786432 | tf_op jit(solution)/shard_map/all_to_all | solution.py:340
  29.9 3.0 %collective-permute-start.4 = (f32[2,2,3,8,128]{4,3,2,1,0:T(8,128)S(1)}, f32[2,2,3,8,128]{4,3,2,1,0:T(8,128)S(1)}, u32[]{:S(2)}, u32[]{:S(2)}) collective-permute-start(f32[2,2,3,8,128]{4,3,2,1,0:T(8,128)S(1)} %slice.4.own), channel_id=1, source_target_pairs={{1,0},{2,1},{3,2},{4,3},{5,4},{6,5},{7,6},{8,7},{9,8},{10,9},{11,1... | collective-permute-start | bytes 147464 | tf_op jit(solution)/shard_map/ppermute | solution.py:304
  33.0 1.6 %collective-permute-done.5.left = f32[2,2,3,8,128]{4,3,2,1,0:T(8,128)S(1)} collective-permute-done((f32[2,2,3,8,128]{4,3,2,1,0:T(8,128)S(1)}, f32[2,2,3,8,128]{4,3,2,1,0:T(8,128)S(1)}, u32[]{:S(2)}, u32[]{:S(2)}) %collective-permute-start.5) | collective-permute-done | bytes 49184 | tf_op jit(solution)/shard_map/ppermute | solution.py:305
  35.1 3.0 %collective-permute-start.6 = (f32[3,3,8,128]{3,2,1,0:T(8,128)S(1)}, f32[3,3,8,128]{3,2,1,0:T(8,128)S(1)}, u32[]{:S(2)}, u32[]{:S(2)}) collective-permute-start(f32[3,3,8,128]{3,2,1,0:T(8,128)S(1)} %get-tuple-element.34.own.rest_1_), channel_id=1, source_target_pairs={{1,0},{2,1},{3,2},{4,3},{5,4},{6,5},{7,6},{8,7},{9,8},{10,9},{11,1... | collective-permute-start | bytes 110600 | tf_op jit(solution)/shard_map/ppermute | solution.py:304
  38.0 1.6 %collective-permute-done.7.left = f32[3,3,8,128]{3,2,1,0:T(8,128)S(1)} collective-permute-done((f32[3,3,8,128]{3,2,1,0:T(8,128)S(1)}, f32[3,3,8,128]{3,2,1,0:T(8,128)S(1)}, u32[]{:S(2)}, u32[]{:S(2)}) %collective-permute-start.7) | collective-permute-done | bytes 36896 | tf_op jit(solution)/shard_map/ppermute | solution.py:305
  40.1 3.0 %collective-permute-start.8 = (f32[3,3,8,128]{3,2,1,0:T(8,128)S(1)}, f32[3,3,8,128]{3,2,1,0:T(8,128)S(1)}, u32[]{:S(2)}, u32[]{:S(2)}) collective-permute-start(f32[3,3,8,128]{3,2,1,0:T(8,128)S(1)} %get-tuple-element.36.own.rest_3_), channel_id=1, source_target_pairs={{1,0},{2,1},{3,2},{4,3},{5,4},{6,5},{7,6},{8,7},{9,8},{10,9},{11,1... | collective-permute-start | bytes 110600 | tf_op jit(solution)/shard_map/ppermute | solution.py:304
  43.1 1.6 %collective-permute-done.9.left = f32[3,3,8,128]{3,2,1,0:T(8,128)S(1)} collective-permute-done((f32[3,3,8,128]{3,2,1,0:T(8,128)S(1)}, f32[3,3,8,128]{3,2,1,0:T(8,128)S(1)}, u32[]{:S(2)}, u32[]{:S(2)}) %collective-permute-start.9) | collective-permute-done | bytes 36896 | tf_op jit(solution)/shard_map/ppermute | solution.py:305
  45.2 3.0 %collective-permute-start.10 = (f32[3,3,8,128]{3,2,1,0:T(8,128)S(1)}, f32[3,3,8,128]{3,2,1,0:T(8,128)S(1)}, u32[]{:S(2)}, u32[]{:S(2)}) collective-permute-start(f32[3,3,8,128]{3,2,1,0:T(8,128)S(1)} %get-tuple-element.38.own.rest_5_), channel_id=1, source_target_pairs={{1,0},{2,1},{3,2},{4,3},{5,4},{6,5},{7,6},{8,7},{9,8},{10,9},{11,1... | collective-permute-start | bytes 110600 | tf_op jit(solution)/shard_map/ppermute | solution.py:304
  48.2 1.6 %collective-permute-done.11.left = f32[3,3,8,128]{3,2,1,0:T(8,128)S(1)} collective-permute-done((f32[3,3,8,128]{3,2,1,0:T(8,128)S(1)}, f32[3,3,8,128]{3,2,1,0:T(8,128)S(1)}, u32[]{:S(2)}, u32[]{:S(2)}) %collective-permute-start.11) | collective-permute-done | bytes 36896 | tf_op jit(solution)/shard_map/ppermute | solution.py:305
  50.3 3.0 %collective-permute-start.12 = (f32[3,3,8,128]{3,2,1,0:T(8,128)S(1)}, f32[3,3,8,128]{3,2,1,0:T(8,128)S(1)}, u32[]{:S(2)}, u32[]{:S(2)}) collective-permute-start(f32[3,3,8,128]{3,2,1,0:T(8,128)S(1)} %get-tuple-element.40.own.rest_7_), channel_id=1, source_target_pairs={{1,0},{2,1},{3,2},{4,3},{5,4},{6,5},{7,6},{8,7},{9,8},{10,9},{11,1... | collective-permute-start | bytes 110600 | tf_op jit(solution)/shard_map/ppermute | solution.py:304
  53.2 1.6 %collective-permute-done.13.left = f32[3,3,8,128]{3,2,1,0:T(8,128)S(1)} collective-permute-done((f32[3,3,8,128]{3,2,1,0:T(8,128)S(1)}, f32[3,3,8,128]{3,2,1,0:T(8,128)S(1)}, u32[]{:S(2)}, u32[]{:S(2)}) %collective-permute-start.13) | collective-permute-done | bytes 36896 | tf_op jit(solution)/shard_map/ppermute | solution.py:305
  55.3 3.0 %collective-permute-start.14 = (f32[3,3,8,128]{3,2,1,0:T(8,128)S(1)}, f32[3,3,8,128]{3,2,1,0:T(8,128)S(1)}, u32[]{:S(2)}, u32[]{:S(2)}) collective-permute-start(f32[3,3,8,128]{3,2,1,0:T(8,128)S(1)} %get-tuple-element.42.own.rest_9_), channel_id=1, source_target_pairs={{1,0},{2,1},{3,2},{4,3},{5,4},{6,5},{7,6},{8,7},{9,8},{10,9},{11,1... | collective-permute-start | bytes 110600 | tf_op jit(solution)/shard_map/ppermute | solution.py:304
  58.3 1.6 %collective-permute-done.15.left = f32[3,3,8,128]{3,2,1,0:T(8,128)S(1)} collective-permute-done((f32[3,3,8,128]{3,2,1,0:T(8,128)S(1)}, f32[3,3,8,128]{3,2,1,0:T(8,128)S(1)}, u32[]{:S(2)}, u32[]{:S(2)}) %collective-permute-start.15) | collective-permute-done | bytes 36896 | tf_op jit(solution)/shard_map/ppermute | solution.py:305
  60.4 3.0 %collective-permute-start.16 = (f32[3,3,8,128]{3,2,1,0:T(8,128)S(1)}, f32[3,3,8,128]{3,2,1,0:T(8,128)S(1)}, u32[]{:S(2)}, u32[]{:S(2)}) collective-permute-start(f32[3,3,8,128]{3,2,1,0:T(8,128)S(1)} %get-tuple-element.44.own.rest_11_), channel_id=1, source_target_pairs={{1,0},{2,1},{3,2},{4,3},{5,4},{6,5},{7,6},{8,7},{9,8},{10,9},{11,1... | collective-permute-start | bytes 110600 | tf_op jit(solution)/shard_map/ppermute | solution.py:304
  63.4 1.6 %collective-permute-done.17.left = f32[3,3,8,128]{3,2,1,0:T(8,128)S(1)} collective-permute-done((f32[3,3,8,128]{3,2,1,0:T(8,128)S(1)}, f32[3,3,8,128]{3,2,1,0:T(8,128)S(1)}, u32[]{:S(2)}, u32[]{:S(2)}) %collective-permute-start.17) | collective-permute-done | bytes 36896 | tf_op jit(solution)/shard_map/ppermute | solution.py:305
  65.5 3.0 %collective-permute-start.18 = (f32[1,3,8,128]{3,2,1,0:T(8,128)S(1)}, f32[1,3,8,128]{3,2,1,0:T(8,128)S(1)}, u32[]{:S(2)}, u32[]{:S(2)}) collective-permute-start(f32[1,3,8,128]{3,2,1,0:T(8,128)S(1)} %get-tuple-element.47.below), channel_id=1, source_target_pairs={{1,0},{2,1},{3,2},{4,3},{5,4},{6,5},{7,6},{8,7},{9,8},{10,9},{11,1... | collective-permute-start | bytes 36872 | tf_op jit(solution)/shard_map/ppermute | solution.py:304
  68.6 1.2 %collective-permute-done.19.rest_1_ = f32[1,3,8,128]{3,2,1,0:T(8,128)S(1)} collective-permute-done((f32[1,3,8,128]{3,2,1,0:T(8,128)S(1)}, f32[1,3,8,128]{3,2,1,0:T(8,128)S(1)}, u32[]{:S(2)}, u32[]{:S(2)}) %collective-permute-start.19) | collective-permute-done | bytes 12320 | tf_op jit(solution)/shard_map/ppermute | solution.py:305
  70.1 12.0 %all_to_all.11.sent = f32[16,3,8,128]{3,2,1,0:T(8,128)S(1)} all-to-all(f32[16,3,8,128]{3,2,1,0:T(8,128)S(1)} %shard_map.48), channel_id=1, replica_groups=mesh['tm'=16,'space'=32] {'tm'}, dimensions={0} | all-to-all | bytes 393216 | tf_op jit(solution)/shard_map/all_to_all | solution.py:356
  82.1 0.8 shard_map.49
  (35 shorter events, 4.4 us)
Async XLA Ops:
  0.0 14.1 %collective-permute-start.1 = (f32[3,2,16,512]{3,2,1,0:T(8,128)}, f32[3,2,16,512]{3,2,1,0:T(8,128)S(1)}, u32[]{:S(2)}, u32[]{:S(2)}) collective-permute-start(f32[3,2,16,512]{3,2,1,0:T(8,128)} %bitcast.2), channel_id=1, source_target_pairs={{0,1},{1,2},{2,3},{3,4},{4,5},{5,6},{6,7},{7,8},{8,9},{9,10},{10,1... | collective-permute-start | bytes 589832 | tf_op jit(solution)/shard_map/ppermute | solution.py:305
  0.0 14.1 %collective-permute-start = (f32[3,2,16,512]{3,2,1,0:T(8,128)}, f32[3,2,16,512]{3,2,1,0:T(8,128)S(1)}, u32[]{:S(2)}, u32[]{:S(2)}) collective-permute-start(f32[3,2,16,512]{3,2,1,0:T(8,128)} %bitcast.3), channel_id=1, source_target_pairs={{1,0},{2,1},{3,2},{4,3},{5,4},{6,5},{7,6},{8,7},{9,8},{10,9},{11,1... | collective-permute-start | bytes 589832 | tf_op jit(solution)/shard_map/ppermute | solution.py:304
  8.9 5.1 %collective-permute-start.3 = (f32[2,16,512]{2,1,0:T(8,128)}, f32[2,16,512]{2,1,0:T(8,128)S(1)}, u32[]{:S(2)}, u32[]{:S(2)}) collective-permute-start(f32[2,16,512]{2,1,0:T(8,128)} %param.4), channel_id=1, source_target_pairs={{0,1},{1,2},{2,3},{3,4},{4,5},{5,6},{6,7},{7,8},{8,9},{9,10},{10,1... | collective-permute-start | bytes 196616 | tf_op jit(solution)/shard_map/ppermute | solution.py:305
  8.9 5.2 %collective-permute-start.2 = (f32[2,16,512]{2,1,0:T(8,128)}, f32[2,16,512]{2,1,0:T(8,128)S(1)}, u32[]{:S(2)}, u32[]{:S(2)}) collective-permute-start(f32[2,16,512]{2,1,0:T(8,128)} %param.4), channel_id=1, source_target_pairs={{1,0},{2,1},{3,2},{4,3},{5,4},{6,5},{7,6},{8,7},{9,8},{10,9},{11,1... | collective-permute-start | bytes 196616 | tf_op jit(solution)/shard_map/ppermute | solution.py:304
  11.9 1.0 %copy-start = (f32[3]{0:T(128)S(1)}, f32[3]{0:T(128)}, u32[]{:S(2)}) copy-start(f32[3]{0:T(128)} %applied.1) | copy-start | bytes 40
  29.9 4.7 %collective-permute-start.5 = (f32[2,2,3,8,128]{4,3,2,1,0:T(8,128)S(1)}, f32[2,2,3,8,128]{4,3,2,1,0:T(8,128)S(1)}, u32[]{:S(2)}, u32[]{:S(2)}) collective-permute-start(f32[2,2,3,8,128]{4,3,2,1,0:T(8,128)S(1)} %slice.4.own), channel_id=1, source_target_pairs={{0,1},{1,2},{2,3},{3,4},{4,5},{5,6},{6,7},{7,8},{8,9},{9,10},{10,1... | collective-permute-start | bytes 147464 | tf_op jit(solution)/shard_map/ppermute | solution.py:305
  29.9 4.7 %collective-permute-start.4 = (f32[2,2,3,8,128]{4,3,2,1,0:T(8,128)S(1)}, f32[2,2,3,8,128]{4,3,2,1,0:T(8,128)S(1)}, u32[]{:S(2)}, u32[]{:S(2)}) collective-permute-start(f32[2,2,3,8,128]{4,3,2,1,0:T(8,128)S(1)} %slice.4.own), channel_id=1, source_target_pairs={{1,0},{2,1},{3,2},{4,3},{5,4},{6,5},{7,6},{8,7},{9,8},{10,9},{11,1... | collective-permute-start | bytes 147464 | tf_op jit(solution)/shard_map/ppermute | solution.py:304
  35.1 4.6 %collective-permute-start.7 = (f32[3,3,8,128]{3,2,1,0:T(8,128)S(1)}, f32[3,3,8,128]{3,2,1,0:T(8,128)S(1)}, u32[]{:S(2)}, u32[]{:S(2)}) collective-permute-start(f32[3,3,8,128]{3,2,1,0:T(8,128)S(1)} %get-tuple-element.35), channel_id=1, source_target_pairs={{0,1},{1,2},{2,3},{3,4},{4,5},{5,6},{6,7},{7,8},{8,9},{9,10},{10,1... | collective-permute-start | bytes 110600 | tf_op jit(solution)/shard_map/ppermute | solution.py:305
  35.1 4.6 %collective-permute-start.6 = (f32[3,3,8,128]{3,2,1,0:T(8,128)S(1)}, f32[3,3,8,128]{3,2,1,0:T(8,128)S(1)}, u32[]{:S(2)}, u32[]{:S(2)}) collective-permute-start(f32[3,3,8,128]{3,2,1,0:T(8,128)S(1)} %get-tuple-element.34.own.rest_1_), channel_id=1, source_target_pairs={{1,0},{2,1},{3,2},{4,3},{5,4},{6,5},{7,6},{8,7},{9,8},{10,9},{11,1... | collective-permute-start | bytes 110600 | tf_op jit(solution)/shard_map/ppermute | solution.py:304
  40.1 4.6 %collective-permute-start.9 = (f32[3,3,8,128]{3,2,1,0:T(8,128)S(1)}, f32[3,3,8,128]{3,2,1,0:T(8,128)S(1)}, u32[]{:S(2)}, u32[]{:S(2)}) collective-permute-start(f32[3,3,8,128]{3,2,1,0:T(8,128)S(1)} %get-tuple-element.37), channel_id=1, source_target_pairs={{0,1},{1,2},{2,3},{3,4},{4,5},{5,6},{6,7},{7,8},{8,9},{9,10},{10,1... | collective-permute-start | bytes 110600 | tf_op jit(solution)/shard_map/ppermute | solution.py:305
  40.1 4.6 %collective-permute-start.8 = (f32[3,3,8,128]{3,2,1,0:T(8,128)S(1)}, f32[3,3,8,128]{3,2,1,0:T(8,128)S(1)}, u32[]{:S(2)}, u32[]{:S(2)}) collective-permute-start(f32[3,3,8,128]{3,2,1,0:T(8,128)S(1)} %get-tuple-element.36.own.rest_3_), channel_id=1, source_target_pairs={{1,0},{2,1},{3,2},{4,3},{5,4},{6,5},{7,6},{8,7},{9,8},{10,9},{11,1... | collective-permute-start | bytes 110600 | tf_op jit(solution)/shard_map/ppermute | solution.py:304
  45.2 4.6 %collective-permute-start.11 = (f32[3,3,8,128]{3,2,1,0:T(8,128)S(1)}, f32[3,3,8,128]{3,2,1,0:T(8,128)S(1)}, u32[]{:S(2)}, u32[]{:S(2)}) collective-permute-start(f32[3,3,8,128]{3,2,1,0:T(8,128)S(1)} %get-tuple-element.39), channel_id=1, source_target_pairs={{0,1},{1,2},{2,3},{3,4},{4,5},{5,6},{6,7},{7,8},{8,9},{9,10},{10,1... | collective-permute-start | bytes 110600 | tf_op jit(solution)/shard_map/ppermute | solution.py:305
  45.2 4.6 %collective-permute-start.10 = (f32[3,3,8,128]{3,2,1,0:T(8,128)S(1)}, f32[3,3,8,128]{3,2,1,0:T(8,128)S(1)}, u32[]{:S(2)}, u32[]{:S(2)}) collective-permute-start(f32[3,3,8,128]{3,2,1,0:T(8,128)S(1)} %get-tuple-element.38.own.rest_5_), channel_id=1, source_target_pairs={{1,0},{2,1},{3,2},{4,3},{5,4},{6,5},{7,6},{8,7},{9,8},{10,9},{11,1... | collective-permute-start | bytes 110600 | tf_op jit(solution)/shard_map/ppermute | solution.py:304
  50.2 4.6 %collective-permute-start.13 = (f32[3,3,8,128]{3,2,1,0:T(8,128)S(1)}, f32[3,3,8,128]{3,2,1,0:T(8,128)S(1)}, u32[]{:S(2)}, u32[]{:S(2)}) collective-permute-start(f32[3,3,8,128]{3,2,1,0:T(8,128)S(1)} %get-tuple-element.41), channel_id=1, source_target_pairs={{0,1},{1,2},{2,3},{3,4},{4,5},{5,6},{6,7},{7,8},{8,9},{9,10},{10,1... | collective-permute-start | bytes 110600 | tf_op jit(solution)/shard_map/ppermute | solution.py:305
  50.3 4.6 %collective-permute-start.12 = (f32[3,3,8,128]{3,2,1,0:T(8,128)S(1)}, f32[3,3,8,128]{3,2,1,0:T(8,128)S(1)}, u32[]{:S(2)}, u32[]{:S(2)}) collective-permute-start(f32[3,3,8,128]{3,2,1,0:T(8,128)S(1)} %get-tuple-element.40.own.rest_7_), channel_id=1, source_target_pairs={{1,0},{2,1},{3,2},{4,3},{5,4},{6,5},{7,6},{8,7},{9,8},{10,9},{11,1... | collective-permute-start | bytes 110600 | tf_op jit(solution)/shard_map/ppermute | solution.py:304
  55.3 4.6 %collective-permute-start.15 = (f32[3,3,8,128]{3,2,1,0:T(8,128)S(1)}, f32[3,3,8,128]{3,2,1,0:T(8,128)S(1)}, u32[]{:S(2)}, u32[]{:S(2)}) collective-permute-start(f32[3,3,8,128]{3,2,1,0:T(8,128)S(1)} %get-tuple-element.43), channel_id=1, source_target_pairs={{0,1},{1,2},{2,3},{3,4},{4,5},{5,6},{6,7},{7,8},{8,9},{9,10},{10,1... | collective-permute-start | bytes 110600 | tf_op jit(solution)/shard_map/ppermute | solution.py:305
  55.3 4.6 %collective-permute-start.14 = (f32[3,3,8,128]{3,2,1,0:T(8,128)S(1)}, f32[3,3,8,128]{3,2,1,0:T(8,128)S(1)}, u32[]{:S(2)}, u32[]{:S(2)}) collective-permute-start(f32[3,3,8,128]{3,2,1,0:T(8,128)S(1)} %get-tuple-element.42.own.rest_9_), channel_id=1, source_target_pairs={{1,0},{2,1},{3,2},{4,3},{5,4},{6,5},{7,6},{8,7},{9,8},{10,9},{11,1... | collective-permute-start | bytes 110600 | tf_op jit(solution)/shard_map/ppermute | solution.py:304
  60.4 4.6 %collective-permute-start.17 = (f32[3,3,8,128]{3,2,1,0:T(8,128)S(1)}, f32[3,3,8,128]{3,2,1,0:T(8,128)S(1)}, u32[]{:S(2)}, u32[]{:S(2)}) collective-permute-start(f32[3,3,8,128]{3,2,1,0:T(8,128)S(1)} %get-tuple-element.45), channel_id=1, source_target_pairs={{0,1},{1,2},{2,3},{3,4},{4,5},{5,6},{6,7},{7,8},{8,9},{9,10},{10,1... | collective-permute-start | bytes 110600 | tf_op jit(solution)/shard_map/ppermute | solution.py:305
  60.4 4.6 %collective-permute-start.16 = (f32[3,3,8,128]{3,2,1,0:T(8,128)S(1)}, f32[3,3,8,128]{3,2,1,0:T(8,128)S(1)}, u32[]{:S(2)}, u32[]{:S(2)}) collective-permute-start(f32[3,3,8,128]{3,2,1,0:T(8,128)S(1)} %get-tuple-element.44.own.rest_11_), channel_id=1, source_target_pairs={{1,0},{2,1},{3,2},{4,3},{5,4},{6,5},{7,6},{8,7},{9,8},{10,9},{11,1... | collective-permute-start | bytes 110600 | tf_op jit(solution)/shard_map/ppermute | solution.py:304
  65.4 4.4 %collective-permute-start.19 = (f32[1,3,8,128]{3,2,1,0:T(8,128)S(1)}, f32[1,3,8,128]{3,2,1,0:T(8,128)S(1)}, u32[]{:S(2)}, u32[]{:S(2)}) collective-permute-start(f32[1,3,8,128]{3,2,1,0:T(8,128)S(1)} %get-tuple-element.46.above), channel_id=1, source_target_pairs={{0,1},{1,2},{2,3},{3,4},{4,5},{5,6},{6,7},{7,8},{8,9},{9,10},{10,1... | collective-permute-start | bytes 36872 | tf_op jit(solution)/shard_map/ppermute | solution.py:305
  65.5 4.4 %collective-permute-start.18 = (f32[1,3,8,128]{3,2,1,0:T(8,128)S(1)}, f32[1,3,8,128]{3,2,1,0:T(8,128)S(1)}, u32[]{:S(2)}, u32[]{:S(2)}) collective-permute-start(f32[1,3,8,128]{3,2,1,0:T(8,128)S(1)} %get-tuple-element.47.below), channel_id=1, source_target_pairs={{1,0},{2,1},{3,2},{4,3},{5,4},{6,5},{7,6},{8,7},{9,8},{10,9},{11,1... | collective-permute-start | bytes 36872 | tf_op jit(solution)/shard_map/ppermute | solution.py:304

commit v10 on v9

--- a/solution.py
+++ b/solution.py
@@ -90,13 +90,13 @@
         for x in range(2):
             for q in range(layers.shape[2]):
                 at = slice(128 * q, 128 * (q + 1))
-                layers[comp, x, q] = aniso[x, :, at] if comp == 3 else spins[comp, x, :, at]
+                layers[comp, x, q] = aniso[x, :, at] if comp == 3 else spins[comp][x, :, at]
                 for parity in range(2):
                     out[comp, x, parity, :, at] = layers[comp, x, q, pl.ds(parity, 8, stride=2), :]
 
 
 def prepare(slab, applied, out, field, layers):
-    by_parity(slab, slab.at[3], out, layers)
+    by_parity([slab.at[c] for c in range(3)], slab.at[3], out, layers)
     for c in range(3):
         field[c] = jnp.full(field.shape[1:], applied[c], F32)
 
@@ -109,9 +109,9 @@
     return load
 
 
-def prologue(own, right, left, right_a, left_a, field, payload, sides, layers):
-    by_parity(left, left_a, sides.at[0], layers.at[0])
-    by_parity(right, right_a, sides.at[1], layers.at[1])
+def prologue(own, right_x, right_y, right_z, right_a, left, left_a, field, payload, sides, layers):
+    by_parity([left.at[c] for c in range(3)], left_a, sides.at[0], layers.at[0])
+    by_parity((right_x, right_y, right_z), right_a, sides.at[1], layers.at[1])
     load = beside(own, sides)
     applied = [jnp.concatenate([field[c]] * layers.shape[3], axis=1) for c in range(3)]
 
@@ -297,12 +297,19 @@
             out[0, comp, :, :, 128 * q : 128 * (q + 1)] = layers[comp, :, q]
 
 
+def from_below(array):
+    count = lax.axis_size("space")
+    return lax.ppermute(array, "space", [(i, (i + 1) % count) for i in range(count)])
+
+
+def from_above(array):
+    count = lax.axis_size("space")
+    return lax.ppermute(array, "space", [((i + 1) % count, i) for i in range(count)])
+
+
 def both_sides(to_above, to_below):
-    count = lax.axis_size("space")
-    up = [(i, (i + 1) % count) for i in range(count)]
-    down = [(j, i) for i, j in up]
-    from_above = lax.ppermute(to_below, "space", down)
-    return from_above, lax.ppermute(to_above, "space", up)
+    right = from_above(to_below)
+    return right, from_below(to_above)
 
 
 def call(kernel, shapes, *args, scratch=(), **more):
@@ -320,9 +327,10 @@
     slices = lax.axis_size("tm")
     width = starts.shape[-1]
     layers = (4, 2, width // 128, 16, 128)
-    slab = jnp.concatenate([starts[0], anisotropy[None]], axis=0)
-    right, left = both_sides(starts[0], starts[0])
-    right_a, left_a = both_sides(anisotropy, anisotropy)
+    (slab,) = lax.optimization_barrier((jnp.concatenate([starts[0], anisotropy[None]], axis=0),))
+    parts = [slab[c] for c in range(4)]
+    rights = [from_above(part) for part in parts]
+    left, left_a = from_below(starts[0]), from_below(anisotropy)
     own, field = call(
         prepare,
         [(4, 2, 2, 8, width), (3, 8, 128)],
@@ -333,7 +341,7 @@
     payload, sides = call(
         prologue,
         [(slices, 2, 3, 8, 128), (2, 4, 2, 2, 8, width)],
-        *(own, right, left, right_a, left_a, field),
+        *(own, *rights, left, left_a, field),
         scratch=[(2, *layers)],
     )
     (windows,) = call(window, [(7, 8, 128)], own, sides)

time: 83.1 us -> 84.7 us (1.019)
    ppermute x20 -> x22, waiting for transfers between devices: 13.4 us -> 14.2 us  [the longest x10 12.6 us: from_below(): lax.ppermute(array, 'space', [(i, (i + 1) % count) for i in range(count)])]
    ppermute x20 -> x22, starting transfers between devices: 35.8 us -> 35.7 us  [the longest x12 33.6 us: from_above(): lax.ppermute(array, 'space', [((i + 1) % count, i) for i in range(count)])]
  transfers between devices with their start and end apart: 20 -> 22, of which waited for: 11 -> 11; matrix products, arithmetic and copies ran while one was open for 1% -> 1% of each run, Pallas kernels for 1% -> 1%
where the time goes in v10:
time: 84.7 us; the launch traced here: 84.5 us
  starting transfers between devices  35.7 us (42%)
  blocking collectives  27.3 us (32%)
  waiting for transfers between devices  14.2 us (17%)
  Pallas kernels  6.1 us (7%)
  other arithmetic  0.98 us (1%)
    ppermute x12, starting transfers between devices, from_above(): lax.ppermute(array, 'space', [((i + 1) % count, i) for i in range(count)])  33.6 us
    all_to_all x1, blocking collectives, per_device(): corr = lax.all_to_all(payload, 'tm', 0, 0, tiled=True)  15.3 us
    ppermute x10, waiting for transfers between devices, from_below(): lax.ppermute(array, 'space', [(i, (i + 1) % count) for i in range(count)])  12.6 us
    all_to_all x1, blocking collectives, per_device(): sent = lax.all_to_all(sent, 'tm', 0, 0, tiled=True)  12 us
    pallas_call x13, Pallas kernels, call(): pl.pallas_call(kernel, out_shape=[jax.ShapeDtypeStruct(s, F32) for s in s...  6.1 us
    ppermute x10, starting transfers between devices, from_below(): lax.ppermute(array, 'space', [(i, (i + 1) % count) for i in range(count)])  2.16 us
  transfers between devices with their start and end apart: 22, of which 11 were waited for; matrix products, arithmetic and copies ran while one was open for 1% of the time, Pallas kernels for 1%

profile of v10, /device:TPU:2, one launch (start us, length us, event | category | flops | bytes accessed | tf_op | source)
XLA Modules:
  0.0 84.5 jit_solution(2979197310658897829)
XLA Ops:
  0.0 2.0 %collective-permute-start.4 = (f32[3,2,16,512]{3,2,1,0:T(8,128)}, f32[3,2,16,512]{3,2,1,0:T(8,128)S(1)}, u32[]{:S(2)}, u32[]{:S(2)}) collective-permute-start(f32[3,2,16,512]{3,2,1,0:T(8,128)} %bitcast.10), channel_id=1, source_target_pairs={{0,1},{1,2},{2,3},{3,4},{4,5},{5,6},{6,7},{7,8},{8,9},{9,10},{10,1... | collective-permute-start | bytes 589832 | tf_op jit(solution)/shard_map/ppermute | solution.py:302
  2.0 1.0 %pad_maximum_fusion.slab = f32[4,2,16,512]{3,2,1,0:T(8,128)S(1)} fusion(f32[1,2,16,512]{3,2,1,0:T(8,128)} %bitcast.12, f32[3,2,16,512]{3,2,1,0:T(8,128)} %bitcast.11), kind=kLoop, calls=%fused_computation | loop fusion | flops 65536 | bytes 524288 | tf_op jit(solution)/shard_map/concatenate | solution.py:330
  3.1 6.9 %collective-permute-start.3 = (f32[2,16,512]{2,1,0:T(8,128)S(1)}, f32[2,16,512]{2,1,0:T(8,128)S(1)}, u32[]{:S(2)}, u32[]{:S(2)}) collective-permute-start(f32[2,16,512]{2,1,0:T(8,128)S(1)} %get-tuple-element.55), channel_id=1, source_target_pairs={{1,0},{2,1},{3,2},{4,3},{5,4},{6,5},{7,6},{8,7},{9,8},{10,9},{11,1... | collective-permute-start | bytes 196616 | tf_op jit(solution)/shard_map/ppermute | solution.py:307
  10.7 1.8 %collective-permute-start.1 = (f32[2,16,512]{2,1,0:T(8,128)S(1)}, f32[2,16,512]{2,1,0:T(8,128)S(1)}, u32[]{:S(2)}, u32[]{:S(2)}) collective-permute-start(f32[2,16,512]{2,1,0:T(8,128)S(1)} %get-tuple-element.57), channel_id=1, source_target_pairs={{1,0},{2,1},{3,2},{4,3},{5,4},{6,5},{7,6},{8,7},{9,8},{10,9},{11,1... | collective-permute-start | bytes 196616 | tf_op jit(solution)/shard_map/ppermute | solution.py:307
  13.5 0.8 collective-permute-done.1.right_y
  14.9 1.2 %shard_map.38 = (f32[16,2,3,8,128]{4,3,2,1,0:T(8,128)S(1)}, f32[2,4,2,2,8,512]{5,4,3,2,1,0:T(8,128)S(1)}) custom-call(f32[4,2,2,8,512]{4,3,2,1,0:T(8,128)S(1)} %get-tuple-element.30.own, f32[2,16,512]{2,1,0:T(8,128)S(1)} %collective-permute-done.right_x, f32[2,16,512]{2,1,0:T(8,128)S(1)} %collective-permute-done.1.right_y, ...), custom_call_target="tpu_custom_call" | custom-call | tf_op jit(solution)/shard_map/pallas_call | solution.py:316
  16.2 15.3 %all_to_all.10.corr.rest_2_ = f32[16,2,3,8,128]{4,3,2,1,0:T(8,128)S(1)} all-to-all(f32[16,2,3,8,128]{4,3,2,1,0:T(8,128)S(1)} %get-tuple-element.32), channel_id=1, replica_groups=mesh['tm'=16,'space'=32] {'tm'}, dimensions={0} | all-to-all | bytes 786432 | tf_op jit(solution)/shard_map/all_to_all | solution.py:348
  31.5 3.0 %collective-permute-start.6 = (f32[2,2,3,8,128]{4,3,2,1,0:T(8,128)S(1)}, f32[2,2,3,8,128]{4,3,2,1,0:T(8,128)S(1)}, u32[]{:S(2)}, u32[]{:S(2)}) collective-permute-start(f32[2,2,3,8,128]{4,3,2,1,0:T(8,128)S(1)} %slice.24.own), channel_id=1, source_target_pairs={{1,0},{2,1},{3,2},{4,3},{5,4},{6,5},{7,6},{8,7},{9,8},{10,9},{11,1... | collective-permute-start | bytes 147464 | tf_op jit(solution)/shard_map/ppermute | solution.py:307
  34.6 1.6 %collective-permute-done.7.left = f32[2,2,3,8,128]{4,3,2,1,0:T(8,128)S(1)} collective-permute-done((f32[2,2,3,8,128]{4,3,2,1,0:T(8,128)S(1)}, f32[2,2,3,8,128]{4,3,2,1,0:T(8,128)S(1)}, u32[]{:S(2)}, u32[]{:S(2)}) %collective-permute-start.7) | collective-permute-done | bytes 49184 | tf_op jit(solution)/shard_map/ppermute | solution.py:302
  36.7 3.0 %collective-permute-start.8 = (f32[3,3,8,128]{3,2,1,0:T(8,128)S(1)}, f32[3,3,8,128]{3,2,1,0:T(8,128)S(1)}, u32[]{:S(2)}, u32[]{:S(2)}) collective-permute-start(f32[3,3,8,128]{3,2,1,0:T(8,128)S(1)} %get-tuple-element.34.own.rest_1_), channel_id=1, source_target_pairs={{1,0},{2,1},{3,2},{4,3},{5,4},{6,5},{7,6},{8,7},{9,8},{10,9},{11,1... | collective-permute-start | bytes 110600 | tf_op jit(solution)/shard_map/ppermute | solution.py:307
  39.7 1.6 %collective-permute-done.9.left = f32[3,3,8,128]{3,2,1,0:T(8,128)S(1)} collective-permute-done((f32[3,3,8,128]{3,2,1,0:T(8,128)S(1)}, f32[3,3,8,128]{3,2,1,0:T(8,128)S(1)}, u32[]{:S(2)}, u32[]{:S(2)}) %collective-permute-start.9) | collective-permute-done | bytes 36896 | tf_op jit(solution)/shard_map/ppermute | solution.py:302
  41.7 3.0 %collective-permute-start.10 = (f32[3,3,8,128]{3,2,1,0:T(8,128)S(1)}, f32[3,3,8,128]{3,2,1,0:T(8,128)S(1)}, u32[]{:S(2)}, u32[]{:S(2)}) collective-permute-start(f32[3,3,8,128]{3,2,1,0:T(8,128)S(1)} %get-tuple-element.36.own.rest_3_), channel_id=1, source_target_pairs={{1,0},{2,1},{3,2},{4,3},{5,4},{6,5},{7,6},{8,7},{9,8},{10,9},{11,1... | collective-permute-start | bytes 110600 | tf_op jit(solution)/shard_map/ppermute | solution.py:307
  44.7 1.6 %collective-permute-done.11.left = f32[3,3,8,128]{3,2,1,0:T(8,128)S(1)} collective-permute-done((f32[3,3,8,128]{3,2,1,0:T(8,128)S(1)}, f32[3,3,8,128]{3,2,1,0:T(8,128)S(1)}, u32[]{:S(2)}, u32[]{:S(2)}) %collective-permute-start.11) | collective-permute-done | bytes 36896 | tf_op jit(solution)/shard_map/ppermute | solution.py:302
  46.8 3.0 %collective-permute-start.12 = (f32[3,3,8,128]{3,2,1,0:T(8,128)S(1)}, f32[3,3,8,128]{3,2,1,0:T(8,128)S(1)}, u32[]{:S(2)}, u32[]{:S(2)}) collective-permute-start(f32[3,3,8,128]{3,2,1,0:T(8,128)S(1)} %get-tuple-element.38.own.rest_5_), channel_id=1, source_target_pairs={{1,0},{2,1},{3,2},{4,3},{5,4},{6,5},{7,6},{8,7},{9,8},{10,9},{11,1... | collective-permute-start | bytes 110600 | tf_op jit(solution)/shard_map/ppermute | solution.py:307
  49.8 1.6 %collective-permute-done.13.left = f32[3,3,8,128]{3,2,1,0:T(8,128)S(1)} collective-permute-done((f32[3,3,8,128]{3,2,1,0:T(8,128)S(1)}, f32[3,3,8,128]{3,2,1,0:T(8,128)S(1)}, u32[]{:S(2)}, u32[]{:S(2)}) %collective-permute-start.13) | collective-permute-done | bytes 36896 | tf_op jit(solution)/shard_map/ppermute | solution.py:302
  51.9 3.0 %collective-permute-start.14 = (f32[3,3,8,128]{3,2,1,0:T(8,128)S(1)}, f32[3,3,8,128]{3,2,1,0:T(8,128)S(1)}, u32[]{:S(2)}, u32[]{:S(2)}) collective-permute-start(f32[3,3,8,128]{3,2,1,0:T(8,128)S(1)} %get-tuple-element.40.own.rest_7_), channel_id=1, source_target_pairs={{1,0},{2,1},{3,2},{4,3},{5,4},{6,5},{7,6},{8,7},{9,8},{10,9},{11,1... | collective-permute-start | bytes 110600 | tf_op jit(solution)/shard_map/ppermute | solution.py:307
  54.8 1.6 %collective-permute-done.15.left = f32[3,3,8,128]{3,2,1,0:T(8,128)S(1)} collective-permute-done((f32[3,3,8,128]{3,2,1,0:T(8,128)S(1)}, f32[3,3,8,128]{3,2,1,0:T(8,128)S(1)}, u32[]{:S(2)}, u32[]{:S(2)}) %collective-permute-start.15) | collective-permute-done | bytes 36896 | tf_op jit(solution)/shard_map/ppermute | solution.py:302
  56.9 3.0 %collective-permute-start.16 = (f32[3,3,8,128]{3,2,1,0:T(8,128)S(1)}, f32[3,3,8,128]{3,2,1,0:T(8,128)S(1)}, u32[]{:S(2)}, u32[]{:S(2)}) collective-permute-start(f32[3,3,8,128]{3,2,1,0:T(8,128)S(1)} %get-tuple-element.42.own.rest_9_), channel_id=1, source_target_pairs={{1,0},{2,1},{3,2},{4,3},{5,4},{6,5},{7,6},{8,7},{9,8},{10,9},{11,1... | collective-permute-start | bytes 110600 | tf_op jit(solution)/shard_map/ppermute | solution.py:307
  59.9 1.6 %collective-permute-done.17.left = f32[3,3,8,128]{3,2,1,0:T(8,128)S(1)} collective-permute-done((f32[3,3,8,128]{3,2,1,0:T(8,128)S(1)}, f32[3,3,8,128]{3,2,1,0:T(8,128)S(1)}, u32[]{:S(2)}, u32[]{:S(2)}) %collective-permute-start.17) | collective-permute-done | bytes 36896 | tf_op jit(solution)/shard_map/ppermute | solution.py:302
  62.0 3.0 %collective-permute-start.18 = (f32[3,3,8,128]{3,2,1,0:T(8,128)S(1)}, f32[3,3,8,128]{3,2,1,0:T(8,128)S(1)}, u32[]{:S(2)}, u32[]{:S(2)}) collective-permute-start(f32[3,3,8,128]{3,2,1,0:T(8,128)S(1)} %get-tuple-element.44.own.rest_11_), channel_id=1, source_target_pairs={{1,0},{2,1},{3,2},{4,3},{5,4},{6,5},{7,6},{8,7},{9,8},{10,9},{11,1... | collective-permute-start | bytes 110600 | tf_op jit(solution)/shard_map/ppermute | solution.py:307
  65.0 1.6 %collective-permute-done.19.left = f32[3,3,8,128]{3,2,1,0:T(8,128)S(1)} collective-permute-done((f32[3,3,8,128]{3,2,1,0:T(8,128)S(1)}, f32[3,3,8,128]{3,2,1,0:T(8,128)S(1)}, u32[]{:S(2)}, u32[]{:S(2)}) %collective-permute-start.19) | collective-permute-done | bytes 36896 | tf_op jit(solution)/shard_map/ppermute | solution.py:302
  67.1 3.0 %collective-permute-start.20 = (f32[1,3,8,128]{3,2,1,0:T(8,128)S(1)}, f32[1,3,8,128]{3,2,1,0:T(8,128)S(1)}, u32[]{:S(2)}, u32[]{:S(2)}) collective-permute-start(f32[1,3,8,128]{3,2,1,0:T(8,128)S(1)} %get-tuple-element.47.below), channel_id=1, source_target_pairs={{1,0},{2,1},{3,2},{4,3},{5,4},{6,5},{7,6},{8,7},{9,8},{10,9},{11,1... | collective-permute-start | bytes 36872 | tf_op jit(solution)/shard_map/ppermute | solution.py:307
  70.2 1.2 %collective-permute-done.21.rest_1_ = f32[1,3,8,128]{3,2,1,0:T(8,128)S(1)} collective-permute-done((f32[1,3,8,128]{3,2,1,0:T(8,128)S(1)}, f32[1,3,8,128]{3,2,1,0:T(8,128)S(1)}, u32[]{:S(2)}, u32[]{:S(2)}) %collective-permute-start.21) | collective-permute-done | bytes 12320 | tf_op jit(solution)/shard_map/ppermute | solution.py:302
  71.7 12.0 %all_to_all.11.sent = f32[16,3,8,128]{3,2,1,0:T(8,128)S(1)} all-to-all(f32[16,3,8,128]{3,2,1,0:T(8,128)S(1)} %shard_map.48), channel_id=1, replica_groups=mesh['tm'=16,'space'=32] {'tm'}, dimensions={0} | all-to-all | bytes 393216 | tf_op jit(solution)/shard_map/all_to_all | solution.py:364
  (40 shorter events, 7.0 us)
Async XLA Ops:
  0.0 12.4 %collective-permute-start.5 = (f32[2,16,512]{2,1,0:T(8,128)}, f32[2,16,512]{2,1,0:T(8,128)S(1)}, u32[]{:S(2)}, u32[]{:S(2)}) collective-permute-start(f32[2,16,512]{2,1,0:T(8,128)} %param.4), channel_id=1, source_target_pairs={{0,1},{1,2},{2,3},{3,4},{4,5},{5,6},{6,7},{7,8},{8,9},{9,10},{10,1... | collective-permute-start | bytes 196616 | tf_op jit(solution)/shard_map/ppermute | solution.py:302
  0.0 14.9 %collective-permute-start.4 = (f32[3,2,16,512]{3,2,1,0:T(8,128)}, f32[3,2,16,512]{3,2,1,0:T(8,128)S(1)}, u32[]{:S(2)}, u32[]{:S(2)}) collective-permute-start(f32[3,2,16,512]{3,2,1,0:T(8,128)} %bitcast.10), channel_id=1, source_target_pairs={{0,1},{1,2},{2,3},{3,4},{4,5},{5,6},{6,7},{7,8},{8,9},{9,10},{10,1... | collective-permute-start | bytes 589832 | tf_op jit(solution)/shard_map/ppermute | solution.py:302
  3.1 10.4 %collective-permute-start.3 = (f32[2,16,512]{2,1,0:T(8,128)S(1)}, f32[2,16,512]{2,1,0:T(8,128)S(1)}, u32[]{:S(2)}, u32[]{:S(2)}) collective-permute-start(f32[2,16,512]{2,1,0:T(8,128)S(1)} %get-tuple-element.55), channel_id=1, source_target_pairs={{1,0},{2,1},{3,2},{4,3},{5,4},{6,5},{7,6},{8,7},{9,8},{10,9},{11,1... | collective-permute-start | bytes 196616 | tf_op jit(solution)/shard_map/ppermute | solution.py:307
  10.0 3.5 %collective-permute-start.2 = (f32[2,16,512]{2,1,0:T(8,128)S(1)}, f32[2,16,512]{2,1,0:T(8,128)S(1)}, u32[]{:S(2)}, u32[]{:S(2)}) collective-permute-start(f32[2,16,512]{2,1,0:T(8,128)S(1)} %get-tuple-element.56), channel_id=1, source_target_pairs={{1,0},{2,1},{3,2},{4,3},{5,4},{6,5},{7,6},{8,7},{9,8},{10,9},{11,1... | collective-permute-start | bytes 196616 | tf_op jit(solution)/shard_map/ppermute | solution.py:307
  10.7 2.3 %copy-start = (f32[3]{0:T(128)S(1)}, f32[3]{0:T(128)}, u32[]{:S(2)}) copy-start(f32[3]{0:T(128)} %applied.1) | copy-start | bytes 40
  10.7 3.7 %collective-permute-start.1 = (f32[2,16,512]{2,1,0:T(8,128)S(1)}, f32[2,16,512]{2,1,0:T(8,128)S(1)}, u32[]{:S(2)}, u32[]{:S(2)}) collective-permute-start(f32[2,16,512]{2,1,0:T(8,128)S(1)} %get-tuple-element.57), channel_id=1, source_target_pairs={{1,0},{2,1},{3,2},{4,3},{5,4},{6,5},{7,6},{8,7},{9,8},{10,9},{11,1... | collective-permute-start | bytes 196616 | tf_op jit(solution)/shard_map/ppermute | solution.py:307
  12.4 2.5 %collective-permute-start = (f32[2,16,512]{2,1,0:T(8,128)S(1)}, f32[2,16,512]{2,1,0:T(8,128)S(1)}, u32[]{:S(2)}, u32[]{:S(2)}) collective-permute-start(f32[2,16,512]{2,1,0:T(8,128)S(1)} %get-tuple-element.58), channel_id=1, source_target_pairs={{1,0},{2,1},{3,2},{4,3},{5,4},{6,5},{7,6},{8,7},{9,8},{10,9},{11,1... | collective-permute-start | bytes 196616 | tf_op jit(solution)/shard_map/ppermute | solution.py:307
  31.5 4.7 %collective-permute-start.7 = (f32[2,2,3,8,128]{4,3,2,1,0:T(8,128)S(1)}, f32[2,2,3,8,128]{4,3,2,1,0:T(8,128)S(1)}, u32[]{:S(2)}, u32[]{:S(2)}) collective-permute-start(f32[2,2,3,8,128]{4,3,2,1,0:T(8,128)S(1)} %slice.24.own), channel_id=1, source_target_pairs={{0,1},{1,2},{2,3},{3,4},{4,5},{5,6},{6,7},{7,8},{8,9},{9,10},{10,1... | collective-permute-start | bytes 147464 | tf_op jit(solution)/shard_map/ppermute | solution.py:302
  31.5 4.7 %collective-permute-start.6 = (f32[2,2,3,8,128]{4,3,2,1,0:T(8,128)S(1)}, f32[2,2,3,8,128]{4,3,2,1,0:T(8,128)S(1)}, u32[]{:S(2)}, u32[]{:S(2)}) collective-permute-start(f32[2,2,3,8,128]{4,3,2,1,0:T(8,128)S(1)} %slice.24.own), channel_id=1, source_target_pairs={{1,0},{2,1},{3,2},{4,3},{5,4},{6,5},{7,6},{8,7},{9,8},{10,9},{11,1... | collective-permute-start | bytes 147464 | tf_op jit(solution)/shard_map/ppermute | solution.py:307
  36.7 4.6 %collective-permute-start.9 = (f32[3,3,8,128]{3,2,1,0:T(8,128)S(1)}, f32[3,3,8,128]{3,2,1,0:T(8,128)S(1)}, u32[]{:S(2)}, u32[]{:S(2)}) collective-permute-start(f32[3,3,8,128]{3,2,1,0:T(8,128)S(1)} %get-tuple-element.35), channel_id=1, source_target_pairs={{0,1},{1,2},{2,3},{3,4},{4,5},{5,6},{6,7},{7,8},{8,9},{9,10},{10,1... | collective-permute-start | bytes 110600 | tf_op jit(solution)/shard_map/ppermute | solution.py:302
  36.7 4.6 %collective-permute-start.8 = (f32[3,3,8,128]{3,2,1,0:T(8,128)S(1)}, f32[3,3,8,128]{3,2,1,0:T(8,128)S(1)}, u32[]{:S(2)}, u32[]{:S(2)}) collective-permute-start(f32[3,3,8,128]{3,2,1,0:T(8,128)S(1)} %get-tuple-element.34.own.rest_1_), channel_id=1, source_target_pairs={{1,0},{2,1},{3,2},{4,3},{5,4},{6,5},{7,6},{8,7},{9,8},{10,9},{11,1... | collective-permute-start | bytes 110600 | tf_op jit(solution)/shard_map/ppermute | solution.py:307
  41.7 4.6 %collective-permute-start.11 = (f32[3,3,8,128]{3,2,1,0:T(8,128)S(1)}, f32[3,3,8,128]{3,2,1,0:T(8,128)S(1)}, u32[]{:S(2)}, u32[]{:S(2)}) collective-permute-start(f32[3,3,8,128]{3,2,1,0:T(8,128)S(1)} %get-tuple-element.37), channel_id=1, source_target_pairs={{0,1},{1,2},{2,3},{3,4},{4,5},{5,6},{6,7},{7,8},{8,9},{9,10},{10,1... | collective-permute-start | bytes 110600 | tf_op jit(solution)/shard_map/ppermute | solution.py:302
  41.7 4.6 %collective-permute-start.10 = (f32[3,3,8,128]{3,2,1,0:T(8,128)S(1)}, f32[3,3,8,128]{3,2,1,0:T(8,128)S(1)}, u32[]{:S(2)}, u32[]{:S(2)}) collective-permute-start(f32[3,3,8,128]{3,2,1,0:T(8,128)S(1)} %get-tuple-element.36.own.rest_3_), channel_id=1, source_target_pairs={{1,0},{2,1},{3,2},{4,3},{5,4},{6,5},{7,6},{8,7},{9,8},{10,9},{11,1... | collective-permute-start | bytes 110600 | tf_op jit(solution)/shard_map/ppermute | solution.py:307
  46.8 4.6 %collective-permute-start.13 = (f32[3,3,8,128]{3,2,1,0:T(8,128)S(1)}, f32[3,3,8,128]{3,2,1,0:T(8,128)S(1)}, u32[]{:S(2)}, u32[]{:S(2)}) collective-permute-start(f32[3,3,8,128]{3,2,1,0:T(8,128)S(1)} %get-tuple-element.39), channel_id=1, source_target_pairs={{0,1},{1,2},{2,3},{3,4},{4,5},{5,6},{6,7},{7,8},{8,9},{9,10},{10,1... | collective-permute-start | bytes 110600 | tf_op jit(solution)/shard_map/ppermute | solution.py:302
  46.8 4.6 %collective-permute-start.12 = (f32[3,3,8,128]{3,2,1,0:T(8,128)S(1)}, f32[3,3,8,128]{3,2,1,0:T(8,128)S(1)}, u32[]{:S(2)}, u32[]{:S(2)}) collective-permute-start(f32[3,3,8,128]{3,2,1,0:T(8,128)S(1)} %get-tuple-element.38.own.rest_5_), channel_id=1, source_target_pairs={{1,0},{2,1},{3,2},{4,3},{5,4},{6,5},{7,6},{8,7},{9,8},{10,9},{11,1... | collective-permute-start | bytes 110600 | tf_op jit(solution)/shard_map/ppermute | solution.py:307
  51.8 4.6 %collective-permute-start.15 = (f32[3,3,8,128]{3,2,1,0:T(8,128)S(1)}, f32[3,3,8,128]{3,2,1,0:T(8,128)S(1)}, u32[]{:S(2)}, u32[]{:S(2)}) collective-permute-start(f32[3,3,8,128]{3,2,1,0:T(8,128)S(1)} %get-tuple-element.41), channel_id=1, source_target_pairs={{0,1},{1,2},{2,3},{3,4},{4,5},{5,6},{6,7},{7,8},{8,9},{9,10},{10,1... | collective-permute-start | bytes 110600 | tf_op jit(solution)/shard_map/ppermute | solution.py:302
  51.9 4.6 %collective-permute-start.14 = (f32[3,3,8,128]{3,2,1,0:T(8,128)S(1)}, f32[3,3,8,128]{3,2,1,0:T(8,128)S(1)}, u32[]{:S(2)}, u32[]{:S(2)}) collective-permute-start(f32[3,3,8,128]{3,2,1,0:T(8,128)S(1)} %get-tuple-element.40.own.rest_7_), channel_id=1, source_target_pairs={{1,0},{2,1},{3,2},{4,3},{5,4},{6,5},{7,6},{8,7},{9,8},{10,9},{11,1... | collective-permute-start | bytes 110600 | tf_op jit(solution)/shard_map/ppermute | solution.py:307
  56.9 4.6 %collective-permute-start.17 = (f32[3,3,8,128]{3,2,1,0:T(8,128)S(1)}, f32[3,3,8,128]{3,2,1,0:T(8,128)S(1)}, u32[]{:S(2)}, u32[]{:S(2)}) collective-permute-start(f32[3,3,8,128]{3,2,1,0:T(8,128)S(1)} %get-tuple-element.43), channel_id=1, source_target_pairs={{0,1},{1,2},{2,3},{3,4},{4,5},{5,6},{6,7},{7,8},{8,9},{9,10},{10,1... | collective-permute-start | bytes 110600 | tf_op jit(solution)/shard_map/ppermute | solution.py:302
  56.9 4.6 %collective-permute-start.16 = (f32[3,3,8,128]{3,2,1,0:T(8,128)S(1)}, f32[3,3,8,128]{3,2,1,0:T(8,128)S(1)}, u32[]{:S(2)}, u32[]{:S(2)}) collective-permute-start(f32[3,3,8,128]{3,2,1,0:T(8,128)S(1)} %get-tuple-element.42.own.rest_9_), channel_id=1, source_target_pairs={{1,0},{2,1},{3,2},{4,3},{5,4},{6,5},{7,6},{8,7},{9,8},{10,9},{11,1... | collective-permute-start | bytes 110600 | tf_op jit(solution)/shard_map/ppermute | solution.py:307
  62.0 4.6 %collective-permute-start.19 = (f32[3,3,8,128]{3,2,1,0:T(8,128)S(1)}, f32[3,3,8,128]{3,2,1,0:T(8,128)S(1)}, u32[]{:S(2)}, u32[]{:S(2)}) collective-permute-start(f32[3,3,8,128]{3,2,1,0:T(8,128)S(1)} %get-tuple-element.45), channel_id=1, source_target_pairs={{0,1},{1,2},{2,3},{3,4},{4,5},{5,6},{6,7},{7,8},{8,9},{9,10},{10,1... | collective-permute-start | bytes 110600 | tf_op jit(solution)/shard_map/ppermute | solution.py:302
  62.0 4.6 %collective-permute-start.18 = (f32[3,3,8,128]{3,2,1,0:T(8,128)S(1)}, f32[3,3,8,128]{3,2,1,0:T(8,128)S(1)}, u32[]{:S(2)}, u32[]{:S(2)}) collective-permute-start(f32[3,3,8,128]{3,2,1,0:T(8,128)S(1)} %get-tuple-element.44.own.rest_11_), channel_id=1, source_target_pairs={{1,0},{2,1},{3,2},{4,3},{5,4},{6,5},{7,6},{8,7},{9,8},{10,9},{11,1... | collective-permute-start | bytes 110600 | tf_op jit(solution)/shard_map/ppermute | solution.py:307
  67.0 4.4 %collective-permute-start.21 = (f32[1,3,8,128]{3,2,1,0:T(8,128)S(1)}, f32[1,3,8,128]{3,2,1,0:T(8,128)S(1)}, u32[]{:S(2)}, u32[]{:S(2)}) collective-permute-start(f32[1,3,8,128]{3,2,1,0:T(8,128)S(1)} %get-tuple-element.46.above), channel_id=1, source_target_pairs={{0,1},{1,2},{2,3},{3,4},{4,5},{5,6},{6,7},{7,8},{8,9},{9,10},{10,1... | collective-permute-start | bytes 36872 | tf_op jit(solution)/shard_map/ppermute | solution.py:302
  67.1 4.4 %collective-permute-start.20 = (f32[1,3,8,128]{3,2,1,0:T(8,128)S(1)}, f32[1,3,8,128]{3,2,1,0:T(8,128)S(1)}, u32[]{:S(2)}, u32[]{:S(2)}) collective-permute-start(f32[1,3,8,128]{3,2,1,0:T(8,128)S(1)} %get-tuple-element.47.below), channel_id=1, source_target_pairs={{1,0},{2,1},{3,2},{4,3},{5,4},{6,5},{7,6},{8,7},{9,8},{10,9},{11,1... | collective-permute-start | bytes 36872 | tf_op jit(solution)/shard_map/ppermute | solution.py:307

commit v11 on v9

--- a/solution.py
+++ b/solution.py
@@ -109,7 +109,7 @@
     return load
 
 
-def prologue(own, right, left, right_a, left_a, field, payload, sides, layers):
+def prologue(own, right, left_a, right_a, left, field, payload, sides, layers):
     by_parity(left, left_a, sides.at[0], layers.at[0])
     by_parity(right, right_a, sides.at[1], layers.at[1])
     load = beside(own, sides)
@@ -333,7 +333,7 @@
     payload, sides = call(
         prologue,
         [(slices, 2, 3, 8, 128), (2, 4, 2, 2, 8, width)],
-        *(own, right, left, right_a, left_a, field),
+        *(own, right, left_a, right_a, left, field),
         scratch=[(2, *layers)],
     )
     (windows,) = call(window, [(7, 8, 128)], own, sides)

time: 83.1 us -> 83.7 us (level)
  waiting for transfers between devices: 13.4 us -> 16.2 us
  starting transfers between devices: 35.8 us -> 33.5 us
    ppermute x10, starting transfers between devices: 35.6 us -> 33.3 us  [both_sides(): from_above = lax.ppermute(to_below, 'space', down)]
    ppermute x10, waiting for transfers between devices: 0.24 us -> 2.11 us  [both_sides(): from_above = lax.ppermute(to_below, 'space', down)]
    ppermute x10, waiting for transfers between devices: 13.1 us -> 14.1 us  [both_sides(): return (from_above, lax.ppermute(to_above, 'space', up))]
where the time goes in v11:
time: 83.7 us; the launch traced here: 83.5 us
  starting transfers between devices  33.5 us (40%)
  blocking collectives  26.5 us (32%)
  waiting for transfers between devices  16.2 us (19%)
  Pallas kernels  6.11 us (7%)
  other arithmetic  0.99 us (1%)
    ppermute x10, starting transfers between devices, both_sides(): from_above = lax.ppermute(to_below, 'space', down)  33.3 us
    all_to_all x1, blocking collectives, per_device(): corr = lax.all_to_all(payload, 'tm', 0, 0, tiled=True)  14.5 us
    ppermute x10, waiting for transfers between devices, both_sides(): return (from_above, lax.ppermute(to_above, 'space', up))  14.1 us
    all_to_all x1, blocking collectives, per_device(): sent = lax.all_to_all(sent, 'tm', 0, 0, tiled=True)  12 us
    pallas_call x13, Pallas kernels, call(): pl.pallas_call(kernel, out_shape=[jax.ShapeDtypeStruct(s, F32) for s in s...  6.11 us
    ppermute x10, waiting for transfers between devices, both_sides(): from_above = lax.ppermute(to_below, 'space', down)  2.11 us
  transfers between devices with their start and end apart: 20, of which 11 were waited for; matrix products, arithmetic and copies ran while one was open for 1% of the time, Pallas kernels for 1%

profile of v11, /device:TPU:2, one launch (start us, length us, event | category | flops | bytes accessed | tf_op | source)
XLA Modules:
  0.0 83.5 jit_solution(10876674527672764067)
XLA Ops:
  0.0 8.9 %collective-permute-start = (f32[3,2,16,512]{3,2,1,0:T(8,128)}, f32[3,2,16,512]{3,2,1,0:T(8,128)S(1)}, u32[]{:S(2)}, u32[]{:S(2)}) collective-permute-start(f32[3,2,16,512]{3,2,1,0:T(8,128)} %bitcast.3), channel_id=1, source_target_pairs={{1,0},{2,1},{3,2},{4,3},{5,4},{6,5},{7,6},{8,7},{9,8},{10,9},{11,1... | collective-permute-start | bytes 589832 | tf_op jit(solution)/shard_map/ppermute | solution.py:304
  9.6 1.0 %pad_maximum_fusion.slab = f32[4,2,16,512]{3,2,1,0:T(8,128)S(1)} fusion(f32[1,2,16,512]{3,2,1,0:T(8,128)} %bitcast.5, f32[3,2,16,512]{3,2,1,0:T(8,128)} %bitcast.4), kind=kLoop, calls=%fused_computation | loop fusion | flops 65536 | bytes 524288 | tf_op jit(solution)/shard_map/concatenate | solution.py:323
  11.2 1.9 %collective-permute-done.2.right_a = f32[2,16,512]{2,1,0:T(8,128)S(1)} collective-permute-done((f32[2,16,512]{2,1,0:T(8,128)}, f32[2,16,512]{2,1,0:T(8,128)S(1)}, u32[]{:S(2)}, u32[]{:S(2)}) %collective-permute-start.2) | collective-permute-done | bytes 65568 | tf_op jit(solution)/shard_map/ppermute | solution.py:304
  13.1 1.6 %collective-permute-done.1.left_a = f32[2,16,512]{2,1,0:T(8,128)S(1)} collective-permute-done((f32[2,16,512]{2,1,0:T(8,128)}, f32[2,16,512]{2,1,0:T(8,128)S(1)}, u32[]{:S(2)}, u32[]{:S(2)}) %collective-permute-start.1) | collective-permute-done | bytes 65568 | tf_op jit(solution)/shard_map/ppermute | solution.py:305
  14.7 1.2 %shard_map.38 = (f32[16,2,3,8,128]{4,3,2,1,0:T(8,128)S(1)}, f32[2,4,2,2,8,512]{5,4,3,2,1,0:T(8,128)S(1)}) custom-call(f32[4,2,2,8,512]{4,3,2,1,0:T(8,128)S(1)} %get-tuple-element.30.own, f32[3,2,16,512]{3,2,1,0:T(8,128)S(1)} %collective-permute-done.right, f32[2,16,512]{2,1,0:T(8,128)S(1)} %collective-permute-done.1.left_a, ...), custom_call_target="tpu_custom_call" | custom-call | tf_op jit(solution)/shard_map/pallas_call | solution.py:309
  16.0 14.5 %all_to_all.10.corr.rest_2_ = f32[16,2,3,8,128]{4,3,2,1,0:T(8,128)S(1)} all-to-all(f32[16,2,3,8,128]{4,3,2,1,0:T(8,128)S(1)} %get-tuple-element.32), channel_id=1, replica_groups=mesh['tm'=16,'space'=32] {'tm'}, dimensions={0} | all-to-all | bytes 786432 | tf_op jit(solution)/shard_map/all_to_all | solution.py:340
  30.5 3.0 %collective-permute-start.4 = (f32[2,2,3,8,128]{4,3,2,1,0:T(8,128)S(1)}, f32[2,2,3,8,128]{4,3,2,1,0:T(8,128)S(1)}, u32[]{:S(2)}, u32[]{:S(2)}) collective-permute-start(f32[2,2,3,8,128]{4,3,2,1,0:T(8,128)S(1)} %slice.4.own), channel_id=1, source_target_pairs={{1,0},{2,1},{3,2},{4,3},{5,4},{6,5},{7,6},{8,7},{9,8},{10,9},{11,1... | collective-permute-start | bytes 147464 | tf_op jit(solution)/shard_map/ppermute | solution.py:304
  33.6 1.6 %collective-permute-done.5.left = f32[2,2,3,8,128]{4,3,2,1,0:T(8,128)S(1)} collective-permute-done((f32[2,2,3,8,128]{4,3,2,1,0:T(8,128)S(1)}, f32[2,2,3,8,128]{4,3,2,1,0:T(8,128)S(1)}, u32[]{:S(2)}, u32[]{:S(2)}) %collective-permute-start.5) | collective-permute-done | bytes 49184 | tf_op jit(solution)/shard_map/ppermute | solution.py:305
  35.7 3.0 %collective-permute-start.6 = (f32[3,3,8,128]{3,2,1,0:T(8,128)S(1)}, f32[3,3,8,128]{3,2,1,0:T(8,128)S(1)}, u32[]{:S(2)}, u32[]{:S(2)}) collective-permute-start(f32[3,3,8,128]{3,2,1,0:T(8,128)S(1)} %get-tuple-element.34.own.rest_1_), channel_id=1, source_target_pairs={{1,0},{2,1},{3,2},{4,3},{5,4},{6,5},{7,6},{8,7},{9,8},{10,9},{11,1... | collective-permute-start | bytes 110600 | tf_op jit(solution)/shard_map/ppermute | solution.py:304
  38.7 1.6 %collective-permute-done.7.left = f32[3,3,8,128]{3,2,1,0:T(8,128)S(1)} collective-permute-done((f32[3,3,8,128]{3,2,1,0:T(8,128)S(1)}, f32[3,3,8,128]{3,2,1,0:T(8,128)S(1)}, u32[]{:S(2)}, u32[]{:S(2)}) %collective-permute-start.7) | collective-permute-done | bytes 36896 | tf_op jit(solution)/shard_map/ppermute | solution.py:305
  40.8 3.0 %collective-permute-start.8 = (f32[3,3,8,128]{3,2,1,0:T(8,128)S(1)}, f32[3,3,8,128]{3,2,1,0:T(8,128)S(1)}, u32[]{:S(2)}, u32[]{:S(2)}) collective-permute-start(f32[3,3,8,128]{3,2,1,0:T(8,128)S(1)} %get-tuple-element.36.own.rest_3_), channel_id=1, source_target_pairs={{1,0},{2,1},{3,2},{4,3},{5,4},{6,5},{7,6},{8,7},{9,8},{10,9},{11,1... | collective-permute-start | bytes 110600 | tf_op jit(solution)/shard_map/ppermute | solution.py:304
  43.7 1.6 %collective-permute-done.9.left = f32[3,3,8,128]{3,2,1,0:T(8,128)S(1)} collective-permute-done((f32[3,3,8,128]{3,2,1,0:T(8,128)S(1)}, f32[3,3,8,128]{3,2,1,0:T(8,128)S(1)}, u32[]{:S(2)}, u32[]{:S(2)}) %collective-permute-start.9) | collective-permute-done | bytes 36896 | tf_op jit(solution)/shard_map/ppermute | solution.py:305
  45.8 3.0 %collective-permute-start.10 = (f32[3,3,8,128]{3,2,1,0:T(8,128)S(1)}, f32[3,3,8,128]{3,2,1,0:T(8,128)S(1)}, u32[]{:S(2)}, u32[]{:S(2)}) collective-permute-start(f32[3,3,8,128]{3,2,1,0:T(8,128)S(1)} %get-tuple-element.38.own.rest_5_), channel_id=1, source_target_pairs={{1,0},{2,1},{3,2},{4,3},{5,4},{6,5},{7,6},{8,7},{9,8},{10,9},{11,1... | collective-permute-start | bytes 110600 | tf_op jit(solution)/shard_map/ppermute | solution.py:304
  48.8 1.6 %collective-permute-done.11.left = f32[3,3,8,128]{3,2,1,0:T(8,128)S(1)} collective-permute-done((f32[3,3,8,128]{3,2,1,0:T(8,128)S(1)}, f32[3,3,8,128]{3,2,1,0:T(8,128)S(1)}, u32[]{:S(2)}, u32[]{:S(2)}) %collective-permute-start.11) | collective-permute-done | bytes 36896 | tf_op jit(solution)/shard_map/ppermute | solution.py:305
  50.9 3.0 %collective-permute-start.12 = (f32[3,3,8,128]{3,2,1,0:T(8,128)S(1)}, f32[3,3,8,128]{3,2,1,0:T(8,128)S(1)}, u32[]{:S(2)}, u32[]{:S(2)}) collective-permute-start(f32[3,3,8,128]{3,2,1,0:T(8,128)S(1)} %get-tuple-element.40.own.rest_7_), channel_id=1, source_target_pairs={{1,0},{2,1},{3,2},{4,3},{5,4},{6,5},{7,6},{8,7},{9,8},{10,9},{11,1... | collective-permute-start | bytes 110600 | tf_op jit(solution)/shard_map/ppermute | solution.py:304
  53.9 1.6 %collective-permute-done.13.left = f32[3,3,8,128]{3,2,1,0:T(8,128)S(1)} collective-permute-done((f32[3,3,8,128]{3,2,1,0:T(8,128)S(1)}, f32[3,3,8,128]{3,2,1,0:T(8,128)S(1)}, u32[]{:S(2)}, u32[]{:S(2)}) %collective-permute-start.13) | collective-permute-done | bytes 36896 | tf_op jit(solution)/shard_map/ppermute | solution.py:305
  55.9 3.0 %collective-permute-start.14 = (f32[3,3,8,128]{3,2,1,0:T(8,128)S(1)}, f32[3,3,8,128]{3,2,1,0:T(8,128)S(1)}, u32[]{:S(2)}, u32[]{:S(2)}) collective-permute-start(f32[3,3,8,128]{3,2,1,0:T(8,128)S(1)} %get-tuple-element.42.own.rest_9_), channel_id=1, source_target_pairs={{1,0},{2,1},{3,2},{4,3},{5,4},{6,5},{7,6},{8,7},{9,8},{10,9},{11,1... | collective-permute-start | bytes 110600 | tf_op jit(solution)/shard_map/ppermute | solution.py:304
  58.9 1.6 %collective-permute-done.15.left = f32[3,3,8,128]{3,2,1,0:T(8,128)S(1)} collective-permute-done((f32[3,3,8,128]{3,2,1,0:T(8,128)S(1)}, f32[3,3,8,128]{3,2,1,0:T(8,128)S(1)}, u32[]{:S(2)}, u32[]{:S(2)}) %collective-permute-start.15) | collective-permute-done | bytes 36896 | tf_op jit(solution)/shard_map/ppermute | solution.py:305
  61.0 3.0 %collective-permute-start.16 = (f32[3,3,8,128]{3,2,1,0:T(8,128)S(1)}, f32[3,3,8,128]{3,2,1,0:T(8,128)S(1)}, u32[]{:S(2)}, u32[]{:S(2)}) collective-permute-start(f32[3,3,8,128]{3,2,1,0:T(8,128)S(1)} %get-tuple-element.44.own.rest_11_), channel_id=1, source_target_pairs={{1,0},{2,1},{3,2},{4,3},{5,4},{6,5},{7,6},{8,7},{9,8},{10,9},{11,1... | collective-permute-start | bytes 110600 | tf_op jit(solution)/shard_map/ppermute | solution.py:304
  64.0 1.6 %collective-permute-done.17.left = f32[3,3,8,128]{3,2,1,0:T(8,128)S(1)} collective-permute-done((f32[3,3,8,128]{3,2,1,0:T(8,128)S(1)}, f32[3,3,8,128]{3,2,1,0:T(8,128)S(1)}, u32[]{:S(2)}, u32[]{:S(2)}) %collective-permute-start.17) | collective-permute-done | bytes 36896 | tf_op jit(solution)/shard_map/ppermute | solution.py:305
  66.1 3.0 %collective-permute-start.18 = (f32[1,3,8,128]{3,2,1,0:T(8,128)S(1)}, f32[1,3,8,128]{3,2,1,0:T(8,128)S(1)}, u32[]{:S(2)}, u32[]{:S(2)}) collective-permute-start(f32[1,3,8,128]{3,2,1,0:T(8,128)S(1)} %get-tuple-element.47.below), channel_id=1, source_target_pairs={{1,0},{2,1},{3,2},{4,3},{5,4},{6,5},{7,6},{8,7},{9,8},{10,9},{11,1... | collective-permute-start | bytes 36872 | tf_op jit(solution)/shard_map/ppermute | solution.py:304
  69.2 1.2 %collective-permute-done.19.rest_1_ = f32[1,3,8,128]{3,2,1,0:T(8,128)S(1)} collective-permute-done((f32[1,3,8,128]{3,2,1,0:T(8,128)S(1)}, f32[1,3,8,128]{3,2,1,0:T(8,128)S(1)}, u32[]{:S(2)}, u32[]{:S(2)}) %collective-permute-start.19) | collective-permute-done | bytes 12320 | tf_op jit(solution)/shard_map/ppermute | solution.py:305
  70.7 12.0 %all_to_all.11.sent = f32[16,3,8,128]{3,2,1,0:T(8,128)S(1)} all-to-all(f32[16,3,8,128]{3,2,1,0:T(8,128)S(1)} %shard_map.48), channel_id=1, replica_groups=mesh['tm'=16,'space'=32] {'tm'}, dimensions={0} | all-to-all | bytes 393216 | tf_op jit(solution)/shard_map/all_to_all | solution.py:356
  82.7 0.8 shard_map.49
  (35 shorter events, 5.0 us)
Async XLA Ops:
  0.0 14.7 %collective-permute-start.3 = (f32[3,2,16,512]{3,2,1,0:T(8,128)}, f32[3,2,16,512]{3,2,1,0:T(8,128)S(1)}, u32[]{:S(2)}, u32[]{:S(2)}) collective-permute-start(f32[3,2,16,512]{3,2,1,0:T(8,128)} %bitcast.2), channel_id=1, source_target_pairs={{0,1},{1,2},{2,3},{3,4},{4,5},{5,6},{6,7},{7,8},{8,9},{9,10},{10,1... | collective-permute-start | bytes 589832 | tf_op jit(solution)/shard_map/ppermute | solution.py:305
  0.0 14.7 %collective-permute-start = (f32[3,2,16,512]{3,2,1,0:T(8,128)}, f32[3,2,16,512]{3,2,1,0:T(8,128)S(1)}, u32[]{:S(2)}, u32[]{:S(2)}) collective-permute-start(f32[3,2,16,512]{3,2,1,0:T(8,128)} %bitcast.3), channel_id=1, source_target_pairs={{1,0},{2,1},{3,2},{4,3},{5,4},{6,5},{7,6},{8,7},{9,8},{10,9},{11,1... | collective-permute-start | bytes 589832 | tf_op jit(solution)/shard_map/ppermute | solution.py:304
  8.9 4.2 %collective-permute-start.2 = (f32[2,16,512]{2,1,0:T(8,128)}, f32[2,16,512]{2,1,0:T(8,128)S(1)}, u32[]{:S(2)}, u32[]{:S(2)}) collective-permute-start(f32[2,16,512]{2,1,0:T(8,128)} %param.4), channel_id=1, source_target_pairs={{1,0},{2,1},{3,2},{4,3},{5,4},{6,5},{7,6},{8,7},{9,8},{10,9},{11,1... | collective-permute-start | bytes 196616 | tf_op jit(solution)/shard_map/ppermute | solution.py:304
  9.6 5.1 %collective-permute-start.1 = (f32[2,16,512]{2,1,0:T(8,128)}, f32[2,16,512]{2,1,0:T(8,128)S(1)}, u32[]{:S(2)}, u32[]{:S(2)}) collective-permute-start(f32[2,16,512]{2,1,0:T(8,128)} %param.4), channel_id=1, source_target_pairs={{0,1},{1,2},{2,3},{3,4},{4,5},{5,6},{6,7},{7,8},{8,9},{9,10},{10,1... | collective-permute-start | bytes 196616 | tf_op jit(solution)/shard_map/ppermute | solution.py:305
  9.6 1.0 %copy-start = (f32[3]{0:T(128)S(1)}, f32[3]{0:T(128)}, u32[]{:S(2)}) copy-start(f32[3]{0:T(128)} %applied.1) | copy-start | bytes 40
  30.5 4.7 %collective-permute-start.5 = (f32[2,2,3,8,128]{4,3,2,1,0:T(8,128)S(1)}, f32[2,2,3,8,128]{4,3,2,1,0:T(8,128)S(1)}, u32[]{:S(2)}, u32[]{:S(2)}) collective-permute-start(f32[2,2,3,8,128]{4,3,2,1,0:T(8,128)S(1)} %slice.4.own), channel_id=1, source_target_pairs={{0,1},{1,2},{2,3},{3,4},{4,5},{5,6},{6,7},{7,8},{8,9},{9,10},{10,1... | collective-permute-start | bytes 147464 | tf_op jit(solution)/shard_map/ppermute | solution.py:305
  30.5 4.7 %collective-permute-start.4 = (f32[2,2,3,8,128]{4,3,2,1,0:T(8,128)S(1)}, f32[2,2,3,8,128]{4,3,2,1,0:T(8,128)S(1)}, u32[]{:S(2)}, u32[]{:S(2)}) collective-permute-start(f32[2,2,3,8,128]{4,3,2,1,0:T(8,128)S(1)} %slice.4.own), channel_id=1, source_target_pairs={{1,0},{2,1},{3,2},{4,3},{5,4},{6,5},{7,6},{8,7},{9,8},{10,9},{11,1... | collective-permute-start | bytes 147464 | tf_op jit(solution)/shard_map/ppermute | solution.py:304
  35.7 4.6 %collective-permute-start.7 = (f32[3,3,8,128]{3,2,1,0:T(8,128)S(1)}, f32[3,3,8,128]{3,2,1,0:T(8,128)S(1)}, u32[]{:S(2)}, u32[]{:S(2)}) collective-permute-start(f32[3,3,8,128]{3,2,1,0:T(8,128)S(1)} %get-tuple-element.35), channel_id=1, source_target_pairs={{0,1},{1,2},{2,3},{3,4},{4,5},{5,6},{6,7},{7,8},{8,9},{9,10},{10,1... | collective-permute-start | bytes 110600 | tf_op jit(solution)/shard_map/ppermute | solution.py:305
  35.7 4.6 %collective-permute-start.6 = (f32[3,3,8,128]{3,2,1,0:T(8,128)S(1)}, f32[3,3,8,128]{3,2,1,0:T(8,128)S(1)}, u32[]{:S(2)}, u32[]{:S(2)}) collective-permute-start(f32[3,3,8,128]{3,2,1,0:T(8,128)S(1)} %get-tuple-element.34.own.rest_1_), channel_id=1, source_target_pairs={{1,0},{2,1},{3,2},{4,3},{5,4},{6,5},{7,6},{8,7},{9,8},{10,9},{11,1... | collective-permute-start | bytes 110600 | tf_op jit(solution)/shard_map/ppermute | solution.py:304
  40.7 4.6 %collective-permute-start.9 = (f32[3,3,8,128]{3,2,1,0:T(8,128)S(1)}, f32[3,3,8,128]{3,2,1,0:T(8,128)S(1)}, u32[]{:S(2)}, u32[]{:S(2)}) collective-permute-start(f32[3,3,8,128]{3,2,1,0:T(8,128)S(1)} %get-tuple-element.37), channel_id=1, source_target_pairs={{0,1},{1,2},{2,3},{3,4},{4,5},{5,6},{6,7},{7,8},{8,9},{9,10},{10,1... | collective-permute-start | bytes 110600 | tf_op jit(solution)/shard_map/ppermute | solution.py:305
  40.8 4.6 %collective-permute-start.8 = (f32[3,3,8,128]{3,2,1,0:T(8,128)S(1)}, f32[3,3,8,128]{3,2,1,0:T(8,128)S(1)}, u32[]{:S(2)}, u32[]{:S(2)}) collective-permute-start(f32[3,3,8,128]{3,2,1,0:T(8,128)S(1)} %get-tuple-element.36.own.rest_3_), channel_id=1, source_target_pairs={{1,0},{2,1},{3,2},{4,3},{5,4},{6,5},{7,6},{8,7},{9,8},{10,9},{11,1... | collective-permute-start | bytes 110600 | tf_op jit(solution)/shard_map/ppermute | solution.py:304
  45.8 4.6 %collective-permute-start.11 = (f32[3,3,8,128]{3,2,1,0:T(8,128)S(1)}, f32[3,3,8,128]{3,2,1,0:T(8,128)S(1)}, u32[]{:S(2)}, u32[]{:S(2)}) collective-permute-start(f32[3,3,8,128]{3,2,1,0:T(8,128)S(1)} %get-tuple-element.39), channel_id=1, source_target_pairs={{0,1},{1,2},{2,3},{3,4},{4,5},{5,6},{6,7},{7,8},{8,9},{9,10},{10,1... | collective-permute-start | bytes 110600 | tf_op jit(solution)/shard_map/ppermute | solution.py:305
  45.8 4.6 %collective-permute-start.10 = (f32[3,3,8,128]{3,2,1,0:T(8,128)S(1)}, f32[3,3,8,128]{3,2,1,0:T(8,128)S(1)}, u32[]{:S(2)}, u32[]{:S(2)}) collective-permute-start(f32[3,3,8,128]{3,2,1,0:T(8,128)S(1)} %get-tuple-element.38.own.rest_5_), channel_id=1, source_target_pairs={{1,0},{2,1},{3,2},{4,3},{5,4},{6,5},{7,6},{8,7},{9,8},{10,9},{11,1... | collective-permute-start | bytes 110600 | tf_op jit(solution)/shard_map/ppermute | solution.py:304
  50.9 4.6 %collective-permute-start.13 = (f32[3,3,8,128]{3,2,1,0:T(8,128)S(1)}, f32[3,3,8,128]{3,2,1,0:T(8,128)S(1)}, u32[]{:S(2)}, u32[]{:S(2)}) collective-permute-start(f32[3,3,8,128]{3,2,1,0:T(8,128)S(1)} %get-tuple-element.41), channel_id=1, source_target_pairs={{0,1},{1,2},{2,3},{3,4},{4,5},{5,6},{6,7},{7,8},{8,9},{9,10},{10,1... | collective-permute-start | bytes 110600 | tf_op jit(solution)/shard_map/ppermute | solution.py:305
  50.9 4.6 %collective-permute-start.12 = (f32[3,3,8,128]{3,2,1,0:T(8,128)S(1)}, f32[3,3,8,128]{3,2,1,0:T(8,128)S(1)}, u32[]{:S(2)}, u32[]{:S(2)}) collective-permute-start(f32[3,3,8,128]{3,2,1,0:T(8,128)S(1)} %get-tuple-element.40.own.rest_7_), channel_id=1, source_target_pairs={{1,0},{2,1},{3,2},{4,3},{5,4},{6,5},{7,6},{8,7},{9,8},{10,9},{11,1... | collective-permute-start | bytes 110600 | tf_op jit(solution)/shard_map/ppermute | solution.py:304
  55.9 4.6 %collective-permute-start.15 = (f32[3,3,8,128]{3,2,1,0:T(8,128)S(1)}, f32[3,3,8,128]{3,2,1,0:T(8,128)S(1)}, u32[]{:S(2)}, u32[]{:S(2)}) collective-permute-start(f32[3,3,8,128]{3,2,1,0:T(8,128)S(1)} %get-tuple-element.43), channel_id=1, source_target_pairs={{0,1},{1,2},{2,3},{3,4},{4,5},{5,6},{6,7},{7,8},{8,9},{9,10},{10,1... | collective-permute-start | bytes 110600 | tf_op jit(solution)/shard_map/ppermute | solution.py:305
  55.9 4.6 %collective-permute-start.14 = (f32[3,3,8,128]{3,2,1,0:T(8,128)S(1)}, f32[3,3,8,128]{3,2,1,0:T(8,128)S(1)}, u32[]{:S(2)}, u32[]{:S(2)}) collective-permute-start(f32[3,3,8,128]{3,2,1,0:T(8,128)S(1)} %get-tuple-element.42.own.rest_9_), channel_id=1, source_target_pairs={{1,0},{2,1},{3,2},{4,3},{5,4},{6,5},{7,6},{8,7},{9,8},{10,9},{11,1... | collective-permute-start | bytes 110600 | tf_op jit(solution)/shard_map/ppermute | solution.py:304
  61.0 4.6 %collective-permute-start.17 = (f32[3,3,8,128]{3,2,1,0:T(8,128)S(1)}, f32[3,3,8,128]{3,2,1,0:T(8,128)S(1)}, u32[]{:S(2)}, u32[]{:S(2)}) collective-permute-start(f32[3,3,8,128]{3,2,1,0:T(8,128)S(1)} %get-tuple-element.45), channel_id=1, source_target_pairs={{0,1},{1,2},{2,3},{3,4},{4,5},{5,6},{6,7},{7,8},{8,9},{9,10},{10,1... | collective-permute-start | bytes 110600 | tf_op jit(solution)/shard_map/ppermute | solution.py:305
  61.0 4.6 %collective-permute-start.16 = (f32[3,3,8,128]{3,2,1,0:T(8,128)S(1)}, f32[3,3,8,128]{3,2,1,0:T(8,128)S(1)}, u32[]{:S(2)}, u32[]{:S(2)}) collective-permute-start(f32[3,3,8,128]{3,2,1,0:T(8,128)S(1)} %get-tuple-element.44.own.rest_11_), channel_id=1, source_target_pairs={{1,0},{2,1},{3,2},{4,3},{5,4},{6,5},{7,6},{8,7},{9,8},{10,9},{11,1... | collective-permute-start | bytes 110600 | tf_op jit(solution)/shard_map/ppermute | solution.py:304
  66.0 4.4 %collective-permute-start.19 = (f32[1,3,8,128]{3,2,1,0:T(8,128)S(1)}, f32[1,3,8,128]{3,2,1,0:T(8,128)S(1)}, u32[]{:S(2)}, u32[]{:S(2)}) collective-permute-start(f32[1,3,8,128]{3,2,1,0:T(8,128)S(1)} %get-tuple-element.46.above), channel_id=1, source_target_pairs={{0,1},{1,2},{2,3},{3,4},{4,5},{5,6},{6,7},{7,8},{8,9},{9,10},{10,1... | collective-permute-start | bytes 36872 | tf_op jit(solution)/shard_map/ppermute | solution.py:305
  66.1 4.4 %collective-permute-start.18 = (f32[1,3,8,128]{3,2,1,0:T(8,128)S(1)}, f32[1,3,8,128]{3,2,1,0:T(8,128)S(1)}, u32[]{:S(2)}, u32[]{:S(2)}) collective-permute-start(f32[1,3,8,128]{3,2,1,0:T(8,128)S(1)} %get-tuple-element.47.below), channel_id=1, source_target_pairs={{1,0},{2,1},{3,2},{4,3},{5,4},{6,5},{7,6},{8,7},{9,8},{10,9},{11,1... | collective-permute-start | bytes 36872 | tf_op jit(solution)/shard_map/ppermute | solution.py:304

commit v12 on v9

--- a/solution.py
+++ b/solution.py
@@ -92,7 +92,8 @@
                 at = slice(128 * q, 128 * (q + 1))
                 layers[comp, x, q] = aniso[x, :, at] if comp == 3 else spins[comp, x, :, at]
                 for parity in range(2):
-                    out[comp, x, parity, :, at] = layers[comp, x, q, pl.ds(parity, 8, stride=2), :]
+                    tile = layers[comp, x, q, pl.ds(parity, 8, stride=2), :]
+                    out[comp, x, parity, :, at] = 2.0 * tile if comp == 3 else tile
 
 
 def prepare(slab, applied, out, field, layers):
@@ -120,10 +121,10 @@
     odd = {x: [load(c, x, 1) for c in range(3)] for x in planes}
 
     def aniso_even(x):
-        return 2.0 * load(3, x, 0)
+        return load(3, x, 0)
 
     def aniso_odd(x):
-        return 2.0 * load(3, x, 1)
+        return load(3, x, 1)
 
     sides = (aniso_even, aniso_odd, applied)
     first_e, first_o = rates(even, odd, *sides, range(-2, 3), range(-1, 4))
@@ -174,7 +175,7 @@
         @pl.when(row == at)
         def _():
             for k in range(6):
-                even, odd = (tiles_of(2.0 * load(3, k - 2, parity)) for parity in range(2))
+                even, odd = (tiles_of(load(3, k - 2, parity)) for parity in range(2))
                 windows[k] = cut(even, [turn(t, 64) for t in odd], at)
 
 
@@ -233,8 +234,9 @@
         below, above = own
         spins = {-1: triple(left, 0), 0: triple(below, 0), 1: triple(above, 0), 2: triple(right, 0)}
     elif start:
-        spins = {base + k: triple(ref, 0, k) for ref, base in ((left, -2), (own, 0), (right, 2)) for k in range(2)}
-        extra = {-1: triple(left, 1, 1), 2: triple(right, 1, 0)}
+        spins = {base + k: triple(ref, k) for ref, base in ((own, 0), (right, 2)) for k in range(2)}
+        spins |= {k - 2: triple(left, 0, k) for k in range(2)}
+        extra = {-1: triple(left, 1, 1), 2: triple(right, 2)}
     else:
         spins = {base + k: triple(ref, k) for ref, base in ((left, -2), (own, 0), (right, 2)) for k in range(2)}
         extra = {-1: triple(left, 2), 2: triple(right, 2)}
@@ -338,7 +340,7 @@
     )
     (windows,) = call(window, [(7, 8, 128)], own, sides)
     corr = lax.all_to_all(payload, "tm", 0, 0, tiled=True)
-    up = down = corr[:2]
+    up, down = corr[:2], corr.reshape(-1, *corr.shape[2:])[:3]
     kept = []
     blocks = slices // 2
     for block in range(blocks - 1):

time: 83.1 us -> 83 us (level)
    ppermute x10, waiting for transfers between devices: 13.1 us -> 11.6 us  [both_sides(): return (from_above, lax.ppermute(to_above, 'space', up))]
    ppermute x10, waiting for transfers between devices: 0.24 us -> 1.71 us  [both_sides(): from_above = lax.ppermute(to_below, 'space', down)]
  transfers between devices with their start and end apart: 20 -> 20, of which waited for: 11 -> 12; matrix products, arithmetic and copies ran while one was open for 1% -> 1% of each run, Pallas kernels for 1% -> 1%
where the time goes in v12:
time: 83 us; the launch traced here: 82.9 us
  starting transfers between devices  35.7 us (43%)
  blocking collectives  26.5 us (32%)
  waiting for transfers between devices  13.4 us (16%)
  Pallas kernels  6.1 us (7%)
  other arithmetic  0.99 us (1%)
    ppermute x10, starting transfers between devices, both_sides(): from_above = lax.ppermute(to_below, 'space', down)  35.6 us
    all_to_all x1, blocking collectives, per_device(): corr = lax.all_to_all(payload, 'tm', 0, 0, tiled=True)  14.5 us
    all_to_all x1, blocking collectives, per_device(): sent = lax.all_to_all(sent, 'tm', 0, 0, tiled=True)  12 us
    ppermute x10, waiting for transfers between devices, both_sides(): return (from_above, lax.ppermute(to_above, 'space', up))  11.6 us
    pallas_call x13, Pallas kernels, call(): pl.pallas_call(kernel, out_shape=[jax.ShapeDtypeStruct(s, F32) for s in s...  6.1 us
    ppermute x10, waiting for transfers between devices, both_sides(): from_above = lax.ppermute(to_below, 'space', down)  1.71 us
  transfers between devices with their start and end apart: 20, of which 12 were waited for; matrix products, arithmetic and copies ran while one was open for 1% of the time, Pallas kernels for 1%

profile of v12, /device:TPU:2, one launch (start us, length us, event | category | flops | bytes accessed | tf_op | source)
XLA Modules:
  0.0 82.9 jit_solution(13798968715626343854)
XLA Ops:
  0.0 8.9 %collective-permute-start = (f32[3,2,16,512]{3,2,1,0:T(8,128)}, f32[3,2,16,512]{3,2,1,0:T(8,128)S(1)}, u32[]{:S(2)}, u32[]{:S(2)}) collective-permute-start(f32[3,2,16,512]{3,2,1,0:T(8,128)} %bitcast.5), channel_id=1, source_target_pairs={{1,0},{2,1},{3,2},{4,3},{5,4},{6,5},{7,6},{8,7},{9,8},{10,9},{11,1... | collective-permute-start | bytes 589832 | tf_op jit(solution)/shard_map/ppermute | solution.py:306
  8.9 3.0 %collective-permute-start.2 = (f32[2,16,512]{2,1,0:T(8,128)}, f32[2,16,512]{2,1,0:T(8,128)S(1)}, u32[]{:S(2)}, u32[]{:S(2)}) collective-permute-start(f32[2,16,512]{2,1,0:T(8,128)} %param.4), channel_id=1, source_target_pairs={{1,0},{2,1},{3,2},{4,3},{5,4},{6,5},{7,6},{8,7},{9,8},{10,9},{11,1... | collective-permute-start | bytes 196616 | tf_op jit(solution)/shard_map/ppermute | solution.py:306
  11.9 1.0 %pad_maximum_fusion.slab = f32[4,2,16,512]{3,2,1,0:T(8,128)S(1)} fusion(f32[1,2,16,512]{3,2,1,0:T(8,128)} %bitcast.7, f32[3,2,16,512]{3,2,1,0:T(8,128)} %bitcast.6), kind=kLoop, calls=%fused_computation | loop fusion | flops 65536 | bytes 524288 | tf_op jit(solution)/shard_map/concatenate | solution.py:325
  12.9 0.6 shard_map.37
  14.1 1.2 %shard_map.38 = (f32[16,2,3,8,128]{4,3,2,1,0:T(8,128)S(1)}, f32[2,4,2,2,8,512]{5,4,3,2,1,0:T(8,128)S(1)}) custom-call(f32[4,2,2,8,512]{4,3,2,1,0:T(8,128)S(1)} %get-tuple-element.30.own, f32[3,2,16,512]{3,2,1,0:T(8,128)S(1)} %collective-permute-done.right, f32[3,2,16,512]{3,2,1,0:T(8,128)S(1)} %collective-permute-done.1.left, ...), custom_call_target="tpu_custom_call" | custom-call | tf_op jit(solution)/shard_map/pallas_call | solution.py:311
  15.4 14.5 %all_to_all.10.corr.rest_2_ = f32[16,2,3,8,128]{4,3,2,1,0:T(8,128)S(1)} all-to-all(f32[16,2,3,8,128]{4,3,2,1,0:T(8,128)S(1)} %get-tuple-element.32), channel_id=1, replica_groups=mesh['tm'=16,'space'=32] {'tm'}, dimensions={0} | all-to-all | bytes 786432 | tf_op jit(solution)/shard_map/all_to_all | solution.py:342
  29.9 2.9 %collective-permute-start.4 = (f32[3,3,8,128]{3,2,1,0:T(8,128)S(1)}, f32[3,3,8,128]{3,2,1,0:T(8,128)S(1)}, u32[]{:S(2)}, u32[]{:S(2)}) collective-permute-start(f32[3,3,8,128]{3,2,1,0:T(8,128)S(1)} %slice.8.own), channel_id=1, source_target_pairs={{1,0},{2,1},{3,2},{4,3},{5,4},{6,5},{7,6},{8,7},{9,8},{10,9},{11,1... | collective-permute-start | bytes 110600 | tf_op jit(solution)/shard_map/ppermute | solution.py:306
  33.0 1.5 %collective-permute-done.4.right = f32[3,3,8,128]{3,2,1,0:T(8,128)S(1)} collective-permute-done((f32[3,3,8,128]{3,2,1,0:T(8,128)S(1)}, f32[3,3,8,128]{3,2,1,0:T(8,128)S(1)}, u32[]{:S(2)}, u32[]{:S(2)}) %collective-permute-start.4) | collective-permute-done | bytes 36896 | tf_op jit(solution)/shard_map/ppermute | solution.py:306
  35.1 2.9 %collective-permute-start.6 = (f32[3,3,8,128]{3,2,1,0:T(8,128)S(1)}, f32[3,3,8,128]{3,2,1,0:T(8,128)S(1)}, u32[]{:S(2)}, u32[]{:S(2)}) collective-permute-start(f32[3,3,8,128]{3,2,1,0:T(8,128)S(1)} %get-tuple-element.34.own.rest_1_), channel_id=1, source_target_pairs={{1,0},{2,1},{3,2},{4,3},{5,4},{6,5},{7,6},{8,7},{9,8},{10,9},{11,1... | collective-permute-start | bytes 110600 | tf_op jit(solution)/shard_map/ppermute | solution.py:306
  38.0 1.6 %collective-permute-done.7.left = f32[3,3,8,128]{3,2,1,0:T(8,128)S(1)} collective-permute-done((f32[3,3,8,128]{3,2,1,0:T(8,128)S(1)}, f32[3,3,8,128]{3,2,1,0:T(8,128)S(1)}, u32[]{:S(2)}, u32[]{:S(2)}) %collective-permute-start.7) | collective-permute-done | bytes 36896 | tf_op jit(solution)/shard_map/ppermute | solution.py:307
  40.1 3.0 %collective-permute-start.8 = (f32[3,3,8,128]{3,2,1,0:T(8,128)S(1)}, f32[3,3,8,128]{3,2,1,0:T(8,128)S(1)}, u32[]{:S(2)}, u32[]{:S(2)}) collective-permute-start(f32[3,3,8,128]{3,2,1,0:T(8,128)S(1)} %get-tuple-element.36.own.rest_3_), channel_id=1, source_target_pairs={{1,0},{2,1},{3,2},{4,3},{5,4},{6,5},{7,6},{8,7},{9,8},{10,9},{11,1... | collective-permute-start | bytes 110600 | tf_op jit(solution)/shard_map/ppermute | solution.py:306
  43.1 1.6 %collective-permute-done.9.left = f32[3,3,8,128]{3,2,1,0:T(8,128)S(1)} collective-permute-done((f32[3,3,8,128]{3,2,1,0:T(8,128)S(1)}, f32[3,3,8,128]{3,2,1,0:T(8,128)S(1)}, u32[]{:S(2)}, u32[]{:S(2)}) %collective-permute-start.9) | collective-permute-done | bytes 36896 | tf_op jit(solution)/shard_map/ppermute | solution.py:307
  45.2 3.0 %collective-permute-start.10 = (f32[3,3,8,128]{3,2,1,0:T(8,128)S(1)}, f32[3,3,8,128]{3,2,1,0:T(8,128)S(1)}, u32[]{:S(2)}, u32[]{:S(2)}) collective-permute-start(f32[3,3,8,128]{3,2,1,0:T(8,128)S(1)} %get-tuple-element.38.own.rest_5_), channel_id=1, source_target_pairs={{1,0},{2,1},{3,2},{4,3},{5,4},{6,5},{7,6},{8,7},{9,8},{10,9},{11,1... | collective-permute-start | bytes 110600 | tf_op jit(solution)/shard_map/ppermute | solution.py:306
  48.1 1.6 %collective-permute-done.11.left = f32[3,3,8,128]{3,2,1,0:T(8,128)S(1)} collective-permute-done((f32[3,3,8,128]{3,2,1,0:T(8,128)S(1)}, f32[3,3,8,128]{3,2,1,0:T(8,128)S(1)}, u32[]{:S(2)}, u32[]{:S(2)}) %collective-permute-start.11) | collective-permute-done | bytes 36896 | tf_op jit(solution)/shard_map/ppermute | solution.py:307
  50.2 3.0 %collective-permute-start.12 = (f32[3,3,8,128]{3,2,1,0:T(8,128)S(1)}, f32[3,3,8,128]{3,2,1,0:T(8,128)S(1)}, u32[]{:S(2)}, u32[]{:S(2)}) collective-permute-start(f32[3,3,8,128]{3,2,1,0:T(8,128)S(1)} %get-tuple-element.40.own.rest_7_), channel_id=1, source_target_pairs={{1,0},{2,1},{3,2},{4,3},{5,4},{6,5},{7,6},{8,7},{9,8},{10,9},{11,1... | collective-permute-start | bytes 110600 | tf_op jit(solution)/shard_map/ppermute | solution.py:306
  53.2 1.6 %collective-permute-done.13.left = f32[3,3,8,128]{3,2,1,0:T(8,128)S(1)} collective-permute-done((f32[3,3,8,128]{3,2,1,0:T(8,128)S(1)}, f32[3,3,8,128]{3,2,1,0:T(8,128)S(1)}, u32[]{:S(2)}, u32[]{:S(2)}) %collective-permute-start.13) | collective-permute-done | bytes 36896 | tf_op jit(solution)/shard_map/ppermute | solution.py:307
  55.3 3.0 %collective-permute-start.14 = (f32[3,3,8,128]{3,2,1,0:T(8,128)S(1)}, f32[3,3,8,128]{3,2,1,0:T(8,128)S(1)}, u32[]{:S(2)}, u32[]{:S(2)}) collective-permute-start(f32[3,3,8,128]{3,2,1,0:T(8,128)S(1)} %get-tuple-element.42.own.rest_9_), channel_id=1, source_target_pairs={{1,0},{2,1},{3,2},{4,3},{5,4},{6,5},{7,6},{8,7},{9,8},{10,9},{11,1... | collective-permute-start | bytes 110600 | tf_op jit(solution)/shard_map/ppermute | solution.py:306
  58.3 1.6 %collective-permute-done.15.left = f32[3,3,8,128]{3,2,1,0:T(8,128)S(1)} collective-permute-done((f32[3,3,8,128]{3,2,1,0:T(8,128)S(1)}, f32[3,3,8,128]{3,2,1,0:T(8,128)S(1)}, u32[]{:S(2)}, u32[]{:S(2)}) %collective-permute-start.15) | collective-permute-done | bytes 36896 | tf_op jit(solution)/shard_map/ppermute | solution.py:307
  60.4 3.0 %collective-permute-start.16 = (f32[3,3,8,128]{3,2,1,0:T(8,128)S(1)}, f32[3,3,8,128]{3,2,1,0:T(8,128)S(1)}, u32[]{:S(2)}, u32[]{:S(2)}) collective-permute-start(f32[3,3,8,128]{3,2,1,0:T(8,128)S(1)} %get-tuple-element.44.own.rest_11_), channel_id=1, source_target_pairs={{1,0},{2,1},{3,2},{4,3},{5,4},{6,5},{7,6},{8,7},{9,8},{10,9},{11,1... | collective-permute-start | bytes 110600 | tf_op jit(solution)/shard_map/ppermute | solution.py:306
  63.3 1.6 %collective-permute-done.17.left = f32[3,3,8,128]{3,2,1,0:T(8,128)S(1)} collective-permute-done((f32[3,3,8,128]{3,2,1,0:T(8,128)S(1)}, f32[3,3,8,128]{3,2,1,0:T(8,128)S(1)}, u32[]{:S(2)}, u32[]{:S(2)}) %collective-permute-start.17) | collective-permute-done | bytes 36896 | tf_op jit(solution)/shard_map/ppermute | solution.py:307
  65.4 3.0 %collective-permute-start.18 = (f32[1,3,8,128]{3,2,1,0:T(8,128)S(1)}, f32[1,3,8,128]{3,2,1,0:T(8,128)S(1)}, u32[]{:S(2)}, u32[]{:S(2)}) collective-permute-start(f32[1,3,8,128]{3,2,1,0:T(8,128)S(1)} %get-tuple-element.47.below), channel_id=1, source_target_pairs={{1,0},{2,1},{3,2},{4,3},{5,4},{6,5},{7,6},{8,7},{9,8},{10,9},{11,1... | collective-permute-start | bytes 36872 | tf_op jit(solution)/shard_map/ppermute | solution.py:306
  68.5 1.2 %collective-permute-done.19.rest_1_ = f32[1,3,8,128]{3,2,1,0:T(8,128)S(1)} collective-permute-done((f32[1,3,8,128]{3,2,1,0:T(8,128)S(1)}, f32[1,3,8,128]{3,2,1,0:T(8,128)S(1)}, u32[]{:S(2)}, u32[]{:S(2)}) %collective-permute-start.19) | collective-permute-done | bytes 12320 | tf_op jit(solution)/shard_map/ppermute | solution.py:307
  70.1 12.0 %all_to_all.11.sent = f32[16,3,8,128]{3,2,1,0:T(8,128)S(1)} all-to-all(f32[16,3,8,128]{3,2,1,0:T(8,128)S(1)} %shard_map.48), channel_id=1, replica_groups=mesh['tm'=16,'space'=32] {'tm'}, dimensions={0} | all-to-all | bytes 393216 | tf_op jit(solution)/shard_map/all_to_all | solution.py:358
  82.0 0.8 shard_map.49
  (36 shorter events, 4.5 us)
Async XLA Ops:
  0.0 14.1 %collective-permute-start.1 = (f32[3,2,16,512]{3,2,1,0:T(8,128)}, f32[3,2,16,512]{3,2,1,0:T(8,128)S(1)}, u32[]{:S(2)}, u32[]{:S(2)}) collective-permute-start(f32[3,2,16,512]{3,2,1,0:T(8,128)} %bitcast.4), channel_id=1, source_target_pairs={{0,1},{1,2},{2,3},{3,4},{4,5},{5,6},{6,7},{7,8},{8,9},{9,10},{10,1... | collective-permute-start | bytes 589832 | tf_op jit(solution)/shard_map/ppermute | solution.py:307
  0.0 14.1 %collective-permute-start = (f32[3,2,16,512]{3,2,1,0:T(8,128)}, f32[3,2,16,512]{3,2,1,0:T(8,128)S(1)}, u32[]{:S(2)}, u32[]{:S(2)}) collective-permute-start(f32[3,2,16,512]{3,2,1,0:T(8,128)} %bitcast.5), channel_id=1, source_target_pairs={{1,0},{2,1},{3,2},{4,3},{5,4},{6,5},{7,6},{8,7},{9,8},{10,9},{11,1... | collective-permute-start | bytes 589832 | tf_op jit(solution)/shard_map/ppermute | solution.py:306
  8.9 5.1 %collective-permute-start.3 = (f32[2,16,512]{2,1,0:T(8,128)}, f32[2,16,512]{2,1,0:T(8,128)S(1)}, u32[]{:S(2)}, u32[]{:S(2)}) collective-permute-start(f32[2,16,512]{2,1,0:T(8,128)} %param.4), channel_id=1, source_target_pairs={{0,1},{1,2},{2,3},{3,4},{4,5},{5,6},{6,7},{7,8},{8,9},{9,10},{10,1... | collective-permute-start | bytes 196616 | tf_op jit(solution)/shard_map/ppermute | solution.py:307
  8.9 5.2 %collective-permute-start.2 = (f32[2,16,512]{2,1,0:T(8,128)}, f32[2,16,512]{2,1,0:T(8,128)S(1)}, u32[]{:S(2)}, u32[]{:S(2)}) collective-permute-start(f32[2,16,512]{2,1,0:T(8,128)} %param.4), channel_id=1, source_target_pairs={{1,0},{2,1},{3,2},{4,3},{5,4},{6,5},{7,6},{8,7},{9,8},{10,9},{11,1... | collective-permute-start | bytes 196616 | tf_op jit(solution)/shard_map/ppermute | solution.py:306
  11.9 1.0 %copy-start = (f32[3]{0:T(128)S(1)}, f32[3]{0:T(128)}, u32[]{:S(2)}) copy-start(f32[3]{0:T(128)} %applied.1) | copy-start | bytes 40
  29.9 4.7 %collective-permute-start.5 = (f32[2,2,3,8,128]{4,3,2,1,0:T(8,128)S(1)}, f32[2,2,3,8,128]{4,3,2,1,0:T(8,128)S(1)}, u32[]{:S(2)}, u32[]{:S(2)}) collective-permute-start(f32[2,2,3,8,128]{4,3,2,1,0:T(8,128)S(1)} %slice.9), channel_id=1, source_target_pairs={{0,1},{1,2},{2,3},{3,4},{4,5},{5,6},{6,7},{7,8},{8,9},{9,10},{10,1... | collective-permute-start | bytes 147464 | tf_op jit(solution)/shard_map/ppermute | solution.py:307
  29.9 4.6 %collective-permute-start.4 = (f32[3,3,8,128]{3,2,1,0:T(8,128)S(1)}, f32[3,3,8,128]{3,2,1,0:T(8,128)S(1)}, u32[]{:S(2)}, u32[]{:S(2)}) collective-permute-start(f32[3,3,8,128]{3,2,1,0:T(8,128)S(1)} %slice.8.own), channel_id=1, source_target_pairs={{1,0},{2,1},{3,2},{4,3},{5,4},{6,5},{7,6},{8,7},{9,8},{10,9},{11,1... | collective-permute-start | bytes 110600 | tf_op jit(solution)/shard_map/ppermute | solution.py:306
  35.0 4.6 %collective-permute-start.7 = (f32[3,3,8,128]{3,2,1,0:T(8,128)S(1)}, f32[3,3,8,128]{3,2,1,0:T(8,128)S(1)}, u32[]{:S(2)}, u32[]{:S(2)}) collective-permute-start(f32[3,3,8,128]{3,2,1,0:T(8,128)S(1)} %get-tuple-element.35), channel_id=1, source_target_pairs={{0,1},{1,2},{2,3},{3,4},{4,5},{5,6},{6,7},{7,8},{8,9},{9,10},{10,1... | collective-permute-start | bytes 110600 | tf_op jit(solution)/shard_map/ppermute | solution.py:307
  35.1 4.6 %collective-permute-start.6 = (f32[3,3,8,128]{3,2,1,0:T(8,128)S(1)}, f32[3,3,8,128]{3,2,1,0:T(8,128)S(1)}, u32[]{:S(2)}, u32[]{:S(2)}) collective-permute-start(f32[3,3,8,128]{3,2,1,0:T(8,128)S(1)} %get-tuple-element.34.own.rest_1_), channel_id=1, source_target_pairs={{1,0},{2,1},{3,2},{4,3},{5,4},{6,5},{7,6},{8,7},{9,8},{10,9},{11,1... | collective-permute-start | bytes 110600 | tf_op jit(solution)/shard_map/ppermute | solution.py:306
  40.1 4.6 %collective-permute-start.9 = (f32[3,3,8,128]{3,2,1,0:T(8,128)S(1)}, f32[3,3,8,128]{3,2,1,0:T(8,128)S(1)}, u32[]{:S(2)}, u32[]{:S(2)}) collective-permute-start(f32[3,3,8,128]{3,2,1,0:T(8,128)S(1)} %get-tuple-element.37), channel_id=1, source_target_pairs={{0,1},{1,2},{2,3},{3,4},{4,5},{5,6},{6,7},{7,8},{8,9},{9,10},{10,1... | collective-permute-start | bytes 110600 | tf_op jit(solution)/shard_map/ppermute | solution.py:307
  40.1 4.6 %collective-permute-start.8 = (f32[3,3,8,128]{3,2,1,0:T(8,128)S(1)}, f32[3,3,8,128]{3,2,1,0:T(8,128)S(1)}, u32[]{:S(2)}, u32[]{:S(2)}) collective-permute-start(f32[3,3,8,128]{3,2,1,0:T(8,128)S(1)} %get-tuple-element.36.own.rest_3_), channel_id=1, source_target_pairs={{1,0},{2,1},{3,2},{4,3},{5,4},{6,5},{7,6},{8,7},{9,8},{10,9},{11,1... | collective-permute-start | bytes 110600 | tf_op jit(solution)/shard_map/ppermute | solution.py:306
  45.1 4.6 %collective-permute-start.11 = (f32[3,3,8,128]{3,2,1,0:T(8,128)S(1)}, f32[3,3,8,128]{3,2,1,0:T(8,128)S(1)}, u32[]{:S(2)}, u32[]{:S(2)}) collective-permute-start(f32[3,3,8,128]{3,2,1,0:T(8,128)S(1)} %get-tuple-element.39), channel_id=1, source_target_pairs={{0,1},{1,2},{2,3},{3,4},{4,5},{5,6},{6,7},{7,8},{8,9},{9,10},{10,1... | collective-permute-start | bytes 110600 | tf_op jit(solution)/shard_map/ppermute | solution.py:307
  45.2 4.6 %collective-permute-start.10 = (f32[3,3,8,128]{3,2,1,0:T(8,128)S(1)}, f32[3,3,8,128]{3,2,1,0:T(8,128)S(1)}, u32[]{:S(2)}, u32[]{:S(2)}) collective-permute-start(f32[3,3,8,128]{3,2,1,0:T(8,128)S(1)} %get-tuple-element.38.own.rest_5_), channel_id=1, source_target_pairs={{1,0},{2,1},{3,2},{4,3},{5,4},{6,5},{7,6},{8,7},{9,8},{10,9},{11,1... | collective-permute-start | bytes 110600 | tf_op jit(solution)/shard_map/ppermute | solution.py:306
  50.2 4.6 %collective-permute-start.13 = (f32[3,3,8,128]{3,2,1,0:T(8,128)S(1)}, f32[3,3,8,128]{3,2,1,0:T(8,128)S(1)}, u32[]{:S(2)}, u32[]{:S(2)}) collective-permute-start(f32[3,3,8,128]{3,2,1,0:T(8,128)S(1)} %get-tuple-element.41), channel_id=1, source_target_pairs={{0,1},{1,2},{2,3},{3,4},{4,5},{5,6},{6,7},{7,8},{8,9},{9,10},{10,1... | collective-permute-start | bytes 110600 | tf_op jit(solution)/shard_map/ppermute | solution.py:307
  50.2 4.6 %collective-permute-start.12 = (f32[3,3,8,128]{3,2,1,0:T(8,128)S(1)}, f32[3,3,8,128]{3,2,1,0:T(8,128)S(1)}, u32[]{:S(2)}, u32[]{:S(2)}) collective-permute-start(f32[3,3,8,128]{3,2,1,0:T(8,128)S(1)} %get-tuple-element.40.own.rest_7_), channel_id=1, source_target_pairs={{1,0},{2,1},{3,2},{4,3},{5,4},{6,5},{7,6},{8,7},{9,8},{10,9},{11,1... | collective-permute-start | bytes 110600 | tf_op jit(solution)/shard_map/ppermute | solution.py:306
  55.3 4.6 %collective-permute-start.15 = (f32[3,3,8,128]{3,2,1,0:T(8,128)S(1)}, f32[3,3,8,128]{3,2,1,0:T(8,128)S(1)}, u32[]{:S(2)}, u32[]{:S(2)}) collective-permute-start(f32[3,3,8,128]{3,2,1,0:T(8,128)S(1)} %get-tuple-element.43), channel_id=1, source_target_pairs={{0,1},{1,2},{2,3},{3,4},{4,5},{5,6},{6,7},{7,8},{8,9},{9,10},{10,1... | collective-permute-start | bytes 110600 | tf_op jit(solution)/shard_map/ppermute | solution.py:307
  55.3 4.6 %collective-permute-start.14 = (f32[3,3,8,128]{3,2,1,0:T(8,128)S(1)}, f32[3,3,8,128]{3,2,1,0:T(8,128)S(1)}, u32[]{:S(2)}, u32[]{:S(2)}) collective-permute-start(f32[3,3,8,128]{3,2,1,0:T(8,128)S(1)} %get-tuple-element.42.own.rest_9_), channel_id=1, source_target_pairs={{1,0},{2,1},{3,2},{4,3},{5,4},{6,5},{7,6},{8,7},{9,8},{10,9},{11,1... | collective-permute-start | bytes 110600 | tf_op jit(solution)/shard_map/ppermute | solution.py:306
  60.3 4.6 %collective-permute-start.17 = (f32[3,3,8,128]{3,2,1,0:T(8,128)S(1)}, f32[3,3,8,128]{3,2,1,0:T(8,128)S(1)}, u32[]{:S(2)}, u32[]{:S(2)}) collective-permute-start(f32[3,3,8,128]{3,2,1,0:T(8,128)S(1)} %get-tuple-element.45), channel_id=1, source_target_pairs={{0,1},{1,2},{2,3},{3,4},{4,5},{5,6},{6,7},{7,8},{8,9},{9,10},{10,1... | collective-permute-start | bytes 110600 | tf_op jit(solution)/shard_map/ppermute | solution.py:307
  60.4 4.6 %collective-permute-start.16 = (f32[3,3,8,128]{3,2,1,0:T(8,128)S(1)}, f32[3,3,8,128]{3,2,1,0:T(8,128)S(1)}, u32[]{:S(2)}, u32[]{:S(2)}) collective-permute-start(f32[3,3,8,128]{3,2,1,0:T(8,128)S(1)} %get-tuple-element.44.own.rest_11_), channel_id=1, source_target_pairs={{1,0},{2,1},{3,2},{4,3},{5,4},{6,5},{7,6},{8,7},{9,8},{10,9},{11,1... | collective-permute-start | bytes 110600 | tf_op jit(solution)/shard_map/ppermute | solution.py:306
  65.4 4.4 %collective-permute-start.19 = (f32[1,3,8,128]{3,2,1,0:T(8,128)S(1)}, f32[1,3,8,128]{3,2,1,0:T(8,128)S(1)}, u32[]{:S(2)}, u32[]{:S(2)}) collective-permute-start(f32[1,3,8,128]{3,2,1,0:T(8,128)S(1)} %get-tuple-element.46.above), channel_id=1, source_target_pairs={{0,1},{1,2},{2,3},{3,4},{4,5},{5,6},{6,7},{7,8},{8,9},{9,10},{10,1... | collective-permute-start | bytes 36872 | tf_op jit(solution)/shard_map/ppermute | solution.py:307
  65.4 4.4 %collective-permute-start.18 = (f32[1,3,8,128]{3,2,1,0:T(8,128)S(1)}, f32[1,3,8,128]{3,2,1,0:T(8,128)S(1)}, u32[]{:S(2)}, u32[]{:S(2)}) collective-permute-start(f32[1,3,8,128]{3,2,1,0:T(8,128)S(1)} %get-tuple-element.47.below), channel_id=1, source_target_pairs={{1,0},{2,1},{3,2},{4,3},{5,4},{6,5},{7,6},{8,7},{9,8},{10,9},{11,1... | collective-permute-start | bytes 36872 | tf_op jit(solution)/shard_map/ppermute | solution.py:306

commit v13 on v12

--- a/solution.py
+++ b/solution.py
@@ -85,49 +85,65 @@
     return pltpu.roll(x, by, axis=1) if by else x
 
 
-def by_parity(spins, aniso, out, layers):
+def by_parity(planes, out, layers, scale=None):
+    for x in range(2):
+        for q in range(layers.shape[1]):
+            at = slice(128 * q, 128 * (q + 1))
+            layers[x, q] = planes[x, :, at]
+            for parity in range(2):
+                tile = layers[x, q, pl.ds(parity, 8, stride=2), :]
+                out[x, parity, :, at] = tile if scale is None else scale * tile
+
+
+def prepare(slab, applied, out, field, layers):
     for comp in range(4):
-        for x in range(2):
-            for q in range(layers.shape[2]):
-                at = slice(128 * q, 128 * (q + 1))
-                layers[comp, x, q] = aniso[x, :, at] if comp == 3 else spins[comp, x, :, at]
-                for parity in range(2):
-                    tile = layers[comp, x, q, pl.ds(parity, 8, stride=2), :]
-                    out[comp, x, parity, :, at] = 2.0 * tile if comp == 3 else tile
-
-
-def prepare(slab, applied, out, field, layers):
-    by_parity(slab, slab.at[3], out, layers)
+        by_parity(slab.at[comp], out.at[comp], layers.at[comp], 2.0 if comp == 3 else None)
     for c in range(3):
         field[c] = jnp.full(field.shape[1:], applied[c], F32)
 
 
-def beside(own, sides):
+def beside(own, sides, first=0):
     def load(comp, plane, parity):
-        ref, at = (sides.at[0], plane + 2) if plane < 0 else (own, plane) if plane < 2 else (sides.at[1], plane - 2)
-        return ref[comp, at, parity]
+        if 0 <= plane < 2:
+            return own[comp, plane, parity]
+        return sides[int(plane > 1), comp - first, plane % 2, parity]
 
     return load
 
 
-def prologue(own, right, left, right_a, left_a, field, payload, sides, layers):
-    by_parity(left, left_a, sides.at[0], layers.at[0])
-    by_parity(right, right_a, sides.at[1], layers.at[1])
+def first_sums(own, right, left, sides, near, layers):
+    for side, spins in enumerate((left, right)):
+        for comp in range(3):
+            by_parity(spins.at[comp], sides.at[side, comp], layers.at[side, comp])
     load = beside(own, sides)
-    applied = [jnp.concatenate([field[c]] * layers.shape[3], axis=1) for c in range(3)]
+    even = {x: [load(c, x, 0) for c in range(3)] for x in range(-2, 4)}
+    odd = {x: [load(c, x, 1) for c in range(3)] for x in range(-2, 4)}
+    for k in range(5):
+        for c, value in enumerate(near_even(odd[k - 2], odd[k - 1])):
+            near[0, k, c] = value
+        for c, value in enumerate(near_odd(even[k - 2], even[k - 1])):
+            near[1, k, c] = value
+
+
+def prologue(own, sides, near, right_a, left_a, field, payload, aniso, layers):
+    by_parity(left_a, aniso.at[0, 0], layers.at[0], 2.0)
+    by_parity(right_a, aniso.at[1, 0], layers.at[1], 2.0)
+    load, load_a = beside(own, sides), beside(own, aniso, 3)
+    applied = [jnp.concatenate([field[c]] * layers.shape[2], axis=1) for c in range(3)]
 
     planes = range(-2, 4)
     even = {x: [load(c, x, 0) for c in range(3)] for x in planes}
     odd = {x: [load(c, x, 1) for c in range(3)] for x in planes}
 
     def aniso_even(x):
-        return load(3, x, 0)
+        return load_a(3, x, 0)
 
     def aniso_odd(x):
-        return load(3, x, 1)
+        return load_a(3, x, 1)
 
     sides = (aniso_even, aniso_odd, applied)
-    first_e, first_o = rates(even, odd, *sides, range(-2, 3), range(-1, 4))
+    first_e = {x: bare_rate(even[x], [near[0, x + 2, c] for c in range(3)], aniso_even(x), applied) for x in range(-2, 3)}
+    first_o = {x: bare_rate(odd[x], [near[1, x + 1, c] for c in range(3)], aniso_odd(x), applied) for x in range(-1, 4)}
     pred_e, pred_o = ahead(even, first_e, STEP), ahead(odd, first_o, STEP)
     second_e, second_o = rates(pred_e, pred_o, *sides, range(-1, 3), range(-1, 3))
     fine_e = finish(even, first_e, second_e, STEP, range(-1, 3))
@@ -166,8 +182,8 @@
     return (lax.broadcasted_iota(jnp.int32, (8, 128), 1) + 16 - 32 * (row % 4)) & 127
 
 
-def window(own, sides, windows):
-    load = beside(own, sides)
+def window(own, aniso, windows):
+    load = beside(own, aniso, 3)
     row = lax.axis_index("tm")
     windows[6] = logical_lane(row).astype(F32)
     for at in range(own.shape[-1] // 32):
@@ -332,13 +348,19 @@
         scratch=[layers],
         in_specs=[VMEM, pl.BlockSpec(memory_space=pltpu.SMEM)],
     )
-    payload, sides = call(
+    sides, near = call(
+        first_sums,
+        [(2, 3, 2, 2, 8, width), (2, 5, 3, 8, width)],
+        *(own, right, left),
+        scratch=[(2, *layers)],
+    )
+    payload, aniso = call(
         prologue,
-        [(slices, 2, 3, 8, 128), (2, 4, 2, 2, 8, width)],
-        *(own, right, left, right_a, left_a, field),
-        scratch=[(2, *layers)],
-    )
-    (windows,) = call(window, [(7, 8, 128)], own, sides)
+        [(slices, 2, 3, 8, 128), (2, 1, 2, 2, 8, width)],
+        *(own, sides, near, right_a, left_a, field),
+        scratch=[(2, *layers[1:])],
+    )
+    (windows,) = call(window, [(7, 8, 128)], own, aniso)
     corr = lax.all_to_all(payload, "tm", 0, 0, tiled=True)
     up, down = corr[:2], corr.reshape(-1, *corr.shape[2:])[:3]
     kept = []

time: 83 us -> 82.8 us (level)
    pallas_call x13 -> x14, Pallas kernels: 6.1 us -> 6.14 us  [call(): pl.pallas_call(kernel, out_shape=[jax.ShapeDtypeStruct(s, F32) for s in s...]
where the time goes in v13:
time: 82.8 us; the launch traced here: 82.7 us
  starting transfers between devices  35.7 us (43%)
  blocking collectives  26.5 us (32%)
  waiting for transfers between devices  13.1 us (16%)
  Pallas kernels  6.14 us (7%)
  other arithmetic  0.99 us (1%)
    ppermute x10, starting transfers between devices, both_sides(): from_above = lax.ppermute(to_below, 'space', down)  35.6 us
    all_to_all x1, blocking collectives, per_device(): corr = lax.all_to_all(payload, 'tm', 0, 0, tiled=True)  14.5 us
    all_to_all x1, blocking collectives, per_device(): sent = lax.all_to_all(sent, 'tm', 0, 0, tiled=True)  12 us
    ppermute x10, waiting for transfers between devices, both_sides(): return (from_above, lax.ppermute(to_above, 'space', up))  11.4 us
    pallas_call x14, Pallas kernels, call(): pl.pallas_call(kernel, out_shape=[jax.ShapeDtypeStruct(s, F32) for s in s...  6.14 us
    ppermute x10, waiting for transfers between devices, both_sides(): from_above = lax.ppermute(to_below, 'space', down)  1.71 us
  transfers between devices with their start and end apart: 20, of which 12 were waited for; matrix products, arithmetic and copies ran while one was open for 1% of the time, Pallas kernels for 1%

profile of v13, /device:TPU:2, one launch (start us, length us, event | category | flops | bytes accessed | tf_op | source)
XLA Modules:
  0.0 82.7 jit_solution(16002096311737212331)
XLA Ops:
  0.0 8.9 %collective-permute-start = (f32[3,2,16,512]{3,2,1,0:T(8,128)}, f32[3,2,16,512]{3,2,1,0:T(8,128)S(1)}, u32[]{:S(2)}, u32[]{:S(2)}) collective-permute-start(f32[3,2,16,512]{3,2,1,0:T(8,128)} %bitcast.5), channel_id=1, source_target_pairs={{1,0},{2,1},{3,2},{4,3},{5,4},{6,5},{7,6},{8,7},{9,8},{10,9},{11,1... | collective-permute-start | bytes 589832 | tf_op jit(solution)/shard_map/ppermute | solution.py:322
  8.9 3.0 %collective-permute-start.2 = (f32[2,16,512]{2,1,0:T(8,128)}, f32[2,16,512]{2,1,0:T(8,128)S(1)}, u32[]{:S(2)}, u32[]{:S(2)}) collective-permute-start(f32[2,16,512]{2,1,0:T(8,128)} %param.4), channel_id=1, source_target_pairs={{1,0},{2,1},{3,2},{4,3},{5,4},{6,5},{7,6},{8,7},{9,8},{10,9},{11,1... | collective-permute-start | bytes 196616 | tf_op jit(solution)/shard_map/ppermute | solution.py:322
  11.9 1.0 %pad_maximum_fusion.slab = f32[4,2,16,512]{3,2,1,0:T(8,128)S(1)} fusion(f32[1,2,16,512]{3,2,1,0:T(8,128)} %bitcast.7, f32[3,2,16,512]{3,2,1,0:T(8,128)} %bitcast.6), kind=kLoop, calls=%fused_computation | loop fusion | flops 65536 | bytes 524288 | tf_op jit(solution)/shard_map/concatenate | solution.py:341
  12.9 0.6 shard_map.37
  14.1 1.0 %shard_map.39 = (f32[16,2,3,8,128]{4,3,2,1,0:T(8,128)S(1)}, f32[2,1,2,2,8,512]{5,4,3,2,1,0:T(8,128)S(1)}) custom-call(f32[4,2,2,8,512]{4,3,2,1,0:T(8,128)S(1)} %get-tuple-element.32.own, f32[2,3,2,2,8,512]{5,4,3,2,1,0:T(8,128)S(1)} %get-tuple-element.33.sides, f32[2,5,3,8,512]{4,3,2,1,0:T(8,128)S(1)} %get-tuple-element.34.near, ...), custom_call_target="tpu_custom_call" | custom-call | tf_op jit(solution)/shard_map/pallas_call | solution.py:327
  15.2 14.5 %all_to_all.10.corr.rest_2_ = f32[16,2,3,8,128]{4,3,2,1,0:T(8,128)S(1)} all-to-all(f32[16,2,3,8,128]{4,3,2,1,0:T(8,128)S(1)} %get-tuple-element.36), channel_id=1, replica_groups=mesh['tm'=16,'space'=32] {'tm'}, dimensions={0} | all-to-all | bytes 786432 | tf_op jit(solution)/shard_map/all_to_all | solution.py:364
  29.7 2.9 %collective-permute-start.4 = (f32[3,3,8,128]{3,2,1,0:T(8,128)S(1)}, f32[3,3,8,128]{3,2,1,0:T(8,128)S(1)}, u32[]{:S(2)}, u32[]{:S(2)}) collective-permute-start(f32[3,3,8,128]{3,2,1,0:T(8,128)S(1)} %slice.8.own), channel_id=1, source_target_pairs={{1,0},{2,1},{3,2},{4,3},{5,4},{6,5},{7,6},{8,7},{9,8},{10,9},{11,1... | collective-permute-start | bytes 110600 | tf_op jit(solution)/shard_map/ppermute | solution.py:322
  32.8 1.5 %collective-permute-done.4.right = f32[3,3,8,128]{3,2,1,0:T(8,128)S(1)} collective-permute-done((f32[3,3,8,128]{3,2,1,0:T(8,128)S(1)}, f32[3,3,8,128]{3,2,1,0:T(8,128)S(1)}, u32[]{:S(2)}, u32[]{:S(2)}) %collective-permute-start.4) | collective-permute-done | bytes 36896 | tf_op jit(solution)/shard_map/ppermute | solution.py:322
  34.9 2.9 %collective-permute-start.6 = (f32[3,3,8,128]{3,2,1,0:T(8,128)S(1)}, f32[3,3,8,128]{3,2,1,0:T(8,128)S(1)}, u32[]{:S(2)}, u32[]{:S(2)}) collective-permute-start(f32[3,3,8,128]{3,2,1,0:T(8,128)S(1)} %get-tuple-element.38.own.rest_1_), channel_id=1, source_target_pairs={{1,0},{2,1},{3,2},{4,3},{5,4},{6,5},{7,6},{8,7},{9,8},{10,9},{11,1... | collective-permute-start | bytes 110600 | tf_op jit(solution)/shard_map/ppermute | solution.py:322
  37.8 1.6 %collective-permute-done.7.left = f32[3,3,8,128]{3,2,1,0:T(8,128)S(1)} collective-permute-done((f32[3,3,8,128]{3,2,1,0:T(8,128)S(1)}, f32[3,3,8,128]{3,2,1,0:T(8,128)S(1)}, u32[]{:S(2)}, u32[]{:S(2)}) %collective-permute-start.7) | collective-permute-done | bytes 36896 | tf_op jit(solution)/shard_map/ppermute | solution.py:323
  39.9 3.0 %collective-permute-start.8 = (f32[3,3,8,128]{3,2,1,0:T(8,128)S(1)}, f32[3,3,8,128]{3,2,1,0:T(8,128)S(1)}, u32[]{:S(2)}, u32[]{:S(2)}) collective-permute-start(f32[3,3,8,128]{3,2,1,0:T(8,128)S(1)} %get-tuple-element.40.own.rest_3_), channel_id=1, source_target_pairs={{1,0},{2,1},{3,2},{4,3},{5,4},{6,5},{7,6},{8,7},{9,8},{10,9},{11,1... | collective-permute-start | bytes 110600 | tf_op jit(solution)/shard_map/ppermute | solution.py:322
  42.9 1.6 %collective-permute-done.9.left = f32[3,3,8,128]{3,2,1,0:T(8,128)S(1)} collective-permute-done((f32[3,3,8,128]{3,2,1,0:T(8,128)S(1)}, f32[3,3,8,128]{3,2,1,0:T(8,128)S(1)}, u32[]{:S(2)}, u32[]{:S(2)}) %collective-permute-start.9) | collective-permute-done | bytes 36896 | tf_op jit(solution)/shard_map/ppermute | solution.py:323
  45.0 3.0 %collective-permute-start.10 = (f32[3,3,8,128]{3,2,1,0:T(8,128)S(1)}, f32[3,3,8,128]{3,2,1,0:T(8,128)S(1)}, u32[]{:S(2)}, u32[]{:S(2)}) collective-permute-start(f32[3,3,8,128]{3,2,1,0:T(8,128)S(1)} %get-tuple-element.42.own.rest_5_), channel_id=1, source_target_pairs={{1,0},{2,1},{3,2},{4,3},{5,4},{6,5},{7,6},{8,7},{9,8},{10,9},{11,1... | collective-permute-start | bytes 110600 | tf_op jit(solution)/shard_map/ppermute | solution.py:322
  47.9 1.6 %collective-permute-done.11.left = f32[3,3,8,128]{3,2,1,0:T(8,128)S(1)} collective-permute-done((f32[3,3,8,128]{3,2,1,0:T(8,128)S(1)}, f32[3,3,8,128]{3,2,1,0:T(8,128)S(1)}, u32[]{:S(2)}, u32[]{:S(2)}) %collective-permute-start.11) | collective-permute-done | bytes 36896 | tf_op jit(solution)/shard_map/ppermute | solution.py:323
  50.0 3.0 %collective-permute-start.12 = (f32[3,3,8,128]{3,2,1,0:T(8,128)S(1)}, f32[3,3,8,128]{3,2,1,0:T(8,128)S(1)}, u32[]{:S(2)}, u32[]{:S(2)}) collective-permute-start(f32[3,3,8,128]{3,2,1,0:T(8,128)S(1)} %get-tuple-element.44.own.rest_7_), channel_id=1, source_target_pairs={{1,0},{2,1},{3,2},{4,3},{5,4},{6,5},{7,6},{8,7},{9,8},{10,9},{11,1... | collective-permute-start | bytes 110600 | tf_op jit(solution)/shard_map/ppermute | solution.py:322
  53.0 1.6 %collective-permute-done.13.left = f32[3,3,8,128]{3,2,1,0:T(8,128)S(1)} collective-permute-done((f32[3,3,8,128]{3,2,1,0:T(8,128)S(1)}, f32[3,3,8,128]{3,2,1,0:T(8,128)S(1)}, u32[]{:S(2)}, u32[]{:S(2)}) %collective-permute-start.13) | collective-permute-done | bytes 36896 | tf_op jit(solution)/shard_map/ppermute | solution.py:323
  55.1 3.0 %collective-permute-start.14 = (f32[3,3,8,128]{3,2,1,0:T(8,128)S(1)}, f32[3,3,8,128]{3,2,1,0:T(8,128)S(1)}, u32[]{:S(2)}, u32[]{:S(2)}) collective-permute-start(f32[3,3,8,128]{3,2,1,0:T(8,128)S(1)} %get-tuple-element.46.own.rest_9_), channel_id=1, source_target_pairs={{1,0},{2,1},{3,2},{4,3},{5,4},{6,5},{7,6},{8,7},{9,8},{10,9},{11,1... | collective-permute-start | bytes 110600 | tf_op jit(solution)/shard_map/ppermute | solution.py:322
  58.1 1.6 %collective-permute-done.15.left = f32[3,3,8,128]{3,2,1,0:T(8,128)S(1)} collective-permute-done((f32[3,3,8,128]{3,2,1,0:T(8,128)S(1)}, f32[3,3,8,128]{3,2,1,0:T(8,128)S(1)}, u32[]{:S(2)}, u32[]{:S(2)}) %collective-permute-start.15) | collective-permute-done | bytes 36896 | tf_op jit(solution)/shard_map/ppermute | solution.py:323
  60.2 3.0 %collective-permute-start.16 = (f32[3,3,8,128]{3,2,1,0:T(8,128)S(1)}, f32[3,3,8,128]{3,2,1,0:T(8,128)S(1)}, u32[]{:S(2)}, u32[]{:S(2)}) collective-permute-start(f32[3,3,8,128]{3,2,1,0:T(8,128)S(1)} %get-tuple-element.48.own.rest_11_), channel_id=1, source_target_pairs={{1,0},{2,1},{3,2},{4,3},{5,4},{6,5},{7,6},{8,7},{9,8},{10,9},{11,1... | collective-permute-start | bytes 110600 | tf_op jit(solution)/shard_map/ppermute | solution.py:322
  63.1 1.6 %collective-permute-done.17.left = f32[3,3,8,128]{3,2,1,0:T(8,128)S(1)} collective-permute-done((f32[3,3,8,128]{3,2,1,0:T(8,128)S(1)}, f32[3,3,8,128]{3,2,1,0:T(8,128)S(1)}, u32[]{:S(2)}, u32[]{:S(2)}) %collective-permute-start.17) | collective-permute-done | bytes 36896 | tf_op jit(solution)/shard_map/ppermute | solution.py:323
  65.2 3.0 %collective-permute-start.18 = (f32[1,3,8,128]{3,2,1,0:T(8,128)S(1)}, f32[1,3,8,128]{3,2,1,0:T(8,128)S(1)}, u32[]{:S(2)}, u32[]{:S(2)}) collective-permute-start(f32[1,3,8,128]{3,2,1,0:T(8,128)S(1)} %get-tuple-element.51.below), channel_id=1, source_target_pairs={{1,0},{2,1},{3,2},{4,3},{5,4},{6,5},{7,6},{8,7},{9,8},{10,9},{11,1... | collective-permute-start | bytes 36872 | tf_op jit(solution)/shard_map/ppermute | solution.py:322
  68.3 1.2 %collective-permute-done.19.rest_1_ = f32[1,3,8,128]{3,2,1,0:T(8,128)S(1)} collective-permute-done((f32[1,3,8,128]{3,2,1,0:T(8,128)S(1)}, f32[1,3,8,128]{3,2,1,0:T(8,128)S(1)}, u32[]{:S(2)}, u32[]{:S(2)}) %collective-permute-start.19) | collective-permute-done | bytes 12320 | tf_op jit(solution)/shard_map/ppermute | solution.py:323
  69.9 12.0 %all_to_all.11.sent = f32[16,3,8,128]{3,2,1,0:T(8,128)S(1)} all-to-all(f32[16,3,8,128]{3,2,1,0:T(8,128)S(1)} %shard_map.49), channel_id=1, replica_groups=mesh['tm'=16,'space'=32] {'tm'}, dimensions={0} | all-to-all | bytes 393216 | tf_op jit(solution)/shard_map/all_to_all | solution.py:380
  81.8 0.8 shard_map.50
  (37 shorter events, 4.5 us)
Async XLA Ops:
  0.0 13.5 %collective-permute-start.1 = (f32[3,2,16,512]{3,2,1,0:T(8,128)}, f32[3,2,16,512]{3,2,1,0:T(8,128)S(1)}, u32[]{:S(2)}, u32[]{:S(2)}) collective-permute-start(f32[3,2,16,512]{3,2,1,0:T(8,128)} %bitcast.4), channel_id=1, source_target_pairs={{0,1},{1,2},{2,3},{3,4},{4,5},{5,6},{6,7},{7,8},{8,9},{9,10},{10,1... | collective-permute-start | bytes 589832 | tf_op jit(solution)/shard_map/ppermute | solution.py:323
  0.0 13.5 %collective-permute-start = (f32[3,2,16,512]{3,2,1,0:T(8,128)}, f32[3,2,16,512]{3,2,1,0:T(8,128)S(1)}, u32[]{:S(2)}, u32[]{:S(2)}) collective-permute-start(f32[3,2,16,512]{3,2,1,0:T(8,128)} %bitcast.5), channel_id=1, source_target_pairs={{1,0},{2,1},{3,2},{4,3},{5,4},{6,5},{7,6},{8,7},{9,8},{10,9},{11,1... | collective-permute-start | bytes 589832 | tf_op jit(solution)/shard_map/ppermute | solution.py:322
  8.9 5.1 %collective-permute-start.3 = (f32[2,16,512]{2,1,0:T(8,128)}, f32[2,16,512]{2,1,0:T(8,128)S(1)}, u32[]{:S(2)}, u32[]{:S(2)}) collective-permute-start(f32[2,16,512]{2,1,0:T(8,128)} %param.4), channel_id=1, source_target_pairs={{0,1},{1,2},{2,3},{3,4},{4,5},{5,6},{6,7},{7,8},{8,9},{9,10},{10,1... | collective-permute-start | bytes 196616 | tf_op jit(solution)/shard_map/ppermute | solution.py:323
  8.9 5.2 %collective-permute-start.2 = (f32[2,16,512]{2,1,0:T(8,128)}, f32[2,16,512]{2,1,0:T(8,128)S(1)}, u32[]{:S(2)}, u32[]{:S(2)}) collective-permute-start(f32[2,16,512]{2,1,0:T(8,128)} %param.4), channel_id=1, source_target_pairs={{1,0},{2,1},{3,2},{4,3},{5,4},{6,5},{7,6},{8,7},{9,8},{10,9},{11,1... | collective-permute-start | bytes 196616 | tf_op jit(solution)/shard_map/ppermute | solution.py:322
  11.9 1.0 %copy-start = (f32[3]{0:T(128)S(1)}, f32[3]{0:T(128)}, u32[]{:S(2)}) copy-start(f32[3]{0:T(128)} %applied.1) | copy-start | bytes 40
  29.7 4.7 %collective-permute-start.5 = (f32[2,2,3,8,128]{4,3,2,1,0:T(8,128)S(1)}, f32[2,2,3,8,128]{4,3,2,1,0:T(8,128)S(1)}, u32[]{:S(2)}, u32[]{:S(2)}) collective-permute-start(f32[2,2,3,8,128]{4,3,2,1,0:T(8,128)S(1)} %slice.9), channel_id=1, source_target_pairs={{0,1},{1,2},{2,3},{3,4},{4,5},{5,6},{6,7},{7,8},{8,9},{9,10},{10,1... | collective-permute-start | bytes 147464 | tf_op jit(solution)/shard_map/ppermute | solution.py:323
  29.7 4.6 %collective-permute-start.4 = (f32[3,3,8,128]{3,2,1,0:T(8,128)S(1)}, f32[3,3,8,128]{3,2,1,0:T(8,128)S(1)}, u32[]{:S(2)}, u32[]{:S(2)}) collective-permute-start(f32[3,3,8,128]{3,2,1,0:T(8,128)S(1)} %slice.8.own), channel_id=1, source_target_pairs={{1,0},{2,1},{3,2},{4,3},{5,4},{6,5},{7,6},{8,7},{9,8},{10,9},{11,1... | collective-permute-start | bytes 110600 | tf_op jit(solution)/shard_map/ppermute | solution.py:322
  34.8 4.6 %collective-permute-start.7 = (f32[3,3,8,128]{3,2,1,0:T(8,128)S(1)}, f32[3,3,8,128]{3,2,1,0:T(8,128)S(1)}, u32[]{:S(2)}, u32[]{:S(2)}) collective-permute-start(f32[3,3,8,128]{3,2,1,0:T(8,128)S(1)} %get-tuple-element.39), channel_id=1, source_target_pairs={{0,1},{1,2},{2,3},{3,4},{4,5},{5,6},{6,7},{7,8},{8,9},{9,10},{10,1... | collective-permute-start | bytes 110600 | tf_op jit(solution)/shard_map/ppermute | solution.py:323
  34.9 4.6 %collective-permute-start.6 = (f32[3,3,8,128]{3,2,1,0:T(8,128)S(1)}, f32[3,3,8,128]{3,2,1,0:T(8,128)S(1)}, u32[]{:S(2)}, u32[]{:S(2)}) collective-permute-start(f32[3,3,8,128]{3,2,1,0:T(8,128)S(1)} %get-tuple-element.38.own.rest_1_), channel_id=1, source_target_pairs={{1,0},{2,1},{3,2},{4,3},{5,4},{6,5},{7,6},{8,7},{9,8},{10,9},{11,1... | collective-permute-start | bytes 110600 | tf_op jit(solution)/shard_map/ppermute | solution.py:322
  39.9 4.6 %collective-permute-start.9 = (f32[3,3,8,128]{3,2,1,0:T(8,128)S(1)}, f32[3,3,8,128]{3,2,1,0:T(8,128)S(1)}, u32[]{:S(2)}, u32[]{:S(2)}) collective-permute-start(f32[3,3,8,128]{3,2,1,0:T(8,128)S(1)} %get-tuple-element.41), channel_id=1, source_target_pairs={{0,1},{1,2},{2,3},{3,4},{4,5},{5,6},{6,7},{7,8},{8,9},{9,10},{10,1... | collective-permute-start | bytes 110600 | tf_op jit(solution)/shard_map/ppermute | solution.py:323
  39.9 4.6 %collective-permute-start.8 = (f32[3,3,8,128]{3,2,1,0:T(8,128)S(1)}, f32[3,3,8,128]{3,2,1,0:T(8,128)S(1)}, u32[]{:S(2)}, u32[]{:S(2)}) collective-permute-start(f32[3,3,8,128]{3,2,1,0:T(8,128)S(1)} %get-tuple-element.40.own.rest_3_), channel_id=1, source_target_pairs={{1,0},{2,1},{3,2},{4,3},{5,4},{6,5},{7,6},{8,7},{9,8},{10,9},{11,1... | collective-permute-start | bytes 110600 | tf_op jit(solution)/shard_map/ppermute | solution.py:322
  44.9 4.6 %collective-permute-start.11 = (f32[3,3,8,128]{3,2,1,0:T(8,128)S(1)}, f32[3,3,8,128]{3,2,1,0:T(8,128)S(1)}, u32[]{:S(2)}, u32[]{:S(2)}) collective-permute-start(f32[3,3,8,128]{3,2,1,0:T(8,128)S(1)} %get-tuple-element.43), channel_id=1, source_target_pairs={{0,1},{1,2},{2,3},{3,4},{4,5},{5,6},{6,7},{7,8},{8,9},{9,10},{10,1... | collective-permute-start | bytes 110600 | tf_op jit(solution)/shard_map/ppermute | solution.py:323
  45.0 4.6 %collective-permute-start.10 = (f32[3,3,8,128]{3,2,1,0:T(8,128)S(1)}, f32[3,3,8,128]{3,2,1,0:T(8,128)S(1)}, u32[]{:S(2)}, u32[]{:S(2)}) collective-permute-start(f32[3,3,8,128]{3,2,1,0:T(8,128)S(1)} %get-tuple-element.42.own.rest_5_), channel_id=1, source_target_pairs={{1,0},{2,1},{3,2},{4,3},{5,4},{6,5},{7,6},{8,7},{9,8},{10,9},{11,1... | collective-permute-start | bytes 110600 | tf_op jit(solution)/shard_map/ppermute | solution.py:322
  50.0 4.6 %collective-permute-start.13 = (f32[3,3,8,128]{3,2,1,0:T(8,128)S(1)}, f32[3,3,8,128]{3,2,1,0:T(8,128)S(1)}, u32[]{:S(2)}, u32[]{:S(2)}) collective-permute-start(f32[3,3,8,128]{3,2,1,0:T(8,128)S(1)} %get-tuple-element.45), channel_id=1, source_target_pairs={{0,1},{1,2},{2,3},{3,4},{4,5},{5,6},{6,7},{7,8},{8,9},{9,10},{10,1... | collective-permute-start | bytes 110600 | tf_op jit(solution)/shard_map/ppermute | solution.py:323
  50.0 4.6 %collective-permute-start.12 = (f32[3,3,8,128]{3,2,1,0:T(8,128)S(1)}, f32[3,3,8,128]{3,2,1,0:T(8,128)S(1)}, u32[]{:S(2)}, u32[]{:S(2)}) collective-permute-start(f32[3,3,8,128]{3,2,1,0:T(8,128)S(1)} %get-tuple-element.44.own.rest_7_), channel_id=1, source_target_pairs={{1,0},{2,1},{3,2},{4,3},{5,4},{6,5},{7,6},{8,7},{9,8},{10,9},{11,1... | collective-permute-start | bytes 110600 | tf_op jit(solution)/shard_map/ppermute | solution.py:322
  55.1 4.6 %collective-permute-start.15 = (f32[3,3,8,128]{3,2,1,0:T(8,128)S(1)}, f32[3,3,8,128]{3,2,1,0:T(8,128)S(1)}, u32[]{:S(2)}, u32[]{:S(2)}) collective-permute-start(f32[3,3,8,128]{3,2,1,0:T(8,128)S(1)} %get-tuple-element.47), channel_id=1, source_target_pairs={{0,1},{1,2},{2,3},{3,4},{4,5},{5,6},{6,7},{7,8},{8,9},{9,10},{10,1... | collective-permute-start | bytes 110600 | tf_op jit(solution)/shard_map/ppermute | solution.py:323
  55.1 4.6 %collective-permute-start.14 = (f32[3,3,8,128]{3,2,1,0:T(8,128)S(1)}, f32[3,3,8,128]{3,2,1,0:T(8,128)S(1)}, u32[]{:S(2)}, u32[]{:S(2)}) collective-permute-start(f32[3,3,8,128]{3,2,1,0:T(8,128)S(1)} %get-tuple-element.46.own.rest_9_), channel_id=1, source_target_pairs={{1,0},{2,1},{3,2},{4,3},{5,4},{6,5},{7,6},{8,7},{9,8},{10,9},{11,1... | collective-permute-start | bytes 110600 | tf_op jit(solution)/shard_map/ppermute | solution.py:322
  60.1 4.6 %collective-permute-start.17 = (f32[3,3,8,128]{3,2,1,0:T(8,128)S(1)}, f32[3,3,8,128]{3,2,1,0:T(8,128)S(1)}, u32[]{:S(2)}, u32[]{:S(2)}) collective-permute-start(f32[3,3,8,128]{3,2,1,0:T(8,128)S(1)} %get-tuple-element.49), channel_id=1, source_target_pairs={{0,1},{1,2},{2,3},{3,4},{4,5},{5,6},{6,7},{7,8},{8,9},{9,10},{10,1... | collective-permute-start | bytes 110600 | tf_op jit(solution)/shard_map/ppermute | solution.py:323
  60.2 4.6 %collective-permute-start.16 = (f32[3,3,8,128]{3,2,1,0:T(8,128)S(1)}, f32[3,3,8,128]{3,2,1,0:T(8,128)S(1)}, u32[]{:S(2)}, u32[]{:S(2)}) collective-permute-start(f32[3,3,8,128]{3,2,1,0:T(8,128)S(1)} %get-tuple-element.48.own.rest_11_), channel_id=1, source_target_pairs={{1,0},{2,1},{3,2},{4,3},{5,4},{6,5},{7,6},{8,7},{9,8},{10,9},{11,1... | collective-permute-start | bytes 110600 | tf_op jit(solution)/shard_map/ppermute | solution.py:322
  65.2 4.4 %collective-permute-start.19 = (f32[1,3,8,128]{3,2,1,0:T(8,128)S(1)}, f32[1,3,8,128]{3,2,1,0:T(8,128)S(1)}, u32[]{:S(2)}, u32[]{:S(2)}) collective-permute-start(f32[1,3,8,128]{3,2,1,0:T(8,128)S(1)} %get-tuple-element.50.above), channel_id=1, source_target_pairs={{0,1},{1,2},{2,3},{3,4},{4,5},{5,6},{6,7},{7,8},{8,9},{9,10},{10,1... | collective-permute-start | bytes 36872 | tf_op jit(solution)/shard_map/ppermute | solution.py:323
  65.2 4.4 %collective-permute-start.18 = (f32[1,3,8,128]{3,2,1,0:T(8,128)S(1)}, f32[1,3,8,128]{3,2,1,0:T(8,128)S(1)}, u32[]{:S(2)}, u32[]{:S(2)}) collective-permute-start(f32[1,3,8,128]{3,2,1,0:T(8,128)S(1)} %get-tuple-element.51.below), channel_id=1, source_target_pairs={{1,0},{2,1},{3,2},{4,3},{5,4},{6,5},{7,6},{8,7},{9,8},{10,9},{11,1... | collective-permute-start | bytes 36872 | tf_op jit(solution)/shard_map/ppermute | solution.py:322

commit v14 on v13

--- a/solution.py
+++ b/solution.py
@@ -111,7 +111,7 @@
     return load
 
 
-def first_sums(own, right, left, sides, near, layers):
+def first_sums(own, right, left, field, sides, near, inner, outer, layers):
     for side, spins in enumerate((left, right)):
         for comp in range(3):
             by_parity(spins.at[comp], sides.at[side, comp], layers.at[side, comp])
@@ -123,9 +123,20 @@
             near[0, k, c] = value
         for c, value in enumerate(near_odd(even[k - 2], even[k - 1])):
             near[1, k, c] = value
-
-
-def prologue(own, sides, near, right_a, left_a, field, payload, aniso, layers):
+    applied = [jnp.concatenate([field[c]] * layers.shape[3], axis=1) for c in range(3)]
+    sides_own = (lambda x: load(3, x, 0), lambda x: load(3, x, 1), applied)
+    first_e, first_o = rates(even, odd, *sides_own, range(2), range(2))
+    for x in range(2):
+        for c in range(3):
+            inner[0, x, c], inner[1, x, c] = first_e[x][c], first_o[x][c]
+    for k, length in enumerate((STEP, COARSE)):
+        pred_e, pred_o = ahead(even, first_e, length), ahead(odd, first_o, length)
+        second_e, second_o = rates(pred_e, pred_o, *sides_own, (0,), (1,))
+        for c in range(3):
+            outer[k, 0, c], outer[k, 1, c] = second_e[0][c], second_o[1][c]
+
+
+def prologue(own, sides, near, inner, outer, right_a, left_a, field, payload, aniso, layers):
     by_parity(left_a, aniso.at[0, 0], layers.at[0], 2.0)
     by_parity(right_a, aniso.at[1, 0], layers.at[1], 2.0)
     load, load_a = beside(own, sides), beside(own, aniso, 3)
@@ -142,15 +153,21 @@
         return load_a(3, x, 1)
 
     sides = (aniso_even, aniso_odd, applied)
-    first_e = {x: bare_rate(even[x], [near[0, x + 2, c] for c in range(3)], aniso_even(x), applied) for x in range(-2, 3)}
-    first_o = {x: bare_rate(odd[x], [near[1, x + 1, c] for c in range(3)], aniso_odd(x), applied) for x in range(-1, 4)}
+    first_e = {x: [inner[0, x, c] for c in range(3)] for x in range(2)}
+    first_o = {x: [inner[1, x, c] for c in range(3)] for x in range(2)}
+    for x in (-2, -1, 2):
+        first_e[x] = bare_rate(even[x], [near[0, x + 2, c] for c in range(3)], aniso_even(x), applied)
+    for x in (-1, 2, 3):
+        first_o[x] = bare_rate(odd[x], [near[1, x + 1, c] for c in range(3)], aniso_odd(x), applied)
     pred_e, pred_o = ahead(even, first_e, STEP), ahead(odd, first_o, STEP)
-    second_e, second_o = rates(pred_e, pred_o, *sides, range(-1, 3), range(-1, 3))
+    second_e, second_o = rates(pred_e, pred_o, *sides, (-1, 1, 2), (-1, 0, 2))
+    second_e[0], second_o[1] = ([outer[0, k, c] for c in range(3)] for k in range(2))
     fine_e = finish(even, first_e, second_e, STEP, range(-1, 3))
     fine_o = finish(odd, first_o, second_o, STEP, range(-1, 3))
     fine_e, fine_o = heun(fine_e, fine_o, *sides, STEP, -1, 2)
     pred_e, pred_o = ahead(even, first_e, COARSE), ahead(odd, first_o, COARSE)
-    second_e, second_o = rates(pred_e, pred_o, *sides, range(2), range(2))
+    second_e, second_o = rates(pred_e, pred_o, *sides, (1,), (0,))
+    second_e[0], second_o[1] = ([outer[1, k, c] for c in range(3)] for k in range(2))
     coarse_e = finish(even, first_e, second_e, COARSE, range(2))
     coarse_o = finish(odd, first_o, second_o, COARSE, range(2))
 
@@ -348,16 +365,16 @@
         scratch=[layers],
         in_specs=[VMEM, pl.BlockSpec(memory_space=pltpu.SMEM)],
     )
-    sides, near = call(
+    sides, near, inner, outer = call(
         first_sums,
-        [(2, 3, 2, 2, 8, width), (2, 5, 3, 8, width)],
-        *(own, right, left),
+        [(2, 3, 2, 2, 8, width), (2, 5, 3, 8, width), (2, 2, 3, 8, width), (2, 2, 3, 8, width)],
+        *(own, right, left, field),
         scratch=[(2, *layers)],
     )
     payload, aniso = call(
         prologue,
         [(slices, 2, 3, 8, 128), (2, 1, 2, 2, 8, width)],
-        *(own, sides, near, right_a, left_a, field),
+        *(own, sides, near, inner, outer, right_a, left_a, field),
         scratch=[(2, *layers[1:])],
     )
     (windows,) = call(window, [(7, 8, 128)], own, aniso)

time: 82.8 us -> 82.7 us (level)
  transfers between devices with their start and end apart: 20 -> 20, of which waited for: 12 -> 12; matrix products, arithmetic and copies ran while one was open for 1% -> 1% of each run, Pallas kernels for 1% -> 2%
where the time goes in v14:
time: 82.7 us; the launch traced here: 82.5 us
  starting transfers between devices  35.7 us (43%)
  blocking collectives  26.5 us (32%)
  waiting for transfers between devices  12.9 us (16%)
  Pallas kernels  6.15 us (7%)
  other arithmetic  0.99 us (1%)
    ppermute x10, starting transfers between devices, both_sides(): from_above = lax.ppermute(to_below, 'space', down)  35.6 us
    all_to_all x1, blocking collectives, per_device(): corr = lax.all_to_all(payload, 'tm', 0, 0, tiled=True)  14.5 us
    all_to_all x1, blocking collectives, per_device(): sent = lax.all_to_all(sent, 'tm', 0, 0, tiled=True)  12 us
    ppermute x10, waiting for transfers between devices, both_sides(): return (from_above, lax.ppermute(to_above, 'space', up))  11.2 us
    pallas_call x14, Pallas kernels, call(): pl.pallas_call(kernel, out_shape=[jax.ShapeDtypeStruct(s, F32) for s in s...  6.15 us
    ppermute x10, waiting for transfers between devices, both_sides(): from_above = lax.ppermute(to_below, 'space', down)  1.71 us
  transfers between devices with their start and end apart: 20, of which 12 were waited for; matrix products, arithmetic and copies ran while one was open for 1% of the time, Pallas kernels for 2%

profile of v14, /device:TPU:2, one launch (start us, length us, event | category | flops | bytes accessed | tf_op | source)
XLA Modules:
  0.0 82.5 jit_solution(11408889879344984221)
XLA Ops:
  0.0 8.9 %collective-permute-start = (f32[3,2,16,512]{3,2,1,0:T(8,128)}, f32[3,2,16,512]{3,2,1,0:T(8,128)S(1)}, u32[]{:S(2)}, u32[]{:S(2)}) collective-permute-start(f32[3,2,16,512]{3,2,1,0:T(8,128)} %bitcast.5), channel_id=1, source_target_pairs={{1,0},{2,1},{3,2},{4,3},{5,4},{6,5},{7,6},{8,7},{9,8},{10,9},{11,1... | collective-permute-start | bytes 589832 | tf_op jit(solution)/shard_map/ppermute | solution.py:339
  8.9 3.0 %collective-permute-start.2 = (f32[2,16,512]{2,1,0:T(8,128)}, f32[2,16,512]{2,1,0:T(8,128)S(1)}, u32[]{:S(2)}, u32[]{:S(2)}) collective-permute-start(f32[2,16,512]{2,1,0:T(8,128)} %param.4), channel_id=1, source_target_pairs={{1,0},{2,1},{3,2},{4,3},{5,4},{6,5},{7,6},{8,7},{9,8},{10,9},{11,1... | collective-permute-start | bytes 196616 | tf_op jit(solution)/shard_map/ppermute | solution.py:339
  11.9 1.0 %pad_maximum_fusion.slab = f32[4,2,16,512]{3,2,1,0:T(8,128)S(1)} fusion(f32[1,2,16,512]{3,2,1,0:T(8,128)} %bitcast.7, f32[3,2,16,512]{3,2,1,0:T(8,128)} %bitcast.6), kind=kLoop, calls=%fused_computation | loop fusion | flops 65536 | bytes 524288 | tf_op jit(solution)/shard_map/concatenate | solution.py:358
  12.9 0.6 shard_map.37
  14.1 0.9 %shard_map.39 = (f32[16,2,3,8,128]{4,3,2,1,0:T(8,128)S(1)}, f32[2,1,2,2,8,512]{5,4,3,2,1,0:T(8,128)S(1)}) custom-call(f32[4,2,2,8,512]{4,3,2,1,0:T(8,128)S(1)} %get-tuple-element.34.own, f32[2,3,2,2,8,512]{5,4,3,2,1,0:T(8,128)S(1)} %get-tuple-element.36.sides, f32[2,5,3,8,512]{4,3,2,1,0:T(8,128)S(1)} %get-tuple-element.37.near, ...), custom_call_target="tpu_custom_call" | custom-call | tf_op jit(solution)/shard_map/pallas_call | solution.py:344
  15.0 14.5 %all_to_all.10.corr.rest_2_ = f32[16,2,3,8,128]{4,3,2,1,0:T(8,128)S(1)} all-to-all(f32[16,2,3,8,128]{4,3,2,1,0:T(8,128)S(1)} %get-tuple-element.40), channel_id=1, replica_groups=mesh['tm'=16,'space'=32] {'tm'}, dimensions={0} | all-to-all | bytes 786432 | tf_op jit(solution)/shard_map/all_to_all | solution.py:381
  29.5 2.9 %collective-permute-start.4 = (f32[3,3,8,128]{3,2,1,0:T(8,128)S(1)}, f32[3,3,8,128]{3,2,1,0:T(8,128)S(1)}, u32[]{:S(2)}, u32[]{:S(2)}) collective-permute-start(f32[3,3,8,128]{3,2,1,0:T(8,128)S(1)} %slice.8.own), channel_id=1, source_target_pairs={{1,0},{2,1},{3,2},{4,3},{5,4},{6,5},{7,6},{8,7},{9,8},{10,9},{11,1... | collective-permute-start | bytes 110600 | tf_op jit(solution)/shard_map/ppermute | solution.py:339
  32.6 1.5 %collective-permute-done.4.right = f32[3,3,8,128]{3,2,1,0:T(8,128)S(1)} collective-permute-done((f32[3,3,8,128]{3,2,1,0:T(8,128)S(1)}, f32[3,3,8,128]{3,2,1,0:T(8,128)S(1)}, u32[]{:S(2)}, u32[]{:S(2)}) %collective-permute-start.4) | collective-permute-done | bytes 36896 | tf_op jit(solution)/shard_map/ppermute | solution.py:339
  34.7 2.9 %collective-permute-start.6 = (f32[3,3,8,128]{3,2,1,0:T(8,128)S(1)}, f32[3,3,8,128]{3,2,1,0:T(8,128)S(1)}, u32[]{:S(2)}, u32[]{:S(2)}) collective-permute-start(f32[3,3,8,128]{3,2,1,0:T(8,128)S(1)} %get-tuple-element.42.own.rest_1_), channel_id=1, source_target_pairs={{1,0},{2,1},{3,2},{4,3},{5,4},{6,5},{7,6},{8,7},{9,8},{10,9},{11,1... | collective-permute-start | bytes 110600 | tf_op jit(solution)/shard_map/ppermute | solution.py:339
  37.6 1.6 %collective-permute-done.7.left = f32[3,3,8,128]{3,2,1,0:T(8,128)S(1)} collective-permute-done((f32[3,3,8,128]{3,2,1,0:T(8,128)S(1)}, f32[3,3,8,128]{3,2,1,0:T(8,128)S(1)}, u32[]{:S(2)}, u32[]{:S(2)}) %collective-permute-start.7) | collective-permute-done | bytes 36896 | tf_op jit(solution)/shard_map/ppermute | solution.py:340
  39.7 3.0 %collective-permute-start.8 = (f32[3,3,8,128]{3,2,1,0:T(8,128)S(1)}, f32[3,3,8,128]{3,2,1,0:T(8,128)S(1)}, u32[]{:S(2)}, u32[]{:S(2)}) collective-permute-start(f32[3,3,8,128]{3,2,1,0:T(8,128)S(1)} %get-tuple-element.44.own.rest_3_), channel_id=1, source_target_pairs={{1,0},{2,1},{3,2},{4,3},{5,4},{6,5},{7,6},{8,7},{9,8},{10,9},{11,1... | collective-permute-start | bytes 110600 | tf_op jit(solution)/shard_map/ppermute | solution.py:339
  42.7 1.6 %collective-permute-done.9.left = f32[3,3,8,128]{3,2,1,0:T(8,128)S(1)} collective-permute-done((f32[3,3,8,128]{3,2,1,0:T(8,128)S(1)}, f32[3,3,8,128]{3,2,1,0:T(8,128)S(1)}, u32[]{:S(2)}, u32[]{:S(2)}) %collective-permute-start.9) | collective-permute-done | bytes 36896 | tf_op jit(solution)/shard_map/ppermute | solution.py:340
  44.8 3.0 %collective-permute-start.10 = (f32[3,3,8,128]{3,2,1,0:T(8,128)S(1)}, f32[3,3,8,128]{3,2,1,0:T(8,128)S(1)}, u32[]{:S(2)}, u32[]{:S(2)}) collective-permute-start(f32[3,3,8,128]{3,2,1,0:T(8,128)S(1)} %get-tuple-element.46.own.rest_5_), channel_id=1, source_target_pairs={{1,0},{2,1},{3,2},{4,3},{5,4},{6,5},{7,6},{8,7},{9,8},{10,9},{11,1... | collective-permute-start | bytes 110600 | tf_op jit(solution)/shard_map/ppermute | solution.py:339
  47.8 1.6 %collective-permute-done.11.left = f32[3,3,8,128]{3,2,1,0:T(8,128)S(1)} collective-permute-done((f32[3,3,8,128]{3,2,1,0:T(8,128)S(1)}, f32[3,3,8,128]{3,2,1,0:T(8,128)S(1)}, u32[]{:S(2)}, u32[]{:S(2)}) %collective-permute-start.11) | collective-permute-done | bytes 36896 | tf_op jit(solution)/shard_map/ppermute | solution.py:340
  49.9 3.0 %collective-permute-start.12 = (f32[3,3,8,128]{3,2,1,0:T(8,128)S(1)}, f32[3,3,8,128]{3,2,1,0:T(8,128)S(1)}, u32[]{:S(2)}, u32[]{:S(2)}) collective-permute-start(f32[3,3,8,128]{3,2,1,0:T(8,128)S(1)} %get-tuple-element.48.own.rest_7_), channel_id=1, source_target_pairs={{1,0},{2,1},{3,2},{4,3},{5,4},{6,5},{7,6},{8,7},{9,8},{10,9},{11,1... | collective-permute-start | bytes 110600 | tf_op jit(solution)/shard_map/ppermute | solution.py:339
  52.8 1.6 %collective-permute-done.13.left = f32[3,3,8,128]{3,2,1,0:T(8,128)S(1)} collective-permute-done((f32[3,3,8,128]{3,2,1,0:T(8,128)S(1)}, f32[3,3,8,128]{3,2,1,0:T(8,128)S(1)}, u32[]{:S(2)}, u32[]{:S(2)}) %collective-permute-start.13) | collective-permute-done | bytes 36896 | tf_op jit(solution)/shard_map/ppermute | solution.py:340
  54.9 3.0 %collective-permute-start.14 = (f32[3,3,8,128]{3,2,1,0:T(8,128)S(1)}, f32[3,3,8,128]{3,2,1,0:T(8,128)S(1)}, u32[]{:S(2)}, u32[]{:S(2)}) collective-permute-start(f32[3,3,8,128]{3,2,1,0:T(8,128)S(1)} %get-tuple-element.50.own.rest_9_), channel_id=1, source_target_pairs={{1,0},{2,1},{3,2},{4,3},{5,4},{6,5},{7,6},{8,7},{9,8},{10,9},{11,1... | collective-permute-start | bytes 110600 | tf_op jit(solution)/shard_map/ppermute | solution.py:339
  57.9 1.6 %collective-permute-done.15.left = f32[3,3,8,128]{3,2,1,0:T(8,128)S(1)} collective-permute-done((f32[3,3,8,128]{3,2,1,0:T(8,128)S(1)}, f32[3,3,8,128]{3,2,1,0:T(8,128)S(1)}, u32[]{:S(2)}, u32[]{:S(2)}) %collective-permute-start.15) | collective-permute-done | bytes 36896 | tf_op jit(solution)/shard_map/ppermute | solution.py:340
  60.0 3.0 %collective-permute-start.16 = (f32[3,3,8,128]{3,2,1,0:T(8,128)S(1)}, f32[3,3,8,128]{3,2,1,0:T(8,128)S(1)}, u32[]{:S(2)}, u32[]{:S(2)}) collective-permute-start(f32[3,3,8,128]{3,2,1,0:T(8,128)S(1)} %get-tuple-element.52.own.rest_11_), channel_id=1, source_target_pairs={{1,0},{2,1},{3,2},{4,3},{5,4},{6,5},{7,6},{8,7},{9,8},{10,9},{11,1... | collective-permute-start | bytes 110600 | tf_op jit(solution)/shard_map/ppermute | solution.py:339
  63.0 1.6 %collective-permute-done.17.left = f32[3,3,8,128]{3,2,1,0:T(8,128)S(1)} collective-permute-done((f32[3,3,8,128]{3,2,1,0:T(8,128)S(1)}, f32[3,3,8,128]{3,2,1,0:T(8,128)S(1)}, u32[]{:S(2)}, u32[]{:S(2)}) %collective-permute-start.17) | collective-permute-done | bytes 36896 | tf_op jit(solution)/shard_map/ppermute | solution.py:340
  65.1 3.0 %collective-permute-start.18 = (f32[1,3,8,128]{3,2,1,0:T(8,128)S(1)}, f32[1,3,8,128]{3,2,1,0:T(8,128)S(1)}, u32[]{:S(2)}, u32[]{:S(2)}) collective-permute-start(f32[1,3,8,128]{3,2,1,0:T(8,128)S(1)} %get-tuple-element.55.below), channel_id=1, source_target_pairs={{1,0},{2,1},{3,2},{4,3},{5,4},{6,5},{7,6},{8,7},{9,8},{10,9},{11,1... | collective-permute-start | bytes 36872 | tf_op jit(solution)/shard_map/ppermute | solution.py:339
  68.2 1.2 %collective-permute-done.19.rest_1_ = f32[1,3,8,128]{3,2,1,0:T(8,128)S(1)} collective-permute-done((f32[1,3,8,128]{3,2,1,0:T(8,128)S(1)}, f32[1,3,8,128]{3,2,1,0:T(8,128)S(1)}, u32[]{:S(2)}, u32[]{:S(2)}) %collective-permute-start.19) | collective-permute-done | bytes 12320 | tf_op jit(solution)/shard_map/ppermute | solution.py:340
  69.7 12.0 %all_to_all.11.sent = f32[16,3,8,128]{3,2,1,0:T(8,128)S(1)} all-to-all(f32[16,3,8,128]{3,2,1,0:T(8,128)S(1)} %shard_map.49), channel_id=1, replica_groups=mesh['tm'=16,'space'=32] {'tm'}, dimensions={0} | all-to-all | bytes 393216 | tf_op jit(solution)/shard_map/all_to_all | solution.py:397
  81.7 0.8 shard_map.50
  (37 shorter events, 4.5 us)
Async XLA Ops:
  0.0 13.5 %collective-permute-start.1 = (f32[3,2,16,512]{3,2,1,0:T(8,128)}, f32[3,2,16,512]{3,2,1,0:T(8,128)S(1)}, u32[]{:S(2)}, u32[]{:S(2)}) collective-permute-start(f32[3,2,16,512]{3,2,1,0:T(8,128)} %bitcast.4), channel_id=1, source_target_pairs={{0,1},{1,2},{2,3},{3,4},{4,5},{5,6},{6,7},{7,8},{8,9},{9,10},{10,1... | collective-permute-start | bytes 589832 | tf_op jit(solution)/shard_map/ppermute | solution.py:340
  0.0 13.5 %collective-permute-start = (f32[3,2,16,512]{3,2,1,0:T(8,128)}, f32[3,2,16,512]{3,2,1,0:T(8,128)S(1)}, u32[]{:S(2)}, u32[]{:S(2)}) collective-permute-start(f32[3,2,16,512]{3,2,1,0:T(8,128)} %bitcast.5), channel_id=1, source_target_pairs={{1,0},{2,1},{3,2},{4,3},{5,4},{6,5},{7,6},{8,7},{9,8},{10,9},{11,1... | collective-permute-start | bytes 589832 | tf_op jit(solution)/shard_map/ppermute | solution.py:339
  8.9 5.1 %collective-permute-start.3 = (f32[2,16,512]{2,1,0:T(8,128)}, f32[2,16,512]{2,1,0:T(8,128)S(1)}, u32[]{:S(2)}, u32[]{:S(2)}) collective-permute-start(f32[2,16,512]{2,1,0:T(8,128)} %param.4), channel_id=1, source_target_pairs={{0,1},{1,2},{2,3},{3,4},{4,5},{5,6},{6,7},{7,8},{8,9},{9,10},{10,1... | collective-permute-start | bytes 196616 | tf_op jit(solution)/shard_map/ppermute | solution.py:340
  8.9 5.2 %collective-permute-start.2 = (f32[2,16,512]{2,1,0:T(8,128)}, f32[2,16,512]{2,1,0:T(8,128)S(1)}, u32[]{:S(2)}, u32[]{:S(2)}) collective-permute-start(f32[2,16,512]{2,1,0:T(8,128)} %param.4), channel_id=1, source_target_pairs={{1,0},{2,1},{3,2},{4,3},{5,4},{6,5},{7,6},{8,7},{9,8},{10,9},{11,1... | collective-permute-start | bytes 196616 | tf_op jit(solution)/shard_map/ppermute | solution.py:339
  11.9 1.0 %copy-start = (f32[3]{0:T(128)S(1)}, f32[3]{0:T(128)}, u32[]{:S(2)}) copy-start(f32[3]{0:T(128)} %applied.1) | copy-start | bytes 40
  29.5 4.7 %collective-permute-start.5 = (f32[2,2,3,8,128]{4,3,2,1,0:T(8,128)S(1)}, f32[2,2,3,8,128]{4,3,2,1,0:T(8,128)S(1)}, u32[]{:S(2)}, u32[]{:S(2)}) collective-permute-start(f32[2,2,3,8,128]{4,3,2,1,0:T(8,128)S(1)} %slice.9), channel_id=1, source_target_pairs={{0,1},{1,2},{2,3},{3,4},{4,5},{5,6},{6,7},{7,8},{8,9},{9,10},{10,1... | collective-permute-start | bytes 147464 | tf_op jit(solution)/shard_map/ppermute | solution.py:340
  29.5 4.6 %collective-permute-start.4 = (f32[3,3,8,128]{3,2,1,0:T(8,128)S(1)}, f32[3,3,8,128]{3,2,1,0:T(8,128)S(1)}, u32[]{:S(2)}, u32[]{:S(2)}) collective-permute-start(f32[3,3,8,128]{3,2,1,0:T(8,128)S(1)} %slice.8.own), channel_id=1, source_target_pairs={{1,0},{2,1},{3,2},{4,3},{5,4},{6,5},{7,6},{8,7},{9,8},{10,9},{11,1... | collective-permute-start | bytes 110600 | tf_op jit(solution)/shard_map/ppermute | solution.py:339
  34.7 4.6 %collective-permute-start.7 = (f32[3,3,8,128]{3,2,1,0:T(8,128)S(1)}, f32[3,3,8,128]{3,2,1,0:T(8,128)S(1)}, u32[]{:S(2)}, u32[]{:S(2)}) collective-permute-start(f32[3,3,8,128]{3,2,1,0:T(8,128)S(1)} %get-tuple-element.43), channel_id=1, source_target_pairs={{0,1},{1,2},{2,3},{3,4},{4,5},{5,6},{6,7},{7,8},{8,9},{9,10},{10,1... | collective-permute-start | bytes 110600 | tf_op jit(solution)/shard_map/ppermute | solution.py:340
  34.7 4.6 %collective-permute-start.6 = (f32[3,3,8,128]{3,2,1,0:T(8,128)S(1)}, f32[3,3,8,128]{3,2,1,0:T(8,128)S(1)}, u32[]{:S(2)}, u32[]{:S(2)}) collective-permute-start(f32[3,3,8,128]{3,2,1,0:T(8,128)S(1)} %get-tuple-element.42.own.rest_1_), channel_id=1, source_target_pairs={{1,0},{2,1},{3,2},{4,3},{5,4},{6,5},{7,6},{8,7},{9,8},{10,9},{11,1... | collective-permute-start | bytes 110600 | tf_op jit(solution)/shard_map/ppermute | solution.py:339
  39.7 4.6 %collective-permute-start.9 = (f32[3,3,8,128]{3,2,1,0:T(8,128)S(1)}, f32[3,3,8,128]{3,2,1,0:T(8,128)S(1)}, u32[]{:S(2)}, u32[]{:S(2)}) collective-permute-start(f32[3,3,8,128]{3,2,1,0:T(8,128)S(1)} %get-tuple-element.45), channel_id=1, source_target_pairs={{0,1},{1,2},{2,3},{3,4},{4,5},{5,6},{6,7},{7,8},{8,9},{9,10},{10,1... | collective-permute-start | bytes 110600 | tf_op jit(solution)/shard_map/ppermute | solution.py:340
  39.7 4.6 %collective-permute-start.8 = (f32[3,3,8,128]{3,2,1,0:T(8,128)S(1)}, f32[3,3,8,128]{3,2,1,0:T(8,128)S(1)}, u32[]{:S(2)}, u32[]{:S(2)}) collective-permute-start(f32[3,3,8,128]{3,2,1,0:T(8,128)S(1)} %get-tuple-element.44.own.rest_3_), channel_id=1, source_target_pairs={{1,0},{2,1},{3,2},{4,3},{5,4},{6,5},{7,6},{8,7},{9,8},{10,9},{11,1... | collective-permute-start | bytes 110600 | tf_op jit(solution)/shard_map/ppermute | solution.py:339
  44.8 4.6 %collective-permute-start.11 = (f32[3,3,8,128]{3,2,1,0:T(8,128)S(1)}, f32[3,3,8,128]{3,2,1,0:T(8,128)S(1)}, u32[]{:S(2)}, u32[]{:S(2)}) collective-permute-start(f32[3,3,8,128]{3,2,1,0:T(8,128)S(1)} %get-tuple-element.47), channel_id=1, source_target_pairs={{0,1},{1,2},{2,3},{3,4},{4,5},{5,6},{6,7},{7,8},{8,9},{9,10},{10,1... | collective-permute-start | bytes 110600 | tf_op jit(solution)/shard_map/ppermute | solution.py:340
  44.8 4.6 %collective-permute-start.10 = (f32[3,3,8,128]{3,2,1,0:T(8,128)S(1)}, f32[3,3,8,128]{3,2,1,0:T(8,128)S(1)}, u32[]{:S(2)}, u32[]{:S(2)}) collective-permute-start(f32[3,3,8,128]{3,2,1,0:T(8,128)S(1)} %get-tuple-element.46.own.rest_5_), channel_id=1, source_target_pairs={{1,0},{2,1},{3,2},{4,3},{5,4},{6,5},{7,6},{8,7},{9,8},{10,9},{11,1... | collective-permute-start | bytes 110600 | tf_op jit(solution)/shard_map/ppermute | solution.py:339
  49.8 4.6 %collective-permute-start.13 = (f32[3,3,8,128]{3,2,1,0:T(8,128)S(1)}, f32[3,3,8,128]{3,2,1,0:T(8,128)S(1)}, u32[]{:S(2)}, u32[]{:S(2)}) collective-permute-start(f32[3,3,8,128]{3,2,1,0:T(8,128)S(1)} %get-tuple-element.49), channel_id=1, source_target_pairs={{0,1},{1,2},{2,3},{3,4},{4,5},{5,6},{6,7},{7,8},{8,9},{9,10},{10,1... | collective-permute-start | bytes 110600 | tf_op jit(solution)/shard_map/ppermute | solution.py:340
  49.9 4.6 %collective-permute-start.12 = (f32[3,3,8,128]{3,2,1,0:T(8,128)S(1)}, f32[3,3,8,128]{3,2,1,0:T(8,128)S(1)}, u32[]{:S(2)}, u32[]{:S(2)}) collective-permute-start(f32[3,3,8,128]{3,2,1,0:T(8,128)S(1)} %get-tuple-element.48.own.rest_7_), channel_id=1, source_target_pairs={{1,0},{2,1},{3,2},{4,3},{5,4},{6,5},{7,6},{8,7},{9,8},{10,9},{11,1... | collective-permute-start | bytes 110600 | tf_op jit(solution)/shard_map/ppermute | solution.py:339
  54.9 4.6 %collective-permute-start.15 = (f32[3,3,8,128]{3,2,1,0:T(8,128)S(1)}, f32[3,3,8,128]{3,2,1,0:T(8,128)S(1)}, u32[]{:S(2)}, u32[]{:S(2)}) collective-permute-start(f32[3,3,8,128]{3,2,1,0:T(8,128)S(1)} %get-tuple-element.51), channel_id=1, source_target_pairs={{0,1},{1,2},{2,3},{3,4},{4,5},{5,6},{6,7},{7,8},{8,9},{9,10},{10,1... | collective-permute-start | bytes 110600 | tf_op jit(solution)/shard_map/ppermute | solution.py:340
  54.9 4.6 %collective-permute-start.14 = (f32[3,3,8,128]{3,2,1,0:T(8,128)S(1)}, f32[3,3,8,128]{3,2,1,0:T(8,128)S(1)}, u32[]{:S(2)}, u32[]{:S(2)}) collective-permute-start(f32[3,3,8,128]{3,2,1,0:T(8,128)S(1)} %get-tuple-element.50.own.rest_9_), channel_id=1, source_target_pairs={{1,0},{2,1},{3,2},{4,3},{5,4},{6,5},{7,6},{8,7},{9,8},{10,9},{11,1... | collective-permute-start | bytes 110600 | tf_op jit(solution)/shard_map/ppermute | solution.py:339
  60.0 4.6 %collective-permute-start.17 = (f32[3,3,8,128]{3,2,1,0:T(8,128)S(1)}, f32[3,3,8,128]{3,2,1,0:T(8,128)S(1)}, u32[]{:S(2)}, u32[]{:S(2)}) collective-permute-start(f32[3,3,8,128]{3,2,1,0:T(8,128)S(1)} %get-tuple-element.53), channel_id=1, source_target_pairs={{0,1},{1,2},{2,3},{3,4},{4,5},{5,6},{6,7},{7,8},{8,9},{9,10},{10,1... | collective-permute-start | bytes 110600 | tf_op jit(solution)/shard_map/ppermute | solution.py:340
  60.0 4.6 %collective-permute-start.16 = (f32[3,3,8,128]{3,2,1,0:T(8,128)S(1)}, f32[3,3,8,128]{3,2,1,0:T(8,128)S(1)}, u32[]{:S(2)}, u32[]{:S(2)}) collective-permute-start(f32[3,3,8,128]{3,2,1,0:T(8,128)S(1)} %get-tuple-element.52.own.rest_11_), channel_id=1, source_target_pairs={{1,0},{2,1},{3,2},{4,3},{5,4},{6,5},{7,6},{8,7},{9,8},{10,9},{11,1... | collective-permute-start | bytes 110600 | tf_op jit(solution)/shard_map/ppermute | solution.py:339
  65.0 4.4 %collective-permute-start.19 = (f32[1,3,8,128]{3,2,1,0:T(8,128)S(1)}, f32[1,3,8,128]{3,2,1,0:T(8,128)S(1)}, u32[]{:S(2)}, u32[]{:S(2)}) collective-permute-start(f32[1,3,8,128]{3,2,1,0:T(8,128)S(1)} %get-tuple-element.54.above), channel_id=1, source_target_pairs={{0,1},{1,2},{2,3},{3,4},{4,5},{5,6},{6,7},{7,8},{8,9},{9,10},{10,1... | collective-permute-start | bytes 36872 | tf_op jit(solution)/shard_map/ppermute | solution.py:340
  65.1 4.4 %collective-permute-start.18 = (f32[1,3,8,128]{3,2,1,0:T(8,128)S(1)}, f32[1,3,8,128]{3,2,1,0:T(8,128)S(1)}, u32[]{:S(2)}, u32[]{:S(2)}) collective-permute-start(f32[1,3,8,128]{3,2,1,0:T(8,128)S(1)} %get-tuple-element.55.below), channel_id=1, source_target_pairs={{1,0},{2,1},{3,2},{4,3},{5,4},{6,5},{7,6},{8,7},{9,8},{10,9},{11,1... | collective-permute-start | bytes 36872 | tf_op jit(solution)/shard_map/ppermute | solution.py:339

commit v15 on v14

--- a/solution.py
+++ b/solution.py
@@ -118,9 +118,10 @@
     load = beside(own, sides)
     even = {x: [load(c, x, 0) for c in range(3)] for x in range(-2, 4)}
     odd = {x: [load(c, x, 1) for c in range(3)] for x in range(-2, 4)}
-    for k in range(5):
+    for k in (0, 1, 4):
         for c, value in enumerate(near_even(odd[k - 2], odd[k - 1])):
             near[0, k, c] = value
+    for k in (0, 3, 4):
         for c, value in enumerate(near_odd(even[k - 2], even[k - 1])):
             near[1, k, c] = value
     applied = [jnp.concatenate([field[c]] * layers.shape[3], axis=1) for c in range(3)]

time: 82.7 us -> 82.7 us (level)
  no operation moved by 1% of the time
where the time goes in v15:
time: 82.7 us; the launch traced here: 82.5 us
  starting transfers between devices  35.7 us (43%)
  blocking collectives  26.5 us (32%)
  waiting for transfers between devices  12.9 us (16%)
  Pallas kernels  6.2 us (7%)
  other arithmetic  0.99 us (1%)
    ppermute x10, starting transfers between devices, both_sides(): from_above = lax.ppermute(to_below, 'space', down)  35.6 us
    all_to_all x1, blocking collectives, per_device(): corr = lax.all_to_all(payload, 'tm', 0, 0, tiled=True)  14.5 us
    all_to_all x1, blocking collectives, per_device(): sent = lax.all_to_all(sent, 'tm', 0, 0, tiled=True)  12 us
    ppermute x10, waiting for transfers between devices, both_sides(): return (from_above, lax.ppermute(to_above, 'space', up))  11.2 us
    pallas_call x14, Pallas kernels, call(): pl.pallas_call(kernel, out_shape=[jax.ShapeDtypeStruct(s, F32) for s in s...  6.2 us
    ppermute x10, waiting for transfers between devices, both_sides(): from_above = lax.ppermute(to_below, 'space', down)  1.71 us
  transfers between devices with their start and end apart: 20, of which 12 were waited for; matrix products, arithmetic and copies ran while one was open for 1% of the time, Pallas kernels for 2%

profile of v15, /device:TPU:2, one launch (start us, length us, event | category | flops | bytes accessed | tf_op | source)
XLA Modules:
  0.0 82.5 jit_solution(16787968602212527166)
XLA Ops:
  0.0 8.9 %collective-permute-start = (f32[3,2,16,512]{3,2,1,0:T(8,128)}, f32[3,2,16,512]{3,2,1,0:T(8,128)S(1)}, u32[]{:S(2)}, u32[]{:S(2)}) collective-permute-start(f32[3,2,16,512]{3,2,1,0:T(8,128)} %bitcast.5), channel_id=1, source_target_pairs={{1,0},{2,1},{3,2},{4,3},{5,4},{6,5},{7,6},{8,7},{9,8},{10,9},{11,1... | collective-permute-start | bytes 589832 | tf_op jit(solution)/shard_map/ppermute | solution.py:340
  8.9 3.0 %collective-permute-start.2 = (f32[2,16,512]{2,1,0:T(8,128)}, f32[2,16,512]{2,1,0:T(8,128)S(1)}, u32[]{:S(2)}, u32[]{:S(2)}) collective-permute-start(f32[2,16,512]{2,1,0:T(8,128)} %param.4), channel_id=1, source_target_pairs={{1,0},{2,1},{3,2},{4,3},{5,4},{6,5},{7,6},{8,7},{9,8},{10,9},{11,1... | collective-permute-start | bytes 196616 | tf_op jit(solution)/shard_map/ppermute | solution.py:340
  11.9 1.0 %pad_maximum_fusion.slab = f32[4,2,16,512]{3,2,1,0:T(8,128)S(1)} fusion(f32[1,2,16,512]{3,2,1,0:T(8,128)} %bitcast.7, f32[3,2,16,512]{3,2,1,0:T(8,128)} %bitcast.6), kind=kLoop, calls=%fused_computation | loop fusion | flops 65536 | bytes 524288 | tf_op jit(solution)/shard_map/concatenate | solution.py:359
  12.9 0.6 shard_map.37
  14.1 0.9 %shard_map.39 = (f32[16,2,3,8,128]{4,3,2,1,0:T(8,128)S(1)}, f32[2,1,2,2,8,512]{5,4,3,2,1,0:T(8,128)S(1)}) custom-call(f32[4,2,2,8,512]{4,3,2,1,0:T(8,128)S(1)} %get-tuple-element.34.own, f32[2,3,2,2,8,512]{5,4,3,2,1,0:T(8,128)S(1)} %get-tuple-element.36.sides, f32[2,5,3,8,512]{4,3,2,1,0:T(8,128)S(1)} %get-tuple-element.37.near, ...), custom_call_target="tpu_custom_call" | custom-call | tf_op jit(solution)/shard_map/pallas_call | solution.py:345
  15.0 14.5 %all_to_all.10.corr.rest_2_ = f32[16,2,3,8,128]{4,3,2,1,0:T(8,128)S(1)} all-to-all(f32[16,2,3,8,128]{4,3,2,1,0:T(8,128)S(1)} %get-tuple-element.40), channel_id=1, replica_groups=mesh['tm'=16,'space'=32] {'tm'}, dimensions={0} | all-to-all | bytes 786432 | tf_op jit(solution)/shard_map/all_to_all | solution.py:382
  29.5 2.9 %collective-permute-start.4 = (f32[3,3,8,128]{3,2,1,0:T(8,128)S(1)}, f32[3,3,8,128]{3,2,1,0:T(8,128)S(1)}, u32[]{:S(2)}, u32[]{:S(2)}) collective-permute-start(f32[3,3,8,128]{3,2,1,0:T(8,128)S(1)} %slice.8.own), channel_id=1, source_target_pairs={{1,0},{2,1},{3,2},{4,3},{5,4},{6,5},{7,6},{8,7},{9,8},{10,9},{11,1... | collective-permute-start | bytes 110600 | tf_op jit(solution)/shard_map/ppermute | solution.py:340
  32.6 1.5 %collective-permute-done.4.right = f32[3,3,8,128]{3,2,1,0:T(8,128)S(1)} collective-permute-done((f32[3,3,8,128]{3,2,1,0:T(8,128)S(1)}, f32[3,3,8,128]{3,2,1,0:T(8,128)S(1)}, u32[]{:S(2)}, u32[]{:S(2)}) %collective-permute-start.4) | collective-permute-done | bytes 36896 | tf_op jit(solution)/shard_map/ppermute | solution.py:340
  34.7 2.9 %collective-permute-start.6 = (f32[3,3,8,128]{3,2,1,0:T(8,128)S(1)}, f32[3,3,8,128]{3,2,1,0:T(8,128)S(1)}, u32[]{:S(2)}, u32[]{:S(2)}) collective-permute-start(f32[3,3,8,128]{3,2,1,0:T(8,128)S(1)} %get-tuple-element.42.own.rest_1_), channel_id=1, source_target_pairs={{1,0},{2,1},{3,2},{4,3},{5,4},{6,5},{7,6},{8,7},{9,8},{10,9},{11,1... | collective-permute-start | bytes 110600 | tf_op jit(solution)/shard_map/ppermute | solution.py:340
  37.6 1.6 %collective-permute-done.7.left = f32[3,3,8,128]{3,2,1,0:T(8,128)S(1)} collective-permute-done((f32[3,3,8,128]{3,2,1,0:T(8,128)S(1)}, f32[3,3,8,128]{3,2,1,0:T(8,128)S(1)}, u32[]{:S(2)}, u32[]{:S(2)}) %collective-permute-start.7) | collective-permute-done | bytes 36896 | tf_op jit(solution)/shard_map/ppermute | solution.py:341
  39.7 3.0 %collective-permute-start.8 = (f32[3,3,8,128]{3,2,1,0:T(8,128)S(1)}, f32[3,3,8,128]{3,2,1,0:T(8,128)S(1)}, u32[]{:S(2)}, u32[]{:S(2)}) collective-permute-start(f32[3,3,8,128]{3,2,1,0:T(8,128)S(1)} %get-tuple-element.44.own.rest_3_), channel_id=1, source_target_pairs={{1,0},{2,1},{3,2},{4,3},{5,4},{6,5},{7,6},{8,7},{9,8},{10,9},{11,1... | collective-permute-start | bytes 110600 | tf_op jit(solution)/shard_map/ppermute | solution.py:340
  42.7 1.6 %collective-permute-done.9.left = f32[3,3,8,128]{3,2,1,0:T(8,128)S(1)} collective-permute-done((f32[3,3,8,128]{3,2,1,0:T(8,128)S(1)}, f32[3,3,8,128]{3,2,1,0:T(8,128)S(1)}, u32[]{:S(2)}, u32[]{:S(2)}) %collective-permute-start.9) | collective-permute-done | bytes 36896 | tf_op jit(solution)/shard_map/ppermute | solution.py:341
  44.8 3.0 %collective-permute-start.10 = (f32[3,3,8,128]{3,2,1,0:T(8,128)S(1)}, f32[3,3,8,128]{3,2,1,0:T(8,128)S(1)}, u32[]{:S(2)}, u32[]{:S(2)}) collective-permute-start(f32[3,3,8,128]{3,2,1,0:T(8,128)S(1)} %get-tuple-element.46.own.rest_5_), channel_id=1, source_target_pairs={{1,0},{2,1},{3,2},{4,3},{5,4},{6,5},{7,6},{8,7},{9,8},{10,9},{11,1... | collective-permute-start | bytes 110600 | tf_op jit(solution)/shard_map/ppermute | solution.py:340
  47.8 1.6 %collective-permute-done.11.left = f32[3,3,8,128]{3,2,1,0:T(8,128)S(1)} collective-permute-done((f32[3,3,8,128]{3,2,1,0:T(8,128)S(1)}, f32[3,3,8,128]{3,2,1,0:T(8,128)S(1)}, u32[]{:S(2)}, u32[]{:S(2)}) %collective-permute-start.11) | collective-permute-done | bytes 36896 | tf_op jit(solution)/shard_map/ppermute | solution.py:341
  49.9 3.0 %collective-permute-start.12 = (f32[3,3,8,128]{3,2,1,0:T(8,128)S(1)}, f32[3,3,8,128]{3,2,1,0:T(8,128)S(1)}, u32[]{:S(2)}, u32[]{:S(2)}) collective-permute-start(f32[3,3,8,128]{3,2,1,0:T(8,128)S(1)} %get-tuple-element.48.own.rest_7_), channel_id=1, source_target_pairs={{1,0},{2,1},{3,2},{4,3},{5,4},{6,5},{7,6},{8,7},{9,8},{10,9},{11,1... | collective-permute-start | bytes 110600 | tf_op jit(solution)/shard_map/ppermute | solution.py:340
  52.8 1.6 %collective-permute-done.13.left = f32[3,3,8,128]{3,2,1,0:T(8,128)S(1)} collective-permute-done((f32[3,3,8,128]{3,2,1,0:T(8,128)S(1)}, f32[3,3,8,128]{3,2,1,0:T(8,128)S(1)}, u32[]{:S(2)}, u32[]{:S(2)}) %collective-permute-start.13) | collective-permute-done | bytes 36896 | tf_op jit(solution)/shard_map/ppermute | solution.py:341
  54.9 3.0 %collective-permute-start.14 = (f32[3,3,8,128]{3,2,1,0:T(8,128)S(1)}, f32[3,3,8,128]{3,2,1,0:T(8,128)S(1)}, u32[]{:S(2)}, u32[]{:S(2)}) collective-permute-start(f32[3,3,8,128]{3,2,1,0:T(8,128)S(1)} %get-tuple-element.50.own.rest_9_), channel_id=1, source_target_pairs={{1,0},{2,1},{3,2},{4,3},{5,4},{6,5},{7,6},{8,7},{9,8},{10,9},{11,1... | collective-permute-start | bytes 110600 | tf_op jit(solution)/shard_map/ppermute | solution.py:340
  57.9 1.6 %collective-permute-done.15.left = f32[3,3,8,128]{3,2,1,0:T(8,128)S(1)} collective-permute-done((f32[3,3,8,128]{3,2,1,0:T(8,128)S(1)}, f32[3,3,8,128]{3,2,1,0:T(8,128)S(1)}, u32[]{:S(2)}, u32[]{:S(2)}) %collective-permute-start.15) | collective-permute-done | bytes 36896 | tf_op jit(solution)/shard_map/ppermute | solution.py:341
  60.0 3.0 %collective-permute-start.16 = (f32[3,3,8,128]{3,2,1,0:T(8,128)S(1)}, f32[3,3,8,128]{3,2,1,0:T(8,128)S(1)}, u32[]{:S(2)}, u32[]{:S(2)}) collective-permute-start(f32[3,3,8,128]{3,2,1,0:T(8,128)S(1)} %get-tuple-element.52.own.rest_11_), channel_id=1, source_target_pairs={{1,0},{2,1},{3,2},{4,3},{5,4},{6,5},{7,6},{8,7},{9,8},{10,9},{11,1... | collective-permute-start | bytes 110600 | tf_op jit(solution)/shard_map/ppermute | solution.py:340
  63.0 1.6 %collective-permute-done.17.left = f32[3,3,8,128]{3,2,1,0:T(8,128)S(1)} collective-permute-done((f32[3,3,8,128]{3,2,1,0:T(8,128)S(1)}, f32[3,3,8,128]{3,2,1,0:T(8,128)S(1)}, u32[]{:S(2)}, u32[]{:S(2)}) %collective-permute-start.17) | collective-permute-done | bytes 36896 | tf_op jit(solution)/shard_map/ppermute | solution.py:341
  65.1 3.0 %collective-permute-start.18 = (f32[1,3,8,128]{3,2,1,0:T(8,128)S(1)}, f32[1,3,8,128]{3,2,1,0:T(8,128)S(1)}, u32[]{:S(2)}, u32[]{:S(2)}) collective-permute-start(f32[1,3,8,128]{3,2,1,0:T(8,128)S(1)} %get-tuple-element.55.below), channel_id=1, source_target_pairs={{1,0},{2,1},{3,2},{4,3},{5,4},{6,5},{7,6},{8,7},{9,8},{10,9},{11,1... | collective-permute-start | bytes 36872 | tf_op jit(solution)/shard_map/ppermute | solution.py:340
  68.2 1.2 %collective-permute-done.19.rest_1_ = f32[1,3,8,128]{3,2,1,0:T(8,128)S(1)} collective-permute-done((f32[1,3,8,128]{3,2,1,0:T(8,128)S(1)}, f32[1,3,8,128]{3,2,1,0:T(8,128)S(1)}, u32[]{:S(2)}, u32[]{:S(2)}) %collective-permute-start.19) | collective-permute-done | bytes 12320 | tf_op jit(solution)/shard_map/ppermute | solution.py:341
  69.7 12.0 %all_to_all.11.sent = f32[16,3,8,128]{3,2,1,0:T(8,128)S(1)} all-to-all(f32[16,3,8,128]{3,2,1,0:T(8,128)S(1)} %shard_map.49), channel_id=1, replica_groups=mesh['tm'=16,'space'=32] {'tm'}, dimensions={0} | all-to-all | bytes 393216 | tf_op jit(solution)/shard_map/all_to_all | solution.py:398
  81.7 0.8 shard_map.50
  (37 shorter events, 4.5 us)
Async XLA Ops:
  0.0 13.5 %collective-permute-start.1 = (f32[3,2,16,512]{3,2,1,0:T(8,128)}, f32[3,2,16,512]{3,2,1,0:T(8,128)S(1)}, u32[]{:S(2)}, u32[]{:S(2)}) collective-permute-start(f32[3,2,16,512]{3,2,1,0:T(8,128)} %bitcast.4), channel_id=1, source_target_pairs={{0,1},{1,2},{2,3},{3,4},{4,5},{5,6},{6,7},{7,8},{8,9},{9,10},{10,1... | collective-permute-start | bytes 589832 | tf_op jit(solution)/shard_map/ppermute | solution.py:341
  0.0 13.5 %collective-permute-start = (f32[3,2,16,512]{3,2,1,0:T(8,128)}, f32[3,2,16,512]{3,2,1,0:T(8,128)S(1)}, u32[]{:S(2)}, u32[]{:S(2)}) collective-permute-start(f32[3,2,16,512]{3,2,1,0:T(8,128)} %bitcast.5), channel_id=1, source_target_pairs={{1,0},{2,1},{3,2},{4,3},{5,4},{6,5},{7,6},{8,7},{9,8},{10,9},{11,1... | collective-permute-start | bytes 589832 | tf_op jit(solution)/shard_map/ppermute | solution.py:340
  8.9 5.1 %collective-permute-start.3 = (f32[2,16,512]{2,1,0:T(8,128)}, f32[2,16,512]{2,1,0:T(8,128)S(1)}, u32[]{:S(2)}, u32[]{:S(2)}) collective-permute-start(f32[2,16,512]{2,1,0:T(8,128)} %param.4), channel_id=1, source_target_pairs={{0,1},{1,2},{2,3},{3,4},{4,5},{5,6},{6,7},{7,8},{8,9},{9,10},{10,1... | collective-permute-start | bytes 196616 | tf_op jit(solution)/shard_map/ppermute | solution.py:341
  8.9 5.2 %collective-permute-start.2 = (f32[2,16,512]{2,1,0:T(8,128)}, f32[2,16,512]{2,1,0:T(8,128)S(1)}, u32[]{:S(2)}, u32[]{:S(2)}) collective-permute-start(f32[2,16,512]{2,1,0:T(8,128)} %param.4), channel_id=1, source_target_pairs={{1,0},{2,1},{3,2},{4,3},{5,4},{6,5},{7,6},{8,7},{9,8},{10,9},{11,1... | collective-permute-start | bytes 196616 | tf_op jit(solution)/shard_map/ppermute | solution.py:340
  11.9 1.0 %copy-start = (f32[3]{0:T(128)S(1)}, f32[3]{0:T(128)}, u32[]{:S(2)}) copy-start(f32[3]{0:T(128)} %applied.1) | copy-start | bytes 40
  29.5 4.7 %collective-permute-start.5 = (f32[2,2,3,8,128]{4,3,2,1,0:T(8,128)S(1)}, f32[2,2,3,8,128]{4,3,2,1,0:T(8,128)S(1)}, u32[]{:S(2)}, u32[]{:S(2)}) collective-permute-start(f32[2,2,3,8,128]{4,3,2,1,0:T(8,128)S(1)} %slice.9), channel_id=1, source_target_pairs={{0,1},{1,2},{2,3},{3,4},{4,5},{5,6},{6,7},{7,8},{8,9},{9,10},{10,1... | collective-permute-start | bytes 147464 | tf_op jit(solution)/shard_map/ppermute | solution.py:341
  29.5 4.6 %collective-permute-start.4 = (f32[3,3,8,128]{3,2,1,0:T(8,128)S(1)}, f32[3,3,8,128]{3,2,1,0:T(8,128)S(1)}, u32[]{:S(2)}, u32[]{:S(2)}) collective-permute-start(f32[3,3,8,128]{3,2,1,0:T(8,128)S(1)} %slice.8.own), channel_id=1, source_target_pairs={{1,0},{2,1},{3,2},{4,3},{5,4},{6,5},{7,6},{8,7},{9,8},{10,9},{11,1... | collective-permute-start | bytes 110600 | tf_op jit(solution)/shard_map/ppermute | solution.py:340
  34.7 4.6 %collective-permute-start.7 = (f32[3,3,8,128]{3,2,1,0:T(8,128)S(1)}, f32[3,3,8,128]{3,2,1,0:T(8,128)S(1)}, u32[]{:S(2)}, u32[]{:S(2)}) collective-permute-start(f32[3,3,8,128]{3,2,1,0:T(8,128)S(1)} %get-tuple-element.43), channel_id=1, source_target_pairs={{0,1},{1,2},{2,3},{3,4},{4,5},{5,6},{6,7},{7,8},{8,9},{9,10},{10,1... | collective-permute-start | bytes 110600 | tf_op jit(solution)/shard_map/ppermute | solution.py:341
  34.7 4.6 %collective-permute-start.6 = (f32[3,3,8,128]{3,2,1,0:T(8,128)S(1)}, f32[3,3,8,128]{3,2,1,0:T(8,128)S(1)}, u32[]{:S(2)}, u32[]{:S(2)}) collective-permute-start(f32[3,3,8,128]{3,2,1,0:T(8,128)S(1)} %get-tuple-element.42.own.rest_1_), channel_id=1, source_target_pairs={{1,0},{2,1},{3,2},{4,3},{5,4},{6,5},{7,6},{8,7},{9,8},{10,9},{11,1... | collective-permute-start | bytes 110600 | tf_op jit(solution)/shard_map/ppermute | solution.py:340
  39.7 4.6 %collective-permute-start.9 = (f32[3,3,8,128]{3,2,1,0:T(8,128)S(1)}, f32[3,3,8,128]{3,2,1,0:T(8,128)S(1)}, u32[]{:S(2)}, u32[]{:S(2)}) collective-permute-start(f32[3,3,8,128]{3,2,1,0:T(8,128)S(1)} %get-tuple-element.45), channel_id=1, source_target_pairs={{0,1},{1,2},{2,3},{3,4},{4,5},{5,6},{6,7},{7,8},{8,9},{9,10},{10,1... | collective-permute-start | bytes 110600 | tf_op jit(solution)/shard_map/ppermute | solution.py:341
  39.7 4.6 %collective-permute-start.8 = (f32[3,3,8,128]{3,2,1,0:T(8,128)S(1)}, f32[3,3,8,128]{3,2,1,0:T(8,128)S(1)}, u32[]{:S(2)}, u32[]{:S(2)}) collective-permute-start(f32[3,3,8,128]{3,2,1,0:T(8,128)S(1)} %get-tuple-element.44.own.rest_3_), channel_id=1, source_target_pairs={{1,0},{2,1},{3,2},{4,3},{5,4},{6,5},{7,6},{8,7},{9,8},{10,9},{11,1... | collective-permute-start | bytes 110600 | tf_op jit(solution)/shard_map/ppermute | solution.py:340
  44.8 4.6 %collective-permute-start.11 = (f32[3,3,8,128]{3,2,1,0:T(8,128)S(1)}, f32[3,3,8,128]{3,2,1,0:T(8,128)S(1)}, u32[]{:S(2)}, u32[]{:S(2)}) collective-permute-start(f32[3,3,8,128]{3,2,1,0:T(8,128)S(1)} %get-tuple-element.47), channel_id=1, source_target_pairs={{0,1},{1,2},{2,3},{3,4},{4,5},{5,6},{6,7},{7,8},{8,9},{9,10},{10,1... | collective-permute-start | bytes 110600 | tf_op jit(solution)/shard_map/ppermute | solution.py:341
  44.8 4.6 %collective-permute-start.10 = (f32[3,3,8,128]{3,2,1,0:T(8,128)S(1)}, f32[3,3,8,128]{3,2,1,0:T(8,128)S(1)}, u32[]{:S(2)}, u32[]{:S(2)}) collective-permute-start(f32[3,3,8,128]{3,2,1,0:T(8,128)S(1)} %get-tuple-element.46.own.rest_5_), channel_id=1, source_target_pairs={{1,0},{2,1},{3,2},{4,3},{5,4},{6,5},{7,6},{8,7},{9,8},{10,9},{11,1... | collective-permute-start | bytes 110600 | tf_op jit(solution)/shard_map/ppermute | solution.py:340
  49.8 4.6 %collective-permute-start.13 = (f32[3,3,8,128]{3,2,1,0:T(8,128)S(1)}, f32[3,3,8,128]{3,2,1,0:T(8,128)S(1)}, u32[]{:S(2)}, u32[]{:S(2)}) collective-permute-start(f32[3,3,8,128]{3,2,1,0:T(8,128)S(1)} %get-tuple-element.49), channel_id=1, source_target_pairs={{0,1},{1,2},{2,3},{3,4},{4,5},{5,6},{6,7},{7,8},{8,9},{9,10},{10,1... | collective-permute-start | bytes 110600 | tf_op jit(solution)/shard_map/ppermute | solution.py:341
  49.9 4.6 %collective-permute-start.12 = (f32[3,3,8,128]{3,2,1,0:T(8,128)S(1)}, f32[3,3,8,128]{3,2,1,0:T(8,128)S(1)}, u32[]{:S(2)}, u32[]{:S(2)}) collective-permute-start(f32[3,3,8,128]{3,2,1,0:T(8,128)S(1)} %get-tuple-element.48.own.rest_7_), channel_id=1, source_target_pairs={{1,0},{2,1},{3,2},{4,3},{5,4},{6,5},{7,6},{8,7},{9,8},{10,9},{11,1... | collective-permute-start | bytes 110600 | tf_op jit(solution)/shard_map/ppermute | solution.py:340
  54.9 4.6 %collective-permute-start.15 = (f32[3,3,8,128]{3,2,1,0:T(8,128)S(1)}, f32[3,3,8,128]{3,2,1,0:T(8,128)S(1)}, u32[]{:S(2)}, u32[]{:S(2)}) collective-permute-start(f32[3,3,8,128]{3,2,1,0:T(8,128)S(1)} %get-tuple-element.51), channel_id=1, source_target_pairs={{0,1},{1,2},{2,3},{3,4},{4,5},{5,6},{6,7},{7,8},{8,9},{9,10},{10,1... | collective-permute-start | bytes 110600 | tf_op jit(solution)/shard_map/ppermute | solution.py:341
  54.9 4.6 %collective-permute-start.14 = (f32[3,3,8,128]{3,2,1,0:T(8,128)S(1)}, f32[3,3,8,128]{3,2,1,0:T(8,128)S(1)}, u32[]{:S(2)}, u32[]{:S(2)}) collective-permute-start(f32[3,3,8,128]{3,2,1,0:T(8,128)S(1)} %get-tuple-element.50.own.rest_9_), channel_id=1, source_target_pairs={{1,0},{2,1},{3,2},{4,3},{5,4},{6,5},{7,6},{8,7},{9,8},{10,9},{11,1... | collective-permute-start | bytes 110600 | tf_op jit(solution)/shard_map/ppermute | solution.py:340
  60.0 4.6 %collective-permute-start.17 = (f32[3,3,8,128]{3,2,1,0:T(8,128)S(1)}, f32[3,3,8,128]{3,2,1,0:T(8,128)S(1)}, u32[]{:S(2)}, u32[]{:S(2)}) collective-permute-start(f32[3,3,8,128]{3,2,1,0:T(8,128)S(1)} %get-tuple-element.53), channel_id=1, source_target_pairs={{0,1},{1,2},{2,3},{3,4},{4,5},{5,6},{6,7},{7,8},{8,9},{9,10},{10,1... | collective-permute-start | bytes 110600 | tf_op jit(solution)/shard_map/ppermute | solution.py:341
  60.0 4.6 %collective-permute-start.16 = (f32[3,3,8,128]{3,2,1,0:T(8,128)S(1)}, f32[3,3,8,128]{3,2,1,0:T(8,128)S(1)}, u32[]{:S(2)}, u32[]{:S(2)}) collective-permute-start(f32[3,3,8,128]{3,2,1,0:T(8,128)S(1)} %get-tuple-element.52.own.rest_11_), channel_id=1, source_target_pairs={{1,0},{2,1},{3,2},{4,3},{5,4},{6,5},{7,6},{8,7},{9,8},{10,9},{11,1... | collective-permute-start | bytes 110600 | tf_op jit(solution)/shard_map/ppermute | solution.py:340
  65.0 4.4 %collective-permute-start.19 = (f32[1,3,8,128]{3,2,1,0:T(8,128)S(1)}, f32[1,3,8,128]{3,2,1,0:T(8,128)S(1)}, u32[]{:S(2)}, u32[]{:S(2)}) collective-permute-start(f32[1,3,8,128]{3,2,1,0:T(8,128)S(1)} %get-tuple-element.54.above), channel_id=1, source_target_pairs={{0,1},{1,2},{2,3},{3,4},{4,5},{5,6},{6,7},{7,8},{8,9},{9,10},{10,1... | collective-permute-start | bytes 36872 | tf_op jit(solution)/shard_map/ppermute | solution.py:341
  65.1 4.4 %collective-permute-start.18 = (f32[1,3,8,128]{3,2,1,0:T(8,128)S(1)}, f32[1,3,8,128]{3,2,1,0:T(8,128)S(1)}, u32[]{:S(2)}, u32[]{:S(2)}) collective-permute-start(f32[1,3,8,128]{3,2,1,0:T(8,128)S(1)} %get-tuple-element.55.below), channel_id=1, source_target_pairs={{1,0},{2,1},{3,2},{4,3},{5,4},{6,5},{7,6},{8,7},{9,8},{10,9},{11,1... | collective-permute-start | bytes 36872 | tf_op jit(solution)/shard_map/ppermute | solution.py:340
